TPU v7x, 32 devices: a whole 2x2x4 slice. The times are simulated.
32 devices in a mesh: dp: 16 (over z, y, core), tensor: 2 (over x).
Axes of the slice: x: 2, y: 2, z: 4, core: 2. Of those that a mesh axis runs over, the one named last changes fastest.
Arguments:
- tokens: bfloat16 [8192, 768], P('dp'), may hold values from -6 to 6
- seg_ids: int32 [8192], P('dp'), may hold values from 0 to 2, as said below
- positions: int32 [8192], P('dp'), may hold values from 0 to 382, as said below
- gain_attn: bfloat16 [768], P('dp'), may hold values from 0.25 to 1.75
- w_qkv: bfloat16 [768, 3, 768], P('dp', None, 'tensor'), may hold values from -0.21875 to 0.21875
- w_attn_out: bfloat16 [768, 768], P('tensor', 'dp'), may hold values from -1.75 to 1.75
- gain_mlp: bfloat16 [768], P('dp'), may hold values from 0.25 to 1.75
- w_in: bfloat16 [768, 2, 1152], P('dp', None, 'tensor'), may hold values from -0.21875 to 0.21875
- w_mlp_out: bfloat16 [1152, 768], P('tensor', 'dp'), may hold values from -0.375 to 0.375
- cotangent: bfloat16 [8192, 768], P('dp'), may hold values from -8 to 8
Outputs:
- output: bfloat16 [8192, 768], P('dp')
- grad_input: float32 [8192, 768], P('dp')
- grad_gain_attn: float32 [768], P('dp')
- grad_qkv: float32 [768, 3, 768], P('dp', None, 'tensor')
- grad_attn_out: float32 [768, 768], P('tensor', 'dp')
- grad_gain_mlp: float32 [768], P('dp')
- grad_in: float32 [768, 2, 1152], P('dp', None, 'tensor')
- grad_mlp_out: float32 [1152, 768], P('tensor', 'dp')
Inputs may be any that keep to these rules, and one draw needn't show every extreme that they name: `seg_ids`: within each aligned run of 512 tokens (one sequence) the ids never fall and take each of 0, 1 and 2 once as a run; the document numbered 1 contains the tokens 512 / 2 - 1 and 256 of its sequence. `positions`: 0 at the first token of each sequence and wherever seg_ids changes, else one more than at the token before; some document is 383 tokens long, and none is longer.
All inputs are finite; a program needn't handle non-finite values.
Results may differ from a plain program's by a relative error of at most 0.019.
Values may be sent and summed in bfloat16 or wider, within the bound.
No kernel may reach another device: no remote copies, remote signals or barrier semaphores. Data moves between devices by JAX's collectives and lax.ppermute only.
A program may use at most 128 MiB of HBM per device.

v0:
```python
import jax
import jax.numpy as jnp
from jax import lax
from jax.sharding import PartitionSpec as P

HD = 64
HALF = 64


EPSILON = 1e-05
THETA = 10000.0
MASKED = -1e30


def normalize(values):
    average = jnp.mean(values, axis=-1, keepdims=True)
    centered = values - average
    variance = jnp.mean(centered * centered, axis=-1, keepdims=True)
    inverse = lax.rsqrt(variance + EPSILON)
    return (centered * inverse, inverse)


def norm_back(upstream, normed, inverse, gain):
    scaled = upstream * gain
    first = jnp.mean(scaled, axis=-1, keepdims=True)
    second = jnp.mean(scaled * normed, axis=-1, keepdims=True)
    return (inverse * (scaled - first - normed * second), jnp.sum(upstream * normed, axis=0))


def rope_tables(positions, size):
    frequency = THETA ** (-jnp.arange(0, size, 2).astype(jnp.float32) / size)
    angle = positions.astype(jnp.float32)[:, None] * frequency[None, :]
    angle = jnp.concatenate([angle, angle], axis=-1)
    return (jnp.cos(angle)[:, None, :], jnp.sin(angle)[:, None, :])


def rotate_half(values):
    middle = values.shape[-1] // 2
    return jnp.concatenate([-values[..., middle:], values[..., :middle]], axis=-1)


def rotate(values, cosine, sine):
    return values * cosine + rotate_half(values) * sine


def rotate_back(values, cosine, sine):
    return values * cosine - rotate_half(values * sine)


def gated(active, factor):
    return jax.nn.gelu(active, approximate=False) * factor


def per_device(
    tokens, seg_ids, positions, gain_attn, w_qkv, w_attn_out, gain_mlp, w_in, w_mlp_out, cotangent
):
    count = tokens.shape[0]
    width = tokens.shape[1]
    inner = w_qkv.shape[2]
    heads_here = inner // HD
    hidden = w_in.shape[2]
    gain_one, whole_qkv, whole_out, gain_two, whole_in, whole_down = (
        lax.all_gather(gain_attn, "dp", axis=0, tiled=True),
        lax.all_gather(w_qkv, "dp", axis=0, tiled=True),
        lax.all_gather(w_attn_out, "dp", axis=1, tiled=True),
        lax.all_gather(gain_mlp, "dp", axis=0, tiled=True),
        lax.all_gather(w_in, "dp", axis=0, tiled=True),
        lax.all_gather(w_mlp_out, "dp", axis=1, tiled=True),
    )
    inputs = tokens.astype(jnp.float32)
    normed_one, inverse_one = normalize(inputs)
    gain_one = gain_one.astype(jnp.float32)
    lowered_one = (normed_one * gain_one).astype(jnp.bfloat16)
    matrix_qkv = whole_qkv.reshape(width, 3 * inner)
    projected = jnp.dot(lowered_one, matrix_qkv, preferred_element_type=jnp.float32)
    projected = projected.reshape(count, 3, heads_here, HD)
    cosine, sine = rope_tables(positions, HD)
    query = rotate(projected[:, 0], cosine, sine).astype(jnp.bfloat16)
    keys = rotate(projected[:, 1], cosine, sine).astype(jnp.bfloat16)
    values = projected[:, 2].astype(jnp.bfloat16)
    wide_keys = jnp.pad(keys, ((HALF, HALF), (0, 0), (0, 0)))
    wide_values = jnp.pad(values, ((HALF, HALF), (0, 0), (0, 0)))
    wide_segments = jnp.pad(seg_ids, (HALF, HALF), constant_values=-1)
    block = min(512, count)
    span = block + 2 * HALF
    scale = HD ** (-0.5)
    offsets = jnp.arange(span)[None, :] - HALF - jnp.arange(block)[:, None]
    near = jnp.abs(offsets) <= HALF

    def scores_of():
        allowed = near & (seg_ids[:, None] == wide_segments[None, :])
        scores = (
            jnp.einsum("qhd,khd->hqk", query, wide_keys, preferred_element_type=jnp.float32) * scale
        )
        return (jnp.where(allowed[None], scores, MASKED), allowed)

    start = 0
    scores, allowed = scores_of()
    peak = jnp.max(scores, axis=-1, keepdims=True)
    powers = jnp.exp(scores - peak)
    total = jnp.sum(powers, axis=-1, keepdims=True)
    shares = (powers / total).astype(jnp.bfloat16)
    log_sums = [peak + jnp.log(total)]
    contexts = jnp.einsum("hqk,khd->qhd", shares, wide_values, preferred_element_type=jnp.float32)
    context = contexts.astype(jnp.bfloat16).reshape(count, inner)
    attn_part = jnp.dot(context, whole_out, preferred_element_type=jnp.float32)
    middle = inputs + lax.psum(attn_part.astype(jnp.bfloat16), "tensor").astype(jnp.float32)
    normed_two, inverse_two = normalize(middle)
    gain_two = gain_two.astype(jnp.float32)
    lowered_two = (normed_two * gain_two).astype(jnp.bfloat16)
    matrix_in = whole_in.reshape(width, 2 * hidden)
    gates = jnp.dot(lowered_two, matrix_in, preferred_element_type=jnp.float32).reshape(
        count, 2, hidden
    )
    active = gates[:, 0]
    factor = gates[:, 1]
    mixed = gated(active, factor).astype(jnp.bfloat16)
    mlp_part = jnp.dot(mixed, whole_down, preferred_element_type=jnp.float32)
    output = (
        middle + lax.psum(mlp_part.astype(jnp.bfloat16), "tensor").astype(jnp.float32)
    ).astype(jnp.bfloat16)
    grad_down = jnp.dot(mixed.T, cotangent, preferred_element_type=jnp.float32)
    grad_mixed = jnp.dot(cotangent, whole_down.T, preferred_element_type=jnp.float32)
    unused, pull = jax.vjp(gated, active, factor)
    grad_active, grad_factor = pull(grad_mixed)
    grad_gates = (
        jnp.stack([grad_active, grad_factor], axis=1)
        .astype(jnp.bfloat16)
        .reshape(count, 2 * hidden)
    )
    grad_in = jnp.dot(lowered_two.T, grad_gates, preferred_element_type=jnp.float32).reshape(
        width, 2, hidden
    )
    partial_two = jnp.dot(grad_gates, matrix_in.T, preferred_element_type=jnp.float32)
    grad_lowered_two = lax.psum(partial_two.astype(jnp.bfloat16), "tensor").astype(jnp.float32)
    grad_norm_two, grad_gain_two = norm_back(grad_lowered_two, normed_two, inverse_two, gain_two)
    grad_middle = cotangent.astype(jnp.float32) + grad_norm_two
    grad_branch = grad_middle.astype(jnp.bfloat16)
    grad_out = jnp.dot(context.T, grad_branch, preferred_element_type=jnp.float32)
    grad_context = jnp.dot(grad_branch, whole_out.T, preferred_element_type=jnp.float32)
    grad_context = grad_context.astype(jnp.bfloat16).reshape(count, heads_here, HD)
    query_grads = []
    grad_keys = jnp.zeros((count + 2 * HALF, heads_here, HD), jnp.float32)
    grad_values = jnp.zeros((count + 2 * HALF, heads_here, HD), jnp.float32)
    for number, start in enumerate(range(0, count, block)):
        scores, allowed = scores_of()
        shares = jnp.where(allowed[None], jnp.exp(scores - log_sums[number]), 0.0)
        grad_shares = jnp.einsum(
            "qhd,khd->hqk", grad_context, wide_values, preferred_element_type=jnp.float32
        )
        grad_values = grad_values.at[start : start + span].add(
            jnp.einsum(
                "hqk,qhd->khd",
                shares.astype(jnp.bfloat16),
                grad_context,
                preferred_element_type=jnp.float32,
            )
        )
        row_sums = jnp.sum(shares * grad_shares, axis=-1, keepdims=True)
        grad_scores = (shares * (grad_shares - row_sums)).astype(jnp.bfloat16)
        query_grads.append(
            jnp.einsum("hqk,khd->qhd", grad_scores, wide_keys, preferred_element_type=jnp.float32)
            * scale
        )
        grad_keys = grad_keys.at[start : start + span].add(
            jnp.einsum("hqk,qhd->khd", grad_scores, query, preferred_element_type=jnp.float32)
            * scale
        )
    grad_query = rotate_back(query_grads[0], cosine, sine)
    grad_key_pre = rotate_back(grad_keys[HALF : HALF + count], cosine, sine)
    grad_projected = (
        jnp.stack(
            [
                grad_query.reshape(count, inner),
                grad_key_pre.reshape(count, inner),
                grad_values[HALF : HALF + count].reshape(count, inner),
            ],
            axis=1,
        )
        .astype(jnp.bfloat16)
        .reshape(count, 3 * inner)
    )
    grad_qkv = jnp.dot(lowered_one.T, grad_projected, preferred_element_type=jnp.float32).reshape(
        width, 3, inner
    )
    partial_one = jnp.dot(grad_projected, matrix_qkv.T, preferred_element_type=jnp.float32)
    grad_lowered_one = lax.psum(partial_one.astype(jnp.bfloat16), "tensor").astype(jnp.float32)
    grad_norm_one, grad_gain_one = norm_back(grad_lowered_one, normed_one, inverse_one, gain_one)
    grad_input = grad_middle + grad_norm_one
    sum_one, sum_qkv, sum_out, sum_two, sum_in, sum_down = (
        lax.psum_scatter(grad_gain_one, "dp", scatter_dimension=0, tiled=True),
        lax.psum_scatter(grad_qkv, "dp", scatter_dimension=0, tiled=True),
        lax.psum_scatter(grad_out, "dp", scatter_dimension=1, tiled=True),
        lax.psum_scatter(grad_gain_two, "dp", scatter_dimension=0, tiled=True),
        lax.psum_scatter(grad_in, "dp", scatter_dimension=0, tiled=True),
        lax.psum_scatter(grad_down, "dp", scatter_dimension=1, tiled=True),
    )
    return (output, grad_input, sum_one, sum_qkv, sum_out, sum_two, sum_in, sum_down)


def solution(mesh):
    return jax.shard_map(
        per_device,
        mesh=mesh,
        in_specs=(
            P("dp", None),
            P("dp"),
            P("dp"),
            P("dp"),
            P("dp", None, "tensor"),
            P("tensor", "dp"),
            P("dp"),
            P("dp", None, "tensor"),
            P("tensor", "dp"),
            P("dp", None),
        ),
        out_specs=(
            P("dp", None),
            P("dp", None),
            P("dp"),
            P("dp", None, "tensor"),
            P("tensor", "dp"),
            P("dp"),
            P("dp", None, "tensor"),
            P("tensor", "dp"),
        ),
        check_vma=False,
    )
```

profile of v0, /device:TPU:0, one launch (start us, length us, event | category | flops | bytes accessed | tf_op | source)
XLA Modules:
  0.0 546.2 jit_solution(16271605312771953245)
XLA Ops:
  7.3 0.7 all-gather.3.cloned.1.call-update
  8.0 1.6 copy.36
  9.7 0.7 convert_element_type.110
  10.4 1.3 convert_reduce_fusion
  12.1 0.6 fusion.96
  13.8 35.3 %all-reduce.8 = (bf16[768]{0:T(1024)(128)(2,1)S(1)}, bf16[768]{0:T(1024)(128)(2,1)S(1)}) all-reduce(bf16[768]{0:T(1024)(128)(2,1)S(1)} %dynamic-update-slice.5, bf16[768]{0:T(1024)(128)(2,1)S(1)} %dynamic-update-slice.4), channel_id=1, replica_groups=mesh['dp'=16,'tensor'=2] {'dp'}, use_global_device_ids=true, to_apply=%add.4 | all-reduce | flops 1536 | bytes 6144
  49.2 1.0 broadcast_multiply_fusion.2
  50.2 19.0 %all_gather.20 = bf16[384,768]{0,1:T(8,128)(2,1)S(1)} all-gather(bf16[384,48]{0,1:T(8,128)(2,1)S(1)} %copy-done.35), channel_id=1, replica_groups=mesh['dp'=16,'tensor'=2] {'dp'}, dimensions={1}, use_global_device_ids=true | all-gather | bytes 626688 | tf_op jit(solution)/shard_map/all_gather | solution.py:65
  69.8 3.8 copy.35
  73.6 2.7 fusion.65
  76.7 0.9 copy-done.27
  78.1 2.0 fusion.1
  80.1 2.0 fusion
  82.1 1.1 copy-done
  83.2 2.7 fusion.35
  85.9 1.5 convolution_convert_fusion.1
  87.5 23.0 %all_gather.23 = bf16[576,768]{0,1:T(8,128)(2,1)S(1)} all-gather(bf16[576,48]{0,1:T(8,128)(2,1)S(1)} %copy-done.34), channel_id=1, replica_groups=mesh['dp'=16,'tensor'=2] {'dp'}, dimensions={1}, use_global_device_ids=true | all-gather | bytes 940032 | tf_op jit(solution)/shard_map/all_gather | solution.py:68
  110.5 1.0 copy-done.11
  111.5 0.7 fusion.97
  112.2 4.0 copy.37
  116.2 16.4 %all-reduce.14.cloned.1.call-done = bf16[512,768]{1,0:T(8,128)(2,1)} async-done(((bf16[512,768]{1,0:T(8,128)(2,1)}), bf16[512,768]{1,0:T(8,128)(2,1)}) %all-reduce.14.cloned.1.call-update) | async-done | bytes 786448 | tf_op jit(solution)/shard_map/psum | solution.py:107
  132.6 1.6 fusion.34
  134.6 1.3 fusion.15
  135.9 2.8 fusion.47
  140.0 0.7 copy-done.29
  141.2 2.1 bitcast_convert_fusion.1
  143.7 2.1 multiply_convert_fusion.2
  145.8 0.8 copy-done.18
  146.6 1.7 convolution_convert_fusion
  148.4 29.5 %all-reduce.16.cloned.1.call-done = bf16[512,768]{1,0:T(8,128)(2,1)} async-done(((bf16[512,768]{1,0:T(8,128)(2,1)}), bf16[512,768]{1,0:T(8,128)(2,1)}) %all-reduce.16.cloned.1.call-update) | async-done | bytes 786448 | tf_op jit(solution)/shard_map/psum | solution.py:135
  177.9 2.7 fusion.26
  180.6 0.8 fusion.24
  182.2 5.0 fusion.29
  187.4 5.6 %multiply_reduce_fusion = (f32[6,512]{1,0:T(8,128)S(1)}, f32[6,512,640]{2,1,0:T(8,128)}) fusion(f32[6,512]{1,0:T(8,128)S(1)} %log_add_fusion, f32[6,512,640]{2,1,0:T(8,128)S(1)} %bitcast.173, pred[512,640]{1,0:T(8,128)(4,1)S(1)} %fusion.33, bf16[512,6,64]{0,2,1:T(8,128)(2,1)S(1)} %bitcast.181, bf16[512,6,64]{0,2,1:T(8,128)(2,1)S(1)} %copy-done.33), kind=kOutput, calls=%fused_computation.1 | convolution fusion | flops 263451648 | bytes 16867328 | tf_op jit(solution)/shard_map/qhd,khd->hqk/dot_general | solution.py:148
  193.0 0.9 slice.115
  193.9 1.9 copy.40
  195.9 6.8 %multiply_convert_fusion = bf16[6,512,640]{2,1,0:T(8,128)(2,1)S(1)} fusion(f32[6,512,640]{2,1,0:T(8,128)} %get-tuple-element.109, f32[6,512]{1,0:T(8,128)S(1)} %get-tuple-element.108, f32[6,512]{1,0:T(8,128)S(1)} %log_add_fusion, f32[6,512,640]{2,1,0:T(8,128)} %copy-done, pred[512,640]{1,0:T(8,128)(4,1)S(1)} %fusion.33), kind=kLoop, calls=%fused_computation | loop fusion | flops 13762560 | bytes 20013056 | tf_op jit(solution)/shard_map/convert_element_type | solution.py:160
  202.7 1.7 fusion.32
  204.5 1.3 broadcast_multiply_fusion
  205.9 0.8 copy-done.30
  207.0 0.9 copy.38
  207.9 1.6 slice_multiply_fusion.1
  209.6 1.0 maximum_subtract_fusion.1
  210.6 1.9 copy.39
  212.5 3.8 bitcast_convert_fusion
  217.0 4.7 fusion.37
  221.8 1.0 copy-done.22
  222.8 1.7 fusion.75
  224.5 3.5 fusion.98
  228.1 0.9 copy-done.24
  229.1 2.3 maximum_convert_fusion.1
  231.4 2.4 copy.41
  233.8 4.6 fusion.39
  239.0 29.2 %all-reduce.18.cloned.1.call-done = (bf16[512,768]{1,0:T(8,128)(2,1)}, bf16[512,768]{1,0:T(8,128)(2,1)}) async-done(((bf16[512,768]{1,0:T(8,128)(2,1)}, bf16[512,768]{1,0:T(8,128)(2,1)}), (bf16[512,768]{1,0:T(8,128)(2,1)}, bf16[512,768]{1,0:T(8,128)(2,1)})) %all-reduce.18.cloned.1.call-update) | async-done | bytes 1572880 | tf_op jit(solution)/shard_map/psum | solution.py:120
  268.2 2.0 fusion.28
  270.2 33.8 %all-reduce.7 = (f32[768]{0:T(1024)S(1)}, f32[768]{0:T(1024)S(1)}) all-reduce(f32[768]{0:T(1024)S(1)} %get-tuple-element.74, f32[768]{0:T(1024)S(1)} %copy-done.40), channel_id=2, replica_groups=mesh['dp'=16,'tensor'=2] {'dp'}, use_global_device_ids=true, to_apply=%region_16.17.clone | all-reduce | flops 1536 | bytes 12288
  304.0 0.6 dynamic-slice.13
  304.6 0.6 dynamic-slice.15
  305.2 3.5 fusion.20
  308.6 34.0 %reduce-scatter.9.cloned.1.call-done = f32[48,2,576]{2,0,1:T(8,128)} async-done(((f32[768,2,576]{2,0,1:T(8,128)}), f32[48,2,576]{2,0,1:T(8,128)}) %reduce-scatter.9.cloned.1.call-update) | async-done | bytes 221200 | tf_op jit(solution)/shard_map/reduce_scatter | solution.py:195
  342.6 1.8 copy.44
  344.4 59.4 %reduce-scatter.7.cloned.1.call-done = f32[384,48]{0,1:T(8,128)} async-done(((f32[384,768]{0,1:T(8,128)}), f32[384,48]{0,1:T(8,128)}) %reduce-scatter.7.cloned.1.call-update) | async-done | bytes 73744 | tf_op jit(solution)/shard_map/reduce_scatter | solution.py:193
  403.8 64.5 %reduce-scatter.11.cloned.1.call-done = f32[576,48]{0,1:T(8,128)} async-done(((f32[576,768]{0,1:T(8,128)}), f32[576,48]{0,1:T(8,128)}) %reduce-scatter.11.cloned.1.call-update) | async-done | bytes 110608 | tf_op jit(solution)/shard_map/reduce_scatter | solution.py:196
  468.3 71.5 %reduce-scatter.5.cloned.1.call-done = f32[48,3,384]{2,0,1:T(8,128)} async-done(((f32[768,3,384]{2,0,1:T(8,128)}), f32[48,3,384]{2,0,1:T(8,128)}) %reduce-scatter.5.cloned.1.call-update) | async-done | bytes 221200 | tf_op jit(solution)/shard_map/reduce_scatter | solution.py:192
  (137 shorter events, 7.3 us)
Async XLA Ops:
  7.2 4.9 copy-start.42
  7.2 4.5 copy-start.1
  7.2 6.2 %copy-start.43 = (bf16[48]{0:T(256)(128)(2,1)S(1)}, bf16[48]{0:T(256)(128)(2,1)}, u32[]{:S(2)}) copy-start(bf16[48]{0:T(256)(128)(2,1)} %param.24) | copy-start | bytes 292
  7.2 6.4 %copy-start.44 = (bf16[48]{0:T(256)(128)(2,1)S(1)}, bf16[48]{0:T(256)(128)(2,1)}, u32[]{:S(2)}) copy-start(bf16[48]{0:T(256)(128)(2,1)} %param.21) | copy-start | bytes 292
  7.2 43.0 %copy-start.35 = (bf16[384,48]{0,1:T(8,128)(2,1)S(1)}, bf16[384,48]{0,1:T(8,128)(2,1)}, u32[]{:S(2)}) copy-start(bf16[384,48]{0,1:T(8,128)(2,1)} %param.23) | copy-start | bytes 110596
  7.2 62.5 %all-gather.3.cloned.1.call-start = ((), (), s32[]{:S(2)}) async-start(), calls=%async_computation.4 | async-start | bytes 1880064 | tf_op jit(solution)/shard_map/all_gather | solution.py:64
  8.0 104.2 %all-gather.5.cloned.1.call-start = ((), (), s32[]{:S(2)}) async-start(), calls=%async_computation.6 | async-start | bytes 2088960 | tf_op jit(solution)/shard_map/all_gather | solution.py:67
  9.6 59.6 %copy-start.41 = (s32[512]{0:T(512)S(1)}, s32[512]{0:T(512)}, u32[]{:S(2)}) copy-start(s32[512]{0:T(512)} %param.19) | copy-start | bytes 6148
  9.6 123.0 %all-reduce.14.cloned.1.call-start = ((), (), s32[]{:S(2)}) async-start(), calls=%async_computation.5 | async-start | bytes 1572864 | tf_op jit(solution)/shard_map/psum | solution.py:107
  12.1 61.5 %copy-start.38 = (f32[512]{0:T(512)}, f32[512]{0:T(512)S(1)}, u32[]{:S(2)}) copy-start(f32[512]{0:T(512)S(1)} %add_rsqrt_fusion.1) | copy-start | bytes 6148
  50.2 26.6 %copy-start.25 = (f32[512,64]{0,1:T(8,128)}, f32[512,64]{0,1:T(8,128)S(1)}, u32[]{:S(2)}) copy-start(f32[512,64]{0,1:T(8,128)S(1)} %get-tuple-element.103) | copy-start | bytes 393220
  69.2 16.7 %copy-start.9 = (bf16[384,768]{0,1:T(8,128)(2,1)}, bf16[384,768]{0,1:T(8,128)(2,1)S(1)}, u32[]{:S(2)}) copy-start(bf16[384,768]{0,1:T(8,128)(2,1)S(1)} %all_gather.20) | copy-start | bytes 1769476
  76.5 5.6 %copy-start.32 = (bf16[512,6,64]{0,2,1:T(8,128)(2,1)}, bf16[512,6,64]{0,2,1:T(8,128)(2,1)S(1)}, u32[]{:S(2)}) copy-start(bf16[512,6,64]{0,2,1:T(8,128)(2,1)S(1)} %fusion.74) | copy-start | bytes 1179652
  76.5 1.0 copy-start.27
  78.0 2.0 copy-start.13
  78.1 2.0 copy-start.15
  80.1 3.1 copy-start
  85.9 1.6 copy-start.21
  85.9 1.6 copy-start.34
  85.9 25.6 %copy-start.6 = (bf16[512,768]{1,0:T(8,128)(2,1)S(1)}, bf16[512,768]{1,0:T(8,128)(2,1)}, u32[]{:S(2)}) copy-start(bf16[512,768]{1,0:T(8,128)(2,1)} %param.27) | copy-start | bytes 2359300
  87.4 90.4 %all-reduce.16.cloned.1.call-start = ((), (), s32[]{:S(2)}) async-start(), calls=%async_computation.7 | async-start | bytes 1572864 | tf_op jit(solution)/shard_map/psum | solution.py:135
  110.5 1.0 copy-start.11
  132.6 1.6 copy-start.2
  132.6 2.0 copy-start.20
  134.6 46.0 %copy-start.36 = (f32[512]{0:T(512)}, f32[512]{0:T(512)S(1)}, u32[]{:S(2)}) copy-start(f32[512]{0:T(512)S(1)} %add_rsqrt_fusion) | copy-start | bytes 6148
  135.9 2.9 copy-start.3
  138.8 1.0 copy-start.4
  138.8 1.2 copy-start.28
  138.8 2.4 copy-start.19
  139.8 0.8 copy-start.29
  141.2 2.5 copy-start.5
  143.4 124.9 %all-reduce.18.cloned.1.call-start = ((), (), s32[]{:S(2)}) async-start(), calls=%async_computation.12 | async-start | bytes 3145728 | tf_op jit(solution)/shard_map/psum | solution.py:120
  143.7 3.0 copy-start.12
  145.8 0.8 copy-start.18
  177.9 2.7 copy-start.7
  177.9 2.7 copy-start.17
  180.6 1.1 copy-start.10
  181.7 5.6 %slice-start = ((s8[7864320]{0:T(1024)(128)(4,1)}), s8[4194304]{0:T(1024)(128)(4,1)S(1)}, s32[]{:S(2)}) async-start(s8[7864320]{0:T(1024)(128)(4,1)} %bitcast.172), calls=%async_computation.13 | async-start | bytes 8388608
  182.2 5.2 slice-start.1
  182.2 5.2 copy-start.33
  195.9 6.8 %copy-start.16 = (bf16[512,6,64]{0,2,1:T(8,128)(2,1)S(1)}, bf16[512,6,64]{0,2,1:T(8,128)(2,1)}, u32[]{:S(2)}) copy-start(bf16[512,6,64]{0,2,1:T(8,128)(2,1)} %copy-done.15) | copy-start | bytes 1179652
  202.7 1.8 copy-start.14
  202.7 1.8 copy-start.31
  205.8 0.9 copy-start.30
  207.9 1.7 copy-start.8
  207.9 1.7 copy-start.26
  209.6 3.0 copy-start.23
  216.4 0.7 copy-start.37
  216.4 126.2 %reduce-scatter.9.cloned.1.call-start = ((), (), s32[]{:S(2)}) async-start(), calls=%async_computation.10 | async-start | bytes 4177920 | tf_op jit(solution)/shard_map/reduce_scatter | solution.py:195
  221.7 1.1 copy-start.22
  221.7 182.0 %reduce-scatter.7.cloned.1.call-start = ((), (), s32[]{:S(2)}) async-start(), calls=%async_computation.9 | async-start | bytes 1253376 | tf_op jit(solution)/shard_map/reduce_scatter | solution.py:193
  224.5 243.8 %reduce-scatter.11.cloned.1.call-start = ((), (), s32[]{:S(2)}) async-start(), calls=%async_computation.11 | async-start | bytes 2088960 | tf_op jit(solution)/shard_map/reduce_scatter | solution.py:196
  228.1 1.0 copy-start.24
  228.1 311.6 %reduce-scatter.5.cloned.1.call-start = ((), (), s32[]{:S(2)}) async-start(), calls=%async_computation.8 | async-start | bytes 3760128 | tf_op jit(solution)/shard_map/reduce_scatter | solution.py:192
  231.4 2.4 copy-start.39
  238.4 31.8 %copy-start.40 = (f32[768]{0:T(1024)S(1)}, f32[768]{0:T(1024)}, u32[]{:S(2)}) copy-start(f32[768]{0:T(1024)} %get-tuple-element.72) | copy-start | bytes 9220
Sparse Core Ops, SparseCore 0:
  10.4 43.2 all-gather.2
  56.4 40.1 all-gather.4
  99.5 33.0 all-reduce.13
  143.5 34.3 all-reduce.15
  216.5 51.6 all-reduce.17
  272.5 70.1 reduce-scatter.8
  346.8 56.9 reduce-scatter.6
  408.1 60.1 reduce-scatter.10
  472.7 66.9 reduce-scatter.4
where the time goes:
time: 547 us; the launch traced here: 546 us
  waiting for transfers between devices  305 us (56%)
  blocking collectives  111 us (20%)
  matrix products  47.2 us (9%)
  other arithmetic  35 us (6%)
  local copies, waits for them, and re-layouts  31.1 us (6%)
  between operations  15.8 us (3%)
    reduce_scatter x1, waiting for transfers between devices, per_device(): lax.psum_scatter(grad_qkv, 'dp', scatter_dimension=0, tiled=True)  71.5 us
    unnamed x2, blocking collectives  69 us
    reduce_scatter x1, waiting for transfers between devices, per_device(): lax.psum_scatter(grad_down, 'dp', scatter_dimension=1, tiled=True)  64.5 us
    reduce_scatter x1, waiting for transfers between devices, per_device(): lax.psum_scatter(grad_out, 'dp', scatter_dimension=1, tiled=True)  59.4 us
    reduce_scatter x1, waiting for transfers between devices, per_device(): lax.psum_scatter(grad_in, 'dp', scatter_dimension=0, tiled=True)  34 us
    psum x1, waiting for transfers between devices, per_device(): lax.psum(partial_two.astype(jnp.bfloat16), 'tensor').astype(jnp.float32)  29.5 us
    psum x1, waiting for transfers between devices, per_device(): lax.psum(mlp_part.astype(jnp.bfloat16), 'tensor').astype(jnp.float32)  29.2 us
    all_gather x1, blocking collectives, per_device(): lax.all_gather(w_mlp_out, 'dp', axis=1, tiled=True)  23 us
  transfers between devices with their start and end apart: 9, of which 7 were waited for; matrix products, arithmetic and copies ran while one was open for 11% of the time, Pallas kernels for 0%

commit v1 on v0

v1 whole, which is shorter than its diff:
```python
import functools

import jax
import jax.numpy as jnp
from jax import lax
from jax.sharding import PartitionSpec as P

HD = 64
HALF = 64


EPSILON = 1e-05
THETA = 10000.0
MASKED = -1e30


def normalize(values):
    average = jnp.mean(values, axis=-1, keepdims=True)
    centered = values - average
    variance = jnp.mean(centered * centered, axis=-1, keepdims=True)
    inverse = lax.rsqrt(variance + EPSILON)
    return (centered * inverse, inverse)


def rope_tables(positions, size):
    frequency = THETA ** (-jnp.arange(0, size, 2).astype(jnp.float32) / size)
    angle = positions.astype(jnp.float32)[:, None] * frequency[None, :]
    angle = jnp.concatenate([angle, angle], axis=-1)
    return (jnp.cos(angle)[:, None, :], jnp.sin(angle)[:, None, :])


def rotate_half(values):
    middle = values.shape[-1] // 2
    return jnp.concatenate([-values[..., middle:], values[..., :middle]], axis=-1)


def rotate(values, cosine, sine):
    return values * cosine + rotate_half(values) * sine


def rotate_back(values, cosine, sine):
    return values * cosine - rotate_half(values * sine)


def gated(active, factor):
    return jax.nn.gelu(active, approximate=False) * factor


def levels_of(count):
    levels, stride = [], count
    while stride > 1:
        size = 4 if stride % 8 == 0 else 2 if stride % 2 == 0 else stride
        stride //= size
        levels.append((stride, size))
    return levels


def shifted(values, count, level, step):
    stride, size = level
    pairs = []
    for device in range(count):
        digit = (device // stride) % size
        pairs.append((device, device + ((digit + step) % size - digit) * stride))
    return lax.ppermute(values, "dp", pairs)


def gather_rows(shard, count):
    held = shard
    for level in levels_of(count):
        held = jnp.concatenate(
            [held] + [shifted(held, count, level, step) for step in range(1, level[1])], axis=0
        )
    return held


def scatter_rows(partial, count):
    held = partial
    for level in reversed(levels_of(count)):
        size = level[1]
        pieces = held.reshape(size, held.shape[0] // size, held.shape[1])
        total = pieces[0].astype(jnp.float32)
        for step in range(1, size):
            total = total + shifted(pieces[step], count, level, -step).astype(jnp.float32)
        held = lax.optimization_barrier(total.astype(jnp.bfloat16)) if level[0] != levels_of(count)[0][0] else total
    return held


def placement(count, width):
    device = lax.axis_index("dp")
    place = jnp.arange(count)
    owner, weight = jnp.zeros_like(place), 1
    for stride, size in levels_of(count):
        step = (place // weight) % size
        owner = owner + ((device // stride) % size - step + size) % size * stride
        weight *= size
    rows = width // count
    natural = (owner[:, None] * rows + jnp.arange(rows)[None, :]).reshape(width)
    return (natural[None, :] == jnp.arange(width)[:, None]).astype(jnp.bfloat16)


def reorder(values, matrix):
    return jnp.dot(values, matrix, preferred_element_type=jnp.float32)


def restore(values, matrix):
    return lax.dot_general(values, matrix, (((1,), (1,)), ((), ())), preferred_element_type=jnp.float32)


def pair_sum(part):
    own = lax.optimization_barrier(part.astype(jnp.bfloat16))
    other = lax.ppermute(own, "tensor", [(0, 1), (1, 0)])
    return own.astype(jnp.float32) + other.astype(jnp.float32)


def norm_back_scaled(scaled, normed, inverse):
    first = jnp.mean(scaled, axis=-1, keepdims=True)
    second = jnp.mean(scaled * normed, axis=-1, keepdims=True)
    return inverse * (scaled - first - normed * second)


def per_device(
    devices, tokens, seg_ids, positions, gain_attn, w_qkv, w_attn_out, gain_mlp, w_in, w_mlp_out, cotangent
):
    count = tokens.shape[0]
    width = tokens.shape[1]
    inner = w_qkv.shape[2]
    heads_here = inner // HD
    hidden = w_in.shape[2]
    rows = w_qkv.shape[0]
    gain_one = gain_attn.astype(jnp.float32)
    gain_two = gain_mlp.astype(jnp.float32)
    scaled_qkv = (w_qkv.astype(jnp.float32) * gain_one[:, None, None]).astype(jnp.bfloat16)
    scaled_in = (w_in.astype(jnp.float32) * gain_two[:, None, None]).astype(jnp.bfloat16)
    matrix_q, matrix_k, matrix_v = (gather_rows(scaled_qkv[:, i], devices) for i in range(3))
    matrix_qkv = jnp.concatenate([matrix_q, matrix_k, matrix_v], axis=1)
    rest = jnp.concatenate([w_attn_out.T, w_mlp_out.T, scaled_in.reshape(rows, 2 * hidden)], axis=1)
    rest = gather_rows(rest, devices)
    out_rows, down_rows, matrix_in = jnp.split(rest, [inner, inner + hidden], axis=1)

    order = placement(devices, width)
    inputs = reorder(tokens, order)
    upstream = reorder(cotangent, order).astype(jnp.bfloat16)
    normed_one, inverse_one = normalize(inputs)
    lowered_one = normed_one.astype(jnp.bfloat16)
    projected = jnp.dot(lowered_one, matrix_qkv, preferred_element_type=jnp.float32)
    projected = projected.reshape(count, 3, heads_here, HD)
    cosine, sine = rope_tables(positions, HD)
    query = rotate(projected[:, 0], cosine, sine).astype(jnp.bfloat16)
    keys = rotate(projected[:, 1], cosine, sine).astype(jnp.bfloat16)
    values = projected[:, 2].astype(jnp.bfloat16)
    wide_keys = jnp.pad(keys, ((HALF, HALF), (0, 0), (0, 0)))
    wide_values = jnp.pad(values, ((HALF, HALF), (0, 0), (0, 0)))
    wide_segments = jnp.pad(seg_ids, (HALF, HALF), constant_values=-1)
    block = min(512, count)
    span = block + 2 * HALF
    scale = HD ** (-0.5)
    offsets = jnp.arange(span)[None, :] - HALF - jnp.arange(block)[:, None]
    near = jnp.abs(offsets) <= HALF

    def scores_of():
        allowed = near & (seg_ids[:, None] == wide_segments[None, :])
        scores = (
            jnp.einsum("qhd,khd->hqk", query, wide_keys, preferred_element_type=jnp.float32) * scale
        )
        return (jnp.where(allowed[None], scores, MASKED), allowed)

    start = 0
    scores, allowed = scores_of()
    peak = jnp.max(scores, axis=-1, keepdims=True)
    powers = jnp.exp(scores - peak)
    total = jnp.sum(powers, axis=-1, keepdims=True)
    shares = (powers / total).astype(jnp.bfloat16)
    log_sums = [peak + jnp.log(total)]
    contexts = jnp.einsum("hqk,khd->qhd", shares, wide_values, preferred_element_type=jnp.float32)
    context = contexts.astype(jnp.bfloat16).reshape(count, inner)
    attn_part = lax.dot_general(context, out_rows, (((1,), (1,)), ((), ())), preferred_element_type=jnp.float32)
    middle = inputs + pair_sum(attn_part)
    normed_two, inverse_two = normalize(middle)
    lowered_two = normed_two.astype(jnp.bfloat16)
    gates = jnp.dot(lowered_two, matrix_in, preferred_element_type=jnp.float32)
    active, factor = gates[:, :hidden], gates[:, hidden:]
    mixed = gated(active, factor).astype(jnp.bfloat16)
    mlp_part = lax.dot_general(mixed, down_rows, (((1,), (1,)), ((), ())), preferred_element_type=jnp.float32)
    output = (middle + pair_sum(mlp_part)).astype(jnp.bfloat16)
    output = restore(output, order).astype(jnp.bfloat16)
    grad_down = jnp.dot(upstream.T, mixed, preferred_element_type=jnp.float32)
    grad_mixed = jnp.dot(upstream, down_rows, preferred_element_type=jnp.float32)
    unused, pull = jax.vjp(gated, active, factor)
    grad_active, grad_factor = pull(grad_mixed)
    grad_gates = jnp.concatenate([grad_active, grad_factor], axis=1).astype(jnp.bfloat16)
    grad_in = jnp.dot(lowered_two.T, grad_gates, preferred_element_type=jnp.float32)
    mlp_grads = jnp.concatenate([grad_down, grad_in], axis=1).astype(jnp.bfloat16)
    mlp_grads = scatter_rows(mlp_grads, devices)
    partial_two = lax.dot_general(grad_gates, matrix_in, (((1,), (1,)), ((), ())), preferred_element_type=jnp.float32)
    grad_middle = upstream.astype(jnp.float32) + norm_back_scaled(pair_sum(partial_two), normed_two, inverse_two)
    grad_branch = grad_middle.astype(jnp.bfloat16)
    grad_out = jnp.dot(grad_branch.T, context, preferred_element_type=jnp.float32).astype(jnp.bfloat16)
    grad_out = scatter_rows(grad_out, devices)
    grad_context = jnp.dot(grad_branch, out_rows, preferred_element_type=jnp.float32)
    grad_context = grad_context.astype(jnp.bfloat16).reshape(count, heads_here, HD)
    query_grads = []
    grad_keys = jnp.zeros((count + 2 * HALF, heads_here, HD), jnp.float32)
    grad_values = jnp.zeros((count + 2 * HALF, heads_here, HD), jnp.float32)
    for number, start in enumerate(range(0, count, block)):
        scores, allowed = scores_of()
        shares = jnp.where(allowed[None], jnp.exp(scores - log_sums[number]), 0.0)
        grad_shares = jnp.einsum(
            "qhd,khd->hqk", grad_context, wide_values, preferred_element_type=jnp.float32
        )
        grad_values = grad_values.at[start : start + span].add(
            jnp.einsum(
                "hqk,qhd->khd",
                shares.astype(jnp.bfloat16),
                grad_context,
                preferred_element_type=jnp.float32,
            )
        )
        row_sums = jnp.sum(shares * grad_shares, axis=-1, keepdims=True)
        grad_scores = (shares * (grad_shares - row_sums)).astype(jnp.bfloat16)
        query_grads.append(
            jnp.einsum("hqk,khd->qhd", grad_scores, wide_keys, preferred_element_type=jnp.float32)
            * scale
        )
        grad_keys = grad_keys.at[start : start + span].add(
            jnp.einsum("hqk,qhd->khd", grad_scores, query, preferred_element_type=jnp.float32)
            * scale
        )
    grad_query = rotate_back(query_grads[0], cosine, sine)
    grad_key_pre = rotate_back(grad_keys[HALF : HALF + count], cosine, sine)
    grad_projected = (
        jnp.stack(
            [
                grad_query.reshape(count, inner),
                grad_key_pre.reshape(count, inner),
                grad_values[HALF : HALF + count].reshape(count, inner),
            ],
            axis=1,
        )
        .astype(jnp.bfloat16)
        .reshape(count, 3 * inner)
    )
    grad_qkv = jnp.dot(lowered_one.T, grad_projected, preferred_element_type=jnp.float32).astype(jnp.bfloat16)
    grad_qkv = jnp.concatenate([scatter_rows(part, devices) for part in jnp.split(grad_qkv, 3, axis=1)], axis=1)
    partial_one = lax.dot_general(grad_projected, matrix_qkv, (((1,), (1,)), ((), ())), preferred_element_type=jnp.float32)
    grad_input = grad_middle + norm_back_scaled(pair_sum(partial_one), normed_one, inverse_one)
    high = lax.optimization_barrier(grad_input.astype(jnp.bfloat16))
    low = (grad_input - high.astype(jnp.float32)).astype(jnp.bfloat16)
    grad_input = restore(high, order) + restore(low, order)

    sum_qkv = grad_qkv.reshape(rows, 3, inner)
    sum_down = mlp_grads[:, :hidden]
    sum_in = mlp_grads[:, hidden:].reshape(rows, 2, hidden)
    gains = jnp.stack(
        [
            jnp.sum(w_qkv.astype(jnp.float32) * sum_qkv, axis=(1, 2)),
            jnp.sum(w_in.astype(jnp.float32) * sum_in, axis=(1, 2)),
        ]
    )
    gains = gains + lax.ppermute(gains, "tensor", [(0, 1), (1, 0)])
    return (
        output,
        grad_input,
        gains[0],
        sum_qkv * gain_one[:, None, None],
        grad_out.T,
        gains[1],
        sum_in * gain_two[:, None, None],
        sum_down.T,
    )


def solution(mesh):
    return jax.shard_map(
        functools.partial(per_device, mesh.shape["dp"]),
        mesh=mesh,
        in_specs=(
            P("dp", None),
            P("dp"),
            P("dp"),
            P("dp"),
            P("dp", None, "tensor"),
            P("tensor", "dp"),
            P("dp"),
            P("dp", None, "tensor"),
            P("tensor", "dp"),
            P("dp", None),
        ),
        out_specs=(
            P("dp", None),
            P("dp", None),
            P("dp"),
            P("dp", None, "tensor"),
            P("tensor", "dp"),
            P("dp"),
            P("dp", None, "tensor"),
            P("tensor", "dp"),
        ),
        check_vma=False,
    )
```

time: 547 us -> 265 us (0.48)
  waiting for transfers between devices: 305 us -> 59.7 us
  blocking collectives: 111 us -> 0 us
  starting transfers between devices: 0.85 us -> 60 us
  local copies, waits for them, and re-layouts: 31.1 us -> 56.4 us
  between operations: 15.8 us -> 1.74 us
    reduce_scatter x4 -> x0, waiting for transfers between devices: 229 us -> none  [the longest x1 71.5 us: per_device(): lax.psum_scatter(grad_qkv, 'dp', scatter_dimension=0, tiled=True)]
    psum x3 -> x0, waiting for transfers between devices: 75.1 us -> none  [the longest x1 29.5 us: per_device(): lax.psum(partial_two.astype(jnp.bfloat16), 'tensor').astype(jnp.float32)]
    unnamed x2 -> x0, blocking collectives: 69 us -> none
    ppermute x0 -> x50, starting transfers between devices: none -> 60 us  [the longest x45 54.3 us: shifted(): return lax.ppermute(values, 'dp', pairs)]
    ppermute x0 -> x50, waiting for transfers between devices: none -> 59.7 us  [the longest x45 32.8 us: shifted(): return lax.ppermute(values, 'dp', pairs)]
    all_gather x2 -> x0, blocking collectives: 42 us -> none  [the longest x1 23 us: per_device(): lax.all_gather(w_mlp_out, 'dp', axis=1, tiled=True)]
    concatenate x0 -> x11, local copies, waits for them, and re-layouts: none -> 21.5 us  [the longest x9 19.5 us: gather_rows(): jnp.concatenate([held] + [shifted(held, count, level, step) for step in r...]
    all_gather x2 -> x0, local copies, waits for them, and re-layouts: 7.85 us -> none  [the longest x1 4 us: per_device(): lax.all_gather(w_in, 'dp', axis=0, tiled=True)]
  transfers between devices with their start and end apart: 9 -> 50, of which waited for: 7 -> 18; matrix products, arithmetic and copies ran while one was open for 11% -> 39% of each run, Pallas kernels for 0% -> 0%
where the time goes in v1:
time: 265 us; the launch traced here: 260 us
  starting transfers between devices  60 us (23%)
  waiting for transfers between devices  59.7 us (23%)
  local copies, waits for them, and re-layouts  56.4 us (21%)
  matrix products  50.1 us (19%)
  other arithmetic  32.1 us (12%)
    ppermute x45, starting transfers between devices, shifted(): return lax.ppermute(values, 'dp', pairs)  54.3 us
    ppermute x45, waiting for transfers between devices, shifted(): return lax.ppermute(values, 'dp', pairs)  32.8 us
    ppermute x4, waiting for transfers between devices, pair_sum(): other = lax.ppermute(own, 'tensor', [(0, 1), (1, 0)])  24.4 us
    concatenate x9, local copies, waits for them, and re-layouts, gather_rows(): jnp.concatenate([held] + [shifted(held, count, level, step) for step in r...  19.5 us
    unnamed x88, local copies, waits for them, and re-layouts  17.7 us
    ppermute x5, local copies, waits for them, and re-layouts, shifted(): return lax.ppermute(values, 'dp', pairs)  7.68 us
    dot_general x3, matrix products, restore(): lax.dot_general(values, matrix, (((1,), (1,)), ((), ())), preferred_eleme...  6.08 us
  transfers between devices with their start and end apart: 50, of which 18 were waited for; matrix products, arithmetic and copies ran while one was open for 39% of the time, Pallas kernels for 0%

profile of v1, /device:TPU:0, one launch (start us, length us, event | category | flops | bytes accessed | tf_op | source)
XLA Modules:
  0.0 260.0 jit_solution(17179764817954029497)
XLA Ops:
  2.4 5.1 %collective-permute-start.2 = (bf16[48,384]{1,0:T(8,128)(2,1)S(1)}, bf16[48,384]{1,0:T(8,128)(2,1)S(1)}, u32[]{:S(2)}, u32[]{:S(2)}) collective-permute-start(bf16[48,384]{1,0:T(8,128)(2,1)S(1)} %get-tuple-element.117), channel_id=1, source_target_pairs={{0,24},{2,26},{4,28},{6,30},{8,0},{10,2},{12,4},{14,6},{16,8},{18,... | collective-permute-start | bytes 110600 | tf_op jit(solution)/shard_map/ppermute | solution.py:64
  8.5 2.8 %collective-permute-start.12 = (bf16[48,384]{1,0:T(8,128)(2,1)S(1)}, bf16[48,384]{1,0:T(8,128)(2,1)S(1)}, u32[]{:S(2)}, u32[]{:S(2)}) collective-permute-start(bf16[48,384]{1,0:T(8,128)(2,1)S(1)} %get-tuple-element.118), channel_id=1, source_target_pairs={{0,24},{2,26},{4,28},{6,30},{8,0},{10,2},{12,4},{14,6},{16,8},{18,... | collective-permute-start | bytes 110600 | tf_op jit(solution)/shard_map/ppermute | solution.py:64
  22.3 3.8 %collective-permute-start.7 = (bf16[48,384]{1,0:T(8,128)(2,1)S(1)}, bf16[48,384]{1,0:T(8,128)(2,1)S(1)}, u32[]{:S(2)}, u32[]{:S(2)}) collective-permute-start(bf16[48,384]{1,0:T(8,128)(2,1)S(1)} %get-tuple-element.119), channel_id=1, source_target_pairs={{0,24},{2,26},{4,28},{6,30},{8,0},{10,2},{12,4},{14,6},{16,8},{18,... | collective-permute-start | bytes 110600 | tf_op jit(solution)/shard_map/ppermute | solution.py:64
  28.8 3.2 %collective-permute-start.17 = (bf16[48,2112]{1,0:T(8,128)(2,1)S(1)}, bf16[48,2112]{1,0:T(8,128)(2,1)S(1)}, u32[]{:S(2)}, u32[]{:S(2)}) collective-permute-start(bf16[48,2112]{1,0:T(8,128)(2,1)S(1)} %concatenate.101), channel_id=1, source_target_pairs={{0,24},{2,26},{4,28},{6,30},{8,0},{10,2},{12,4},{14,6},{16,8},{18,... | collective-permute-start | bytes 608264 | tf_op jit(solution)/shard_map/ppermute | solution.py:64
  36.0 1.5 collective-permute-start.3
  39.9 2.6 collective-permute-done.3
  42.5 1.5 collective-permute-start.8
  45.5 2.1 collective-permute-done.8
  50.5 1.5 collective-permute-start.18
  57.2 1.7 constant_dynamic-update-slice_fusion.5
  58.9 1.7 constant_dynamic-update-slice_fusion.27
  60.7 1.7 constant_dynamic-update-slice_fusion.16
  62.3 2.5 fusion.61
  66.7 5.1 %fusion.1 = (f32[6,512]{1,0:T(8,128)S(1)}, f32[6,512,640]{2,1,0:T(8,128)}) fusion(pred[512,640]{1,0:T(8,128)(4,1)S(1)} %fusion.36, bf16[512,6,64]{0,2,1:T(8,128)(2,1)S(1)} %get-tuple-element.69, bf16[512,6,64]{0,2,1:T(8,128)(2,1)S(1)} %get-tuple-element.68), kind=kOutput, calls=%fused_computation.7 | convolution fusion | flops 257553408 | bytes 8990720 | tf_op jit(solution)/shard_map/qhd,khd->hqk/dot_general | solution.py:163
  72.9 3.8 %copy.68 = bf16[384,2112]{0,1:T(8,128)(2,1)} copy(bf16[384,2112]{1,0:T(8,128)(2,1)} %constant_dynamic-update-slice_fusion.33) | data formatting | bytes 3244032 | tf_op jit(solution)/shard_map/concatenate | solution.py:70
  76.7 4.5 %fusion = f32[6,512]{1,0:T(8,128)S(1)} fusion(f32[6,512,640]{2,1,0:T(8,128)} %get-tuple-element.147, f32[6,512]{1,0:T(8,128)S(1)} %get-tuple-element.146, pred[512,640]{1,0:T(8,128)(4,1)S(1)} %fusion.36), kind=kLoop, calls=%fused_computation.6 | loop fusion | flops 7861248 | bytes 8216576 | tf_op jit(solution)/shard_map/reduce_sum | solution.py:171
  83.2 3.4 %fusion.40 = bf16[6,64,512]{2,1,0:T(8,128)(2,1)} fusion(f32[6,512,640]{2,1,0:T(8,128)S(1)} %copy-done.2, f32[6,512]{1,0:T(8,128)S(1)} %fusion, f32[6,512]{1,0:T(8,128)S(1)} %get-tuple-element.146, pred[512,640]{1,0:T(8,128)(4,1)S(1)} %fusion.36, bf16[512,6,64]{0,2,1:T(8,128)(2,1)S(1)} %fusion.70), kind=kOutput, calls=%fused_computation.81 | convolution fusion | flops 261685248 | bytes 9003008 | tf_op jit(solution)/shard_map/hqk,khd->qhd/dot_general | solution.py:174
  86.6 2.0 copy.73
  88.5 7.3 %concatenate.104 = bf16[768,2112]{0,1:T(8,128)(2,1)} concatenate(bf16[48,2112]{0,1:T(8,128)(2,1)} %copy.69, bf16[48,2112]{0,1:T(8,128)(2,1)} %copy.70, bf16[48,2112]{0,1:T(8,128)(2,1)} %copy.71, bf16[48,2112]{0,1:T(8,128)(2,1)} %copy.72, bf16[192,2112]{0,1:T(8,128)(2,1)S(1)} %copy.73, bf16[384,2112]{0,1:T(8,128)(2,1)} %collective-permute-done.19), dimensions={0} | concatenate | bytes 6488064 | tf_op jit(solution)/shard_map/concatenate | solution.py:70
  95.8 1.9 convolution_convert_fusion.5
  97.7 1.6 collective-permute-start.20
  100.1 17.6 %collective-permute-done.20 = bf16[512,768]{0,1:T(8,128)(2,1)S(1)} collective-permute-done((bf16[512,768]{0,1:T(8,128)(2,1)S(1)}, bf16[512,768]{0,1:T(8,128)(2,1)S(1)}, u32[]{:S(2)}, u32[]{:S(2)}) %collective-permute-start.20) | collective-permute-done | bytes 786464 | tf_op jit(solution)/shard_map/ppermute | solution.py:111
  118.4 1.8 copy-done.9
  121.5 3.6 %add_convert_fusion.3 = (bf16[512,576]{1,0:T(8,128)(2,1)S(1)}, f32[512,576]{1,0:T(8,128)S(1)}, f32[512,576]{1,0:T(8,128)S(1)}) fusion(f32[512,1152]{1,0:T(8,128)S(1)} %fusion.15, bf16[768,512]{1,0:T(8,128)(2,1)S(1)} %fusion.22, bf16[768,2112]{0,1:T(8,128)(2,1)S(1)} %copy-done.9), kind=kOutput, calls=%fused_computation.61 | convolution fusion | flops 474513408 | bytes 7241728 | tf_op jit(solution)/shard_map/dot_general | solution.py:187
  126.0 2.2 fusion.19
  128.2 1.7 convolution_convert_fusion.3
  129.9 1.5 collective-permute-start.22
  131.4 1.7 convolution_convert_fusion.2
  133.0 1.5 copy.81
  135.2 3.0 %convolution_convert_fusion = bf16[768,1152]{1,0:T(8,128)(2,1)S(1)} fusion(bf16[512,576]{1,0:T(8,128)(2,1)} %copy-done.19, bf16[512,576]{1,0:T(8,128)(2,1)} %copy-done.34, f32[512,768]{0,1:T(8,128)} %copy-done.5, f32[512]{0:T(512)S(1)} %add_rsqrt_fusion, f32[512]{0:T(512)S(1)} %broadcast_multiply_fusion.9), kind=kOutput, calls=%fused_computation.11 | convolution fusion | flops 910393344 | bytes 4526080 | tf_op jit(solution)/shard_map/dot_general | solution.py:191
  139.4 1.5 pad_maximum_fusion.1
  140.9 3.0 %copy.82 = bf16[384,1728]{0,1:T(8,128)(2,1)} copy(bf16[384,1728]{1,0:T(8,128)(2,1)} %pad_maximum_fusion.1) | data formatting | bytes 2654208 | tf_op jit(solution)/shard_map/slice | solution.py:83
  143.8 6.8 %collective-permute-done.22 = bf16[512,768]{0,1:T(8,128)(2,1)} collective-permute-done((bf16[512,768]{0,1:T(8,128)(2,1)}, bf16[512,768]{0,1:T(8,128)(2,1)}, u32[]{:S(2)}, u32[]{:S(2)}) %collective-permute-start.22) | collective-permute-done | bytes 786464 | tf_op jit(solution)/shard_map/ppermute | solution.py:111
  150.6 2.3 fusion.26
  153.0 2.0 bitcast_add_fusion
  155.0 2.0 convolution_convert_fusion.7
  157.7 5.0 %fusion.41 = bf16[640,6,64]{0,2,1:T(8,128)(2,1)S(1)} fusion(bf16[512,6,64]{0,2,1:T(8,128)(2,1)S(1)} %bitcast.108, f32[6,512]{1,0:T(8,128)S(1)} %log_add_fusion, f32[6,512,640]{2,1,0:T(8,128)} %get-tuple-element.147, pred[512,640]{1,0:T(8,128)(4,1)S(1)} %fusion.36), kind=kOutput, calls=%fused_computation.83 | convolution fusion | flops 261734400 | bytes 9089024 | tf_op jit(solution)/shard_map/hqk,qhd->khd/dot_general | solution.py:211
  162.8 3.8 %multiply_reduce_fusion = (f32[6,512]{1,0:T(8,128)S(1)}, f32[6,512,640]{2,1,0:T(8,128)S(1)}) fusion(f32[6,512]{1,0:T(8,128)S(1)} %log_add_fusion, f32[6,512,640]{2,1,0:T(8,128)S(1)} %bitcast.96, pred[512,640]{1,0:T(8,128)(4,1)S(1)} %fusion.36, bf16[512,6,64]{0,2,1:T(8,128)(2,1)S(1)} %bitcast.109, bf16[512,6,64]{0,2,1:T(8,128)(2,1)S(1)} %copy-done.26), kind=kOutput, calls=%fused_computation.1 | convolution fusion | flops 263451648 | bytes 16867328 | tf_op jit(solution)/shard_map/qhd,khd->hqk/dot_general | solution.py:207
  167.6 3.0 %multiply_convert_fusion = bf16[6,512,640]{2,1,0:T(8,128)(2,1)S(1)} fusion(f32[6,512,640]{2,1,0:T(8,128)S(1)} %get-tuple-element.150, f32[6,512]{1,0:T(8,128)S(1)} %get-tuple-element.149, f32[6,512]{1,0:T(8,128)S(1)} %log_add_fusion, f32[6,512,640]{2,1,0:T(8,128)S(1)} %bitcast.96, pred[512,640]{1,0:T(8,128)(4,1)S(1)} %fusion.36), kind=kLoop, calls=%fused_computation | loop fusion | flops 13762560 | bytes 20013056 | tf_op jit(solution)/shard_map/convert_element_type | solution.py:219
  179.8 3.1 %fusion.25 = bf16[512,768]{1,0:T(8,128)(2,1)} fusion(s32[768]{0:T(1024)S(1)} %add.308, f32[512,768]{0,1:T(8,128)S(1)} %copy-done.6, bf16[512,768]{0,1:T(8,128)(2,1)} %collective-permute-done.21, bf16[512,768]{0,1:T(8,128)(2,1)S(1)} %copy-done.33), kind=kOutput, calls=%fused_computation.48 | convolution fusion | flops 606928896 | bytes 3935232 | tf_op jit(solution)/shard_map/dot_general | solution.py:106
  183.0 1.5 collective-permute-start.23
  185.5 1.6 collective-permute-start.30
  187.6 3.8 %collective-permute-done.46 = bf16[192,384]{1,0:T(8,128)(2,1)S(1)} collective-permute-done((bf16[192,384]{1,0:T(8,128)(2,1)S(1)}, bf16[192,384]{1,0:T(8,128)(2,1)S(1)}, u32[]{:S(2)}, u32[]{:S(2)}) %collective-permute-start.46) | collective-permute-done | bytes 147488 | tf_op jit(solution)/shard_map/ppermute | solution.py:64
  191.9 2.6 %collective-permute-done.30 = bf16[192,384]{1,0:T(8,128)(2,1)S(1)} collective-permute-done((bf16[192,384]{1,0:T(8,128)(2,1)S(1)}, bf16[192,384]{1,0:T(8,128)(2,1)S(1)}, u32[]{:S(2)}, u32[]{:S(2)}) %collective-permute-start.30) | collective-permute-done | bytes 147488 | tf_op jit(solution)/shard_map/ppermute | solution.py:64
  194.6 3.1 %collective-permute-start.31 = (bf16[48,384]{1,0:T(8,128)(2,1)S(1)}, bf16[48,384]{1,0:T(8,128)(2,1)S(1)}, u32[]{:S(2)}, u32[]{:S(2)}) collective-permute-start(bf16[48,384]{1,0:T(8,128)(2,1)S(1)} %get-tuple-element.99), channel_id=1, source_target_pairs={{0,24},{2,26},{4,28},{6,30},{8,0},{10,2},{12,4},{14,6},{16,8},{18,... | collective-permute-start | bytes 110600 | tf_op jit(solution)/shard_map/ppermute | solution.py:64
  197.8 1.7 collective-permute-start.33
  199.6 1.9 collective-permute-start.32
  201.6 2.3 collective-permute-start.26
  204.8 2.0 collective-permute-start.27
  206.8 2.8 %collective-permute-start.36 = (bf16[48,384]{1,0:T(8,128)(2,1)S(1)}, bf16[48,384]{1,0:T(8,128)(2,1)S(1)}, u32[]{:S(2)}, u32[]{:S(2)}) collective-permute-start(bf16[48,384]{1,0:T(8,128)(2,1)S(1)} %get-tuple-element.102), channel_id=1, source_target_pairs={{0,24},{2,26},{4,28},{6,30},{8,0},{10,2},{12,4},{14,6},{16,8},{18,... | collective-permute-start | bytes 110600 | tf_op jit(solution)/shard_map/ppermute | solution.py:64
  210.1 2.0 collective-permute-start.37
  212.1 3.4 %collective-permute-start.47 = (bf16[48,384]{1,0:T(8,128)(2,1)S(1)}, bf16[48,384]{1,0:T(8,128)(2,1)S(1)}, u32[]{:S(2)}, u32[]{:S(2)}) collective-permute-start(bf16[48,384]{1,0:T(8,128)(2,1)S(1)} %get-tuple-element.93), channel_id=1, source_target_pairs={{0,24},{2,26},{4,28},{6,30},{8,0},{10,2},{12,4},{14,6},{16,8},{18,... | collective-permute-start | bytes 110600 | tf_op jit(solution)/shard_map/ppermute | solution.py:64
  215.6 1.7 collective-permute-start.48
  217.3 4.0 %collective-permute-done.49 = bf16[48,384]{1,0:T(8,128)(2,1)S(1)} collective-permute-done((bf16[48,384]{1,0:T(8,128)(2,1)S(1)}, bf16[48,384]{1,0:T(8,128)(2,1)S(1)}, u32[]{:S(2)}, u32[]{:S(2)}) %collective-permute-start.49) | collective-permute-done | bytes 36896 | tf_op jit(solution)/shard_map/ppermute | solution.py:64
  222.9 2.6 copy.83
  225.5 2.2 add_convert_fusion
  228.7 1.6 fusion.27
  230.3 1.8 fusion.113
  233.0 7.6 %collective-permute-done.40 = bf16[192,1728]{1,0:T(8,128)(2,1)S(1)} collective-permute-done((bf16[192,1728]{1,0:T(8,128)(2,1)S(1)}, bf16[192,1728]{1,0:T(8,128)(2,1)S(1)}, u32[]{:S(2)}, u32[]{:S(2)}) %collective-permute-start.40) | collective-permute-done | bytes 663584 | tf_op jit(solution)/shard_map/ppermute | solution.py:64
  240.9 2.8 %collective-permute-start.41 = (bf16[48,1728]{1,0:T(8,128)(2,1)S(1)}, bf16[48,1728]{1,0:T(8,128)(2,1)S(1)}, u32[]{:S(2)}, u32[]{:S(2)}) collective-permute-start(bf16[48,1728]{1,0:T(8,128)(2,1)S(1)} %get-tuple-element.86), channel_id=1, source_target_pairs={{0,24},{2,26},{4,28},{6,30},{8,0},{10,2},{12,4},{14,6},{16,8},{18,... | collective-permute-start | bytes 497672 | tf_op jit(solution)/shard_map/ppermute | solution.py:64
  244.2 2.0 fusion.17
  246.8 4.1 %collective-permute-done.43 = bf16[48,1728]{1,0:T(8,128)(2,1)S(1)} collective-permute-done((bf16[48,1728]{1,0:T(8,128)(2,1)S(1)}, bf16[48,1728]{1,0:T(8,128)(2,1)S(1)}, u32[]{:S(2)}, u32[]{:S(2)}) %collective-permute-start.43) | collective-permute-done | bytes 165920 | tf_op jit(solution)/shard_map/ppermute | solution.py:64
  250.9 3.1 %collective-permute-done.42 = bf16[48,1728]{1,0:T(8,128)(2,1)S(1)} collective-permute-done((bf16[48,1728]{1,0:T(8,128)(2,1)S(1)}, bf16[48,1728]{1,0:T(8,128)(2,1)S(1)}, u32[]{:S(2)}, u32[]{:S(2)}) %collective-permute-start.42) | collective-permute-done | bytes 165920 | tf_op jit(solution)/shard_map/ppermute | solution.py:64
  256.8 2.4 collective-permute-done.44
  (251 shorter events, 65.2 us)
Async XLA Ops:
  0.6 17.7 %copy-start = (bf16[512,768]{1,0:T(8,128)(2,1)S(1)}, bf16[512,768]{1,0:T(8,128)(2,1)}, u32[]{:S(2)}) copy-start(bf16[512,768]{1,0:T(8,128)(2,1)} %param.18) | copy-start | bytes 2359300
  2.4 19.9 %collective-permute-start.2 = (bf16[48,384]{1,0:T(8,128)(2,1)S(1)}, bf16[48,384]{1,0:T(8,128)(2,1)S(1)}, u32[]{:S(2)}, u32[]{:S(2)}) collective-permute-start(bf16[48,384]{1,0:T(8,128)(2,1)S(1)} %get-tuple-element.117), channel_id=1, source_target_pairs={{0,24},{2,26},{4,28},{6,30},{8,0},{10,2},{12,4},{14,6},{16,8},{18,... | collective-permute-start | bytes 110600 | tf_op jit(solution)/shard_map/ppermute | solution.py:64
  7.5 14.8 %collective-permute-start.1 = (bf16[48,384]{1,0:T(8,128)(2,1)S(1)}, bf16[48,384]{1,0:T(8,128)(2,1)S(1)}, u32[]{:S(2)}, u32[]{:S(2)}) collective-permute-start(bf16[48,384]{1,0:T(8,128)(2,1)S(1)} %get-tuple-element.117), channel_id=1, source_target_pairs={{0,16},{2,18},{4,20},{6,22},{8,24},{10,26},{12,28},{14,30},{16,0},... | collective-permute-start | bytes 110600 | tf_op jit(solution)/shard_map/ppermute | solution.py:64
  7.5 18.7 %collective-permute-start = (bf16[48,384]{1,0:T(8,128)(2,1)S(1)}, bf16[48,384]{1,0:T(8,128)(2,1)S(1)}, u32[]{:S(2)}, u32[]{:S(2)}) collective-permute-start(bf16[48,384]{1,0:T(8,128)(2,1)S(1)} %get-tuple-element.117), channel_id=1, source_target_pairs={{0,8},{2,10},{4,12},{6,14},{8,16},{10,18},{12,20},{14,22},{16,24},... | collective-permute-start | bytes 110600 | tf_op jit(solution)/shard_map/ppermute | solution.py:64
  8.5 19.6 %collective-permute-start.12 = (bf16[48,384]{1,0:T(8,128)(2,1)S(1)}, bf16[48,384]{1,0:T(8,128)(2,1)S(1)}, u32[]{:S(2)}, u32[]{:S(2)}) collective-permute-start(bf16[48,384]{1,0:T(8,128)(2,1)S(1)} %get-tuple-element.118), channel_id=1, source_target_pairs={{0,24},{2,26},{4,28},{6,30},{8,0},{10,2},{12,4},{14,6},{16,8},{18,... | collective-permute-start | bytes 110600 | tf_op jit(solution)/shard_map/ppermute | solution.py:64
  11.3 17.5 %collective-permute-start.11 = (bf16[48,384]{1,0:T(8,128)(2,1)S(1)}, bf16[48,384]{1,0:T(8,128)(2,1)S(1)}, u32[]{:S(2)}, u32[]{:S(2)}) collective-permute-start(bf16[48,384]{1,0:T(8,128)(2,1)S(1)} %get-tuple-element.118), channel_id=1, source_target_pairs={{0,16},{2,18},{4,20},{6,22},{8,24},{10,26},{12,28},{14,30},{16,0},... | collective-permute-start | bytes 110600 | tf_op jit(solution)/shard_map/ppermute | solution.py:64
  21.3 43.9 %copy-start.13 = (f32[512,64]{0,1:T(8,128)}, f32[512,64]{0,1:T(8,128)S(1)}, u32[]{:S(2)}) copy-start(f32[512,64]{0,1:T(8,128)S(1)} %get-tuple-element.123) | copy-start | bytes 393220
  22.3 9.7 %collective-permute-start.10 = (bf16[48,384]{1,0:T(8,128)(2,1)S(1)}, bf16[48,384]{1,0:T(8,128)(2,1)S(1)}, u32[]{:S(2)}, u32[]{:S(2)}) collective-permute-start(bf16[48,384]{1,0:T(8,128)(2,1)S(1)} %get-tuple-element.118), channel_id=1, source_target_pairs={{0,8},{2,10},{4,12},{6,14},{8,16},{10,18},{12,20},{14,22},{16,24},... | collective-permute-start | bytes 110600 | tf_op jit(solution)/shard_map/ppermute | solution.py:64
  22.3 13.4 %collective-permute-start.7 = (bf16[48,384]{1,0:T(8,128)(2,1)S(1)}, bf16[48,384]{1,0:T(8,128)(2,1)S(1)}, u32[]{:S(2)}, u32[]{:S(2)}) collective-permute-start(bf16[48,384]{1,0:T(8,128)(2,1)S(1)} %get-tuple-element.119), channel_id=1, source_target_pairs={{0,24},{2,26},{4,28},{6,30},{8,0},{10,2},{12,4},{14,6},{16,8},{18,... | collective-permute-start | bytes 110600 | tf_op jit(solution)/shard_map/ppermute | solution.py:64
  26.2 9.8 %collective-permute-start.6 = (bf16[48,384]{1,0:T(8,128)(2,1)S(1)}, bf16[48,384]{1,0:T(8,128)(2,1)S(1)}, u32[]{:S(2)}, u32[]{:S(2)}) collective-permute-start(bf16[48,384]{1,0:T(8,128)(2,1)S(1)} %get-tuple-element.119), channel_id=1, source_target_pairs={{0,16},{2,18},{4,20},{6,22},{8,24},{10,26},{12,28},{14,30},{16,0},... | collective-permute-start | bytes 110600 | tf_op jit(solution)/shard_map/ppermute | solution.py:64
  28.1 9.4 %collective-permute-start.5 = (bf16[48,384]{1,0:T(8,128)(2,1)S(1)}, bf16[48,384]{1,0:T(8,128)(2,1)S(1)}, u32[]{:S(2)}, u32[]{:S(2)}) collective-permute-start(bf16[48,384]{1,0:T(8,128)(2,1)S(1)} %get-tuple-element.119), channel_id=1, source_target_pairs={{0,8},{2,10},{4,12},{6,14},{8,16},{10,18},{12,20},{14,22},{16,24},... | collective-permute-start | bytes 110600 | tf_op jit(solution)/shard_map/ppermute | solution.py:64
  28.8 19.6 %collective-permute-start.17 = (bf16[48,2112]{1,0:T(8,128)(2,1)S(1)}, bf16[48,2112]{1,0:T(8,128)(2,1)S(1)}, u32[]{:S(2)}, u32[]{:S(2)}) collective-permute-start(bf16[48,2112]{1,0:T(8,128)(2,1)S(1)} %concatenate.101), channel_id=1, source_target_pairs={{0,24},{2,26},{4,28},{6,30},{8,0},{10,2},{12,4},{14,6},{16,8},{18,... | collective-permute-start | bytes 608264 | tf_op jit(solution)/shard_map/ppermute | solution.py:64
  32.0 17.5 %collective-permute-start.16 = (bf16[48,2112]{1,0:T(8,128)(2,1)S(1)}, bf16[48,2112]{1,0:T(8,128)(2,1)S(1)}, u32[]{:S(2)}, u32[]{:S(2)}) collective-permute-start(bf16[48,2112]{1,0:T(8,128)(2,1)S(1)} %concatenate.101), channel_id=1, source_target_pairs={{0,16},{2,18},{4,20},{6,22},{8,24},{10,26},{12,28},{14,30},{16,0},... | collective-permute-start | bytes 608264 | tf_op jit(solution)/shard_map/ppermute | solution.py:64
  35.7 13.8 %collective-permute-start.15 = (bf16[48,2112]{1,0:T(8,128)(2,1)S(1)}, bf16[48,2112]{1,0:T(8,128)(2,1)S(1)}, u32[]{:S(2)}, u32[]{:S(2)}) collective-permute-start(bf16[48,2112]{1,0:T(8,128)(2,1)S(1)} %concatenate.101), channel_id=1, source_target_pairs={{0,8},{2,10},{4,12},{6,14},{8,16},{10,18},{12,20},{14,22},{16,24},... | collective-permute-start | bytes 608264 | tf_op jit(solution)/shard_map/ppermute | solution.py:64
  36.0 6.5 %collective-permute-start.3 = (bf16[192,384]{1,0:T(8,128)(2,1)S(1)}, bf16[192,384]{1,0:T(8,128)(2,1)S(1)}, u32[]{:S(2)}, u32[]{:S(2)}) collective-permute-start(bf16[192,384]{1,0:T(8,128)(2,1)S(1)} %pad_maximum_fusion.10), channel_id=1, source_target_pairs={{0,4},{2,6},{4,0},{6,2},{8,12},{10,14},{12,8},{14,10},{16,20},{18,... | collective-permute-start | bytes 442376 | tf_op jit(solution)/shard_map/ppermute | solution.py:64
  37.5 7.3 %collective-permute-start.13 = (bf16[192,384]{1,0:T(8,128)(2,1)S(1)}, bf16[192,384]{1,0:T(8,128)(2,1)S(1)}, u32[]{:S(2)}, u32[]{:S(2)}) collective-permute-start(bf16[192,384]{1,0:T(8,128)(2,1)S(1)} %pad_maximum_fusion.12), channel_id=1, source_target_pairs={{0,4},{2,6},{4,0},{6,2},{8,12},{10,14},{12,8},{14,10},{16,20},{18,... | collective-permute-start | bytes 442376 | tf_op jit(solution)/shard_map/ppermute | solution.py:64
  42.5 5.1 %collective-permute-start.8 = (bf16[192,384]{1,0:T(8,128)(2,1)S(1)}, bf16[192,384]{1,0:T(8,128)(2,1)S(1)}, u32[]{:S(2)}, u32[]{:S(2)}) collective-permute-start(bf16[192,384]{1,0:T(8,128)(2,1)S(1)} %pad_maximum_fusion.11), channel_id=1, source_target_pairs={{0,4},{2,6},{4,0},{6,2},{8,12},{10,14},{12,8},{14,10},{16,20},{18,... | collective-permute-start | bytes 442376 | tf_op jit(solution)/shard_map/ppermute | solution.py:64
  44.8 12.5 %collective-permute-start.4 = (bf16[384,384]{1,0:T(8,128)(2,1)}, bf16[384,384]{1,0:T(8,128)(2,1)}, u32[]{:S(2)}, u32[]{:S(2)}) collective-permute-start(bf16[384,384]{1,0:T(8,128)(2,1)} %get-tuple-element.105), channel_id=1, source_target_pairs={{0,2},{2,0},{4,6},{6,4},{8,10},{10,8},{12,14},{14,12},{16,18},{18,... | collective-permute-start | bytes 884744 | tf_op jit(solution)/shard_map/ppermute | solution.py:64
  47.6 11.3 %collective-permute-start.14 = (bf16[384,384]{1,0:T(8,128)(2,1)}, bf16[384,384]{1,0:T(8,128)(2,1)}, u32[]{:S(2)}, u32[]{:S(2)}) collective-permute-start(bf16[384,384]{1,0:T(8,128)(2,1)} %get-tuple-element.109), channel_id=1, source_target_pairs={{0,2},{2,0},{4,6},{6,4},{8,10},{10,8},{12,14},{14,12},{16,18},{18,... | collective-permute-start | bytes 884744 | tf_op jit(solution)/shard_map/ppermute | solution.py:64
  48.4 12.3 %collective-permute-start.9 = (bf16[384,384]{1,0:T(8,128)(2,1)}, bf16[384,384]{1,0:T(8,128)(2,1)}, u32[]{:S(2)}, u32[]{:S(2)}) collective-permute-start(bf16[384,384]{1,0:T(8,128)(2,1)} %get-tuple-element.107), channel_id=1, source_target_pairs={{0,2},{2,0},{4,6},{6,4},{8,10},{10,8},{12,14},{14,12},{16,18},{18,... | collective-permute-start | bytes 884744 | tf_op jit(solution)/shard_map/ppermute | solution.py:64
  50.5 21.3 %collective-permute-start.18 = (bf16[192,2112]{1,0:T(8,128)(2,1)}, bf16[192,2112]{1,0:T(8,128)(2,1)S(1)}, u32[]{:S(2)}, u32[]{:S(2)}) collective-permute-start(bf16[192,2112]{1,0:T(8,128)(2,1)} %pad_maximum_fusion.4), channel_id=1, source_target_pairs={{0,4},{2,6},{4,0},{6,2},{8,12},{10,14},{12,8},{14,10},{16,20},{18,... | collective-permute-start | bytes 2433032 | tf_op jit(solution)/shard_map/ppermute | solution.py:64
  66.7 5.1 %copy-start.10 = (bf16[512,6,64]{0,2,1:T(8,128)(2,1)}, bf16[512,6,64]{0,2,1:T(8,128)(2,1)S(1)}, u32[]{:S(2)}) copy-start(bf16[512,6,64]{0,2,1:T(8,128)(2,1)S(1)} %get-tuple-element.69) | copy-start | bytes 1179652
  71.8 4.9 %copy-start.12 = (bf16[192,2112]{1,0:T(8,128)(2,1)}, bf16[192,2112]{1,0:T(8,128)(2,1)S(1)}, u32[]{:S(2)}) copy-start(bf16[192,2112]{1,0:T(8,128)(2,1)S(1)} %collective-permute-done.18) | copy-start | bytes 2433028
  76.7 11.9 %collective-permute-start.19 = (bf16[384,2112]{0,1:T(8,128)(2,1)}, bf16[384,2112]{0,1:T(8,128)(2,1)}, u32[]{:S(2)}, u32[]{:S(2)}) collective-permute-start(bf16[384,2112]{0,1:T(8,128)(2,1)} %copy.68), channel_id=1, source_target_pairs={{0,2},{2,0},{4,6},{6,4},{8,10},{10,8},{12,14},{14,12},{16,18},{18,... | collective-permute-start | bytes 4866056 | tf_op jit(solution)/shard_map/ppermute | solution.py:64
  76.7 6.5 %copy-start.2 = (f32[6,512,640]{2,1,0:T(8,128)S(1)}, f32[6,512,640]{2,1,0:T(8,128)}, u32[]{:S(2)}) copy-start(f32[6,512,640]{2,1,0:T(8,128)} %get-tuple-element.147) | copy-start | bytes 23592964
  97.7 20.0 %collective-permute-start.20 = (bf16[512,768]{0,1:T(8,128)(2,1)S(1)}, bf16[512,768]{0,1:T(8,128)(2,1)S(1)}, u32[]{:S(2)}, u32[]{:S(2)}) collective-permute-start(bf16[512,768]{0,1:T(8,128)(2,1)S(1)} %convolution_convert_fusion.5), channel_id=1, source_target_pairs={{0,1},{1,0},{2,3},{3,2},{4,5},{5,4},{6,7},{7,6},{8,9},{9,8},{10,11... | collective-permute-start | bytes 2359304 | tf_op jit(solution)/shard_map/ppermute | solution.py:111
  100.1 31.2 %copy-start.17 = (bf16[768,512]{1,0:T(8,128)(2,1)}, bf16[768,512]{1,0:T(8,128)(2,1)S(1)}, u32[]{:S(2)}) copy-start(bf16[768,512]{1,0:T(8,128)(2,1)S(1)} %fusion.22) | copy-start | bytes 2359300
  129.9 20.8 %collective-permute-start.22 = (bf16[512,768]{0,1:T(8,128)(2,1)}, bf16[512,768]{0,1:T(8,128)(2,1)}, u32[]{:S(2)}, u32[]{:S(2)}) collective-permute-start(bf16[512,768]{0,1:T(8,128)(2,1)} %fusion.19), channel_id=1, source_target_pairs={{0,1},{1,0},{2,3},{3,2},{4,5},{5,4},{6,7},{7,6},{8,9},{9,8},{10,11... | collective-permute-start | bytes 2359304 | tf_op jit(solution)/shard_map/ppermute | solution.py:111
  134.6 44.7 %collective-permute-start.21 = (bf16[512,768]{0,1:T(8,128)(2,1)}, bf16[512,768]{0,1:T(8,128)(2,1)}, u32[]{:S(2)}, u32[]{:S(2)}) collective-permute-start(bf16[512,768]{0,1:T(8,128)(2,1)} %convolution_convert_fusion.3), channel_id=1, source_target_pairs={{0,1},{1,0},{2,3},{3,2},{4,5},{5,4},{6,7},{7,6},{8,9},{9,8},{10,11... | collective-permute-start | bytes 2359304 | tf_op jit(solution)/shard_map/ppermute | solution.py:111
  143.8 9.2 %copy-start.6 = (f32[512,768]{0,1:T(8,128)S(1)}, f32[512,768]{0,1:T(8,128)}, u32[]{:S(2)}) copy-start(f32[512,768]{0,1:T(8,128)} %copy-done.5) | copy-start | bytes 4718596
  143.8 9.2 %copy-start.18 = (bf16[768,512]{1,0:T(8,128)(2,1)S(1)}, bf16[768,512]{1,0:T(8,128)(2,1)}, u32[]{:S(2)}) copy-start(bf16[768,512]{1,0:T(8,128)(2,1)} %copy-done.17) | copy-start | bytes 2359300
  143.8 79.0 %collective-permute-start.39 = (bf16[384,1728]{0,1:T(8,128)(2,1)}, bf16[384,1728]{0,1:T(8,128)(2,1)}, u32[]{:S(2)}, u32[]{:S(2)}) collective-permute-start(bf16[384,1728]{0,1:T(8,128)(2,1)} %copy.82), channel_id=1, source_target_pairs={{0,2},{2,0},{4,6},{6,4},{8,10},{10,8},{12,14},{14,12},{16,18},{18,... | collective-permute-start | bytes 3981320 | tf_op jit(solution)/shard_map/ppermute | solution.py:64
  157.0 5.7 %slice-start = ((s8[7864320]{0:T(1024)(128)(4,1)}), s8[4194304]{0:T(1024)(128)(4,1)S(1)}, s32[]{:S(2)}) async-start(s8[7864320]{0:T(1024)(128)(4,1)} %bitcast.95), calls=%async_computation | async-start | bytes 8388608
  157.7 5.1 %slice-start.1 = ((s8[7864320]{0:T(1024)(128)(4,1)}), s8[3670016]{0:T(1024)(128)(4,1)S(1)}, s32[]{:S(2)}) async-start(s8[7864320]{0:T(1024)(128)(4,1)} %bitcast.95), calls=%async_computation.1 | async-start | bytes 7340032
  157.7 5.1 %copy-start.26 = (bf16[512,6,64]{0,2,1:T(8,128)(2,1)S(1)}, bf16[512,6,64]{0,2,1:T(8,128)(2,1)}, u32[]{:S(2)}) copy-start(bf16[512,6,64]{0,2,1:T(8,128)(2,1)} %copy-done.25) | copy-start | bytes 1179652
  167.4 15.5 %collective-permute-start.45 = (bf16[384,384]{1,0:T(8,128)(2,1)}, bf16[384,384]{1,0:T(8,128)(2,1)S(1)}, u32[]{:S(2)}, u32[]{:S(2)}) collective-permute-start(bf16[384,384]{1,0:T(8,128)(2,1)} %slice.388), channel_id=1, source_target_pairs={{0,2},{2,0},{4,6},{6,4},{8,10},{10,8},{12,14},{14,12},{16,18},{18,... | collective-permute-start | bytes 884744 | tf_op jit(solution)/shard_map/ppermute | solution.py:64
  176.8 7.8 %collective-permute-start.24 = (bf16[384,384]{1,0:T(8,128)(2,1)S(1)}, bf16[384,384]{1,0:T(8,128)(2,1)S(1)}, u32[]{:S(2)}, u32[]{:S(2)}) collective-permute-start(bf16[384,384]{1,0:T(8,128)(2,1)S(1)} %get-tuple-element.75), channel_id=1, source_target_pairs={{0,2},{2,0},{4,6},{6,4},{8,10},{10,8},{12,14},{14,12},{16,18},{18,... | collective-permute-start | bytes 884744 | tf_op jit(solution)/shard_map/ppermute | solution.py:64
  177.3 7.8 %collective-permute-start.34 = (bf16[384,384]{1,0:T(8,128)(2,1)S(1)}, bf16[384,384]{1,0:T(8,128)(2,1)S(1)}, u32[]{:S(2)}, u32[]{:S(2)}) collective-permute-start(bf16[384,384]{1,0:T(8,128)(2,1)S(1)} %get-tuple-element.76), channel_id=1, source_target_pairs={{0,2},{2,0},{4,6},{6,4},{8,10},{10,8},{12,14},{14,12},{16,18},{18,... | collective-permute-start | bytes 884744 | tf_op jit(solution)/shard_map/ppermute | solution.py:64
  179.2 5.9 %collective-permute-start.29 = (bf16[384,384]{1,0:T(8,128)(2,1)S(1)}, bf16[384,384]{1,0:T(8,128)(2,1)S(1)}, u32[]{:S(2)}, u32[]{:S(2)}) collective-permute-start(bf16[384,384]{1,0:T(8,128)(2,1)S(1)} %get-tuple-element.77), channel_id=1, source_target_pairs={{0,2},{2,0},{4,6},{6,4},{8,10},{10,8},{12,14},{14,12},{16,18},{18,... | collective-permute-start | bytes 884744 | tf_op jit(solution)/shard_map/ppermute | solution.py:64
  183.0 45.8 %collective-permute-start.23 = (bf16[512,768]{0,1:T(8,128)(2,1)S(1)}, bf16[512,768]{0,1:T(8,128)(2,1)}, u32[]{:S(2)}, u32[]{:S(2)}) collective-permute-start(bf16[512,768]{0,1:T(8,128)(2,1)S(1)} %convolution_convert_fusion.4), channel_id=1, source_target_pairs={{0,1},{1,0},{2,3},{3,2},{4,5},{5,4},{6,7},{7,6},{8,9},{9,8},{10,11... | collective-permute-start | bytes 2359304 | tf_op jit(solution)/shard_map/ppermute | solution.py:111
  184.6 6.9 %collective-permute-start.46 = (bf16[192,384]{1,0:T(8,128)(2,1)S(1)}, bf16[192,384]{1,0:T(8,128)(2,1)S(1)}, u32[]{:S(2)}, u32[]{:S(2)}) collective-permute-start(bf16[192,384]{1,0:T(8,128)(2,1)S(1)} %slice.390), channel_id=1, source_target_pairs={{0,4},{2,6},{4,0},{6,2},{8,12},{10,14},{12,8},{14,10},{16,20},{18,... | collective-permute-start | bytes 442376 | tf_op jit(solution)/shard_map/ppermute | solution.py:64
  185.5 9.1 %collective-permute-start.30 = (bf16[192,384]{1,0:T(8,128)(2,1)S(1)}, bf16[192,384]{1,0:T(8,128)(2,1)S(1)}, u32[]{:S(2)}, u32[]{:S(2)}) collective-permute-start(bf16[192,384]{1,0:T(8,128)(2,1)S(1)} %slice.365), channel_id=1, source_target_pairs={{0,4},{2,6},{4,0},{6,2},{8,12},{10,14},{12,8},{14,10},{16,20},{18,... | collective-permute-start | bytes 442376 | tf_op jit(solution)/shard_map/ppermute | solution.py:64
  187.1 10.7 %collective-permute-start.25 = (bf16[192,384]{1,0:T(8,128)(2,1)S(1)}, bf16[192,384]{1,0:T(8,128)(2,1)S(1)}, u32[]{:S(2)}, u32[]{:S(2)}) collective-permute-start(bf16[192,384]{1,0:T(8,128)(2,1)S(1)} %slice.357), channel_id=1, source_target_pairs={{0,4},{2,6},{4,0},{6,2},{8,12},{10,14},{12,8},{14,10},{16,20},{18,... | collective-permute-start | bytes 442376 | tf_op jit(solution)/shard_map/ppermute | solution.py:64
  191.4 8.2 %collective-permute-start.35 = (bf16[192,384]{1,0:T(8,128)(2,1)S(1)}, bf16[192,384]{1,0:T(8,128)(2,1)S(1)}, u32[]{:S(2)}, u32[]{:S(2)}) collective-permute-start(bf16[192,384]{1,0:T(8,128)(2,1)S(1)} %slice.373), channel_id=1, source_target_pairs={{0,4},{2,6},{4,0},{6,2},{8,12},{10,14},{12,8},{14,10},{16,20},{18,... | collective-permute-start | bytes 442376 | tf_op jit(solution)/shard_map/ppermute | solution.py:64
  194.6 27.4 %copy-start.23 = (bf16[48,3,384]{2,0,1:T(8,128)(2,1)S(1)}, bf16[48,3,384]{2,0,1:T(8,128)(2,1)}, u32[]{:S(2)}) copy-start(bf16[48,3,384]{2,0,1:T(8,128)(2,1)} %param.22) | copy-start | bytes 331780
  194.6 6.9 %collective-permute-start.31 = (bf16[48,384]{1,0:T(8,128)(2,1)S(1)}, bf16[48,384]{1,0:T(8,128)(2,1)S(1)}, u32[]{:S(2)}, u32[]{:S(2)}) collective-permute-start(bf16[48,384]{1,0:T(8,128)(2,1)S(1)} %get-tuple-element.99), channel_id=1, source_target_pairs={{0,24},{2,26},{4,28},{6,30},{8,0},{10,2},{12,4},{14,6},{16,8},{18,... | collective-permute-start | bytes 110600 | tf_op jit(solution)/shard_map/ppermute | solution.py:64
  197.8 6.1 %collective-permute-start.33 = (bf16[48,384]{1,0:T(8,128)(2,1)S(1)}, bf16[48,384]{1,0:T(8,128)(2,1)S(1)}, u32[]{:S(2)}, u32[]{:S(2)}) collective-permute-start(bf16[48,384]{1,0:T(8,128)(2,1)S(1)} %get-tuple-element.100), channel_id=1, source_target_pairs={{0,8},{2,10},{4,12},{6,14},{8,16},{10,18},{12,20},{14,22},{16,24},... | collective-permute-start | bytes 110600 | tf_op jit(solution)/shard_map/ppermute | solution.py:64
  199.6 5.2 %collective-permute-start.32 = (bf16[48,384]{1,0:T(8,128)(2,1)S(1)}, bf16[48,384]{1,0:T(8,128)(2,1)S(1)}, u32[]{:S(2)}, u32[]{:S(2)}) collective-permute-start(bf16[48,384]{1,0:T(8,128)(2,1)S(1)} %get-tuple-element.101), channel_id=1, source_target_pairs={{0,16},{2,18},{4,20},{6,22},{8,24},{10,26},{12,28},{14,30},{16,0},... | collective-permute-start | bytes 110600 | tf_op jit(solution)/shard_map/ppermute | solution.py:64
  201.6 5.2 %collective-permute-start.26 = (bf16[48,384]{1,0:T(8,128)(2,1)S(1)}, bf16[48,384]{1,0:T(8,128)(2,1)S(1)}, u32[]{:S(2)}, u32[]{:S(2)}) collective-permute-start(bf16[48,384]{1,0:T(8,128)(2,1)S(1)} %get-tuple-element.96), channel_id=1, source_target_pairs={{0,24},{2,26},{4,28},{6,30},{8,0},{10,2},{12,4},{14,6},{16,8},{18,... | collective-permute-start | bytes 110600 | tf_op jit(solution)/shard_map/ppermute | solution.py:64
  203.9 5.9 %collective-permute-start.28 = (bf16[48,384]{1,0:T(8,128)(2,1)S(1)}, bf16[48,384]{1,0:T(8,128)(2,1)S(1)}, u32[]{:S(2)}, u32[]{:S(2)}) collective-permute-start(bf16[48,384]{1,0:T(8,128)(2,1)S(1)} %get-tuple-element.97), channel_id=1, source_target_pairs={{0,8},{2,10},{4,12},{6,14},{8,16},{10,18},{12,20},{14,22},{16,24},... | collective-permute-start | bytes 110600 | tf_op jit(solution)/shard_map/ppermute | solution.py:64
  204.8 5.3 %collective-permute-start.27 = (bf16[48,384]{1,0:T(8,128)(2,1)S(1)}, bf16[48,384]{1,0:T(8,128)(2,1)S(1)}, u32[]{:S(2)}, u32[]{:S(2)}) collective-permute-start(bf16[48,384]{1,0:T(8,128)(2,1)S(1)} %get-tuple-element.98), channel_id=1, source_target_pairs={{0,16},{2,18},{4,20},{6,22},{8,24},{10,26},{12,28},{14,30},{16,0},... | collective-permute-start | bytes 110600 | tf_op jit(solution)/shard_map/ppermute | solution.py:64
  206.8 5.2 %collective-permute-start.36 = (bf16[48,384]{1,0:T(8,128)(2,1)S(1)}, bf16[48,384]{1,0:T(8,128)(2,1)S(1)}, u32[]{:S(2)}, u32[]{:S(2)}) collective-permute-start(bf16[48,384]{1,0:T(8,128)(2,1)S(1)} %get-tuple-element.102), channel_id=1, source_target_pairs={{0,24},{2,26},{4,28},{6,30},{8,0},{10,2},{12,4},{14,6},{16,8},{18,... | collective-permute-start | bytes 110600 | tf_op jit(solution)/shard_map/ppermute | solution.py:64
  209.8 5.8 %collective-permute-start.38 = (bf16[48,384]{1,0:T(8,128)(2,1)S(1)}, bf16[48,384]{1,0:T(8,128)(2,1)S(1)}, u32[]{:S(2)}, u32[]{:S(2)}) collective-permute-start(bf16[48,384]{1,0:T(8,128)(2,1)S(1)} %get-tuple-element.103), channel_id=1, source_target_pairs={{0,8},{2,10},{4,12},{6,14},{8,16},{10,18},{12,20},{14,22},{16,24},... | collective-permute-start | bytes 110600 | tf_op jit(solution)/shard_map/ppermute | solution.py:64
  210.1 5.5 %collective-permute-start.37 = (bf16[48,384]{1,0:T(8,128)(2,1)S(1)}, bf16[48,384]{1,0:T(8,128)(2,1)S(1)}, u32[]{:S(2)}, u32[]{:S(2)}) collective-permute-start(bf16[48,384]{1,0:T(8,128)(2,1)S(1)} %get-tuple-element.104), channel_id=1, source_target_pairs={{0,16},{2,18},{4,20},{6,22},{8,24},{10,26},{12,28},{14,30},{16,0},... | collective-permute-start | bytes 110600 | tf_op jit(solution)/shard_map/ppermute | solution.py:64
  212.1 5.2 %collective-permute-start.47 = (bf16[48,384]{1,0:T(8,128)(2,1)S(1)}, bf16[48,384]{1,0:T(8,128)(2,1)S(1)}, u32[]{:S(2)}, u32[]{:S(2)}) collective-permute-start(bf16[48,384]{1,0:T(8,128)(2,1)S(1)} %get-tuple-element.93), channel_id=1, source_target_pairs={{0,24},{2,26},{4,28},{6,30},{8,0},{10,2},{12,4},{14,6},{16,8},{18,... | collective-permute-start | bytes 110600 | tf_op jit(solution)/shard_map/ppermute | solution.py:64
  215.6 5.8 %collective-permute-start.49 = (bf16[48,384]{1,0:T(8,128)(2,1)S(1)}, bf16[48,384]{1,0:T(8,128)(2,1)S(1)}, u32[]{:S(2)}, u32[]{:S(2)}) collective-permute-start(bf16[48,384]{1,0:T(8,128)(2,1)S(1)} %get-tuple-element.94), channel_id=1, source_target_pairs={{0,8},{2,10},{4,12},{6,14},{8,16},{10,18},{12,20},{14,22},{16,24},... | collective-permute-start | bytes 110600 | tf_op jit(solution)/shard_map/ppermute | solution.py:64
  215.6 5.8 %collective-permute-start.48 = (bf16[48,384]{1,0:T(8,128)(2,1)S(1)}, bf16[48,384]{1,0:T(8,128)(2,1)S(1)}, u32[]{:S(2)}, u32[]{:S(2)}) collective-permute-start(bf16[48,384]{1,0:T(8,128)(2,1)S(1)} %get-tuple-element.95), channel_id=1, source_target_pairs={{0,16},{2,18},{4,20},{6,22},{8,24},{10,26},{12,28},{14,30},{16,0},... | collective-permute-start | bytes 110600 | tf_op jit(solution)/shard_map/ppermute | solution.py:64
  227.8 12.9 %collective-permute-start.40 = (bf16[192,1728]{1,0:T(8,128)(2,1)S(1)}, bf16[192,1728]{1,0:T(8,128)(2,1)S(1)}, u32[]{:S(2)}, u32[]{:S(2)}) collective-permute-start(bf16[192,1728]{1,0:T(8,128)(2,1)S(1)} %slice.381), channel_id=1, source_target_pairs={{0,4},{2,6},{4,0},{6,2},{8,12},{10,14},{12,8},{14,10},{16,20},{18,... | collective-permute-start | bytes 1990664 | tf_op jit(solution)/shard_map/ppermute | solution.py:64
  240.9 6.0 %collective-permute-start.41 = (bf16[48,1728]{1,0:T(8,128)(2,1)S(1)}, bf16[48,1728]{1,0:T(8,128)(2,1)S(1)}, u32[]{:S(2)}, u32[]{:S(2)}) collective-permute-start(bf16[48,1728]{1,0:T(8,128)(2,1)S(1)} %get-tuple-element.86), channel_id=1, source_target_pairs={{0,24},{2,26},{4,28},{6,30},{8,0},{10,2},{12,4},{14,6},{16,8},{18,... | collective-permute-start | bytes 497672 | tf_op jit(solution)/shard_map/ppermute | solution.py:64
  243.6 7.3 %collective-permute-start.43 = (bf16[48,1728]{1,0:T(8,128)(2,1)S(1)}, bf16[48,1728]{1,0:T(8,128)(2,1)S(1)}, u32[]{:S(2)}, u32[]{:S(2)}) collective-permute-start(bf16[48,1728]{1,0:T(8,128)(2,1)S(1)} %get-tuple-element.87), channel_id=1, source_target_pairs={{0,8},{2,10},{4,12},{6,14},{8,16},{10,18},{12,20},{14,22},{16,24},... | collective-permute-start | bytes 497672 | tf_op jit(solution)/shard_map/ppermute | solution.py:64
  243.6 10.5 %collective-permute-start.42 = (bf16[48,1728]{1,0:T(8,128)(2,1)S(1)}, bf16[48,1728]{1,0:T(8,128)(2,1)S(1)}, u32[]{:S(2)}, u32[]{:S(2)}) collective-permute-start(bf16[48,1728]{1,0:T(8,128)(2,1)S(1)} %get-tuple-element.88), channel_id=1, source_target_pairs={{0,16},{2,18},{4,20},{6,22},{8,24},{10,26},{12,28},{14,30},{16,0},... | collective-permute-start | bytes 497672 | tf_op jit(solution)/shard_map/ppermute | solution.py:64
  244.2 15.5 %copy-start.1 = (bf16[512,768]{1,0:T(8,128)(2,1)S(1)}, bf16[512,768]{1,0:T(8,128)(2,1)}, u32[]{:S(2)}) copy-start(bf16[512,768]{1,0:T(8,128)(2,1)} %param.18) | copy-start | bytes 2359300
  246.3 8.2 %copy-start.22 = (bf16[48,2,576]{2,1,0:T(2,128)(2,1)S(1)}, bf16[48,2,576]{2,1,0:T(2,128)(2,1)}, u32[]{:S(2)}) copy-start(bf16[48,2,576]{2,1,0:T(2,128)(2,1)} %param.25) | copy-start | bytes 331780
  255.6 3.6 %collective-permute-start.44 = (f32[2,48]{1,0:T(2,128)S(1)}, f32[2,48]{1,0:T(2,128)S(1)}, u32[]{:S(2)}, u32[]{:S(2)}) collective-permute-start(f32[2,48]{1,0:T(2,128)S(1)} %pad_maximum_fusion.14), channel_id=1, source_target_pairs={{0,1},{1,0},{2,3},{3,2},{4,5},{5,4},{6,7},{7,6},{8,9},{9,8},{10,11... | collective-permute-start | bytes 1160 | tf_op jit(solution)/shard_map/ppermute | solution.py:259
  (23 other events, 38.8 us)

commit v2 on v1

v2 whole, which is shorter than its diff:
```python
import functools

import jax
import jax.numpy as jnp
from jax import lax
from jax.experimental import pallas as pl
from jax.experimental.pallas import tpu as pltpu
from jax.sharding import PartitionSpec as P

HD = 64
HALF = 64
LANES = 128
BLOCK = 128
WINDOW = 256
CHUNKS = 2
PIECES = 4

EPSILON = 1e-05
THETA = 10000.0
MASKED = -1e30
SCALE = HD ** (-0.5)

NN = (((1,), (0,)), ((), ()))
NT = (((1,), (1,)), ((), ()))
TN = (((0,), (0,)), ((), ()))


def product(left, right, dims=NN):
    return lax.dot_general(left, right, dims, preferred_element_type=jnp.float32)


def low(values):
    return values.astype(jnp.bfloat16)


def wide(values):
    return values.astype(jnp.float32)


def levels_of(count):
    levels, stride = [], count
    while stride > 1:
        size = 4 if stride % 8 == 0 else 2 if stride % 2 == 0 else stride
        stride //= size
        levels.append((stride, size))
    return levels


def shifted(values, count, level, step):
    stride, size = level
    pairs = []
    for device in range(count):
        digit = (device // stride) % size
        pairs.append((device, device + ((digit + step) % size - digit) * stride))
    return lax.ppermute(values, "dp", pairs)


def swapped(values):
    return lax.ppermute(values, "tensor", [(0, 1), (1, 0)])


def is_plain(count, rows):
    return levels_of(count) == [(4, 4), (2, 2), (1, 2)] and rows % 16 == 0


def gather_rows(shard, count):
    levels = levels_of(count)
    if is_plain(count, shard.shape[0]):
        first, second, third = levels
        held = stack_rows([shard] + [shifted(shard, count, first, step) for step in range(1, 4)])
        other = shifted(held, count, second, 1)
        return [held, other, shifted(held, count, third, 1), shifted(other, count, third, 1)]
    held = shard
    for level in levels:
        held = jnp.concatenate(
            [held] + [shifted(held, count, level, step) for step in range(1, level[1])], axis=0
        )
    return jnp.split(held, PIECES, axis=0)


def scatter_rows(kept, sent, count, rows):
    levels = levels_of(count)
    if is_plain(count, rows):
        first, second, third = levels
        kept, sent = add_split(kept, shifted(sent, count, third, -1), 2)
        pieces = add_split(kept, shifted(sent, count, second, -1), 4)
        received = [shifted(pieces[step], count, first, -step) for step in range(1, 4)]
        return add_all([pieces[0]] + received)
    held = jnp.concatenate([kept, sent], axis=0)
    for level in reversed(levels):
        size = level[1]
        pieces = held.reshape(size, held.shape[0] // size, held.shape[1])
        total = wide(pieces[0])
        for step in range(1, size):
            total = total + wide(shifted(pieces[step], count, level, -step))
        held = total if level == levels[0] else low(total)
    return held


def placement(count, width):
    device = lax.axis_index("dp")
    place = jnp.arange(count)
    owner, weight = jnp.zeros_like(place), 1
    for stride, size in levels_of(count):
        step = (place // weight) % size
        owner = owner + ((device // stride) % size - step + size) % size * stride
        weight *= size
    rows = width // count
    natural = (owner[:, None] * rows + jnp.arange(rows)[None, :]).reshape(width)
    return low(natural[None, :] == jnp.arange(width)[:, None])


def spec(block, *place):
    return pl.BlockSpec(block, lambda step: place)


def run(body, out_shapes, operands, specs=None, scratch=(), flops=0, limit=40):
    size = sum(a.size * a.dtype.itemsize for a in [*operands, *out_shapes])
    grid = () if specs is None else (1,)
    specs = [None] * len(operands) if specs is None else specs
    specs = [
        pl.BlockSpec(memory_space=pltpu.VMEM) if given is None else given for given in specs
    ]
    return pl.pallas_call(
        body,
        out_shape=out_shapes,
        grid=grid,
        in_specs=specs,
        out_specs=[pl.BlockSpec(memory_space=pltpu.VMEM)] * len(out_shapes),
        scratch_shapes=scratch,
        compiler_params=pltpu.CompilerParams(vmem_limit_bytes=limit * 1024 * 1024),
        cost_estimate=pl.CostEstimate(flops=flops, bytes_accessed=size, transcendentals=0),
    )(*operands)


def half(*shape):
    return jax.ShapeDtypeStruct(shape, jnp.bfloat16)


def full(*shape):
    return jax.ShapeDtypeStruct(shape, jnp.float32)


def stack_rows(pieces):
    rows, width = pieces[0].shape

    def body(*refs):
        for number, ref in enumerate(refs[:-1]):
            refs[-1][number * rows : (number + 1) * rows, :] = ref[...]

    return run(body, [half(rows * len(pieces), width)], pieces)[0]


def add_split(left, right, parts):
    rows, width = left.shape
    rows //= parts

    def body(left_ref, right_ref, *outs):
        for number, out in enumerate(outs):
            part = slice(number * rows, (number + 1) * rows)
            out[...] = low(wide(left_ref[part, :]) + wide(right_ref[part, :]))

    return run(body, [half(rows, width)] * parts, [left, right])


def add_all(pieces):
    def body(*refs):
        total = wide(refs[0][...])
        for ref in refs[1:-1]:
            total = total + wide(ref[...])
        refs[-1][...] = total

    return run(body, [full(*pieces[0].shape)], pieces)[0]


def normalize(values):
    average = jnp.mean(values, axis=-1, keepdims=True)
    centered = values - average
    variance = jnp.mean(centered * centered, axis=-1, keepdims=True)
    inverse = lax.rsqrt(variance + EPSILON)
    return centered * inverse, inverse


def norm_back(scaled, normed, inverse):
    first = jnp.mean(scaled, axis=-1, keepdims=True)
    second = jnp.mean(scaled * normed, axis=-1, keepdims=True)
    return inverse * (scaled - first - normed * second)


def partner(values):
    lane = lax.broadcasted_iota(jnp.int32, values.shape, 1)
    return jnp.where(
        lane % HD < HD // 2,
        pltpu.roll(values, LANES - HD // 2, 1),
        pltpu.roll(values, HD // 2, 1),
    )


def group(number):
    return slice(number * LANES, (number + 1) * LANES)


def rows_of(refs):
    return jnp.concatenate([ref[...] for ref in refs], axis=0)


def both_heads(values):
    lane = lax.broadcasted_iota(jnp.int32, values.shape, 1)
    nothing = jnp.zeros_like(values)
    return jnp.concatenate(
        [jnp.where(lane < HD, values, nothing), jnp.where(lane < HD, nothing, values)], axis=0
    )


def one_pair(values):
    rows = values.shape[0] // 2
    lane = lax.broadcasted_iota(jnp.int32, (rows, values.shape[1]), 1)
    return jnp.where(lane < HD, values[:rows], values[rows:])


def tiles_of(count, inner):
    for block in range(count // BLOCK):
        start = min(max(block * BLOCK - HALF, 0), count - WINDOW)
        for pair in range(inner // LANES):
            number = block * (inner // LANES) + pair
            yield number, pair, slice(block * BLOCK, (block + 1) * BLOCK), slice(start, start + WINDOW)


def prepare(tokens, cotangent, order):
    count, width = tokens.shape

    def body(tokens_ref, cotangent_ref, order_ref, inputs_ref, normed_ref, upstream_ref):
        inputs = product(tokens_ref[...], order_ref[...])
        inputs_ref[...] = low(inputs)
        normed_ref[...] = low(normalize(inputs)[0])
        upstream_ref[...] = low(product(cotangent_ref[...], order_ref[...]))

    return run(
        body, [half(count, width)] * 3, [tokens, cotangent, order], flops=4 * count * width * width
    )


def attend_shares(normed, pieces, cosine, sine, column, row):
    count, width = normed.shape
    inner = pieces[0].shape[1] // 2
    tiles = list(tiles_of(count, inner))

    def body(normed_ref, a, b, c, d, cosine_ref, sine_ref, column_ref, row_ref, query_ref, keys_ref, shares_ref):
        projected = product(normed_ref[...], rows_of((a, b, c, d)))
        cosine, sine = cosine_ref[...], sine_ref[...]
        for number in range(inner // LANES):
            part = projected[:, group(number)]
            query_ref[:, group(number)] = low(part * cosine + partner(part) * sine)
            part = projected[:, group(number + inner // LANES)]
            keys_ref[:, group(number)] = low(part * cosine + partner(part) * sine)
        for number, pair, queries, window in tiles:
            if pair == 0:
                near = lax.broadcasted_iota(jnp.int32, (WINDOW, BLOCK), 0) + window.start
                near = near - lax.broadcasted_iota(jnp.int32, (WINDOW, BLOCK), 1) - queries.start
                allowed = (jnp.abs(near) <= HALF) & (column_ref[window, :] == row_ref[:, queries])
                allowed = jnp.concatenate([allowed.astype(jnp.float32)] * 2, axis=1) > 0.5
            query = both_heads(query_ref[queries, group(pair)])
            scores = product(keys_ref[window, group(pair)], query, NT) * SCALE
            scores = jnp.where(allowed, scores, MASKED)
            powers = jnp.exp(scores - jnp.max(scores, axis=0, keepdims=True))
            total = jnp.sum(powers, axis=0, keepdims=True)
            shares_ref[number] = low(powers * (1.0 / total))

    return run(
        body,
        [half(count, inner), half(count, inner), half(len(tiles), WINDOW, 2 * BLOCK)],
        [normed, *pieces, cosine, sine, column, row],
        flops=4 * count * width * inner + len(tiles) * 4 * WINDOW * BLOCK * LANES,
    )


def attend_values(normed, pieces, shares):
    count, width = normed.shape
    inner = pieces[0].shape[1] // 2
    tiles = list(tiles_of(count, inner))
    rows = count // CHUNKS

    def body(normed_ref, a, b, c, d, shares_ref, values_ref, context_ref, *outs):
        matrix = rows_of((a, b, c, d))
        values_ref[...] = low(product(normed_ref[...], matrix[:, :inner]))
        for number, pair, queries, window in tiles:
            both = product(shares_ref[number], values_ref[window, group(pair)], TN)
            context_ref[queries, group(pair)] = low(one_pair(both))
        for number, out in enumerate(outs):
            part = context_ref[number * rows : (number + 1) * rows, :]
            out[...] = low(product(part, matrix[:, inner:], NT))

    return run(
        body,
        [half(count, inner), half(count, inner)] + [half(rows, width)] * CHUNKS,
        [normed, *pieces, shares],
        flops=4 * count * width * inner + len(tiles) * 4 * WINDOW * BLOCK * LANES,
    )


def feed_forward(number, inputs, upstream, own, other, pieces, hidden):
    count, width = inputs.shape
    rows = count // CHUNKS

    def body(inputs_ref, upstream_ref, own_ref, other_ref, a, b, c, d, e, f, g, h,
             middle_ref, normed_ref, mixed_ref, gates_ref, forward_ref, back_ref):
        middle = wide(inputs_ref[...]) + (wide(own_ref[...]) + wide(other_ref[...]))
        middle_ref[...] = middle
        normed = low(normalize(middle)[0])
        normed_ref[...] = normed
        matrix = rows_of((a, b, c, d))
        down = rows_of((e, f, g, h))
        gates = product(normed, matrix)
        active, factor = gates[:, :hidden], gates[:, hidden:]
        chance = 0.5 + 0.5 * lax.erf(active * 0.7071067811865476)
        bent = active * chance
        mixed = low(bent * factor)
        mixed_ref[...] = mixed
        forward_ref[...] = low(product(mixed, down, NT))
        grad_mixed = product(upstream_ref[...], down)
        slope = chance + active * (0.3989422804014327 * jnp.exp(-0.5 * active * active))
        grad_active = low(grad_mixed * factor * slope)
        grad_factor = low(grad_mixed * bent)
        gates_ref[:, :hidden] = grad_active
        gates_ref[:, hidden:] = grad_factor
        back_ref[...] = low(
            product(grad_active, matrix[:, :hidden], NT) + product(grad_factor, matrix[:, hidden:], NT)
        )

    chunk = spec((rows, width), number, 0)
    return run(
        body,
        [full(rows, width), half(rows, width), half(rows, hidden), half(rows, 2 * hidden), half(rows, width), half(rows, width)],
        [inputs, upstream, own, other, *pieces, *pieces],
        [chunk, chunk, None, None]
        + [spec((width // PIECES, 2 * hidden), 0, 0)] * PIECES
        + [spec((width // PIECES, hidden), 0, 2)] * PIECES,
        flops=2 * rows * width * hidden * 6,
    )


def feed_forward_grads(normed, mixed, gates, upstream):
    count, width = upstream.shape
    hidden = mixed[0].shape[1]

    def body(*refs):
        normed, mixed, gates = (rows_of(refs[i * CHUNKS : (i + 1) * CHUNKS]) for i in range(3))
        upstream = refs[3 * CHUNKS][...]
        for number, out in enumerate(refs[3 * CHUNKS + 1 :]):
            part = slice(number * width // 2, (number + 1) * width // 2)
            out[:, : 2 * hidden] = low(product(normed[:, part], gates, TN))
            out[:, 2 * hidden :] = low(product(upstream[:, part], mixed, TN))

    return run(
        body,
        [half(width // 2, 3 * hidden)] * 2,
        [*normed, *mixed, *gates, upstream],
        flops=2 * count * width * hidden * 3,
    )


def add_output(middle, own, other, order):
    rows, width = middle[0].shape

    def body(*refs):
        order = refs[3 * CHUNKS][...]
        for number in range(CHUNKS):
            middle, own, other = (refs[number + i * CHUNKS][...] for i in range(3))
            total = low(middle + (wide(own) + wide(other)))
            refs[-1][number * rows : (number + 1) * rows, :] = low(product(total, order, NT))

    return run(
        body,
        [half(rows * CHUNKS, width)],
        [*middle, *own, *other, order],
        flops=2 * rows * CHUNKS * width * width,
    )[0]


def attend_back_values(upstream, middle, own, other, pieces, context, shares):
    count, width = upstream.shape
    inner = context.shape[1]
    tiles = list(tiles_of(count, inner))
    rows = count // CHUNKS

    def body(upstream_ref, *refs):
        middle, own, other = (refs[i * CHUNKS : (i + 1) * CHUNKS] for i in range(3))
        refs = refs[3 * CHUNKS :]
        matrix = rows_of(refs[:PIECES])
        context_ref, shares_ref, grad_middle_ref, branch_ref, grad_context_ref, grad_values_ref, total_ref = refs[PIECES:]
        for number in range(CHUNKS):
            part = slice(number * rows, (number + 1) * rows)
            normed, inverse = normalize(middle[number][...])
            scaled = wide(own[number][...]) + wide(other[number][...])
            grad_middle = wide(upstream_ref[part, :]) + norm_back(scaled, normed, inverse)
            grad_middle_ref[part, :] = grad_middle
            branch_ref[part, :] = low(grad_middle)
        grad_context_ref[...] = low(product(branch_ref[...], matrix))
        total_ref[...] = jnp.zeros_like(total_ref)
        for number, pair, queries, window in tiles:
            upper = both_heads(grad_context_ref[queries, group(pair)])
            total_ref[window, group(pair)] += product(shares_ref[number], upper)
        grad_values_ref[...] = low(total_ref[...])

    return run(
        body,
        [full(count, width), half(count, width), half(count, inner), half(count, inner)],
        [upstream, *middle, *own, *other, *pieces, context, shares],
        [None] * (1 + 3 * CHUNKS) + [spec((width // PIECES, inner), 0, 1)] * PIECES + [None] * 2,
        scratch=[pltpu.VMEM((count, inner), jnp.float32)],
        flops=2 * count * width * inner + len(tiles) * 4 * WINDOW * BLOCK * LANES,
    )


def attend_back_shares(query, keys, values, grad_context, shares, grad_values, cosine, sine, query_keys, values_out):
    count, inner = query.shape
    width = query_keys[0].shape[0] * PIECES
    tiles = list(tiles_of(count, inner))

    def body(query_ref, keys_ref, values_ref, grad_context_ref, shares_ref, grad_values_ref, cosine_ref, sine_ref,
             a, b, c, d, e, f, g, h, grad_ref, back_ref, total_ref):
        total_ref[...] = jnp.zeros_like(total_ref)
        cosine, sine = cosine_ref[...], sine_ref[...]
        for number, pair, queries, window in tiles:
            upper = both_heads(grad_context_ref[queries, group(pair)])
            grad_shares = product(values_ref[window, group(pair)], upper, NT)
            shares = wide(shares_ref[number])
            sums = jnp.sum(shares * grad_shares, axis=0, keepdims=True)
            grad_scores = low(shares * (grad_shares - sums))
            grad_query = one_pair(product(grad_scores, keys_ref[window, group(pair)], TN)) * SCALE
            grad_query = grad_query * cosine[queries] - partner(grad_query) * sine[queries]
            grad_ref[queries, group(pair)] = low(grad_query)
            lower = both_heads(query_ref[queries, group(pair)])
            total_ref[window, group(pair)] += product(grad_scores, lower)
        for pair in range(inner // LANES):
            grad_keys = total_ref[:, group(pair)] * SCALE
            grad_keys = grad_keys * cosine - partner(grad_keys) * sine
            grad_ref[:, group(pair + inner // LANES)] = low(grad_keys)
        back = product(grad_ref[...], rows_of((a, b, c, d)), NT)
        back_ref[...] = low(back + product(grad_values_ref[...], rows_of((e, f, g, h)), NT))

    return run(
        body,
        [half(count, 2 * inner), half(count, width)],
        [query, keys, values, grad_context, shares, grad_values, cosine, sine, *query_keys, *values_out],
        [None] * (8 + PIECES) + [spec((width // PIECES, inner), 0, 0)] * PIECES,
        scratch=[pltpu.VMEM((count, inner), jnp.float32)],
        flops=6 * count * width * inner + len(tiles) * 12 * WINDOW * BLOCK * LANES,
    )


def paired_grads(pairs):
    count, width = pairs[0][0].shape
    sizes = [right.shape[1] for _, right in pairs]

    def body(*refs):
        outs = refs[2 * len(pairs) :]
        for number, out in enumerate(outs):
            part = slice(number * width // 2, (number + 1) * width // 2)
            start = 0
            for i, size in enumerate(sizes):
                out[:, start : start + size] = low(product(refs[2 * i][:, part], refs[2 * i + 1][...], TN))
                start += size

    return run(
        body,
        [half(width // 2, sum(sizes))] * 2,
        [array for pair in pairs for array in pair],
        flops=2 * count * width * sum(sizes),
    )


def input_grads(grad_middle, inputs, own, other, order):
    count, width = inputs.shape

    def body(grad_middle_ref, inputs_ref, own_ref, other_ref, order_ref, out_ref):
        normed, inverse = normalize(wide(inputs_ref[...]))
        scaled = wide(own_ref[...]) + wide(other_ref[...])
        total = grad_middle_ref[...] + norm_back(scaled, normed, inverse)
        high = low(total)
        rest = low(total - wide(high))
        out_ref[...] = product(high, order_ref[...], NT) + product(rest, order_ref[...], NT)

    return run(
        body,
        [full(count, width)],
        [grad_middle, inputs, own, other, order],
        flops=4 * count * width * width,
    )[0]


def rope_tables(positions):
    frequency = THETA ** (-jnp.arange(0, HD, 2).astype(jnp.float32) / HD)
    angle = positions.astype(jnp.float32)[:, None] * jnp.tile(frequency, LANES // (HD // 2))[None, :]
    sign = jnp.where(jnp.arange(LANES) % HD < HD // 2, -1.0, 1.0)
    return jnp.cos(angle), jnp.sin(angle) * sign[None, :]


def padded(values, width):
    return jnp.pad(values, ((0, 0), (0, width - values.shape[1])))


def per_device(
    devices, tokens, seg_ids, positions, gain_attn, w_qkv, w_attn_out, gain_mlp, w_in, w_mlp_out, cotangent
):
    width = tokens.shape[1]
    rows, _, inner = w_qkv.shape
    hidden = w_in.shape[2]
    room = -(-hidden // LANES) * LANES
    gain_one, gain_two = wide(gain_attn)[:, None], wide(gain_mlp)[:, None]
    scaled_qkv = [low(wide(w_qkv[:, i]) * gain_one) for i in range(3)]
    scaled_in = [padded(low(wide(w_in[:, i]) * gain_two), room) for i in range(2)]
    shard_one = jnp.concatenate(scaled_qkv[:2], axis=1)
    shard_two = jnp.concatenate([scaled_qkv[2], w_attn_out.T], axis=1)
    shard_three = jnp.concatenate(scaled_in + [padded(w_mlp_out.T, room)], axis=1)
    query_keys = gather_rows(shard_one, devices)
    values_out = gather_rows(shard_two, devices)
    shard_three, _ = lax.optimization_barrier((shard_three, values_out[0]))
    gates_down = gather_rows(shard_three, devices)

    order = placement(devices, width)
    inputs, normed_one, upstream = prepare(tokens, cotangent, order)
    cosine, sine = rope_tables(positions)
    query, keys, shares = attend_shares(
        normed_one, query_keys, cosine, sine, seg_ids[:, None], seg_ids[None, :]
    )
    values, context, *own = attend_values(normed_one, values_out, shares)
    other = [swapped(part) for part in own]
    middle, normed_two, mixed, grad_gates, own_out, own_two = zip(
        *(
            feed_forward(number, inputs, upstream, own[number], other[number], gates_down, room)
            for number in range(CHUNKS)
        )
    )
    other_two = [swapped(part) for part in own_two]
    other_out = [swapped(part) for part in own_out]
    grads_mlp = feed_forward_grads(normed_two, mixed, grad_gates, upstream)
    grads_mlp = scatter_rows(*grads_mlp, devices, rows)
    output = add_output(middle, own_out, other_out, order)
    grad_middle, branch, grad_context, grad_values = attend_back_values(
        upstream, middle, own_two, other_two, values_out, context, shares
    )
    grads_two = scatter_rows(
        *paired_grads([(normed_one, grad_values), (branch, context)]), devices, rows
    )
    grad_query_keys, own_one = attend_back_shares(
        query, keys, values, grad_context, shares, grad_values, cosine, sine, query_keys, values_out
    )
    other_one = swapped(own_one)
    grads_one = scatter_rows(*paired_grads([(normed_one, grad_query_keys)]), devices, rows)
    grad_input = input_grads(grad_middle, inputs, own_one, other_one, order)

    sum_qkv = [grads_one[:, :inner], grads_one[:, inner:], grads_two[:, :inner]]
    sum_in = [grads_mlp[:, :hidden], grads_mlp[:, room : room + hidden]]
    gains = jnp.stack(
        [
            sum(jnp.sum(wide(w_qkv[:, i]) * part, axis=1) for i, part in enumerate(sum_qkv)),
            sum(jnp.sum(wide(w_in[:, i]) * part, axis=1) for i, part in enumerate(sum_in)),
        ]
    )
    gains = gains + swapped(gains)
    return (
        output,
        grad_input,
        gains[0],
        jnp.stack([part * gain_one for part in sum_qkv], axis=1),
        grads_two[:, inner:].T,
        gains[1],
        jnp.stack([part * gain_two for part in sum_in], axis=1),
        grads_mlp[:, 2 * room : 2 * room + hidden].T,
    )


def solution(mesh):
    return jax.shard_map(
        functools.partial(per_device, mesh.shape["dp"]),
        mesh=mesh,
        in_specs=(
            P("dp", None),
            P("dp"),
            P("dp"),
            P("dp"),
            P("dp", None, "tensor"),
            P("tensor", "dp"),
            P("dp"),
            P("dp", None, "tensor"),
            P("tensor", "dp"),
            P("dp", None),
        ),
        out_specs=(
            P("dp", None),
            P("dp", None),
            P("dp"),
            P("dp", None, "tensor"),
            P("tensor", "dp"),
            P("dp"),
            P("dp", None, "tensor"),
            P("tensor", "dp"),
        ),
        check_vma=False,
    )
```

time: 265 us -> 205 us (0.77); the launches traced: 260 us -> 205 us
  matrix products: 50.1 us -> 0 us
  local copies, waits for them, and re-layouts: 56.4 us -> 10.4 us
  waiting for transfers between devices: 59.7 us -> 101 us
  Pallas kernels: 0 us -> 30.4 us
  other arithmetic: 32.1 us -> 7.84 us
  starting transfers between devices: 60 us -> 53.8 us
    dot_general x23 -> x0, matrix products: 50.1 us -> none  [the longest x3 6.08 us: restore(): lax.dot_general(values, matrix, (((1,), (1,)), ((), ())), preferred_eleme...]
    ppermute x45 -> x33, waiting for transfers between devices: 32.8 us -> 65.4 us  [shifted(): return lax.ppermute(values, 'dp', pairs)]
    pallas_call x0 -> x24, Pallas kernels: none -> 30.4 us  [run(): pl.pallas_call(body, out_shape=out_shapes, grid=grid, in_specs=specs, out...]
    concatenate x11 -> x0, local copies, waits for them, and re-layouts: 21.5 us -> none  [the longest x9 19.5 us: gather_rows(): jnp.concatenate([held] + [shifted(held, count, level, step) for step in r...]
    unnamed x88 -> x51, local copies, waits for them, and re-layouts: 17.7 us -> 7.2 us
    convert_element_type x16 -> x6, other arithmetic: 12.2 us -> 2.76 us  [the longest x3 1.39 us: low(): return values.astype(jnp.bfloat16)]
    ppermute x45 -> x33, starting transfers between devices: 54.3 us -> 44.9 us  [shifted(): return lax.ppermute(values, 'dp', pairs)]
    reduce_sum x6 -> x0, other arithmetic: 9.23 us -> none  [the longest x1 4.46 us: per_device(): total = jnp.sum(powers, axis=-1, keepdims=True)]
  transfers between devices with their start and end apart: 50 -> 41, of which waited for: 18 -> 18; matrix products, arithmetic and copies ran while one was open for 39% -> 4% of each run, Pallas kernels for 0% -> 12%
where the time goes in v2:
time: 205 us
  waiting for transfers between devices  101 us (49%)
  starting transfers between devices  53.8 us (26%)
  Pallas kernels  30.4 us (15%)
  local copies, waits for them, and re-layouts  10.4 us (5%)
  other arithmetic  7.84 us (4%)
    ppermute x33, waiting for transfers between devices, shifted(): return lax.ppermute(values, 'dp', pairs)  65.4 us
    ppermute x33, starting transfers between devices, shifted(): return lax.ppermute(values, 'dp', pairs)  44.9 us
    ppermute x8, waiting for transfers between devices, swapped(): return lax.ppermute(values, 'tensor', [(0, 1), (1, 0)])  35.7 us
    pallas_call x24, Pallas kernels, run(): pl.pallas_call(body, out_shape=out_shapes, grid=grid, in_specs=specs, out...  30.4 us
    ppermute x8, starting transfers between devices, swapped(): return lax.ppermute(values, 'tensor', [(0, 1), (1, 0)])  8.83 us
    unnamed x51, local copies, waits for them, and re-layouts  7.2 us
  transfers between devices with their start and end apart: 41, of which 18 were waited for; matrix products, arithmetic and copies ran while one was open for 4% of the time, Pallas kernels for 12%

profile of v2, /device:TPU:0, one launch (start us, length us, event | category | flops | bytes accessed | tf_op | source)
XLA Modules:
  0.0 204.7 jit_solution(7402375816634806507)
XLA Ops:
  1.3 0.9 fusion.12
  3.0 3.0 %collective-permute-start = (bf16[48,768]{1,0:T(8,128)(2,1)S(1)}, bf16[48,768]{1,0:T(8,128)(2,1)S(1)}, u32[]{:S(2)}, u32[]{:S(2)}) collective-permute-start(bf16[48,768]{1,0:T(8,128)(2,1)S(1)} %pad_maximum_fusion.2.refs_0_), channel_id=1, source_target_pairs={{0,8},{2,10},{4,12},{6,14},{8,16},{10,18},{12,20},{14,22},{16,24},... | collective-permute-start | bytes 221192 | tf_op jit(solution)/shard_map/ppermute | solution.py:55
  6.0 2.6 %collective-permute-start.1 = (bf16[48,768]{1,0:T(8,128)(2,1)S(1)}, bf16[48,768]{1,0:T(8,128)(2,1)S(1)}, u32[]{:S(2)}, u32[]{:S(2)}) collective-permute-start(bf16[48,768]{1,0:T(8,128)(2,1)S(1)} %pad_maximum_fusion.2.refs_0_), channel_id=1, source_target_pairs={{0,16},{2,18},{4,20},{6,22},{8,24},{10,26},{12,28},{14,30},{16,0},... | collective-permute-start | bytes 221192 | tf_op jit(solution)/shard_map/ppermute | solution.py:55
  8.6 1.3 collective-permute-start.2
  9.9 1.2 fusion.35
  11.9 0.8 fusion.7.refs_0_
  13.8 1.9 collective-permute-start.13
  15.7 1.9 collective-permute-start.14
  18.3 1.4 collective-permute-start.6
  19.7 1.0 collective-permute-start.7
  20.7 2.6 %collective-permute-done.13.refs_1_ = bf16[48,1920]{1,0:T(8,128)(2,1)S(1)} collective-permute-done((bf16[48,1920]{1,0:T(8,128)(2,1)S(1)}, bf16[48,1920]{1,0:T(8,128)(2,1)S(1)}, u32[]{:S(2)}, u32[]{:S(2)}) %collective-permute-start.13) | collective-permute-done | bytes 184352 | tf_op jit(solution)/shard_map/ppermute | solution.py:55
  23.3 1.3 collective-permute-start.8
  24.6 6.6 %collective-permute-done.14.refs_2_ = bf16[48,1920]{1,0:T(8,128)(2,1)S(1)} collective-permute-done((bf16[48,1920]{1,0:T(8,128)(2,1)S(1)}, bf16[48,1920]{1,0:T(8,128)(2,1)S(1)}, u32[]{:S(2)}, u32[]{:S(2)}) %collective-permute-start.14) | collective-permute-done | bytes 184352 | tf_op jit(solution)/shard_map/ppermute | solution.py:55
  31.3 1.8 collective-permute-start.16
  33.3 5.4 %collective-permute-done.7.refs_2_ = bf16[48,768]{1,0:T(8,128)(2,1)S(1)} collective-permute-done((bf16[48,768]{1,0:T(8,128)(2,1)S(1)}, bf16[48,768]{1,0:T(8,128)(2,1)S(1)}, u32[]{:S(2)}, u32[]{:S(2)}) %collective-permute-start.7) | collective-permute-done | bytes 73760 | tf_op jit(solution)/shard_map/ppermute | solution.py:55
  38.7 1.4 collective-permute-start.9
  40.5 0.8 collective-permute-start.3
  42.0 0.9 copy.21.column_ref
  42.8 1.1 copy-done.14
  43.9 1.1 copy-done.15
  45.1 1.5 shard_map.161
  46.6 10.6 %collective-permute-done.9.b = bf16[192,768]{1,0:T(8,128)(2,1)} collective-permute-done((bf16[192,768]{1,0:T(8,128)(2,1)S(1)}, bf16[192,768]{1,0:T(8,128)(2,1)}, u32[]{:S(2)}, u32[]{:S(2)}) %collective-permute-start.9) | collective-permute-done | bytes 294944 | tf_op jit(solution)/shard_map/ppermute | solution.py:55
  57.8 4.5 %collective-permute-done.3.b.refs_7_.f = bf16[192,768]{1,0:T(8,128)(2,1)S(1)} collective-permute-done((bf16[192,768]{1,0:T(8,128)(2,1)S(1)}, bf16[192,768]{1,0:T(8,128)(2,1)S(1)}, u32[]{:S(2)}, u32[]{:S(2)}) %collective-permute-start.3) | collective-permute-done | bytes 294944 | tf_op jit(solution)/shard_map/ppermute | solution.py:55
  62.7 1.0 fusion.5
  63.8 3.9 %shard_map.164 = (bf16[512,384]{1,0:T(8,128)(2,1)S(1)}, bf16[512,384]{1,0:T(8,128)(2,1)S(1)}, bf16[12,256,256]{2,1,0:T(8,128)(2,1)S(1)}) custom-call(bf16[512,768]{1,0:T(8,128)(2,1)S(1)} %get-tuple-element.63.normed_ref.refs_0_, bf16[192,768]{1,0:T(8,128)(2,1)S(1)} %shard_map.163.a, bf16[192,768]{1,0:T(8,128)(2,1)} %collective-permute-done.9.b, ...), custom_call_target="tpu_custom_call" | custom-call | flops 805306368 | bytes 4853760 | tf_op jit(solution)/shard_map/pallas_call | solution.py:124
  69.2 1.5 shard_map.165
  71.5 1.5 collective-permute-start.19
  73.6 10.0 %collective-permute-done.19.other_ref = bf16[256,768]{1,0:T(8,128)(2,1)S(1)} collective-permute-done((bf16[256,768]{1,0:T(8,128)(2,1)S(1)}, bf16[256,768]{1,0:T(8,128)(2,1)S(1)}, u32[]{:S(2)}, u32[]{:S(2)}) %collective-permute-start.19) | collective-permute-done | bytes 393248 | tf_op jit(solution)/shard_map/ppermute | solution.py:59
  83.5 2.7 %shard_map.168 = (f32[256,768]{1,0:T(8,128)S(1)}, bf16[256,768]{1,0:T(8,128)(2,1)S(1)}, bf16[256,640]{1,0:T(8,128)(2,1)S(1)}, bf16[256,1280]{1,0:T(8,128)(2,1)S(...) custom-call(bf16[512,768]{1,0:T(8,128)(2,1)S(1)} %get-tuple-element.61.inputs_ref, ...), custom_call_target="tpu_custom_call" | custom-call | flops 1509949440 | bytes 11206656 | tf_op jit(solution)/shard_map/pallas_call | solution.py:124
  87.0 4.0 %collective-permute-done.12.other_ref = bf16[256,768]{1,0:T(8,128)(2,1)S(1)} collective-permute-done((bf16[256,768]{1,0:T(8,128)(2,1)S(1)}, bf16[256,768]{1,0:T(8,128)(2,1)S(1)}, u32[]{:S(2)}, u32[]{:S(2)}) %collective-permute-start.12) | collective-permute-done | bytes 393248 | tf_op jit(solution)/shard_map/ppermute | solution.py:59
  91.0 2.7 %shard_map.167 = (f32[256,768]{1,0:T(8,128)S(1)}, bf16[256,768]{1,0:T(8,128)(2,1)S(1)}, bf16[256,640]{1,0:T(8,128)(2,1)S(1)}, bf16[256,1280]{1,0:T(8,128)(2,1)S(...) custom-call(bf16[512,768]{1,0:T(8,128)(2,1)S(1)} %get-tuple-element.61.inputs_ref, ...), custom_call_target="tpu_custom_call" | custom-call | flops 1509949440 | bytes 11206656 | tf_op jit(solution)/shard_map/pallas_call | solution.py:124
  93.7 2.0 shard_map.181
  95.8 1.5 collective-permute-start.23
  97.9 9.9 %collective-permute-done.23.refs_5_ = bf16[256,768]{1,0:T(8,128)(2,1)S(1)} collective-permute-done((bf16[256,768]{1,0:T(8,128)(2,1)S(1)}, bf16[256,768]{1,0:T(8,128)(2,1)S(1)}, u32[]{:S(2)}, u32[]{:S(2)}) %collective-permute-start.23) | collective-permute-done | bytes 393248 | tf_op jit(solution)/shard_map/ppermute | solution.py:59
  107.8 8.0 %collective-permute-done.22.refs_4_ = bf16[256,768]{1,0:T(8,128)(2,1)S(1)} collective-permute-done((bf16[256,768]{1,0:T(8,128)(2,1)S(1)}, bf16[256,768]{1,0:T(8,128)(2,1)S(1)}, u32[]{:S(2)}, u32[]{:S(2)}) %collective-permute-start.22) | collective-permute-done | bytes 393248 | tf_op jit(solution)/shard_map/ppermute | solution.py:59
  115.8 1.0 copy-done.9
  116.8 2.0 shard_map.170
  118.8 5.9 %shard_map.171 = (bf16[512,768]{1,0:T(8,128)(2,1)S(1)}, bf16[512,768]{1,0:T(8,128)(2,1)S(1)}) custom-call(bf16[512,384]{1,0:T(8,128)(2,1)S(1)} %copy-done.3, bf16[512,384]{1,0:T(8,128)(2,1)S(1)} %copy-done.5, bf16[512,384]{1,0:T(8,128)(2,1)S(1)} %copy-done.7, bf16[512,384]{1,0:T(8,128)(2,1)S(1)} %get-tuple-element.79.grad_context_ref, ...), custom_call_target="tpu_custom_call" | custom-call | flops 1509949440 | bytes 7995392 | tf_op jit(solution)/shard_map/pallas_call | solution.py:124
  124.8 0.8 shard_map.173
  125.7 1.0 shard_map.177
  127.3 1.5 collective-permute-start.24
  129.1 1.6 collective-permute-start.36
  131.9 1.5 collective-permute-start.20
  133.6 20.1 %collective-permute-done.26.right_ref = bf16[192,768]{1,0:T(8,128)(2,1)S(1)} collective-permute-done((bf16[192,768]{1,0:T(8,128)(2,1)S(1)}, bf16[192,768]{1,0:T(8,128)(2,1)S(1)}, u32[]{:S(2)}, u32[]{:S(2)}) %collective-permute-start.26) | collective-permute-done | bytes 294944 | tf_op jit(solution)/shard_map/ppermute | solution.py:55
  153.7 1.5 collective-permute-start.31
  155.3 0.8 collective-permute-done.21.refs_5_
  156.1 6.0 %collective-permute-start.27 = (bf16[48,768]{1,0:T(8,128)(2,1)S(1)}, bf16[48,768]{1,0:T(8,128)(2,1)S(1)}, u32[]{:S(2)}, u32[]{:S(2)}) collective-permute-start(bf16[48,768]{1,0:T(8,128)(2,1)S(1)} %get-tuple-element.88), channel_id=1, source_target_pairs={{0,24},{2,26},{4,28},{6,30},{8,0},{10,2},{12,4},{14,6},{16,8},{18,... | collective-permute-start | bytes 221192 | tf_op jit(solution)/shard_map/ppermute | solution.py:55
  162.1 1.5 collective-permute-done.20.refs_4_
  163.6 5.5 %collective-permute-start.28 = (bf16[48,768]{1,0:T(8,128)(2,1)S(1)}, bf16[48,768]{1,0:T(8,128)(2,1)S(1)}, u32[]{:S(2)}, u32[]{:S(2)}) collective-permute-start(bf16[48,768]{1,0:T(8,128)(2,1)S(1)} %get-tuple-element.89), channel_id=1, source_target_pairs={{0,16},{2,18},{4,20},{6,22},{8,24},{10,26},{12,28},{14,30},{16,0},... | collective-permute-start | bytes 221192 | tf_op jit(solution)/shard_map/ppermute | solution.py:55
  169.1 1.7 shard_map.169
  170.8 1.1 collective-permute-start.29
  172.0 2.8 %collective-permute-start.32 = (bf16[48,768]{1,0:T(8,128)(2,1)S(1)}, bf16[48,768]{1,0:T(8,128)(2,1)S(1)}, u32[]{:S(2)}, u32[]{:S(2)}) collective-permute-start(bf16[48,768]{1,0:T(8,128)(2,1)S(1)} %get-tuple-element.97), channel_id=1, source_target_pairs={{0,24},{2,26},{4,28},{6,30},{8,0},{10,2},{12,4},{14,6},{16,8},{18,... | collective-permute-start | bytes 221192 | tf_op jit(solution)/shard_map/ppermute | solution.py:55
  175.0 1.9 collective-permute-start.34
  176.9 3.4 %shard_map.172 = f32[512,768]{1,0:T(8,128)} custom-call(f32[512,768]{1,0:T(8,128)S(1)} %get-tuple-element.75.grad_middle_ref, bf16[512,768]{1,0:T(8,128)(2,1)S(1)} %get-tuple-element.61.inputs_ref, bf16[512,768]{1,0:T(8,128)(2,1)S(1)} %get-tuple-element.81.own_ref, bf16[512,768]{1,0:T(8,128)(2,1)S(1)} %collective-permute-done.24.other_ref, ...), custom_call_target="tpu_custom_call" | custom-call | flops 1207959552 | bytes 6684672 | tf_op jit(solution)/shard_map/pallas_call | solution.py:124
  180.4 2.3 %collective-permute-done.33.refs_2_ = bf16[48,768]{1,0:T(8,128)(2,1)S(1)} collective-permute-done((bf16[48,768]{1,0:T(8,128)(2,1)S(1)}, bf16[48,768]{1,0:T(8,128)(2,1)S(1)}, u32[]{:S(2)}, u32[]{:S(2)}) %collective-permute-start.33) | collective-permute-done | bytes 73760 | tf_op jit(solution)/shard_map/ppermute | solution.py:55
  183.0 0.9 collective-permute-start.37
  184.2 1.5 collective-permute-start.39
  185.8 0.8 slice_bitcast_fusion.1
  187.3 3.0 %collective-permute-done.37.refs_1_ = bf16[48,1920]{1,0:T(8,128)(2,1)S(1)} collective-permute-done((bf16[48,1920]{1,0:T(8,128)(2,1)S(1)}, bf16[48,1920]{1,0:T(8,128)(2,1)S(1)}, u32[]{:S(2)}, u32[]{:S(2)}) %collective-permute-start.37) | collective-permute-done | bytes 184352 | tf_op jit(solution)/shard_map/ppermute | solution.py:55
  190.3 9.3 %collective-permute-done.38.refs_2_ = bf16[48,1920]{1,0:T(8,128)(2,1)S(1)} collective-permute-done((bf16[48,1920]{1,0:T(8,128)(2,1)S(1)}, bf16[48,1920]{1,0:T(8,128)(2,1)S(1)}, u32[]{:S(2)}, u32[]{:S(2)}) %collective-permute-start.38) | collective-permute-done | bytes 184352 | tf_op jit(solution)/shard_map/ppermute | solution.py:55
  199.7 0.8 multiply_bitcast_fusion.1
  200.5 1.2 collective-permute-start.40
  201.8 0.8 copy.24
  202.6 1.6 collective-permute-done.40
  (120 shorter events, 15.4 us)
Async XLA Ops:
  1.3 12.5 %copy-start.22 = (f32[48]{0:T(128)}, f32[48]{0:T(128)S(1)}, u32[]{:S(2)}) copy-start(f32[48]{0:T(128)S(1)} %convert_element_type.76) | copy-start | bytes 580
  3.0 9.8 %collective-permute-start = (bf16[48,768]{1,0:T(8,128)(2,1)S(1)}, bf16[48,768]{1,0:T(8,128)(2,1)S(1)}, u32[]{:S(2)}, u32[]{:S(2)}) collective-permute-start(bf16[48,768]{1,0:T(8,128)(2,1)S(1)} %pad_maximum_fusion.2.refs_0_), channel_id=1, source_target_pairs={{0,8},{2,10},{4,12},{6,14},{8,16},{10,18},{12,20},{14,22},{16,24},... | collective-permute-start | bytes 221192 | tf_op jit(solution)/shard_map/ppermute | solution.py:55
  6.0 7.5 %collective-permute-start.1 = (bf16[48,768]{1,0:T(8,128)(2,1)S(1)}, bf16[48,768]{1,0:T(8,128)(2,1)S(1)}, u32[]{:S(2)}, u32[]{:S(2)}) collective-permute-start(bf16[48,768]{1,0:T(8,128)(2,1)S(1)} %pad_maximum_fusion.2.refs_0_), channel_id=1, source_target_pairs={{0,16},{2,18},{4,20},{6,22},{8,24},{10,26},{12,28},{14,30},{16,0},... | collective-permute-start | bytes 221192 | tf_op jit(solution)/shard_map/ppermute | solution.py:55
  8.6 5.2 %collective-permute-start.2 = (bf16[48,768]{1,0:T(8,128)(2,1)S(1)}, bf16[48,768]{1,0:T(8,128)(2,1)S(1)}, u32[]{:S(2)}, u32[]{:S(2)}) collective-permute-start(bf16[48,768]{1,0:T(8,128)(2,1)S(1)} %pad_maximum_fusion.2.refs_0_), channel_id=1, source_target_pairs={{0,24},{2,26},{4,28},{6,30},{8,0},{10,2},{12,4},{14,6},{16,8},{18,... | collective-permute-start | bytes 221192 | tf_op jit(solution)/shard_map/ppermute | solution.py:55
  11.1 7.2 %copy-start.16 = (bf16[48,1,576]{2,1,0:T(2,128)(2,1)}, bf16[48,1,576]{2,1,0:T(2,128)(2,1)S(1)}, u32[]{:S(2)}) copy-start(bf16[48,1,576]{2,1,0:T(2,128)(2,1)S(1)} %get-tuple-element.150) | copy-start | bytes 165892
  11.1 8.6 %copy-start.18 = (bf16[48,1,576]{2,1,0:T(2,128)(2,1)}, bf16[48,1,576]{2,1,0:T(2,128)(2,1)S(1)}, u32[]{:S(2)}) copy-start(bf16[48,1,576]{2,1,0:T(2,128)(2,1)S(1)} %get-tuple-element.151) | copy-start | bytes 165892
  13.8 9.5 %collective-permute-start.13 = (bf16[48,1920]{1,0:T(8,128)(2,1)S(1)}, bf16[48,1920]{1,0:T(8,128)(2,1)S(1)}, u32[]{:S(2)}, u32[]{:S(2)}) collective-permute-start(bf16[48,1920]{1,0:T(8,128)(2,1)S(1)} %fusion.7.refs_0_), channel_id=1, source_target_pairs={{0,8},{2,10},{4,12},{6,14},{8,16},{10,18},{12,20},{14,22},{16,24},... | collective-permute-start | bytes 552968 | tf_op jit(solution)/shard_map/ppermute | solution.py:55
  15.7 15.6 %collective-permute-start.14 = (bf16[48,1920]{1,0:T(8,128)(2,1)S(1)}, bf16[48,1920]{1,0:T(8,128)(2,1)S(1)}, u32[]{:S(2)}, u32[]{:S(2)}) collective-permute-start(bf16[48,1920]{1,0:T(8,128)(2,1)S(1)} %fusion.7.refs_0_), channel_id=1, source_target_pairs={{0,16},{2,18},{4,20},{6,22},{8,24},{10,26},{12,28},{14,30},{16,0},... | collective-permute-start | bytes 552968 | tf_op jit(solution)/shard_map/ppermute | solution.py:55
  17.6 13.7 %collective-permute-start.15 = (bf16[48,1920]{1,0:T(8,128)(2,1)S(1)}, bf16[48,1920]{1,0:T(8,128)(2,1)S(1)}, u32[]{:S(2)}, u32[]{:S(2)}) collective-permute-start(bf16[48,1920]{1,0:T(8,128)(2,1)S(1)} %fusion.7.refs_0_), channel_id=1, source_target_pairs={{0,24},{2,26},{4,28},{6,30},{8,0},{10,2},{12,4},{14,6},{16,8},{18,... | collective-permute-start | bytes 552968 | tf_op jit(solution)/shard_map/ppermute | solution.py:55
  18.3 15.0 %collective-permute-start.6 = (bf16[48,768]{1,0:T(8,128)(2,1)S(1)}, bf16[48,768]{1,0:T(8,128)(2,1)S(1)}, u32[]{:S(2)}, u32[]{:S(2)}) collective-permute-start(bf16[48,768]{1,0:T(8,128)(2,1)S(1)} %pad_maximum_fusion.3.refs_0_), channel_id=1, source_target_pairs={{0,8},{2,10},{4,12},{6,14},{8,16},{10,18},{12,20},{14,22},{16,24},... | collective-permute-start | bytes 221192 | tf_op jit(solution)/shard_map/ppermute | solution.py:55
  19.7 18.9 %collective-permute-start.7 = (bf16[48,768]{1,0:T(8,128)(2,1)S(1)}, bf16[48,768]{1,0:T(8,128)(2,1)S(1)}, u32[]{:S(2)}, u32[]{:S(2)}) collective-permute-start(bf16[48,768]{1,0:T(8,128)(2,1)S(1)} %pad_maximum_fusion.3.refs_0_), channel_id=1, source_target_pairs={{0,16},{2,18},{4,20},{6,22},{8,24},{10,26},{12,28},{14,30},{16,0},... | collective-permute-start | bytes 221192 | tf_op jit(solution)/shard_map/ppermute | solution.py:55
  20.7 21.2 %copy-start.21 = (s32[512]{0:T(512)S(1)}, s32[512]{0:T(512)}, u32[]{:S(2)}) copy-start(s32[512]{0:T(512)} %param.12) | copy-start | bytes 6148
  20.7 21.2 %copy-start.13 = (s32[512]{0:T(512)S(1)}, s32[512]{0:T(512)}, u32[]{:S(2)}) copy-start(s32[512]{0:T(512)} %param.11) | copy-start | bytes 6148
  23.3 15.3 %collective-permute-start.8 = (bf16[48,768]{1,0:T(8,128)(2,1)S(1)}, bf16[48,768]{1,0:T(8,128)(2,1)S(1)}, u32[]{:S(2)}, u32[]{:S(2)}) collective-permute-start(bf16[48,768]{1,0:T(8,128)(2,1)S(1)} %pad_maximum_fusion.3.refs_0_), channel_id=1, source_target_pairs={{0,24},{2,26},{4,28},{6,30},{8,0},{10,2},{12,4},{14,6},{16,8},{18,... | collective-permute-start | bytes 221192 | tf_op jit(solution)/shard_map/ppermute | solution.py:55
  31.3 30.9 %collective-permute-start.16 = (bf16[192,1920]{1,0:T(8,128)(2,1)S(1)}, bf16[192,1920]{1,0:T(8,128)(2,1)S(1)}, u32[]{:S(2)}, u32[]{:S(2)}) collective-permute-start(bf16[192,1920]{1,0:T(8,128)(2,1)S(1)} %shard_map.166.a.e), channel_id=1, source_target_pairs={{0,4},{2,6},{4,0},{6,2},{8,12},{10,14},{12,8},{14,10},{16,20},{18,... | collective-permute-start | bytes 2211848 | tf_op jit(solution)/shard_map/ppermute | solution.py:55
  38.7 18.5 %collective-permute-start.9 = (bf16[192,768]{1,0:T(8,128)(2,1)S(1)}, bf16[192,768]{1,0:T(8,128)(2,1)}, u32[]{:S(2)}, u32[]{:S(2)}) collective-permute-start(bf16[192,768]{1,0:T(8,128)(2,1)S(1)} %shard_map.163.a), channel_id=1, source_target_pairs={{0,4},{2,6},{4,0},{6,2},{8,12},{10,14},{12,8},{14,10},{16,20},{18,... | collective-permute-start | bytes 884744 | tf_op jit(solution)/shard_map/ppermute | solution.py:55
  40.5 17.3 %collective-permute-start.10 = (bf16[192,768]{1,0:T(8,128)(2,1)S(1)}, bf16[192,768]{1,0:T(8,128)(2,1)}, u32[]{:S(2)}, u32[]{:S(2)}) collective-permute-start(bf16[192,768]{1,0:T(8,128)(2,1)S(1)} %shard_map.163.a), channel_id=1, source_target_pairs={{0,2},{2,0},{4,6},{6,4},{8,10},{10,8},{12,14},{14,12},{16,18},{18,... | collective-permute-start | bytes 884744 | tf_op jit(solution)/shard_map/ppermute | solution.py:55
  40.5 21.7 %collective-permute-start.3 = (bf16[192,768]{1,0:T(8,128)(2,1)S(1)}, bf16[192,768]{1,0:T(8,128)(2,1)S(1)}, u32[]{:S(2)}, u32[]{:S(2)}) collective-permute-start(bf16[192,768]{1,0:T(8,128)(2,1)S(1)} %shard_map.162.a.refs_6_.e), channel_id=1, source_target_pairs={{0,4},{2,6},{4,0},{6,2},{8,12},{10,14},{12,8},{14,10},{16,20},{18,... | collective-permute-start | bytes 884744 | tf_op jit(solution)/shard_map/ppermute | solution.py:55
  42.8 1.1 copy-start.14
  43.9 1.1 copy-start.15
  45.1 17.7 %copy-start.24 = (f32[128]{0:T(128)S(1)}, f32[128]{0:T(128)}, u32[]{:S(2)}) copy-start(f32[128]{0:T(128)} %mul.144) | copy-start | bytes 1540
  45.1 18.7 %copy-start.12 = (s32[512,1]{1,0:T(8,128)S(1)}, s32[512,1]{1,0:T(8,128)}, u32[]{:S(2)}) copy-start(s32[512,1]{1,0:T(8,128)} %copy.21.column_ref) | copy-start | bytes 6148
  57.2 6.6 %collective-permute-start.11 = (bf16[192,768]{1,0:T(8,128)(2,1)}, bf16[192,768]{1,0:T(8,128)(2,1)S(1)}, u32[]{:S(2)}, u32[]{:S(2)}) collective-permute-start(bf16[192,768]{1,0:T(8,128)(2,1)} %collective-permute-done.9.b), channel_id=1, source_target_pairs={{0,2},{2,0},{4,6},{6,4},{8,10},{10,8},{12,14},{14,12},{16,18},{18,... | collective-permute-start | bytes 884744 | tf_op jit(solution)/shard_map/ppermute | solution.py:55
  57.2 12.0 %collective-permute-start.4 = (bf16[192,768]{1,0:T(8,128)(2,1)S(1)}, bf16[192,768]{1,0:T(8,128)(2,1)S(1)}, u32[]{:S(2)}, u32[]{:S(2)}) collective-permute-start(bf16[192,768]{1,0:T(8,128)(2,1)S(1)} %shard_map.162.a.refs_6_.e), channel_id=1, source_target_pairs={{0,2},{2,0},{4,6},{6,4},{8,10},{10,8},{12,14},{14,12},{16,18},{18,... | collective-permute-start | bytes 884744 | tf_op jit(solution)/shard_map/ppermute | solution.py:55
  57.7 15.9 %collective-permute-start.17 = (bf16[192,1920]{1,0:T(8,128)(2,1)S(1)}, bf16[192,1920]{1,0:T(8,128)(2,1)S(1)}, u32[]{:S(2)}, u32[]{:S(2)}) collective-permute-start(bf16[192,1920]{1,0:T(8,128)(2,1)S(1)} %shard_map.166.a.e), channel_id=1, source_target_pairs={{0,2},{2,0},{4,6},{6,4},{8,10},{10,8},{12,14},{14,12},{16,18},{18,... | collective-permute-start | bytes 2211848 | tf_op jit(solution)/shard_map/ppermute | solution.py:55
  62.2 7.0 %collective-permute-start.5 = (bf16[192,768]{1,0:T(8,128)(2,1)S(1)}, bf16[192,768]{1,0:T(8,128)(2,1)S(1)}, u32[]{:S(2)}, u32[]{:S(2)}) collective-permute-start(bf16[192,768]{1,0:T(8,128)(2,1)S(1)} %collective-permute-done.3.b.refs_7_.f), channel_id=1, source_target_pairs={{0,2},{2,0},{4,6},{6,4},{8,10},{10,8},{12,14},{14,12},{16,18},{18,... | collective-permute-start | bytes 884744 | tf_op jit(solution)/shard_map/ppermute | solution.py:55
  62.2 21.3 %collective-permute-start.18 = (bf16[192,1920]{1,0:T(8,128)(2,1)S(1)}, bf16[192,1920]{1,0:T(8,128)(2,1)S(1)}, u32[]{:S(2)}, u32[]{:S(2)}) collective-permute-start(bf16[192,1920]{1,0:T(8,128)(2,1)S(1)} %collective-permute-done.16.b.f), channel_id=1, source_target_pairs={{0,2},{2,0},{4,6},{6,4},{8,10},{10,8},{12,14},{14,12},{16,18},{18,... | collective-permute-start | bytes 2211848 | tf_op jit(solution)/shard_map/ppermute | solution.py:55
  63.8 7.0 %copy-start.10 = (bf16[192,768]{1,0:T(8,128)(2,1)}, bf16[192,768]{1,0:T(8,128)(2,1)S(1)}, u32[]{:S(2)}) copy-start(bf16[192,768]{1,0:T(8,128)(2,1)S(1)} %collective-permute-done.11.d) | copy-start | bytes 884740
  67.7 0.8 copy-start.2
  70.7 0.8 copy-start.6
  71.5 12.0 %collective-permute-start.19 = (bf16[256,768]{1,0:T(8,128)(2,1)S(1)}, bf16[256,768]{1,0:T(8,128)(2,1)S(1)}, u32[]{:S(2)}, u32[]{:S(2)}) collective-permute-start(bf16[256,768]{1,0:T(8,128)(2,1)S(1)} %get-tuple-element.68.own_ref), channel_id=1, source_target_pairs={{0,1},{1,0},{2,3},{3,2},{4,5},{5,4},{6,7},{7,6},{8,9},{9,8},{10,11... | collective-permute-start | bytes 1179656 | tf_op jit(solution)/shard_map/ppermute | solution.py:59
  73.0 18.0 %collective-permute-start.12 = (bf16[256,768]{1,0:T(8,128)(2,1)S(1)}, bf16[256,768]{1,0:T(8,128)(2,1)S(1)}, u32[]{:S(2)}, u32[]{:S(2)}) collective-permute-start(bf16[256,768]{1,0:T(8,128)(2,1)S(1)} %get-tuple-element.65.own_ref), channel_id=1, source_target_pairs={{0,1},{1,0},{2,3},{3,2},{4,5},{5,4},{6,7},{7,6},{8,9},{9,8},{10,11... | collective-permute-start | bytes 1179656 | tf_op jit(solution)/shard_map/ppermute | solution.py:59
  87.0 8.8 %copy-start.8 = (bf16[256,768]{1,0:T(8,128)(2,1)}, bf16[256,768]{1,0:T(8,128)(2,1)S(1)}, u32[]{:S(2)}) copy-start(bf16[256,768]{1,0:T(8,128)(2,1)S(1)} %get-tuple-element.73.refs_3_) | copy-start | bytes 1179652
  95.7 33.0 %collective-permute-start.35 = (bf16[384,1920]{1,0:T(8,128)(2,1)S(1)}, bf16[384,1920]{1,0:T(8,128)(2,1)S(1)}, u32[]{:S(2)}, u32[]{:S(2)}) collective-permute-start(bf16[384,1920]{1,0:T(8,128)(2,1)S(1)} %get-tuple-element.107), channel_id=1, source_target_pairs={{0,2},{2,0},{4,6},{6,4},{8,10},{10,8},{12,14},{14,12},{16,18},{18,... | collective-permute-start | bytes 4423688 | tf_op jit(solution)/shard_map/ppermute | solution.py:55
  95.8 12.0 %collective-permute-start.23 = (bf16[256,768]{1,0:T(8,128)(2,1)S(1)}, bf16[256,768]{1,0:T(8,128)(2,1)S(1)}, u32[]{:S(2)}, u32[]{:S(2)}) collective-permute-start(bf16[256,768]{1,0:T(8,128)(2,1)S(1)} %get-tuple-element.73.refs_3_), channel_id=1, source_target_pairs={{0,1},{1,0},{2,3},{3,2},{4,5},{5,4},{6,7},{7,6},{8,9},{9,8},{10,11... | collective-permute-start | bytes 1179656 | tf_op jit(solution)/shard_map/ppermute | solution.py:59
  97.4 18.4 %collective-permute-start.22 = (bf16[256,768]{1,0:T(8,128)(2,1)S(1)}, bf16[256,768]{1,0:T(8,128)(2,1)S(1)}, u32[]{:S(2)}, u32[]{:S(2)}) collective-permute-start(bf16[256,768]{1,0:T(8,128)(2,1)S(1)} %get-tuple-element.72.refs_2_), channel_id=1, source_target_pairs={{0,1},{1,0},{2,3},{3,2},{4,5},{5,4},{6,7},{7,6},{8,9},{9,8},{10,11... | collective-permute-start | bytes 1179656 | tf_op jit(solution)/shard_map/ppermute | solution.py:59
  115.8 1.0 copy-start.9
  116.8 2.0 copy-start.3
  116.8 2.0 copy-start.5
  116.8 2.1 %copy-start.7 = (bf16[512,384]{1,0:T(8,128)(2,1)S(1)}, bf16[512,384]{1,0:T(8,128)(2,1)}, u32[]{:S(2)}) copy-start(bf16[512,384]{1,0:T(8,128)(2,1)} %copy-done.6) | copy-start | bytes 1179652
  116.8 2.1 %copy-start.11 = (bf16[192,768]{1,0:T(8,128)(2,1)S(1)}, bf16[192,768]{1,0:T(8,128)(2,1)}, u32[]{:S(2)}) copy-start(bf16[192,768]{1,0:T(8,128)(2,1)} %copy-done.10) | copy-start | bytes 884740
  125.6 5.1 %collective-permute-start.25 = (bf16[384,768]{1,0:T(8,128)(2,1)S(1)}, bf16[384,768]{1,0:T(8,128)(2,1)S(1)}, u32[]{:S(2)}, u32[]{:S(2)}) collective-permute-start(bf16[384,768]{1,0:T(8,128)(2,1)S(1)} %get-tuple-element.84), channel_id=1, source_target_pairs={{0,2},{2,0},{4,6},{6,4},{8,10},{10,8},{12,14},{14,12},{16,18},{18,... | collective-permute-start | bytes 1769480 | tf_op jit(solution)/shard_map/ppermute | solution.py:55
  126.7 5.2 %collective-permute-start.30 = (bf16[384,768]{1,0:T(8,128)(2,1)S(1)}, bf16[384,768]{1,0:T(8,128)(2,1)S(1)}, u32[]{:S(2)}, u32[]{:S(2)}) collective-permute-start(bf16[384,768]{1,0:T(8,128)(2,1)S(1)} %get-tuple-element.93), channel_id=1, source_target_pairs={{0,2},{2,0},{4,6},{6,4},{8,10},{10,8},{12,14},{14,12},{16,18},{18,... | collective-permute-start | bytes 1769480 | tf_op jit(solution)/shard_map/ppermute | solution.py:55
  127.3 44.7 %collective-permute-start.24 = (bf16[512,768]{1,0:T(8,128)(2,1)S(1)}, bf16[512,768]{1,0:T(8,128)(2,1)S(1)}, u32[]{:S(2)}, u32[]{:S(2)}) collective-permute-start(bf16[512,768]{1,0:T(8,128)(2,1)S(1)} %get-tuple-element.81.own_ref), channel_id=1, source_target_pairs={{0,1},{1,0},{2,3},{3,2},{4,5},{5,4},{6,7},{7,6},{8,9},{9,8},{10,11... | collective-permute-start | bytes 2359304 | tf_op jit(solution)/shard_map/ppermute | solution.py:59
  128.7 2.6 %copy-start.1 = (bf16[256,768]{1,0:T(8,128)(2,1)S(1)}, bf16[256,768]{1,0:T(8,128)(2,1)}, u32[]{:S(2)}) copy-start(bf16[256,768]{1,0:T(8,128)(2,1)} %copy-done) | copy-start | bytes 1179652
  129.1 53.7 %collective-permute-start.36 = (bf16[192,1920]{1,0:T(8,128)(2,1)S(1)}, bf16[192,1920]{1,0:T(8,128)(2,1)S(1)}, u32[]{:S(2)}, u32[]{:S(2)}) collective-permute-start(bf16[192,1920]{1,0:T(8,128)(2,1)S(1)} %get-tuple-element.109), channel_id=1, source_target_pairs={{0,4},{2,6},{4,0},{6,2},{8,12},{10,14},{12,8},{14,10},{16,20},{18,... | collective-permute-start | bytes 2211848 | tf_op jit(solution)/shard_map/ppermute | solution.py:55
  130.8 22.8 %collective-permute-start.26 = (bf16[192,768]{1,0:T(8,128)(2,1)S(1)}, bf16[192,768]{1,0:T(8,128)(2,1)S(1)}, u32[]{:S(2)}, u32[]{:S(2)}) collective-permute-start(bf16[192,768]{1,0:T(8,128)(2,1)S(1)} %get-tuple-element.86), channel_id=1, source_target_pairs={{0,4},{2,6},{4,0},{6,2},{8,12},{10,14},{12,8},{14,10},{16,20},{18,... | collective-permute-start | bytes 884744 | tf_op jit(solution)/shard_map/ppermute | solution.py:55
  131.4 24.7 %collective-permute-start.21 = (bf16[256,768]{1,0:T(8,128)(2,1)S(1)}, bf16[256,768]{1,0:T(8,128)(2,1)S(1)}, u32[]{:S(2)}, u32[]{:S(2)}) collective-permute-start(bf16[256,768]{1,0:T(8,128)(2,1)S(1)} %copy-done.1), channel_id=1, source_target_pairs={{0,1},{1,0},{2,3},{3,2},{4,5},{5,4},{6,7},{7,6},{8,9},{9,8},{10,11... | collective-permute-start | bytes 1179656 | tf_op jit(solution)/shard_map/ppermute | solution.py:59
  131.9 31.7 %collective-permute-start.20 = (bf16[256,768]{1,0:T(8,128)(2,1)S(1)}, bf16[256,768]{1,0:T(8,128)(2,1)S(1)}, u32[]{:S(2)}, u32[]{:S(2)}) collective-permute-start(bf16[256,768]{1,0:T(8,128)(2,1)S(1)} %get-tuple-element.70.refs_2_), channel_id=1, source_target_pairs={{0,1},{1,0},{2,3},{3,2},{4,5},{5,4},{6,7},{7,6},{8,9},{9,8},{10,11... | collective-permute-start | bytes 1179656 | tf_op jit(solution)/shard_map/ppermute | solution.py:59
  153.7 17.1 %collective-permute-start.31 = (bf16[192,768]{1,0:T(8,128)(2,1)S(1)}, bf16[192,768]{1,0:T(8,128)(2,1)S(1)}, u32[]{:S(2)}, u32[]{:S(2)}) collective-permute-start(bf16[192,768]{1,0:T(8,128)(2,1)S(1)} %get-tuple-element.95), channel_id=1, source_target_pairs={{0,4},{2,6},{4,0},{6,2},{8,12},{10,14},{12,8},{14,10},{16,20},{18,... | collective-permute-start | bytes 884744 | tf_op jit(solution)/shard_map/ppermute | solution.py:55
  156.1 18.7 %collective-permute-start.27 = (bf16[48,768]{1,0:T(8,128)(2,1)S(1)}, bf16[48,768]{1,0:T(8,128)(2,1)S(1)}, u32[]{:S(2)}, u32[]{:S(2)}) collective-permute-start(bf16[48,768]{1,0:T(8,128)(2,1)S(1)} %get-tuple-element.88), channel_id=1, source_target_pairs={{0,24},{2,26},{4,28},{6,30},{8,0},{10,2},{12,4},{14,6},{16,8},{18,... | collective-permute-start | bytes 221192 | tf_op jit(solution)/shard_map/ppermute | solution.py:55
  163.6 11.3 %collective-permute-start.28 = (bf16[48,768]{1,0:T(8,128)(2,1)S(1)}, bf16[48,768]{1,0:T(8,128)(2,1)S(1)}, u32[]{:S(2)}, u32[]{:S(2)}) collective-permute-start(bf16[48,768]{1,0:T(8,128)(2,1)S(1)} %get-tuple-element.89), channel_id=1, source_target_pairs={{0,16},{2,18},{4,20},{6,22},{8,24},{10,26},{12,28},{14,30},{16,0},... | collective-permute-start | bytes 221192 | tf_op jit(solution)/shard_map/ppermute | solution.py:55
  170.8 9.5 %collective-permute-start.29 = (bf16[48,768]{1,0:T(8,128)(2,1)S(1)}, bf16[48,768]{1,0:T(8,128)(2,1)S(1)}, u32[]{:S(2)}, u32[]{:S(2)}) collective-permute-start(bf16[48,768]{1,0:T(8,128)(2,1)S(1)} %get-tuple-element.90), channel_id=1, source_target_pairs={{0,8},{2,10},{4,12},{6,14},{8,16},{10,18},{12,20},{14,22},{16,24},... | collective-permute-start | bytes 221192 | tf_op jit(solution)/shard_map/ppermute | solution.py:55
  172.0 8.4 %collective-permute-start.32 = (bf16[48,768]{1,0:T(8,128)(2,1)S(1)}, bf16[48,768]{1,0:T(8,128)(2,1)S(1)}, u32[]{:S(2)}, u32[]{:S(2)}) collective-permute-start(bf16[48,768]{1,0:T(8,128)(2,1)S(1)} %get-tuple-element.97), channel_id=1, source_target_pairs={{0,24},{2,26},{4,28},{6,30},{8,0},{10,2},{12,4},{14,6},{16,8},{18,... | collective-permute-start | bytes 221192 | tf_op jit(solution)/shard_map/ppermute | solution.py:55
  174.7 8.0 %collective-permute-start.33 = (bf16[48,768]{1,0:T(8,128)(2,1)S(1)}, bf16[48,768]{1,0:T(8,128)(2,1)S(1)}, u32[]{:S(2)}, u32[]{:S(2)}) collective-permute-start(bf16[48,768]{1,0:T(8,128)(2,1)S(1)} %get-tuple-element.98), channel_id=1, source_target_pairs={{0,16},{2,18},{4,20},{6,22},{8,24},{10,26},{12,28},{14,30},{16,0},... | collective-permute-start | bytes 221192 | tf_op jit(solution)/shard_map/ppermute | solution.py:55
  175.0 7.7 %collective-permute-start.34 = (bf16[48,768]{1,0:T(8,128)(2,1)S(1)}, bf16[48,768]{1,0:T(8,128)(2,1)S(1)}, u32[]{:S(2)}, u32[]{:S(2)}) collective-permute-start(bf16[48,768]{1,0:T(8,128)(2,1)S(1)} %get-tuple-element.99), channel_id=1, source_target_pairs={{0,8},{2,10},{4,12},{6,14},{8,16},{10,18},{12,20},{14,22},{16,24},... | collective-permute-start | bytes 221192 | tf_op jit(solution)/shard_map/ppermute | solution.py:55
  180.3 5.4 %copy-start.20 = (bf16[48,3,384]{2,0,1:T(8,128)(2,1)S(1)}, bf16[48,3,384]{2,0,1:T(8,128)(2,1)}, u32[]{:S(2)}) copy-start(bf16[48,3,384]{2,0,1:T(8,128)(2,1)} %param.14) | copy-start | bytes 331780
  180.3 5.4 %copy-start.23 = (f32[48]{0:T(128)S(1)}, f32[48]{0:T(128)}, u32[]{:S(2)}) copy-start(f32[48]{0:T(128)} %copy-done.22) | copy-start | bytes 580
  182.8 16.9 %copy-start.17 = (bf16[48,1,576]{2,1,0:T(2,128)(2,1)S(1)}, bf16[48,1,576]{2,1,0:T(2,128)(2,1)}, u32[]{:S(2)}) copy-start(bf16[48,1,576]{2,1,0:T(2,128)(2,1)} %copy-done.16) | copy-start | bytes 165892
  182.8 16.9 %copy-start.19 = (bf16[48,1,576]{2,1,0:T(2,128)(2,1)S(1)}, bf16[48,1,576]{2,1,0:T(2,128)(2,1)}, u32[]{:S(2)}) copy-start(bf16[48,1,576]{2,1,0:T(2,128)(2,1)} %copy-done.18) | copy-start | bytes 165892
  183.0 7.3 %collective-permute-start.37 = (bf16[48,1920]{1,0:T(8,128)(2,1)S(1)}, bf16[48,1920]{1,0:T(8,128)(2,1)S(1)}, u32[]{:S(2)}, u32[]{:S(2)}) collective-permute-start(bf16[48,1920]{1,0:T(8,128)(2,1)S(1)} %get-tuple-element.111), channel_id=1, source_target_pairs={{0,24},{2,26},{4,28},{6,30},{8,0},{10,2},{12,4},{14,6},{16,8},{18,... | collective-permute-start | bytes 552968 | tf_op jit(solution)/shard_map/ppermute | solution.py:55
  183.8 15.7 %collective-permute-start.38 = (bf16[48,1920]{1,0:T(8,128)(2,1)S(1)}, bf16[48,1920]{1,0:T(8,128)(2,1)S(1)}, u32[]{:S(2)}, u32[]{:S(2)}) collective-permute-start(bf16[48,1920]{1,0:T(8,128)(2,1)S(1)} %get-tuple-element.112), channel_id=1, source_target_pairs={{0,16},{2,18},{4,20},{6,22},{8,24},{10,26},{12,28},{14,30},{16,0},... | collective-permute-start | bytes 552968 | tf_op jit(solution)/shard_map/ppermute | solution.py:55
  184.2 15.4 %collective-permute-start.39 = (bf16[48,1920]{1,0:T(8,128)(2,1)S(1)}, bf16[48,1920]{1,0:T(8,128)(2,1)S(1)}, u32[]{:S(2)}, u32[]{:S(2)}) collective-permute-start(bf16[48,1920]{1,0:T(8,128)(2,1)S(1)} %get-tuple-element.113), channel_id=1, source_target_pairs={{0,8},{2,10},{4,12},{6,14},{8,16},{10,18},{12,20},{14,22},{16,24},... | collective-permute-start | bytes 552968 | tf_op jit(solution)/shard_map/ppermute | solution.py:55
  200.5 3.6 %collective-permute-start.40 = (f32[2,48]{1,0:T(2,128)S(1)}, f32[2,48]{1,0:T(2,128)S(1)}, u32[]{:S(2)}, u32[]{:S(2)}) collective-permute-start(f32[2,48]{1,0:T(2,128)S(1)} %pad_maximum_fusion.4), channel_id=1, source_target_pairs={{0,1},{1,0},{2,3},{3,2},{4,5},{5,4},{6,7},{7,6},{8,9},{9,8},{10,11... | collective-permute-start | bytes 1160 | tf_op jit(solution)/shard_map/ppermute | solution.py:59
  (2 other events, 1.5 us)

commit v3 on v2

v3 whole, which is shorter than its diff:
```python
import functools

import jax
import jax.numpy as jnp
from jax import lax
from jax.experimental import pallas as pl
from jax.experimental.pallas import tpu as pltpu
from jax.sharding import PartitionSpec as P

HD = 64
HALF = 64
LIMIT = 16
SMALL = 4
LANES = 128
BLOCK = 128
WINDOW = 256
PIECES = 4

EPSILON = 1e-05
THETA = 10000.0
MASKED = -1e30
SCALE = HD ** (-0.5)

NN = (((1,), (0,)), ((), ()))
NT = (((1,), (1,)), ((), ()))
TN = (((0,), (0,)), ((), ()))


def product(left, right, dims=NN):
    return lax.dot_general(left, right, dims, preferred_element_type=jnp.float32)


def low(values):
    return values.astype(jnp.bfloat16)


def wide(values):
    return values.astype(jnp.float32)


def levels_of(count):
    levels, stride = [], count
    while stride > 1:
        size = 4 if stride % 8 == 0 else 2 if stride % 2 == 0 else stride
        stride //= size
        levels.append((stride, size))
    return levels


def shifted(values, count, level, step):
    stride, size = level
    pairs = []
    for device in range(count):
        digit = (device // stride) % size
        pairs.append((device, device + ((digit + step) % size - digit) * stride))
    return lax.ppermute(values, "dp", pairs)


def swapped(values):
    return lax.ppermute(values, "tensor", [(0, 1), (1, 0)])


def is_plain(count, rows):
    return levels_of(count) == [(4, 4), (2, 2), (1, 2)] and rows % 16 == 0


def after(values, *others):
    return lax.optimization_barrier((values, *others))[0]


class Gather:
    def __init__(self, shard, count, late=False, tail=False):
        self.count, self.levels, self.late, self.tail = count, levels_of(count), late, tail
        self.plain = is_plain(count, shard.shape[0])
        self.shard = shard
        if not self.plain:
            held = shard
            for level in self.levels:
                held = jnp.concatenate(
                    [held] + [shifted(held, count, level, step) for step in range(1, level[1])], axis=0
                )
            self.pieces = jnp.split(held, PIECES, axis=0)
            self.other = self.pieces[0]
        elif late:
            self.other = shifted(shard, count, self.levels[1], 1)
        else:
            self.received = self.along_first(shard)

    def along_first(self, rows):
        return [shifted(rows, self.count, self.levels[0], step) for step in range(1, 4)]

    def join_rows(self):
        if self.plain:
            self.shard = stack_rows([self.shard, self.other])

    def begin(self, other):
        if self.plain:
            self.shard = after(self.shard, other)
            self.received = self.along_first(self.shard)

    def stack(self):
        if self.plain:
            _, second, third = self.levels
            if self.late:
                held, other = stack_rows([self.shard] + self.received, 2)
            else:
                held = stack_rows([self.shard] + self.received)
                other = self.other = shifted(held, self.count, second, 1)
            self.pieces = [held, other]
            if not self.tail:
                self.share()
        return self.pieces[0]

    def share(self, *others):
        if self.plain:
            self.pieces += [
                shifted(after(part, *others), self.count, self.levels[2], 1) for part in self.pieces
            ]


class Scatter:
    def __init__(self, kept, sent, count, rows):
        self.count, self.levels = count, levels_of(count)
        self.plain = is_plain(count, rows)
        if self.plain:
            self.own, self.other = kept, [shifted(part, count, self.levels[2], -1) for part in sent]
            return
        held = jnp.concatenate([jnp.concatenate(side, axis=1) for side in (kept, sent)], axis=0)
        for level in reversed(self.levels):
            size = level[1]
            pieces = held.reshape(size, held.shape[0] // size, held.shape[1])
            total = wide(pieces[0])
            for step in range(1, size):
                total = total + wide(shifted(pieces[step], count, level, -step))
            held = total if level == self.levels[0] else low(total)
        self.other = self.begun = held
        self.parts = [held]

    def second(self, *others):
        if self.plain:
            self.own, sent = add_split(self.own, self.other, 2)
            self.other = shifted(after(sent, *others), self.count, self.levels[1], -1)

    def third(self):
        if self.plain:
            pieces = add_split([self.own], [self.other], 4)
            self.parts = [pieces[0]]
            for step in range(1, 4):
                self.parts.append(shifted(pieces[step], self.count, self.levels[0], -step))
            self.other, self.begun = self.parts[1:], pieces[0]

def placement(count, width):
    device = lax.axis_index("dp")
    place = jnp.arange(count)
    owner, weight = jnp.zeros_like(place), 1
    for stride, size in levels_of(count):
        step = (place // weight) % size
        owner = owner + ((device // stride) % size - step + size) % size * stride
        weight *= size
    rows = width // count
    natural = (owner[:, None] * rows + jnp.arange(rows)[None, :]).reshape(width)
    return low(natural[None, :] == jnp.arange(width)[:, None])


def spec(block, *place):
    return pl.BlockSpec(block, lambda step: place)


latest = []


def wait_for(*arrays):
    latest.extend(arrays)


def run(body, out_shapes, operands, specs=None, scratch=(), limit=LIMIT, last=False):
    if last:
        limit = 60
        specs = [spec(array.shape, *[0] * array.ndim) for array in operands]
    grid = () if specs is None else (1,)
    specs = [None] * len(operands) if specs is None else specs
    specs = [
        pl.BlockSpec(memory_space=pltpu.VMEM) if given is None else given for given in specs
    ]
    count, waits = len(operands), len(latest)

    def ordered(*refs):
        body(*refs[:count], *refs[count + waits :])

    results = pl.pallas_call(
        ordered,
        out_shape=out_shapes,
        grid=grid,
        in_specs=specs + [pl.BlockSpec(memory_space=pl.ANY)] * waits,
        out_specs=[
            spec(shape.shape, *[0] * len(shape.shape)) if last else pl.BlockSpec(memory_space=pltpu.VMEM)
            for shape in out_shapes
        ],
        scratch_shapes=scratch,
        compiler_params=pltpu.CompilerParams(vmem_limit_bytes=limit * 1024 * 1024),
        cost_estimate=pl.CostEstimate(flops=0, bytes_accessed=0, transcendentals=0),
    )(*operands, *latest)
    latest[:] = [min(results, key=lambda array: array.size)]
    return results


def half(*shape):
    return jax.ShapeDtypeStruct(shape, jnp.bfloat16)


def full(*shape):
    return jax.ShapeDtypeStruct(shape, jnp.float32)


def stack_rows(pieces, parts=1):
    rows, width = pieces[0].shape
    rows //= parts

    def body(*refs):
        for number, ref in enumerate(refs[:-parts]):
            for part, out in enumerate(refs[-parts:]):
                out[number * rows : (number + 1) * rows, :] = ref[part * rows : (part + 1) * rows, :]

    stacked = run(body, [half(rows * len(pieces), width)] * parts, pieces, limit=SMALL)
    return stacked if parts > 1 else stacked[0]


def add_split(left, right, parts):
    rows = left[0].shape[0] // parts
    sizes = [piece.shape[1] for piece in left]

    def body(*refs):
        start = 0
        for i, size in enumerate(sizes):
            for number, out in enumerate(refs[2 * len(sizes) :]):
                part = slice(number * rows, (number + 1) * rows)
                total = wide(refs[i][part, :]) + wide(refs[i + len(sizes)][part, :])
                out[:, start : start + size] = low(total)
            start += size

    return run(body, [half(rows, sum(sizes))] * parts, [*left, *right], limit=SMALL)


def total_of(refs):
    total = wide(refs[0][...])
    for ref in refs[1:]:
        total = total + wide(ref[...])
    return total


def add_all(parts):
    def body(*refs):
        refs[-1][...] = total_of(refs[:-1])

    return run(body, [full(*parts[0].shape)], parts, limit=SMALL)[0]


def finish_feed_forward(active, others, weights, gain, hidden):
    rows, room = active.shape

    def body(active_ref, others_ref, weights_ref, gain_ref, sum_ref, down_ref, share_ref):
        active, factor = active_ref[...], others_ref[:, :room]
        down_ref[...] = others_ref[:, room : room + hidden]
        sum_ref[:, 0, :] = active[:, :hidden] * gain_ref[...]
        sum_ref[:, 1, :] = factor[:, :hidden] * gain_ref[...]
        share = wide(weights_ref[:, :room]) * active + wide(weights_ref[:, room:]) * factor
        share_ref[...] = jnp.sum(share, axis=1, keepdims=True) / gain_ref[...]

    return run(
        body,
        [full(rows, 2, hidden), full(rows, hidden), full(rows, 1)],
        [active, others, weights, gain],
        last=True,
    )


def finish_attention(parts, query_keys, values_out, gain, share):
    rows, inner = values_out.shape[0], values_out.shape[1] // 2

    def body(*refs):
        *parts, query_keys_ref, values_out_ref, gain_ref, other_ref, sum_ref, out_ref, share_ref = refs
        total = total_of(parts)
        for number in range(3):
            sum_ref[:, number, :] = total[:, number * inner : (number + 1) * inner] * gain_ref[...]
        out_ref[...] = total[:, 3 * inner :]
        share = jnp.sum(wide(query_keys_ref[...]) * total[:, : 2 * inner], axis=1, keepdims=True)
        values = wide(values_out_ref[:, :inner]) * total[:, 2 * inner : 3 * inner]
        share = (share + jnp.sum(values, axis=1, keepdims=True)) / gain_ref[...]
        lane = lax.broadcasted_iota(jnp.int32, (rows, 2), 1)
        share_ref[...] = jnp.where(lane == 0, share, other_ref[...])

    return run(
        body,
        [full(rows, 3, inner), full(rows, inner), full(rows, 2)],
        [*parts, query_keys, values_out, gain, share],
        last=True,
    )


def normalize(values):
    average = jnp.mean(values, axis=-1, keepdims=True)
    centered = values - average
    variance = jnp.mean(centered * centered, axis=-1, keepdims=True)
    inverse = lax.rsqrt(variance + EPSILON)
    return centered * inverse, inverse


def norm_back(scaled, normed, inverse):
    first = jnp.mean(scaled, axis=-1, keepdims=True)
    second = jnp.mean(scaled * normed, axis=-1, keepdims=True)
    return inverse * (scaled - first - normed * second)


def partner(values):
    lane = lax.broadcasted_iota(jnp.int32, values.shape, 1)
    return jnp.where(
        lane % HD < HD // 2,
        pltpu.roll(values, LANES - HD // 2, 1),
        pltpu.roll(values, HD // 2, 1),
    )


def group(number):
    return slice(number * LANES, (number + 1) * LANES)


def rows_of(refs):
    return jnp.concatenate([ref[...] for ref in refs], axis=0)


def both_heads(values):
    lane = lax.broadcasted_iota(jnp.int32, values.shape, 1)
    nothing = jnp.zeros_like(values)
    return jnp.concatenate(
        [jnp.where(lane < HD, values, nothing), jnp.where(lane < HD, nothing, values)], axis=0
    )


def one_pair(values):
    rows = values.shape[0] // 2
    lane = lax.broadcasted_iota(jnp.int32, (rows, values.shape[1]), 1)
    return jnp.where(lane < HD, values[:rows], values[rows:])


def tiles_of(count, inner):
    for block in range(count // BLOCK):
        start = min(max(block * BLOCK - HALF, 0), count - WINDOW)
        for pair in range(inner // LANES):
            number = block * (inner // LANES) + pair
            yield number, pair, slice(block * BLOCK, (block + 1) * BLOCK), slice(start, start + WINDOW)


def prepare(tokens, cotangent, order):
    count, width = tokens.shape

    def body(tokens_ref, cotangent_ref, order_ref, inputs_ref, normed_ref, upstream_ref):
        inputs = product(tokens_ref[...], order_ref[...])
        inputs_ref[...] = low(inputs)
        normed_ref[...] = low(normalize(inputs)[0])
        upstream_ref[...] = low(product(cotangent_ref[...], order_ref[...]))

    return run(
        body, [half(count, width)] * 3, [tokens, cotangent, order]
    )


def attend_shares(normed, pieces, cosine, sine, column, row):
    count, width = normed.shape
    inner = pieces[0].shape[1] // 2
    tiles = list(tiles_of(count, inner))

    def body(normed_ref, a, b, c, d, cosine_ref, sine_ref, column_ref, row_ref, query_ref, keys_ref, shares_ref):
        projected = product(normed_ref[...], rows_of((a, b, c, d)))
        cosine, sine = cosine_ref[...], sine_ref[...]
        for number in range(inner // LANES):
            part = projected[:, group(number)]
            query_ref[:, group(number)] = low(part * cosine + partner(part) * sine)
            part = projected[:, group(number + inner // LANES)]
            keys_ref[:, group(number)] = low(part * cosine + partner(part) * sine)
        for number, pair, queries, window in tiles:
            if pair == 0:
                near = lax.broadcasted_iota(jnp.int32, (WINDOW, BLOCK), 0) + window.start
                near = near - lax.broadcasted_iota(jnp.int32, (WINDOW, BLOCK), 1) - queries.start
                allowed = (jnp.abs(near) <= HALF) & (column_ref[window, :] == row_ref[:, queries])
                allowed = jnp.concatenate([allowed.astype(jnp.float32)] * 2, axis=1) > 0.5
            query = both_heads(query_ref[queries, group(pair)])
            scores = product(keys_ref[window, group(pair)], query, NT) * SCALE
            scores = jnp.where(allowed, scores, MASKED)
            powers = jnp.exp(scores - jnp.max(scores, axis=0, keepdims=True))
            total = jnp.sum(powers, axis=0, keepdims=True)
            shares_ref[number] = low(powers * (1.0 / total))

    return run(
        body,
        [half(count, inner), half(count, inner), half(len(tiles), WINDOW, 2 * BLOCK)],
        [normed, *pieces, cosine, sine, column, row],
    )


def attend_values(normed, pieces, shares):
    count, width = normed.shape
    inner = pieces[0].shape[1] // 2
    tiles = list(tiles_of(count, inner))

    def body(normed_ref, a, b, c, d, shares_ref, values_ref, context_ref, out_ref):
        matrix = rows_of((a, b, c, d))
        values_ref[...] = low(product(normed_ref[...], matrix[:, :inner]))
        for number, pair, queries, window in tiles:
            both = product(shares_ref[number], values_ref[window, group(pair)], TN)
            context_ref[queries, group(pair)] = low(one_pair(both))
        out_ref[...] = low(product(context_ref[...], matrix[:, inner:], NT))

    return run(
        body,
        [half(count, inner), half(count, inner), half(count, width)],
        [normed, *pieces, shares],
    )


def feed_forward(inputs, upstream, own, other, gates_in, down):
    count, width = inputs.shape
    hidden = down[0].shape[1]

    def body(inputs_ref, upstream_ref, own_ref, other_ref, a, b, c, d, e, f, g, h,
             middle_ref, normed_ref, mixed_ref, gates_ref, forward_ref, back_ref):
        middle = wide(inputs_ref[...]) + (wide(own_ref[...]) + wide(other_ref[...]))
        middle_ref[...] = middle
        normed = low(normalize(middle)[0])
        normed_ref[...] = normed
        matrix, down = rows_of((a, b, c, d)), rows_of((e, f, g, h))
        gates = product(normed, matrix)
        active, factor = gates[:, :hidden], gates[:, hidden:]
        chance = 0.5 + 0.5 * lax.erf(active * 0.7071067811865476)
        bent = active * chance
        mixed = low(bent * factor)
        mixed_ref[...] = mixed
        forward_ref[...] = low(product(mixed, down, NT))
        grad_mixed = product(upstream_ref[...], down)
        slope = chance + active * (0.3989422804014327 * jnp.exp(-0.5 * active * active))
        gates_ref[:, :hidden] = low(grad_mixed * factor * slope)
        gates_ref[:, hidden:] = low(grad_mixed * bent)
        back_ref[...] = low(product(gates_ref[...], matrix, NT))

    return run(
        body,
        [full(count, width), half(count, width), half(count, hidden), half(count, 2 * hidden)]
        + [half(count, width)] * 2,
        [inputs, upstream, own, other, *gates_in, *down],
    )


def feed_forward_grads(normed, mixed, gates, upstream):
    count, width = upstream.shape
    hidden = mixed.shape[1]

    def body(normed_ref, mixed_ref, gates_ref, upstream_ref, *outs):
        for number in range(2):
            part = slice(number * width // 2, (number + 1) * width // 2)
            active_ref, factor_ref, down_ref = outs[3 * number : 3 * number + 3]
            both = product(normed_ref[:, part], gates_ref[...], TN)
            active_ref[...] = low(both[:, :hidden])
            factor_ref[...] = low(both[:, hidden:])
            down_ref[...] = low(product(upstream_ref[:, part], mixed_ref[...], TN))

    return run(body, [half(width // 2, hidden)] * 6, [normed, mixed, gates, upstream])


def add_output(middle, own, other, order):
    def body(middle_ref, own_ref, other_ref, order_ref, out_ref):
        total = low(middle_ref[...] + (wide(own_ref[...]) + wide(other_ref[...])))
        out_ref[...] = low(product(total, order_ref[...], NT))

    return run(body, [half(*middle.shape)], [middle, own, other, order], last=True)[0]


def attend_back_values(upstream, middle, own, other, pieces, context, shares):
    count, width = upstream.shape
    inner = context.shape[1]
    tiles = list(tiles_of(count, inner))

    def body(upstream_ref, middle_ref, own_ref, other_ref, a, b, c, d, context_ref, shares_ref,
             grad_middle_ref, branch_ref, grad_context_ref, grad_values_ref, total_ref):
        matrix = rows_of((a, b, c, d))
        normed, inverse = normalize(middle_ref[...])
        scaled = wide(own_ref[...]) + wide(other_ref[...])
        grad_middle = wide(upstream_ref[...]) + norm_back(scaled, normed, inverse)
        grad_middle_ref[...] = grad_middle
        branch_ref[...] = low(grad_middle)
        grad_context_ref[...] = low(product(branch_ref[...], matrix))
        total_ref[...] = jnp.zeros_like(total_ref)
        for number, pair, queries, window in tiles:
            upper = both_heads(grad_context_ref[queries, group(pair)])
            total_ref[window, group(pair)] += product(shares_ref[number], upper)
        grad_values_ref[...] = low(total_ref[...])

    return run(
        body,
        [full(count, width), half(count, width), half(count, inner), half(count, inner)],
        [upstream, middle, own, other, *pieces, context, shares],
        [None] * 4 + [spec((width // PIECES, inner), 0, 1)] * PIECES + [None] * 2,
        scratch=[pltpu.VMEM((count, inner), jnp.float32)],
    )


def attend_back_shares(query, keys, values, grad_context, shares, grad_values, cosine, sine, query_keys, values_out):
    count, inner = query.shape
    width = query_keys[0].shape[0] * PIECES
    tiles = list(tiles_of(count, inner))

    def body(query_ref, keys_ref, values_ref, grad_context_ref, shares_ref, grad_values_ref, cosine_ref, sine_ref,
             a, b, c, d, e, f, g, h, grad_ref, back_ref, total_ref):
        total_ref[...] = jnp.zeros_like(total_ref)
        cosine, sine = cosine_ref[...], sine_ref[...]
        for number, pair, queries, window in tiles:
            upper = both_heads(grad_context_ref[queries, group(pair)])
            grad_shares = product(values_ref[window, group(pair)], upper, NT)
            shares = wide(shares_ref[number])
            sums = jnp.sum(shares * grad_shares, axis=0, keepdims=True)
            grad_scores = low(shares * (grad_shares - sums))
            grad_query = one_pair(product(grad_scores, keys_ref[window, group(pair)], TN)) * SCALE
            grad_query = grad_query * cosine[queries] - partner(grad_query) * sine[queries]
            grad_ref[queries, group(pair)] = low(grad_query)
            lower = both_heads(query_ref[queries, group(pair)])
            total_ref[window, group(pair)] += product(grad_scores, lower)
        for pair in range(inner // LANES):
            grad_keys = total_ref[:, group(pair)] * SCALE
            grad_keys = grad_keys * cosine - partner(grad_keys) * sine
            grad_ref[:, group(pair + inner // LANES)] = low(grad_keys)
        back = product(grad_ref[...], rows_of((a, b, c, d)), NT)
        back_ref[...] = low(back + product(grad_values_ref[...], rows_of((e, f, g, h)), NT))

    return run(
        body,
        [half(count, 2 * inner), half(count, width)],
        [query, keys, values, grad_context, shares, grad_values, cosine, sine, *query_keys, *values_out],
        [None] * (8 + PIECES) + [spec((width // PIECES, inner), 0, 0)] * PIECES,
        scratch=[pltpu.VMEM((count, inner), jnp.float32)],
    )


def paired_grads(groups):
    pairs = [pair for group in groups for pair in group]
    count, width = pairs[0][0].shape
    sizes = [sum(right.shape[1] for _, right in group) for group in groups]

    def body(*refs):
        outs, number = refs[2 * len(pairs) :], 0
        for i, group in enumerate(groups):
            start = 0
            for _, right in group:
                size = right.shape[1]
                for side in range(2):
                    part = slice(side * width // 2, (side + 1) * width // 2)
                    both = product(refs[2 * number][:, part], refs[2 * number + 1][...], TN)
                    outs[2 * i + side][:, start : start + size] = low(both)
                start += size
                number += 1

    return run(
        body,
        [half(width // 2, size) for size in sizes for _ in range(2)],
        [array for pair in pairs for array in pair],
    )


def input_grads(grad_middle, inputs, own, other, order):
    count, width = inputs.shape

    def body(grad_middle_ref, inputs_ref, own_ref, other_ref, order_ref, out_ref):
        normed, inverse = normalize(wide(inputs_ref[...]))
        scaled = wide(own_ref[...]) + wide(other_ref[...])
        total = grad_middle_ref[...] + norm_back(scaled, normed, inverse)
        high = low(total)
        rest = low(total - wide(high))
        out_ref[...] = product(high, order_ref[...], NT) + product(rest, order_ref[...], NT)

    return run(
        body,
        [full(count, width)],
        [grad_middle, inputs, own, other, order],
        last=True,
    )[0]


def rope_tables(positions):
    frequency = THETA ** (-jnp.arange(0, HD, 2).astype(jnp.float32) / HD)
    angle = positions.astype(jnp.float32)[:, None] * jnp.tile(frequency, LANES // (HD // 2))[None, :]
    sign = jnp.where(jnp.arange(LANES) % HD < HD // 2, -1.0, 1.0)
    return jnp.cos(angle), jnp.sin(angle) * sign[None, :]


def padded(values, width):
    return jnp.pad(values, ((0, 0), (0, width - values.shape[1])))


def per_device(
    devices, tokens, seg_ids, positions, gain_attn, w_qkv, w_attn_out, gain_mlp, w_in, w_mlp_out, cotangent
):
    width = tokens.shape[1]
    rows, _, inner = w_qkv.shape
    hidden = w_in.shape[2]
    room = -(-hidden // LANES) * LANES
    gain_one, gain_two = wide(gain_attn)[:, None], wide(gain_mlp)[:, None]
    scaled_qkv = [low(wide(w_qkv[:, i]) * gain_one) for i in range(3)]
    scaled_in = [padded(low(wide(w_in[:, i]) * gain_two), room) for i in range(2)]
    shard_one = jnp.concatenate(scaled_qkv[:2], axis=1)
    shard_two = jnp.concatenate([scaled_qkv[2], w_attn_out.T], axis=1)
    shard_three = jnp.concatenate(scaled_in, axis=1)
    shard_four = padded(w_mlp_out.T, room)
    latest.clear()
    query_keys = Gather(shard_one, devices)
    down = Gather(shard_four, devices, late=True)
    order = placement(devices, width)
    cosine, sine = rope_tables(positions)
    column, row = seg_ids[:, None], seg_ids[None, :]
    wait_for(cosine, sine, column)
    inputs, normed_one, upstream = prepare(tokens, cotangent, order)
    down.join_rows()
    held = query_keys.stack()
    values_out = Gather(after(shard_two, held), devices)
    wait_for(query_keys.other)
    held = values_out.stack()
    gates_in = Gather(after(shard_three, held), devices, tail=True)
    query, keys, shares = attend_shares(normed_one, query_keys.pieces, cosine, sine, column, row)
    values, context, own = attend_values(normed_one, values_out.pieces, shares)
    other = swapped(own)
    wait_for(values_out.other)
    held = gates_in.stack()
    down.begin(held)
    wait_for(other)
    gates_in.share(down.stack())
    middle, normed_two, mixed, grad_gates, own_out, own_two = feed_forward(
        inputs, upstream, own, other, gates_in.pieces, down.pieces
    )
    other_two = swapped(own_two)
    grads_mlp = feed_forward_grads(normed_two, mixed, grad_gates, upstream)
    sums_active = Scatter(grads_mlp[:1], grads_mlp[3:4], devices, rows)
    sums_others = Scatter(grads_mlp[1:3], grads_mlp[4:], devices, rows)
    sums_active.second()
    sums_others.second(sums_active.other)
    sums_active.third()
    grad_middle, branch, grad_context, grad_values = attend_back_values(
        upstream, middle, own_two, other_two, values_out.pieces, context, shares
    )
    grad_query_keys, own_one = attend_back_shares(
        query, keys, values, grad_context, shares, grad_values, cosine, sine, query_keys.pieces, values_out.pieces
    )
    other_one = swapped(own_one)
    sum_active = add_all(sums_active.parts)
    wait_for(sums_others.other)
    kept, sent = paired_grads(
        [[(normed_one, grad_query_keys), (normed_one, grad_values), (branch, context)]]
    )
    sums = Scatter([kept], [sent], devices, rows)
    sums_others.third()
    sums.second()
    sum_others = add_all(sums_others.parts)
    wait_for(other_one)
    sums.third()
    other_out = swapped(after(own_out, sums.begun))
    sum_in, sum_down, share = finish_feed_forward(
        sum_active, sum_others, shard_three, gain_two, hidden
    )
    grad_input = input_grads(grad_middle, inputs, own_one, other_one, order)
    sum_qkv, sum_out, share = finish_attention(sums.parts, shard_one, shard_two, gain_one, share)
    output = add_output(middle, own_out, other_out, order)
    gains = after(share, output) + swapped(share)
    return (output, grad_input, gains[:, 0], sum_qkv, sum_out.T, gains[:, 1], sum_in, sum_down.T)


def solution(mesh):
    return jax.shard_map(
        functools.partial(per_device, mesh.shape["dp"]),
        mesh=mesh,
        in_specs=(
            P("dp", None),
            P("dp"),
            P("dp"),
            P("dp"),
            P("dp", None, "tensor"),
            P("tensor", "dp"),
            P("dp"),
            P("dp", None, "tensor"),
            P("tensor", "dp"),
            P("dp", None),
        ),
        out_specs=(
            P("dp", None),
            P("dp", None),
            P("dp"),
            P("dp", None, "tensor"),
            P("tensor", "dp"),
            P("dp"),
            P("dp", None, "tensor"),
            P("tensor", "dp"),
        ),
        check_vma=False,
    )
```

time: 205 us -> 160 us (0.78)
  waiting for transfers between devices: 101 us -> 53.5 us
  Pallas kernels: 30.4 us -> 38 us
  other arithmetic: 7.84 us -> 4.51 us
  starting transfers between devices: 53.8 us -> 50.9 us
    ppermute x8 -> x5, waiting for transfers between devices: 35.7 us -> 4.83 us  [swapped(): return lax.ppermute(values, 'tensor', [(0, 1), (1, 0)])]
    ppermute x33 -> x40, waiting for transfers between devices: 65.4 us -> 48.7 us  [shifted(): return lax.ppermute(values, 'dp', pairs)]
    pallas_call x24 -> x25, Pallas kernels: 30.4 us -> 38 us  [run(): pl.pallas_call(ordered, out_shape=out_shapes, grid=grid, in_specs=specs +...]
    ppermute x8 -> x5, starting transfers between devices: 8.83 us -> 4.74 us  [swapped(): return lax.ppermute(values, 'tensor', [(0, 1), (1, 0)])]
    ppermute x33 -> x40, starting transfers between devices: 44.9 us -> 46.2 us  [shifted(): return lax.ppermute(values, 'dp', pairs)]
    unnamed x51 -> x57, local copies, waits for them, and re-layouts: 7.2 us -> 7.61 us
  transfers between devices with their start and end apart: 41 -> 45, of which waited for: 18 -> 18; matrix products, arithmetic and copies ran while one was open for 4% -> 4% of each run, Pallas kernels for 12% -> 17%
where the time goes in v3:
time: 160 us
  waiting for transfers between devices  53.5 us (33%)
  starting transfers between devices  50.9 us (32%)
  Pallas kernels  38 us (24%)
  local copies, waits for them, and re-layouts  11.6 us (7%)
  other arithmetic  4.51 us (3%)
    ppermute x40, waiting for transfers between devices, shifted(): return lax.ppermute(values, 'dp', pairs)  48.7 us
    ppermute x40, starting transfers between devices, shifted(): return lax.ppermute(values, 'dp', pairs)  46.2 us
    pallas_call x25, Pallas kernels, run(): pl.pallas_call(ordered, out_shape=out_shapes, grid=grid, in_specs=specs +...  38 us
    unnamed x57, local copies, waits for them, and re-layouts  7.61 us
    ppermute x5, waiting for transfers between devices, swapped(): return lax.ppermute(values, 'tensor', [(0, 1), (1, 0)])  4.83 us
    ppermute x5, starting transfers between devices, swapped(): return lax.ppermute(values, 'tensor', [(0, 1), (1, 0)])  4.74 us
  transfers between devices with their start and end apart: 45, of which 18 were waited for; matrix products, arithmetic and copies ran while one was open for 4% of the time, Pallas kernels for 17%

profile of v3, /device:TPU:0, one launch (start us, length us, event | category | flops | bytes accessed | tf_op | source)
XLA Modules:
  0.0 159.8 jit_solution(62065697413461607)
XLA Ops:
  0.7 0.7 convert_bitcast_fusion.1
  1.4 1.5 fusion.8
  3.5 3.0 %collective-permute-start = (bf16[48,768]{1,0:T(8,128)(2,1)}, bf16[48,768]{1,0:T(8,128)(2,1)}, u32[]{:S(2)}, u32[]{:S(2)}) collective-permute-start(bf16[48,768]{1,0:T(8,128)(2,1)} %pad_maximum_fusion.1.refs_0_.refs_4_), channel_id=1, source_target_pairs={{0,8},{2,10},{4,12},{6,14},{8,16},{10,18},{12,20},{14,22},{16,24},... | collective-permute-start | bytes 221192 | tf_op jit(solution)/shard_map/ppermute | solution.py:56
  6.6 2.6 %collective-permute-start.1 = (bf16[48,768]{1,0:T(8,128)(2,1)}, bf16[48,768]{1,0:T(8,128)(2,1)}, u32[]{:S(2)}, u32[]{:S(2)}) collective-permute-start(bf16[48,768]{1,0:T(8,128)(2,1)} %pad_maximum_fusion.1.refs_0_.refs_4_), channel_id=1, source_target_pairs={{0,16},{2,18},{4,20},{6,22},{8,24},{10,26},{12,28},{14,30},{16,0},... | collective-permute-start | bytes 221192 | tf_op jit(solution)/shard_map/ppermute | solution.py:56
  9.2 1.3 collective-permute-start.2
  10.5 1.5 pad.10.refs_0_
  12.0 1.5 collective-permute-start.3
  14.2 1.0 fusion.1
  15.4 1.1 copy-done.13
  16.6 1.5 shard_map.161
  18.1 1.2 shard_map.162.refs_4_.refs_0_
  19.4 1.0 shard_map.163.refs_4_.refs_1_.refs_8_
  21.0 0.7 collective-permute-start.4
  22.0 2.8 %collective-permute-start.6 = (bf16[48,768]{1,0:T(8,128)(2,1)S(1)}, bf16[48,768]{1,0:T(8,128)(2,1)S(1)}, u32[]{:S(2)}, u32[]{:S(2)}) collective-permute-start(bf16[48,768]{1,0:T(8,128)(2,1)S(1)} %pad_maximum_fusion.refs_0_.refs_5_), channel_id=1, source_target_pairs={{0,24},{2,26},{4,28},{6,30},{8,0},{10,2},{12,4},{14,6},{16,8},{18,... | collective-permute-start | bytes 221192 | tf_op jit(solution)/shard_map/ppermute | solution.py:56
  24.8 2.5 %collective-permute-done.4.refs_1_ = bf16[48,768]{1,0:T(8,128)(2,1)S(1)} collective-permute-done((bf16[48,768]{1,0:T(8,128)(2,1)S(1)}, bf16[48,768]{1,0:T(8,128)(2,1)S(1)}, u32[]{:S(2)}, u32[]{:S(2)}) %collective-permute-start.4) | collective-permute-done | bytes 73760 | tf_op jit(solution)/shard_map/ppermute | solution.py:56
  27.3 1.6 collective-permute-done.5.refs_2_
  29.5 1.5 collective-permute-start.8
  31.9 4.4 %collective-permute-done.8.refs_2_.refs_5_.refs_13_ = bf16[192,768]{1,0:T(8,128)(2,1)S(1)} collective-permute-done((bf16[192,768]{1,0:T(8,128)(2,1)S(1)}, bf16[192,768]{1,0:T(8,128)(2,1)S(1)}, u32[]{:S(2)}, u32[]{:S(2)}) %collective-permute-start.8) | collective-permute-done | bytes 294944 | tf_op jit(solution)/shard_map/ppermute | solution.py:56
  36.4 2.8 %shard_map.165 = (bf16[512,384]{1,0:T(8,128)(2,1)S(1)}, bf16[512,384]{1,0:T(8,128)(2,1)S(1)}, bf16[12,256,256]{2,1,0:T(8,128)(2,1)S(1)}) custom-call(bf16[512,768]{1,0:T(8,128)(2,1)S(1)} %get-tuple-element.73.refs_0_.refs_2_, bf16[192,768]{1,0:T(8,128)(2,1)S(1)} %shard_map.163.refs_4_.refs_1_.refs_8_, ...), custom_call_target="tpu_custom_call" | custom-call | tf_op jit(solution)/shard_map/pallas_call | solution.py:190
  39.2 1.7 %shard_map.166 = (bf16[512,384]{1,0:T(8,128)(2,1)S(1)}, bf16[512,384]{1,0:T(8,128)(2,1)S(1)}, bf16[512,768]{1,0:T(8,128)(2,1)S(1)}) custom-call(bf16[512,768]{1,0:T(8,128)(2,1)S(1)} %get-tuple-element.73.refs_0_.refs_2_, bf16[192,768]{1,0:T(8,128)(2,1)S(1)} %shard_map.164.refs_9_.refs_1_.refs_4_.refs_12_, ...), custom_call_target="tpu_custom_call" | custom-call | tf_op jit(solution)/shard_map/pallas_call | solution.py:190
  40.9 1.6 collective-permute-start.13
  42.5 2.2 %collective-permute-start.14 = (bf16[48,1280]{1,0:T(8,128)(2,1)S(1)}, bf16[48,1280]{1,0:T(8,128)(2,1)S(1)}, u32[]{:S(2)}, u32[]{:S(2)}) collective-permute-start(bf16[48,1280]{1,0:T(8,128)(2,1)S(1)} %fusion.4.refs_0_.refs_2_), channel_id=1, source_target_pairs={{0,8},{2,10},{4,12},{6,14},{8,16},{10,18},{12,20},{14,22},{16,24},... | collective-permute-start | bytes 368648 | tf_op jit(solution)/shard_map/ppermute | solution.py:56
  45.2 1.9 %collective-permute-start.16 = (bf16[48,1280]{1,0:T(8,128)(2,1)S(1)}, bf16[48,1280]{1,0:T(8,128)(2,1)S(1)}, u32[]{:S(2)}, u32[]{:S(2)}) collective-permute-start(bf16[48,1280]{1,0:T(8,128)(2,1)S(1)} %fusion.4.refs_0_.refs_2_), channel_id=1, source_target_pairs={{0,24},{2,26},{4,28},{6,30},{8,0},{10,2},{12,4},{14,6},{16,8},{18,... | collective-permute-start | bytes 368648 | tf_op jit(solution)/shard_map/ppermute | solution.py:56
  47.1 3.5 %collective-permute-done.14.refs_1_ = bf16[48,1280]{1,0:T(8,128)(2,1)S(1)} collective-permute-done((bf16[48,1280]{1,0:T(8,128)(2,1)S(1)}, bf16[48,1280]{1,0:T(8,128)(2,1)S(1)}, u32[]{:S(2)}, u32[]{:S(2)}) %collective-permute-start.14) | collective-permute-done | bytes 122912 | tf_op jit(solution)/shard_map/ppermute | solution.py:56
  50.6 4.6 %collective-permute-done.15.refs_2_ = bf16[48,1280]{1,0:T(8,128)(2,1)S(1)} collective-permute-done((bf16[48,1280]{1,0:T(8,128)(2,1)S(1)}, bf16[48,1280]{1,0:T(8,128)(2,1)S(1)}, u32[]{:S(2)}, u32[]{:S(2)}) %collective-permute-start.15) | collective-permute-done | bytes 122912 | tf_op jit(solution)/shard_map/ppermute | solution.py:56
  55.2 1.6 collective-permute-start.17
  56.8 3.1 %collective-permute-start.18 = (bf16[96,640]{1,0:T(8,128)(2,1)S(1)}, bf16[96,640]{1,0:T(8,128)(2,1)S(1)}, u32[]{:S(2)}, u32[]{:S(2)}) collective-permute-start(bf16[96,640]{1,0:T(8,128)(2,1)S(1)} %shard_map.162.refs_4_.refs_0_), channel_id=1, source_target_pairs={{0,8},{2,10},{4,12},{6,14},{8,16},{10,18},{12,20},{14,22},{16,24},... | collective-permute-start | bytes 368648 | tf_op jit(solution)/shard_map/ppermute | solution.py:56
  59.9 0.9 collective-permute-start.19
  60.7 1.5 collective-permute-start.20
  62.2 2.3 %collective-permute-done.18.refs_1_ = bf16[96,640]{1,0:T(8,128)(2,1)S(1)} collective-permute-done((bf16[96,640]{1,0:T(8,128)(2,1)S(1)}, bf16[96,640]{1,0:T(8,128)(2,1)S(1)}, u32[]{:S(2)}, u32[]{:S(2)}) %collective-permute-start.18) | collective-permute-done | bytes 122912 | tf_op jit(solution)/shard_map/ppermute | solution.py:56
  64.5 4.3 %collective-permute-done.19.refs_2_ = bf16[96,640]{1,0:T(8,128)(2,1)S(1)} collective-permute-done((bf16[96,640]{1,0:T(8,128)(2,1)S(1)}, bf16[96,640]{1,0:T(8,128)(2,1)S(1)}, u32[]{:S(2)}, u32[]{:S(2)}) %collective-permute-start.19) | collective-permute-done | bytes 122912 | tf_op jit(solution)/shard_map/ppermute | solution.py:56
  70.0 1.9 %collective-permute-done.23.refs_10_ = bf16[192,640]{1,0:T(8,128)(2,1)S(1)} collective-permute-done((bf16[192,640]{1,0:T(8,128)(2,1)S(1)}, bf16[192,640]{1,0:T(8,128)(2,1)S(1)}, u32[]{:S(2)}, u32[]{:S(2)}) %collective-permute-start.23) | collective-permute-done | bytes 245792 | tf_op jit(solution)/shard_map/ppermute | solution.py:56
  72.2 4.5 %shard_map.169 = (f32[512,768]{1,0:T(8,128)S(1)}, bf16[512,768]{1,0:T(8,128)(2,1)S(1)}, bf16[512,640]{1,0:T(8,128)(2,1)S(1)}, bf16[512,1280]{1,0:T(8,128)(2,1)S(...) custom-call(bf16[512,768]{1,0:T(8,128)(2,1)S(1)} %get-tuple-element.71.refs_2_.refs_0_.refs_1_, ...), custom_call_target="tpu_custom_call" | custom-call | tf_op jit(solution)/shard_map/pallas_call | solution.py:190
  76.7 1.8 %shard_map.170 = (bf16[384,640]{1,0:T(8,128)(2,1)S(1)}, bf16[384,640]{1,0:T(8,128)(2,1)S(1)}, bf16[384,640]{1,0:T(8,128)(2,1)S(1)}, bf16[384,640]{1,0:T(8,128)(2...) custom-call(bf16[512,768]{1,0:T(8,128)(2,1)S(1)} %get-tuple-element.90.refs_0_, ...), custom_call_target="tpu_custom_call" | custom-call | tf_op jit(solution)/shard_map/pallas_call | solution.py:190
  79.8 0.7 collective-permute-done.26.refs_1_
  80.6 0.9 collective-permute-start.27
  82.1 6.5 %collective-permute-done.27.refs_1_ = bf16[192,640]{1,0:T(8,128)(2,1)S(1)} collective-permute-done((bf16[192,640]{1,0:T(8,128)(2,1)S(1)}, bf16[192,640]{1,0:T(8,128)(2,1)S(1)}, u32[]{:S(2)}, u32[]{:S(2)}) %collective-permute-start.27) | collective-permute-done | bytes 245792 | tf_op jit(solution)/shard_map/ppermute | solution.py:56
  88.7 0.9 collective-permute-start.33
  89.6 4.2 %collective-permute-start.30 = (bf16[48,640]{1,0:T(8,128)(2,1)S(1)}, bf16[48,640]{1,0:T(8,128)(2,1)S(1)}, u32[]{:S(2)}, u32[]{:S(2)}) collective-permute-start(bf16[48,640]{1,0:T(8,128)(2,1)S(1)} %get-tuple-element.107), channel_id=1, source_target_pairs={{0,24},{2,26},{4,28},{6,30},{8,0},{10,2},{12,4},{14,6},{16,8},{18,... | collective-permute-start | bytes 184328 | tf_op jit(solution)/shard_map/ppermute | solution.py:56
  94.5 4.6 %collective-permute-done.25.refs_3_ = bf16[512,768]{1,0:T(8,128)(2,1)S(1)} collective-permute-done((bf16[512,768]{1,0:T(8,128)(2,1)S(1)}, bf16[512,768]{1,0:T(8,128)(2,1)S(1)}, u32[]{:S(2)}, u32[]{:S(2)}) %collective-permute-start.25) | collective-permute-done | bytes 786464 | tf_op jit(solution)/shard_map/ppermute | solution.py:60
  99.1 2.0 %shard_map.174 = (f32[512,768]{1,0:T(8,128)S(1)}, bf16[512,768]{1,0:T(8,128)(2,1)S(1)}, bf16[512,384]{1,0:T(8,128)(2,1)S(1)}, bf16[512,384]{1,0:T(8,128)(2,1)S(1)}) custom-call(bf16[512,768]{1,0:T(8,128)(2,1)S(1)} %get-tuple-element.72.refs_1_.refs_3_.refs_0_, f32[512,768]{1,0:T(8,128)S(1)} %get-tuple-element.85.refs_1_.refs_0_, ...), custom_call_target="tpu_custom_call" | custom-call | tf_op jit(solution)/shard_map/pallas_call | solution.py:190
  101.1 1.1 copy-done.9
  102.3 4.9 %shard_map.175 = (bf16[512,768]{1,0:T(8,128)(2,1)S(1)}, bf16[512,768]{1,0:T(8,128)(2,1)S(1)}) custom-call(bf16[512,384]{1,0:T(8,128)(2,1)S(1)} %get-tuple-element.76.refs_6_.refs_0_, bf16[512,384]{1,0:T(8,128)(2,1)S(1)} %get-tuple-element.87.refs_1_, bf16[512,384]{1,0:T(8,128)(2,1)S(1)} %get-tuple-element.79.refs_4_.refs_2_, ...), custom_call_target="tpu_custom_call" | custom-call | tf_op jit(solution)/shard_map/pallas_call | solution.py:190
  107.3 1.6 %shard_map.177 = (bf16[384,1536]{1,0:T(8,128)(2,1)S(1)}, bf16[384,1536]{1,0:T(8,128)(2,1)S(1)}) custom-call(bf16[512,768]{1,0:T(8,128)(2,1)S(1)} %get-tuple-element.73.refs_0_.refs_2_, bf16[512,768]{1,0:T(8,128)(2,1)S(1)} %get-tuple-element.105.refs_4_.refs_1_, bf16[512,768]{1,0:T(8,128)(2,1)S(1)} %get-tuple-element.73.refs_0_.refs_2_, ...), custom_call_target="tpu_custom_call" | custom-call | tf_op jit(solution)/shard_map/pallas_call | solution.py:190
  109.8 2.1 %collective-permute-done.34.refs_1_ = bf16[384,1536]{1,0:T(8,128)(2,1)S(1)} collective-permute-done((bf16[384,1536]{1,0:T(8,128)(2,1)S(1)}, bf16[384,1536]{1,0:T(8,128)(2,1)S(1)}, u32[]{:S(2)}, u32[]{:S(2)}) %collective-permute-start.34) | collective-permute-done | bytes 1179680 | tf_op jit(solution)/shard_map/ppermute | solution.py:56
  112.2 0.9 collective-permute-start.35
  113.1 4.2 %collective-permute-start.36 = (bf16[48,1280]{1,0:T(8,128)(2,1)S(1)}, bf16[48,1280]{1,0:T(8,128)(2,1)S(1)}, u32[]{:S(2)}, u32[]{:S(2)}) collective-permute-start(bf16[48,1280]{1,0:T(8,128)(2,1)S(1)} %get-tuple-element.117), channel_id=1, source_target_pairs={{0,24},{2,26},{4,28},{6,30},{8,0},{10,2},{12,4},{14,6},{16,8},{18,... | collective-permute-start | bytes 368648 | tf_op jit(solution)/shard_map/ppermute | solution.py:56
  117.8 3.2 %collective-permute-done.36.refs_1_ = bf16[48,1280]{1,0:T(8,128)(2,1)S(1)} collective-permute-done((bf16[48,1280]{1,0:T(8,128)(2,1)S(1)}, bf16[48,1280]{1,0:T(8,128)(2,1)S(1)}, u32[]{:S(2)}, u32[]{:S(2)}) %collective-permute-start.36) | collective-permute-done | bytes 122912 | tf_op jit(solution)/shard_map/ppermute | solution.py:56
  121.0 7.7 %collective-permute-done.37.refs_2_ = bf16[48,1280]{1,0:T(8,128)(2,1)S(1)} collective-permute-done((bf16[48,1280]{1,0:T(8,128)(2,1)S(1)}, bf16[48,1280]{1,0:T(8,128)(2,1)S(1)}, u32[]{:S(2)}, u32[]{:S(2)}) %collective-permute-start.37) | collective-permute-done | bytes 122912 | tf_op jit(solution)/shard_map/ppermute | solution.py:56
  129.2 0.8 copy-done.16
  130.5 4.5 %collective-permute-start.41 = (bf16[48,1536]{1,0:T(8,128)(2,1)S(1)}, bf16[48,1536]{1,0:T(8,128)(2,1)S(1)}, u32[]{:S(2)}, u32[]{:S(2)}) collective-permute-start(bf16[48,1536]{1,0:T(8,128)(2,1)S(1)} %get-tuple-element.123), channel_id=1, source_target_pairs={{0,24},{2,26},{4,28},{6,30},{8,0},{10,2},{12,4},{14,6},{16,8},{18,... | collective-permute-start | bytes 442376 | tf_op jit(solution)/shard_map/ppermute | solution.py:56
  135.6 0.7 copy.27.refs_3_
  136.3 0.7 copy.28.refs_6_
  137.0 1.9 %shard_map.182 = (f32[48,2,576]{2,1,0:T(2,128)}, f32[48,576]{1,0:T(8,128)}, f32[48,1]{1,0:T(8,128)}) custom-call(f32[48,640]{1,0:T(8,128)} %copy-done.11, f32[48,1280]{1,0:T(8,128)} %copy-done.8, bf16[48,1280]{1,0:T(8,128)(2,1)} %copy-done.10, f32[48,1]{1,0:T(8,128)} %copy.27.refs_3_, bf16[48,1536]{1,0:T(8,128)(2,1)} %copy-done.16), custom_call_target="tpu_custom_call" | custom-call | tf_op jit(solution)/shard_map/pallas_call | solution.py:190
  138.9 5.8 %shard_map.183.refs_8_ = f32[512,768]{1,0:T(8,128)} custom-call(f32[512,768]{1,0:T(8,128)} %copy-done.9, bf16[512,768]{1,0:T(8,128)(2,1)} %copy-done.1, bf16[512,768]{1,0:T(8,128)(2,1)} %copy-done.14, bf16[512,768]{1,0:T(8,128)(2,1)} %copy-done.7, bf16[768,768]{1,0:T(8,128)(2,1)} %copy-done, f32[48,1]{1,0:T(8,128)} %get-tuple-element.126.refs_5_.refs_7_), custom_call_target="tpu_custom_call" | custom-call | tf_op jit(solution)/shard_map/pallas_call | solution.py:190
  144.7 2.9 %collective-permute-done.42.refs_2_ = bf16[48,1536]{1,0:T(8,128)(2,1)S(1)} collective-permute-done((bf16[48,1536]{1,0:T(8,128)(2,1)S(1)}, bf16[48,1536]{1,0:T(8,128)(2,1)S(1)}, u32[]{:S(2)}, u32[]{:S(2)}) %collective-permute-start.42) | collective-permute-done | bytes 147488 | tf_op jit(solution)/shard_map/ppermute | solution.py:56
  147.6 0.6 copy-done.21
  148.3 0.7 copy-done.22
  149.0 2.2 %shard_map.184 = (f32[48,3,384]{2,1,0:T(4,128)}, f32[48,384]{1,0:T(8,128)}, f32[48,2]{1,0:T(8,128)}) custom-call(bf16[48,1536]{1,0:T(8,128)(2,1)} %copy-done.16, bf16[48,1536]{1,0:T(8,128)(2,1)} %copy-done.20, bf16[48,1536]{1,0:T(8,128)(2,1)} %copy-done.21, bf16[48,1536]{1,0:T(8,128)(2,1)} %copy-done.22, bf16[48,768]{1,0:T(8,128)(2,1)} %pad_maximum_fusion.1.refs_0_.refs_4_, ...), custom_call_target="tpu_custom_call" | custom-call | tf_op jit(solution)/shard_map/pallas_call | solution.py:190
  151.1 1.5 collective-permute-start.44
  152.6 1.7 %copy.29 = f32[48,3,384]{2,0,1:T(8,128)} copy(f32[48,3,384]{2,1,0:T(4,128)} %get-tuple-element.145) | data formatting | bytes 442368
  154.3 0.9 copy-done.18
  155.2 3.9 %shard_map.185 = bf16[512,768]{1,0:T(8,128)(2,1)} custom-call(f32[512,768]{1,0:T(8,128)} %copy-done.2, bf16[512,768]{1,0:T(8,128)(2,1)} %get-tuple-element.122.refs_1_, bf16[512,768]{1,0:T(8,128)(2,1)} %copy-done.18, bf16[768,768]{1,0:T(8,128)(2,1)} %copy-done, f32[48,2]{1,0:T(8,128)} %get-tuple-element.129.refs_4_), custom_call_target="tpu_custom_call" | custom-call | tf_op jit(solution)/shard_map/pallas_call | solution.py:190
  159.1 0.7 slice_reduce_fusion
  (132 shorter events, 12.0 us)
Async XLA Ops:
  0.6 13.6 %copy-start.26 = (s32[512]{0:T(512)S(1)}, s32[512]{0:T(512)}, u32[]{:S(2)}) copy-start(s32[512]{0:T(512)} %param.12) | copy-start | bytes 6148
  0.6 14.6 %copy-start.17 = (s32[512]{0:T(512)S(1)}, s32[512]{0:T(512)}, u32[]{:S(2)}) copy-start(s32[512]{0:T(512)} %param.11) | copy-start | bytes 6148
  0.7 14.8 %copy-start.12 = (bf16[512,768]{1,0:T(8,128)(2,1)S(1)}, bf16[512,768]{1,0:T(8,128)(2,1)}, u32[]{:S(2)}) copy-start(bf16[512,768]{1,0:T(8,128)(2,1)} %refs_0_.1) | copy-start | bytes 2359300
  3.5 15.8 %collective-permute-start = (bf16[48,768]{1,0:T(8,128)(2,1)}, bf16[48,768]{1,0:T(8,128)(2,1)}, u32[]{:S(2)}, u32[]{:S(2)}) collective-permute-start(bf16[48,768]{1,0:T(8,128)(2,1)} %pad_maximum_fusion.1.refs_0_.refs_4_), channel_id=1, source_target_pairs={{0,8},{2,10},{4,12},{6,14},{8,16},{10,18},{12,20},{14,22},{16,24},... | collective-permute-start | bytes 221192 | tf_op jit(solution)/shard_map/ppermute | solution.py:56
  6.6 12.8 %collective-permute-start.1 = (bf16[48,768]{1,0:T(8,128)(2,1)}, bf16[48,768]{1,0:T(8,128)(2,1)}, u32[]{:S(2)}, u32[]{:S(2)}) collective-permute-start(bf16[48,768]{1,0:T(8,128)(2,1)} %pad_maximum_fusion.1.refs_0_.refs_4_), channel_id=1, source_target_pairs={{0,16},{2,18},{4,20},{6,22},{8,24},{10,26},{12,28},{14,30},{16,0},... | collective-permute-start | bytes 221192 | tf_op jit(solution)/shard_map/ppermute | solution.py:56
  9.2 10.2 %collective-permute-start.2 = (bf16[48,768]{1,0:T(8,128)(2,1)}, bf16[48,768]{1,0:T(8,128)(2,1)}, u32[]{:S(2)}, u32[]{:S(2)}) collective-permute-start(bf16[48,768]{1,0:T(8,128)(2,1)} %pad_maximum_fusion.1.refs_0_.refs_4_), channel_id=1, source_target_pairs={{0,24},{2,26},{4,28},{6,30},{8,0},{10,2},{12,4},{14,6},{16,8},{18,... | collective-permute-start | bytes 221192 | tf_op jit(solution)/shard_map/ppermute | solution.py:56
  12.0 6.1 %collective-permute-start.3 = (bf16[48,640]{1,0:T(8,128)(2,1)}, bf16[48,640]{1,0:T(8,128)(2,1)}, u32[]{:S(2)}, u32[]{:S(2)}) collective-permute-start(bf16[48,640]{1,0:T(8,128)(2,1)} %pad.10.refs_0_), channel_id=1, source_target_pairs={{0,4},{2,6},{4,0},{6,2},{8,12},{10,14},{12,8},{14,10},{16,20},{18,... | collective-permute-start | bytes 184328 | tf_op jit(solution)/shard_map/ppermute | solution.py:56
  14.1 3.9 %copy-start = (bf16[768,768]{1,0:T(8,128)(2,1)}, bf16[768,768]{1,0:T(8,128)(2,1)S(1)}, u32[]{:S(2)}) copy-start(bf16[768,768]{1,0:T(8,128)(2,1)S(1)} %fusion.refs_2_.refs_4_.refs_3_) | copy-start | bytes 3538948
  15.2 21.1 %copy-start.3 = (f32[512,128]{1,0:T(8,128)}, f32[512,128]{1,0:T(8,128)S(1)}, u32[]{:S(2)}) copy-start(f32[512,128]{1,0:T(8,128)S(1)} %get-tuple-element.157.refs_4_.refs_6_.refs_7_) | copy-start | bytes 786436
  15.2 21.1 %copy-start.5 = (f32[512,128]{1,0:T(8,128)}, f32[512,128]{1,0:T(8,128)S(1)}, u32[]{:S(2)}) copy-start(f32[512,128]{1,0:T(8,128)S(1)} %get-tuple-element.158.refs_3_.refs_5_.refs_6_) | copy-start | bytes 786436
  18.0 54.2 %copy-start.1 = (bf16[512,768]{1,0:T(8,128)(2,1)}, bf16[512,768]{1,0:T(8,128)(2,1)S(1)}, u32[]{:S(2)}) copy-start(bf16[512,768]{1,0:T(8,128)(2,1)S(1)} %get-tuple-element.71.refs_2_.refs_0_.refs_1_) | copy-start | bytes 2359300
  18.1 2.9 %copy-start.23 = (bf16[48,384]{1,0:T(8,128)(2,1)S(1)}, bf16[48,384]{1,0:T(8,128)(2,1)}, u32[]{:S(2)}) copy-start(bf16[48,384]{1,0:T(8,128)(2,1)} %get-tuple-element.155) | copy-start | bytes 110596
  18.1 2.9 %copy-start.25 = (bf16[384,48]{0,1:T(8,128)(2,1)S(1)}, bf16[384,48]{0,1:T(8,128)(2,1)}, u32[]{:S(2)}) copy-start(bf16[384,48]{0,1:T(8,128)(2,1)} %param.15) | copy-start | bytes 110596
  18.1 13.0 %copy-start.19 = (bf16[48,2,576]{2,1,0:T(2,128)(2,1)S(1)}, bf16[48,2,576]{2,1,0:T(2,128)(2,1)}, u32[]{:S(2)}) copy-start(bf16[48,2,576]{2,1,0:T(2,128)(2,1)} %param.17) | copy-start | bytes 331780
  18.1 18.2 %copy-start.27 = (bf16[48]{0:T(256)(128)(2,1)S(1)}, bf16[48]{0:T(256)(128)(2,1)}, u32[]{:S(2)}) copy-start(bf16[48]{0:T(256)(128)(2,1)} %param.16) | copy-start | bytes 292
  20.4 8.5 %collective-permute-start.7 = (bf16[192,768]{1,0:T(8,128)(2,1)S(1)}, bf16[192,768]{1,0:T(8,128)(2,1)S(1)}, u32[]{:S(2)}, u32[]{:S(2)}) collective-permute-start(bf16[192,768]{1,0:T(8,128)(2,1)S(1)} %shard_map.163.refs_4_.refs_1_.refs_8_), channel_id=1, source_target_pairs={{0,4},{2,6},{4,0},{6,2},{8,12},{10,14},{12,8},{14,10},{16,20},{18,... | collective-permute-start | bytes 884744 | tf_op jit(solution)/shard_map/ppermute | solution.py:56
  21.0 6.3 %collective-permute-start.4 = (bf16[48,768]{1,0:T(8,128)(2,1)S(1)}, bf16[48,768]{1,0:T(8,128)(2,1)S(1)}, u32[]{:S(2)}, u32[]{:S(2)}) collective-permute-start(bf16[48,768]{1,0:T(8,128)(2,1)S(1)} %pad_maximum_fusion.refs_0_.refs_5_), channel_id=1, source_target_pairs={{0,8},{2,10},{4,12},{6,14},{8,16},{10,18},{12,20},{14,22},{16,24},... | collective-permute-start | bytes 221192 | tf_op jit(solution)/shard_map/ppermute | solution.py:56
  21.7 7.2 %collective-permute-start.5 = (bf16[48,768]{1,0:T(8,128)(2,1)S(1)}, bf16[48,768]{1,0:T(8,128)(2,1)S(1)}, u32[]{:S(2)}, u32[]{:S(2)}) collective-permute-start(bf16[48,768]{1,0:T(8,128)(2,1)S(1)} %pad_maximum_fusion.refs_0_.refs_5_), channel_id=1, source_target_pairs={{0,16},{2,18},{4,20},{6,22},{8,24},{10,26},{12,28},{14,30},{16,0},... | collective-permute-start | bytes 221192 | tf_op jit(solution)/shard_map/ppermute | solution.py:56
  22.0 6.8 %collective-permute-start.6 = (bf16[48,768]{1,0:T(8,128)(2,1)S(1)}, bf16[48,768]{1,0:T(8,128)(2,1)S(1)}, u32[]{:S(2)}, u32[]{:S(2)}) collective-permute-start(bf16[48,768]{1,0:T(8,128)(2,1)S(1)} %pad_maximum_fusion.refs_0_.refs_5_), channel_id=1, source_target_pairs={{0,24},{2,26},{4,28},{6,30},{8,0},{10,2},{12,4},{14,6},{16,8},{18,... | collective-permute-start | bytes 221192 | tf_op jit(solution)/shard_map/ppermute | solution.py:56
  29.5 6.7 %collective-permute-start.8 = (bf16[192,768]{1,0:T(8,128)(2,1)S(1)}, bf16[192,768]{1,0:T(8,128)(2,1)S(1)}, u32[]{:S(2)}, u32[]{:S(2)}) collective-permute-start(bf16[192,768]{1,0:T(8,128)(2,1)S(1)} %shard_map.164.refs_9_.refs_1_.refs_4_.refs_12_), channel_id=1, source_target_pairs={{0,4},{2,6},{4,0},{6,2},{8,12},{10,14},{12,8},{14,10},{16,20},{18,... | collective-permute-start | bytes 884744 | tf_op jit(solution)/shard_map/ppermute | solution.py:56
  31.2 5.1 %collective-permute-start.11 = (bf16[192,768]{1,0:T(8,128)(2,1)S(1)}, bf16[192,768]{1,0:T(8,128)(2,1)S(1)}, u32[]{:S(2)}, u32[]{:S(2)}) collective-permute-start(bf16[192,768]{1,0:T(8,128)(2,1)S(1)} %shard_map.163.refs_4_.refs_1_.refs_8_), channel_id=1, source_target_pairs={{0,2},{2,0},{4,6},{6,4},{8,10},{10,8},{12,14},{14,12},{16,18},{18,... | collective-permute-start | bytes 884744 | tf_op jit(solution)/shard_map/ppermute | solution.py:56
  31.3 5.1 %collective-permute-start.12 = (bf16[192,768]{1,0:T(8,128)(2,1)S(1)}, bf16[192,768]{1,0:T(8,128)(2,1)S(1)}, u32[]{:S(2)}, u32[]{:S(2)}) collective-permute-start(bf16[192,768]{1,0:T(8,128)(2,1)S(1)} %collective-permute-done.7.refs_5_.refs_2_.refs_9_), channel_id=1, source_target_pairs={{0,2},{2,0},{4,6},{6,4},{8,10},{10,8},{12,14},{14,12},{16,18},{18,... | collective-permute-start | bytes 884744 | tf_op jit(solution)/shard_map/ppermute | solution.py:56
  31.8 7.4 %collective-permute-start.9 = (bf16[192,768]{1,0:T(8,128)(2,1)S(1)}, bf16[192,768]{1,0:T(8,128)(2,1)S(1)}, u32[]{:S(2)}, u32[]{:S(2)}) collective-permute-start(bf16[192,768]{1,0:T(8,128)(2,1)S(1)} %shard_map.164.refs_9_.refs_1_.refs_4_.refs_12_), channel_id=1, source_target_pairs={{0,2},{2,0},{4,6},{6,4},{8,10},{10,8},{12,14},{14,12},{16,18},{18,... | collective-permute-start | bytes 884744 | tf_op jit(solution)/shard_map/ppermute | solution.py:56
  36.2 2.9 %collective-permute-start.10 = (bf16[192,768]{1,0:T(8,128)(2,1)S(1)}, bf16[192,768]{1,0:T(8,128)(2,1)S(1)}, u32[]{:S(2)}, u32[]{:S(2)}) collective-permute-start(bf16[192,768]{1,0:T(8,128)(2,1)S(1)} %collective-permute-done.8.refs_2_.refs_5_.refs_13_), channel_id=1, source_target_pairs={{0,2},{2,0},{4,6},{6,4},{8,10},{10,8},{12,14},{14,12},{16,18},{18,... | collective-permute-start | bytes 884744 | tf_op jit(solution)/shard_map/ppermute | solution.py:56
  40.9 27.9 %collective-permute-start.13 = (bf16[512,768]{1,0:T(8,128)(2,1)S(1)}, bf16[512,768]{1,0:T(8,128)(2,1)S(1)}, u32[]{:S(2)}, u32[]{:S(2)}) collective-permute-start(bf16[512,768]{1,0:T(8,128)(2,1)S(1)} %get-tuple-element.77.refs_2_), channel_id=1, source_target_pairs={{0,1},{1,0},{2,3},{3,2},{4,5},{5,4},{6,7},{7,6},{8,9},{9,8},{10,11... | collective-permute-start | bytes 2359304 | tf_op jit(solution)/shard_map/ppermute | solution.py:60
  42.4 26.4 %copy-start.10 = (bf16[48,1280]{1,0:T(8,128)(2,1)}, bf16[48,1280]{1,0:T(8,128)(2,1)S(1)}, u32[]{:S(2)}) copy-start(bf16[48,1280]{1,0:T(8,128)(2,1)S(1)} %fusion.4.refs_0_.refs_2_) | copy-start | bytes 368644
  42.5 8.1 %collective-permute-start.14 = (bf16[48,1280]{1,0:T(8,128)(2,1)S(1)}, bf16[48,1280]{1,0:T(8,128)(2,1)S(1)}, u32[]{:S(2)}, u32[]{:S(2)}) collective-permute-start(bf16[48,1280]{1,0:T(8,128)(2,1)S(1)} %fusion.4.refs_0_.refs_2_), channel_id=1, source_target_pairs={{0,8},{2,10},{4,12},{6,14},{8,16},{10,18},{12,20},{14,22},{16,24},... | collective-permute-start | bytes 368648 | tf_op jit(solution)/shard_map/ppermute | solution.py:56
  44.7 10.5 %collective-permute-start.15 = (bf16[48,1280]{1,0:T(8,128)(2,1)S(1)}, bf16[48,1280]{1,0:T(8,128)(2,1)S(1)}, u32[]{:S(2)}, u32[]{:S(2)}) collective-permute-start(bf16[48,1280]{1,0:T(8,128)(2,1)S(1)} %fusion.4.refs_0_.refs_2_), channel_id=1, source_target_pairs={{0,16},{2,18},{4,20},{6,22},{8,24},{10,26},{12,28},{14,30},{16,0},... | collective-permute-start | bytes 368648 | tf_op jit(solution)/shard_map/ppermute | solution.py:56
  45.2 9.9 %collective-permute-start.16 = (bf16[48,1280]{1,0:T(8,128)(2,1)S(1)}, bf16[48,1280]{1,0:T(8,128)(2,1)S(1)}, u32[]{:S(2)}, u32[]{:S(2)}) collective-permute-start(bf16[48,1280]{1,0:T(8,128)(2,1)S(1)} %fusion.4.refs_0_.refs_2_), channel_id=1, source_target_pairs={{0,24},{2,26},{4,28},{6,30},{8,0},{10,2},{12,4},{14,6},{16,8},{18,... | collective-permute-start | bytes 368648 | tf_op jit(solution)/shard_map/ppermute | solution.py:56
  55.2 13.7 %collective-permute-start.17 = (bf16[192,1280]{1,0:T(8,128)(2,1)S(1)}, bf16[192,1280]{1,0:T(8,128)(2,1)S(1)}, u32[]{:S(2)}, u32[]{:S(2)}) collective-permute-start(bf16[192,1280]{1,0:T(8,128)(2,1)S(1)} %shard_map.167.refs_4_), channel_id=1, source_target_pairs={{0,4},{2,6},{4,0},{6,2},{8,12},{10,14},{12,8},{14,10},{16,20},{18,... | collective-permute-start | bytes 1474568 | tf_op jit(solution)/shard_map/ppermute | solution.py:56
  56.8 7.8 %collective-permute-start.18 = (bf16[96,640]{1,0:T(8,128)(2,1)S(1)}, bf16[96,640]{1,0:T(8,128)(2,1)S(1)}, u32[]{:S(2)}, u32[]{:S(2)}) collective-permute-start(bf16[96,640]{1,0:T(8,128)(2,1)S(1)} %shard_map.162.refs_4_.refs_0_), channel_id=1, source_target_pairs={{0,8},{2,10},{4,12},{6,14},{8,16},{10,18},{12,20},{14,22},{16,24},... | collective-permute-start | bytes 368648 | tf_op jit(solution)/shard_map/ppermute | solution.py:56
  59.9 8.9 %collective-permute-start.19 = (bf16[96,640]{1,0:T(8,128)(2,1)S(1)}, bf16[96,640]{1,0:T(8,128)(2,1)S(1)}, u32[]{:S(2)}, u32[]{:S(2)}) collective-permute-start(bf16[96,640]{1,0:T(8,128)(2,1)S(1)} %shard_map.162.refs_4_.refs_0_), channel_id=1, source_target_pairs={{0,16},{2,18},{4,20},{6,22},{8,24},{10,26},{12,28},{14,30},{16,0},... | collective-permute-start | bytes 368648 | tf_op jit(solution)/shard_map/ppermute | solution.py:56
  60.7 8.1 %collective-permute-start.20 = (bf16[96,640]{1,0:T(8,128)(2,1)S(1)}, bf16[96,640]{1,0:T(8,128)(2,1)S(1)}, u32[]{:S(2)}, u32[]{:S(2)}) collective-permute-start(bf16[96,640]{1,0:T(8,128)(2,1)S(1)} %shard_map.162.refs_4_.refs_0_), channel_id=1, source_target_pairs={{0,24},{2,26},{4,28},{6,30},{8,0},{10,2},{12,4},{14,6},{16,8},{18,... | collective-permute-start | bytes 368648 | tf_op jit(solution)/shard_map/ppermute | solution.py:56
  68.9 3.3 %collective-permute-start.22 = (bf16[192,1280]{1,0:T(8,128)(2,1)S(1)}, bf16[192,1280]{1,0:T(8,128)(2,1)S(1)}, u32[]{:S(2)}, u32[]{:S(2)}) collective-permute-start(bf16[192,1280]{1,0:T(8,128)(2,1)S(1)} %collective-permute-done.17.refs_5_), channel_id=1, source_target_pairs={{0,2},{2,0},{4,6},{6,4},{8,10},{10,8},{12,14},{14,12},{16,18},{18,... | collective-permute-start | bytes 1474568 | tf_op jit(solution)/shard_map/ppermute | solution.py:56
  68.9 3.3 %collective-permute-start.21 = (bf16[192,1280]{1,0:T(8,128)(2,1)S(1)}, bf16[192,1280]{1,0:T(8,128)(2,1)S(1)}, u32[]{:S(2)}, u32[]{:S(2)}) collective-permute-start(bf16[192,1280]{1,0:T(8,128)(2,1)S(1)} %shard_map.167.refs_4_), channel_id=1, source_target_pairs={{0,2},{2,0},{4,6},{6,4},{8,10},{10,8},{12,14},{14,12},{16,18},{18,... | collective-permute-start | bytes 1474568 | tf_op jit(solution)/shard_map/ppermute | solution.py:56
  69.4 2.4 %collective-permute-start.23 = (bf16[192,640]{1,0:T(8,128)(2,1)S(1)}, bf16[192,640]{1,0:T(8,128)(2,1)S(1)}, u32[]{:S(2)}, u32[]{:S(2)}) collective-permute-start(bf16[192,640]{1,0:T(8,128)(2,1)S(1)} %get-tuple-element.81.refs_8_.refs_12_), channel_id=1, source_target_pairs={{0,2},{2,0},{4,6},{6,4},{8,10},{10,8},{12,14},{14,12},{16,18},{18,... | collective-permute-start | bytes 737288 | tf_op jit(solution)/shard_map/ppermute | solution.py:56
  69.5 2.7 %collective-permute-start.24 = (bf16[192,640]{1,0:T(8,128)(2,1)S(1)}, bf16[192,640]{1,0:T(8,128)(2,1)S(1)}, u32[]{:S(2)}, u32[]{:S(2)}) collective-permute-start(bf16[192,640]{1,0:T(8,128)(2,1)S(1)} %get-tuple-element.84.refs_9_), channel_id=1, source_target_pairs={{0,2},{2,0},{4,6},{6,4},{8,10},{10,8},{12,14},{14,12},{16,18},{18,... | collective-permute-start | bytes 737288 | tf_op jit(solution)/shard_map/ppermute | solution.py:56
  76.7 22.4 %copy-start.2 = (f32[512,768]{1,0:T(8,128)}, f32[512,768]{1,0:T(8,128)S(1)}, u32[]{:S(2)}) copy-start(f32[512,768]{1,0:T(8,128)S(1)} %get-tuple-element.85.refs_1_.refs_0_) | copy-start | bytes 4718596
  78.6 1.9 %collective-permute-start.26 = (bf16[384,640]{1,0:T(8,128)(2,1)S(1)}, bf16[384,640]{1,0:T(8,128)(2,1)S(1)}, u32[]{:S(2)}, u32[]{:S(2)}) collective-permute-start(bf16[384,640]{1,0:T(8,128)(2,1)S(1)} %get-tuple-element.94), channel_id=1, source_target_pairs={{0,2},{2,0},{4,6},{6,4},{8,10},{10,8},{12,14},{14,12},{16,18},{18,... | collective-permute-start | bytes 1474568 | tf_op jit(solution)/shard_map/ppermute | solution.py:56
  78.8 2.8 %collective-permute-start.28 = (bf16[384,640]{1,0:T(8,128)(2,1)S(1)}, bf16[384,640]{1,0:T(8,128)(2,1)S(1)}, u32[]{:S(2)}, u32[]{:S(2)}) collective-permute-start(bf16[384,640]{1,0:T(8,128)(2,1)S(1)} %get-tuple-element.99), channel_id=1, source_target_pairs={{0,2},{2,0},{4,6},{6,4},{8,10},{10,8},{12,14},{14,12},{16,18},{18,... | collective-permute-start | bytes 1474568 | tf_op jit(solution)/shard_map/ppermute | solution.py:56
  79.1 2.8 %collective-permute-start.29 = (bf16[384,640]{1,0:T(8,128)(2,1)S(1)}, bf16[384,640]{1,0:T(8,128)(2,1)S(1)}, u32[]{:S(2)}, u32[]{:S(2)}) collective-permute-start(bf16[384,640]{1,0:T(8,128)(2,1)S(1)} %get-tuple-element.100), channel_id=1, source_target_pairs={{0,2},{2,0},{4,6},{6,4},{8,10},{10,8},{12,14},{14,12},{16,18},{18,... | collective-permute-start | bytes 1474568 | tf_op jit(solution)/shard_map/ppermute | solution.py:56
  79.3 19.8 %collective-permute-start.25 = (bf16[512,768]{1,0:T(8,128)(2,1)S(1)}, bf16[512,768]{1,0:T(8,128)(2,1)S(1)}, u32[]{:S(2)}, u32[]{:S(2)}) collective-permute-start(bf16[512,768]{1,0:T(8,128)(2,1)S(1)} %get-tuple-element.88.refs_2_), channel_id=1, source_target_pairs={{0,1},{1,0},{2,3},{3,2},{4,5},{5,4},{6,7},{7,6},{8,9},{9,8},{10,11... | collective-permute-start | bytes 2359304 | tf_op jit(solution)/shard_map/ppermute | solution.py:60
  80.6 8.1 %collective-permute-start.27 = (bf16[192,640]{1,0:T(8,128)(2,1)S(1)}, bf16[192,640]{1,0:T(8,128)(2,1)S(1)}, u32[]{:S(2)}, u32[]{:S(2)}) collective-permute-start(bf16[192,640]{1,0:T(8,128)(2,1)S(1)} %get-tuple-element.96), channel_id=1, source_target_pairs={{0,4},{2,6},{4,0},{6,2},{8,12},{10,14},{12,8},{14,10},{16,20},{18,... | collective-permute-start | bytes 737288 | tf_op jit(solution)/shard_map/ppermute | solution.py:56
  88.7 18.6 %collective-permute-start.33 = (bf16[192,1280]{1,0:T(8,128)(2,1)S(1)}, bf16[192,1280]{1,0:T(8,128)(2,1)S(1)}, u32[]{:S(2)}, u32[]{:S(2)}) collective-permute-start(bf16[192,1280]{1,0:T(8,128)(2,1)S(1)} %get-tuple-element.111), channel_id=1, source_target_pairs={{0,4},{2,6},{4,0},{6,2},{8,12},{10,14},{12,8},{14,10},{16,20},{18,... | collective-permute-start | bytes 1474568 | tf_op jit(solution)/shard_map/ppermute | solution.py:56
  89.6 17.6 %collective-permute-start.30 = (bf16[48,640]{1,0:T(8,128)(2,1)S(1)}, bf16[48,640]{1,0:T(8,128)(2,1)S(1)}, u32[]{:S(2)}, u32[]{:S(2)}) collective-permute-start(bf16[48,640]{1,0:T(8,128)(2,1)S(1)} %get-tuple-element.107), channel_id=1, source_target_pairs={{0,24},{2,26},{4,28},{6,30},{8,0},{10,2},{12,4},{14,6},{16,8},{18,... | collective-permute-start | bytes 184328 | tf_op jit(solution)/shard_map/ppermute | solution.py:56
  93.8 13.4 %collective-permute-start.31 = (bf16[48,640]{1,0:T(8,128)(2,1)S(1)}, bf16[48,640]{1,0:T(8,128)(2,1)S(1)}, u32[]{:S(2)}, u32[]{:S(2)}) collective-permute-start(bf16[48,640]{1,0:T(8,128)(2,1)S(1)} %get-tuple-element.108), channel_id=1, source_target_pairs={{0,16},{2,18},{4,20},{6,22},{8,24},{10,26},{12,28},{14,30},{16,0},... | collective-permute-start | bytes 184328 | tf_op jit(solution)/shard_map/ppermute | solution.py:56
  94.3 12.9 %collective-permute-start.32 = (bf16[48,640]{1,0:T(8,128)(2,1)S(1)}, bf16[48,640]{1,0:T(8,128)(2,1)S(1)}, u32[]{:S(2)}, u32[]{:S(2)}) collective-permute-start(bf16[48,640]{1,0:T(8,128)(2,1)S(1)} %get-tuple-element.109), channel_id=1, source_target_pairs={{0,8},{2,10},{4,12},{6,14},{8,16},{10,18},{12,20},{14,22},{16,24},... | collective-permute-start | bytes 184328 | tf_op jit(solution)/shard_map/ppermute | solution.py:56
  99.1 3.2 %copy-start.4 = (f32[512,128]{1,0:T(8,128)S(1)}, f32[512,128]{1,0:T(8,128)}, u32[]{:S(2)}) copy-start(f32[512,128]{1,0:T(8,128)} %copy-done.3) | copy-start | bytes 786436
  99.1 3.2 %copy-start.6 = (f32[512,128]{1,0:T(8,128)S(1)}, f32[512,128]{1,0:T(8,128)}, u32[]{:S(2)}) copy-start(f32[512,128]{1,0:T(8,128)} %copy-done.5) | copy-start | bytes 786436
  109.0 2.9 %collective-permute-start.34 = (bf16[384,1536]{1,0:T(8,128)(2,1)S(1)}, bf16[384,1536]{1,0:T(8,128)(2,1)S(1)}, u32[]{:S(2)}, u32[]{:S(2)}) collective-permute-start(bf16[384,1536]{1,0:T(8,128)(2,1)S(1)} %get-tuple-element.113), channel_id=1, source_target_pairs={{0,2},{2,0},{4,6},{6,4},{8,10},{10,8},{12,14},{14,12},{16,18},{18,... | collective-permute-start | bytes 3538952 | tf_op jit(solution)/shard_map/ppermute | solution.py:56
  109.1 19.9 %collective-permute-start.39 = (bf16[512,768]{1,0:T(8,128)(2,1)S(1)}, bf16[512,768]{1,0:T(8,128)(2,1)S(1)}, u32[]{:S(2)}, u32[]{:S(2)}) collective-permute-start(bf16[512,768]{1,0:T(8,128)(2,1)S(1)} %get-tuple-element.120.refs_2_), channel_id=1, source_target_pairs={{0,1},{1,0},{2,3},{3,2},{4,5},{5,4},{6,7},{7,6},{8,9},{9,8},{10,11... | collective-permute-start | bytes 2359304 | tf_op jit(solution)/shard_map/ppermute | solution.py:60
  112.2 16.9 %collective-permute-start.35 = (bf16[192,1536]{1,0:T(8,128)(2,1)S(1)}, bf16[192,1536]{1,0:T(8,128)(2,1)S(1)}, u32[]{:S(2)}, u32[]{:S(2)}) collective-permute-start(bf16[192,1536]{1,0:T(8,128)(2,1)S(1)} %get-tuple-element.116), channel_id=1, source_target_pairs={{0,4},{2,6},{4,0},{6,2},{8,12},{10,14},{12,8},{14,10},{16,20},{18,... | collective-permute-start | bytes 1769480 | tf_op jit(solution)/shard_map/ppermute | solution.py:56
  113.1 7.9 %collective-permute-start.36 = (bf16[48,1280]{1,0:T(8,128)(2,1)S(1)}, bf16[48,1280]{1,0:T(8,128)(2,1)S(1)}, u32[]{:S(2)}, u32[]{:S(2)}) collective-permute-start(bf16[48,1280]{1,0:T(8,128)(2,1)S(1)} %get-tuple-element.117), channel_id=1, source_target_pairs={{0,24},{2,26},{4,28},{6,30},{8,0},{10,2},{12,4},{14,6},{16,8},{18,... | collective-permute-start | bytes 368648 | tf_op jit(solution)/shard_map/ppermute | solution.py:56
  117.3 11.4 %collective-permute-start.37 = (bf16[48,1280]{1,0:T(8,128)(2,1)S(1)}, bf16[48,1280]{1,0:T(8,128)(2,1)S(1)}, u32[]{:S(2)}, u32[]{:S(2)}) collective-permute-start(bf16[48,1280]{1,0:T(8,128)(2,1)S(1)} %get-tuple-element.118), channel_id=1, source_target_pairs={{0,16},{2,18},{4,20},{6,22},{8,24},{10,26},{12,28},{14,30},{16,0},... | collective-permute-start | bytes 368648 | tf_op jit(solution)/shard_map/ppermute | solution.py:56
  117.8 11.0 %collective-permute-start.38 = (bf16[48,1280]{1,0:T(8,128)(2,1)S(1)}, bf16[48,1280]{1,0:T(8,128)(2,1)S(1)}, u32[]{:S(2)}, u32[]{:S(2)}) collective-permute-start(bf16[48,1280]{1,0:T(8,128)(2,1)S(1)} %get-tuple-element.119), channel_id=1, source_target_pairs={{0,8},{2,10},{4,12},{6,14},{8,16},{10,18},{12,20},{14,22},{16,24},... | collective-permute-start | bytes 368648 | tf_op jit(solution)/shard_map/ppermute | solution.py:56
  128.8 8.2 %copy-start.8 = (f32[48,1280]{1,0:T(8,128)}, f32[48,1280]{1,0:T(8,128)S(1)}, u32[]{:S(2)}) copy-start(f32[48,1280]{1,0:T(8,128)S(1)} %shard_map.180.refs_2_.refs_1_) | copy-start | bytes 737284
  129.0 9.9 %copy-start.7 = (bf16[512,768]{1,0:T(8,128)(2,1)}, bf16[512,768]{1,0:T(8,128)(2,1)S(1)}, u32[]{:S(2)}) copy-start(bf16[512,768]{1,0:T(8,128)(2,1)S(1)} %collective-permute-done.39.refs_3_) | copy-start | bytes 2359300
  129.9 24.4 %collective-permute-start.40 = (bf16[512,768]{1,0:T(8,128)(2,1)}, bf16[512,768]{1,0:T(8,128)(2,1)S(1)}, u32[]{:S(2)}, u32[]{:S(2)}) collective-permute-start(bf16[512,768]{1,0:T(8,128)(2,1)} %get-tuple-element.122.refs_1_), channel_id=1, source_target_pairs={{0,1},{1,0},{2,3},{3,2},{4,5},{5,4},{6,7},{7,6},{8,9},{9,8},{10,11... | collective-permute-start | bytes 2359304 | tf_op jit(solution)/shard_map/ppermute | solution.py:60
  130.5 14.3 %collective-permute-start.41 = (bf16[48,1536]{1,0:T(8,128)(2,1)S(1)}, bf16[48,1536]{1,0:T(8,128)(2,1)S(1)}, u32[]{:S(2)}, u32[]{:S(2)}) collective-permute-start(bf16[48,1536]{1,0:T(8,128)(2,1)S(1)} %get-tuple-element.123), channel_id=1, source_target_pairs={{0,24},{2,26},{4,28},{6,30},{8,0},{10,2},{12,4},{14,6},{16,8},{18,... | collective-permute-start | bytes 442376 | tf_op jit(solution)/shard_map/ppermute | solution.py:56
  135.0 12.6 %collective-permute-start.42 = (bf16[48,1536]{1,0:T(8,128)(2,1)S(1)}, bf16[48,1536]{1,0:T(8,128)(2,1)S(1)}, u32[]{:S(2)}, u32[]{:S(2)}) collective-permute-start(bf16[48,1536]{1,0:T(8,128)(2,1)S(1)} %get-tuple-element.124), channel_id=1, source_target_pairs={{0,16},{2,18},{4,20},{6,22},{8,24},{10,26},{12,28},{14,30},{16,0},... | collective-permute-start | bytes 442376 | tf_op jit(solution)/shard_map/ppermute | solution.py:56
  135.0 12.6 %collective-permute-start.43 = (bf16[48,1536]{1,0:T(8,128)(2,1)S(1)}, bf16[48,1536]{1,0:T(8,128)(2,1)S(1)}, u32[]{:S(2)}, u32[]{:S(2)}) collective-permute-start(bf16[48,1536]{1,0:T(8,128)(2,1)S(1)} %get-tuple-element.125), channel_id=1, source_target_pairs={{0,8},{2,10},{4,12},{6,14},{8,16},{10,18},{12,20},{14,22},{16,24},... | collective-permute-start | bytes 442376 | tf_op jit(solution)/shard_map/ppermute | solution.py:56
  144.7 2.9 %copy-start.20 = (bf16[48,1536]{1,0:T(8,128)(2,1)}, bf16[48,1536]{1,0:T(8,128)(2,1)S(1)}, u32[]{:S(2)}) copy-start(bf16[48,1536]{1,0:T(8,128)(2,1)S(1)} %collective-permute-done.41.refs_1_) | copy-start | bytes 442372
  151.1 8.0 %collective-permute-start.44 = (f32[48,2]{1,0:T(8,128)}, f32[48,2]{1,0:T(8,128)S(1)}, u32[]{:S(2)}, u32[]{:S(2)}) collective-permute-start(f32[48,2]{1,0:T(8,128)} %get-tuple-element.129.refs_4_), channel_id=1, source_target_pairs={{0,1},{1,0},{2,3},{3,2},{4,5},{5,4},{6,7},{7,6},{8,9},{9,8},{10,11... | collective-permute-start | bytes 1160 | tf_op jit(solution)/shard_map/ppermute | solution.py:60
  154.3 4.8 %copy-start.24 = (f32[48,2]{1,0:T(8,128)S(1)}, f32[48,2]{1,0:T(8,128)}, u32[]{:S(2)}) copy-start(f32[48,2]{1,0:T(8,128)} %get-tuple-element.129.refs_4_) | copy-start | bytes 1156
  (9 other events, 9.4 us)

commit v4 on v3

--- a/solution.py
+++ b/solution.py
@@ -14,6 +14,8 @@
 LANES = 128
 BLOCK = 128
 WINDOW = 256
+EARLY = 4
+WEIGHT = 10**10
 PIECES = 4
 
 EPSILON = 1e-05
@@ -98,13 +100,13 @@
             self.shard = after(self.shard, other)
             self.received = self.along_first(self.shard)
 
-    def stack(self):
+    def stack(self, weight=0):
         if self.plain:
             _, second, third = self.levels
             if self.late:
                 held, other = stack_rows([self.shard] + self.received, 2)
             else:
-                held = stack_rows([self.shard] + self.received)
+                held = stack_rows([self.shard] + self.received, weight=weight)
                 other = self.other = shifted(held, self.count, second, 1)
             self.pieces = [held, other]
             if not self.tail:
@@ -133,17 +135,16 @@
             for step in range(1, size):
                 total = total + wide(shifted(pieces[step], count, level, -step))
             held = total if level == self.levels[0] else low(total)
-        self.other = self.begun = held
-        self.parts = [held]
-
-    def second(self, *others):
+        self.other, self.begun, self.parts = [held], held, [held]
+
+    def second(self):
         if self.plain:
-            self.own, sent = add_split(self.own, self.other, 2)
-            self.other = shifted(after(sent, *others), self.count, self.levels[1], -1)
+            self.own, sent = add_halves(self.own, self.other)
+            self.other = [shifted(part, self.count, self.levels[1], -1) for part in sent]
 
     def third(self):
         if self.plain:
-            pieces = add_split([self.own], [self.other], 4)
+            pieces = add_split(self.own, self.other, 4)
             self.parts = [pieces[0]]
             for step in range(1, 4):
                 self.parts.append(shifted(pieces[step], self.count, self.levels[0], -step))
@@ -159,7 +160,8 @@
         weight *= size
     rows = width // count
     natural = (owner[:, None] * rows + jnp.arange(rows)[None, :]).reshape(width)
-    return low(natural[None, :] == jnp.arange(width)[:, None])
+    there = jnp.arange(width)
+    return low(natural[None, :] == there[:, None]), low(natural[:, None] == there[None, :])
 
 
 def spec(block, *place):
@@ -173,7 +175,7 @@
     latest.extend(arrays)
 
 
-def run(body, out_shapes, operands, specs=None, scratch=(), limit=LIMIT, last=False):
+def run(body, out_shapes, operands, specs=None, scratch=(), limit=LIMIT, last=False, weight=0):
     if last:
         limit = 60
         specs = [spec(array.shape, *[0] * array.ndim) for array in operands]
@@ -198,7 +200,7 @@
         ],
         scratch_shapes=scratch,
         compiler_params=pltpu.CompilerParams(vmem_limit_bytes=limit * 1024 * 1024),
-        cost_estimate=pl.CostEstimate(flops=0, bytes_accessed=0, transcendentals=0),
+        cost_estimate=pl.CostEstimate(flops=weight, bytes_accessed=0, transcendentals=0),
     )(*operands, *latest)
     latest[:] = [min(results, key=lambda array: array.size)]
     return results
@@ -212,7 +214,7 @@
     return jax.ShapeDtypeStruct(shape, jnp.float32)
 
 
-def stack_rows(pieces, parts=1):
+def stack_rows(pieces, parts=1, weight=0):
     rows, width = pieces[0].shape
     rows //= parts
 
@@ -221,8 +223,23 @@
             for part, out in enumerate(refs[-parts:]):
                 out[number * rows : (number + 1) * rows, :] = ref[part * rows : (part + 1) * rows, :]
 
-    stacked = run(body, [half(rows * len(pieces), width)] * parts, pieces, limit=SMALL)
+    stacked = run(body, [half(rows * len(pieces), width)] * parts, pieces, limit=SMALL, weight=weight)
     return stacked if parts > 1 else stacked[0]
+
+
+def add_halves(left, right):
+    rows = left[0].shape[0] // 2
+
+    def body(*refs):
+        pieces = len(left)
+        for i in range(pieces):
+            total = wide(refs[i][...]) + wide(refs[i + pieces][...])
+            refs[i + 2 * pieces][...] = low(total[:rows])
+            refs[i + 3 * pieces][...] = low(total[rows:])
+
+    shapes = [half(rows, piece.shape[1]) for piece in left]
+    results = run(body, shapes * 2, [*left, *right], limit=SMALL)
+    return results[: len(left)], results[len(left) :]
 
 
 def add_split(left, right, parts):
@@ -252,47 +269,48 @@
     def body(*refs):
         refs[-1][...] = total_of(refs[:-1])
 
-    return run(body, [full(*parts[0].shape)], parts, limit=SMALL)[0]
-
-
-def finish_feed_forward(active, others, weights, gain, hidden):
-    rows, room = active.shape
-
-    def body(active_ref, others_ref, weights_ref, gain_ref, sum_ref, down_ref, share_ref):
-        active, factor = active_ref[...], others_ref[:, :room]
-        down_ref[...] = others_ref[:, room : room + hidden]
-        sum_ref[:, 0, :] = active[:, :hidden] * gain_ref[...]
-        sum_ref[:, 1, :] = factor[:, :hidden] * gain_ref[...]
-        share = wide(weights_ref[:, :room]) * active + wide(weights_ref[:, room:]) * factor
-        share_ref[...] = jnp.sum(share, axis=1, keepdims=True) / gain_ref[...]
-
-    return run(
-        body,
-        [full(rows, 2, hidden), full(rows, hidden), full(rows, 1)],
-        [active, others, weights, gain],
+    return run(body, [full(*parts[0].shape)], parts, limit=SMALL, weight=WEIGHT)[0]
+
+
+def finish_feed_forward(total, weights, gains, hidden):
+    rows, room = total.shape[0], total.shape[1] // 3
+
+    def body(total_ref, weights_ref, gains_ref, sum_ref, down_ref, columns_ref):
+        gain = gains_ref[:, :1]
+        down_ref[...] = total_ref[:, 2 * room : 2 * room + hidden]
+        sum_ref[0] = total_ref[:, :hidden] * gain
+        sum_ref[1] = total_ref[:, room : room + hidden] * gain
+        share = jnp.sum(wide(weights_ref[...]) * total_ref[:, : 2 * room], axis=1, keepdims=True) / gain
+        lane = lax.broadcasted_iota(jnp.int32, (rows, 2), 1)
+        columns_ref[...] = jnp.where(lane == 0, gains_ref[:, 1:], share)
+
+    return run(
+        body,
+        [full(2, rows, hidden), full(rows, hidden), full(rows, 2)],
+        [total, weights, gains],
         last=True,
     )
 
 
-def finish_attention(parts, query_keys, values_out, gain, share):
+def finish_attention(parts, query_keys, values_out, columns):
     rows, inner = values_out.shape[0], values_out.shape[1] // 2
 
     def body(*refs):
-        *parts, query_keys_ref, values_out_ref, gain_ref, other_ref, sum_ref, out_ref, share_ref = refs
-        total = total_of(parts)
+        *parts, query_keys_ref, values_out_ref, columns_ref, sum_ref, out_ref, share_ref = refs
+        total, gain = total_of(parts), columns_ref[:, :1]
         for number in range(3):
-            sum_ref[:, number, :] = total[:, number * inner : (number + 1) * inner] * gain_ref[...]
+            sum_ref[number] = total[:, number * inner : (number + 1) * inner] * gain
         out_ref[...] = total[:, 3 * inner :]
         share = jnp.sum(wide(query_keys_ref[...]) * total[:, : 2 * inner], axis=1, keepdims=True)
         values = wide(values_out_ref[:, :inner]) * total[:, 2 * inner : 3 * inner]
-        share = (share + jnp.sum(values, axis=1, keepdims=True)) / gain_ref[...]
+        share = (share + jnp.sum(values, axis=1, keepdims=True)) / gain
         lane = lax.broadcasted_iota(jnp.int32, (rows, 2), 1)
-        share_ref[...] = jnp.where(lane == 0, share, other_ref[...])
-
-    return run(
-        body,
-        [full(rows, 3, inner), full(rows, inner), full(rows, 2)],
-        [*parts, query_keys, values_out, gain, share],
+        share_ref[...] = jnp.where(lane == 0, share, columns_ref[...])
+
+    return run(
+        body,
+        [full(3, rows, inner), full(rows, inner), full(rows, 2)],
+        [*parts, query_keys, values_out, columns],
         last=True,
     )
 
@@ -465,12 +483,15 @@
     return run(body, [half(width // 2, hidden)] * 6, [normed, mixed, gates, upstream])
 
 
-def add_output(middle, own, other, order):
-    def body(middle_ref, own_ref, other_ref, order_ref, out_ref):
-        total = low(middle_ref[...] + (wide(own_ref[...]) + wide(other_ref[...])))
-        out_ref[...] = low(product(total, order_ref[...], NT))
-
-    return run(body, [half(*middle.shape)], [middle, own, other, order], last=True)[0]
+def add_output(middle, own, others, order):
+    cut = others[0].shape[0]
+
+    def body(middle_ref, own_ref, upper_ref, lower_ref, order_ref, out_ref):
+        for part, ref in ((slice(0, cut), upper_ref), (slice(cut, None), lower_ref)):
+            total = low(middle_ref[part, :] + (wide(own_ref[part, :]) + wide(ref[...])))
+            out_ref[part, :] = low(product(total, order_ref[...]))
+
+    return run(body, [half(*middle.shape)], [middle, own, *others, order], last=True)[0]
 
 
 def attend_back_values(upstream, middle, own, other, pieces, context, shares):
@@ -572,7 +593,7 @@
         total = grad_middle_ref[...] + norm_back(scaled, normed, inverse)
         high = low(total)
         rest = low(total - wide(high))
-        out_ref[...] = product(high, order_ref[...], NT) + product(rest, order_ref[...], NT)
+        out_ref[...] = product(high, order_ref[...]) + product(rest, order_ref[...])
 
     return run(
         body,
@@ -610,23 +631,23 @@
     latest.clear()
     query_keys = Gather(shard_one, devices)
     down = Gather(shard_four, devices, late=True)
-    order = placement(devices, width)
+    order, back = placement(devices, width)
     cosine, sine = rope_tables(positions)
     column, row = seg_ids[:, None], seg_ids[None, :]
-    wait_for(cosine, sine, column)
-    inputs, normed_one, upstream = prepare(tokens, cotangent, order)
-    down.join_rows()
     held = query_keys.stack()
     values_out = Gather(after(shard_two, held), devices)
     wait_for(query_keys.other)
     held = values_out.stack()
     gates_in = Gather(after(shard_three, held), devices, tail=True)
+    wait_for(cosine, sine, column)
+    inputs, normed_one, upstream = prepare(tokens, cotangent, order)
+    down.join_rows()
     query, keys, shares = attend_shares(normed_one, query_keys.pieces, cosine, sine, column, row)
+    wait_for(values_out.other)
+    held = gates_in.stack(WEIGHT)
+    down.begin(held)
     values, context, own = attend_values(normed_one, values_out.pieces, shares)
     other = swapped(own)
-    wait_for(values_out.other)
-    held = gates_in.stack()
-    down.begin(held)
     wait_for(other)
     gates_in.share(down.stack())
     middle, normed_two, mixed, grad_gates, own_out, own_two = feed_forward(
@@ -634,11 +655,10 @@
     )
     other_two = swapped(own_two)
     grads_mlp = feed_forward_grads(normed_two, mixed, grad_gates, upstream)
-    sums_active = Scatter(grads_mlp[:1], grads_mlp[3:4], devices, rows)
-    sums_others = Scatter(grads_mlp[1:3], grads_mlp[4:], devices, rows)
-    sums_active.second()
-    sums_others.second(sums_active.other)
-    sums_active.third()
+    sums_mlp = Scatter(grads_mlp[:3], grads_mlp[3:], devices, rows)
+    sums_mlp.second()
+    early = own_out.shape[0] // EARLY
+    upper_out = swapped(after(own_out[:early], other_two))
     grad_middle, branch, grad_context, grad_values = attend_back_values(
         upstream, middle, own_two, other_two, values_out.pieces, context, shares
     )
@@ -646,25 +666,25 @@
         query, keys, values, grad_context, shares, grad_values, cosine, sine, query_keys.pieces, values_out.pieces
     )
     other_one = swapped(own_one)
-    sum_active = add_all(sums_active.parts)
-    wait_for(sums_others.other)
+    wait_for(upper_out, *sums_mlp.other)
     kept, sent = paired_grads(
         [[(normed_one, grad_query_keys), (normed_one, grad_values), (branch, context)]]
     )
     sums = Scatter([kept], [sent], devices, rows)
-    sums_others.third()
+    sums_mlp.third()
     sums.second()
-    sum_others = add_all(sums_others.parts)
     wait_for(other_one)
+    sum_mlp = add_all(sums_mlp.parts)
     sums.third()
-    other_out = swapped(after(own_out, sums.begun))
-    sum_in, sum_down, share = finish_feed_forward(
-        sum_active, sum_others, shard_three, gain_two, hidden
-    )
-    grad_input = input_grads(grad_middle, inputs, own_one, other_one, order)
-    sum_qkv, sum_out, share = finish_attention(sums.parts, shard_one, shard_two, gain_one, share)
-    output = add_output(middle, own_out, other_out, order)
+    lower_out = swapped(after(own_out[early:], sums.begun))
+    sum_in, sum_down, columns = finish_feed_forward(
+        sum_mlp, shard_three, jnp.concatenate([gain_two, gain_one], axis=1), hidden
+    )
+    grad_input = input_grads(grad_middle, inputs, own_one, other_one, back)
+    sum_qkv, sum_out, share = finish_attention(sums.parts, shard_one, shard_two, columns)
+    output = add_output(middle, own_out, (upper_out, lower_out), back)
     gains = after(share, output) + swapped(share)
+    sum_qkv, sum_in = (jnp.transpose(array, (1, 0, 2)) for array in (sum_qkv, sum_in))
     return (output, grad_input, gains[:, 0], sum_qkv, sum_out.T, gains[:, 1], sum_in, sum_down.T)
 
 

time: 160 us -> 151 us (0.944)
  starting transfers between devices: 50.9 us -> 46.7 us
  waiting for transfers between devices: 53.5 us -> 51 us
  Pallas kernels: 38 us -> 35.9 us
    ppermute x40 -> x38, waiting for transfers between devices: 48.7 us -> 35.5 us  [shifted(): return lax.ppermute(values, 'dp', pairs)]
    ppermute x5 -> x6, waiting for transfers between devices: 4.83 us -> 15.5 us  [swapped(): return lax.ppermute(values, 'tensor', [(0, 1), (1, 0)])]
    ppermute x40 -> x38, starting transfers between devices: 46.2 us -> 39.2 us  [shifted(): return lax.ppermute(values, 'dp', pairs)]
    ppermute x5 -> x6, starting transfers between devices: 4.74 us -> 7.5 us  [swapped(): return lax.ppermute(values, 'tensor', [(0, 1), (1, 0)])]
    pallas_call x25 -> x22, Pallas kernels: 38 us -> 35.9 us  [run(): pl.pallas_call(ordered, out_shape=out_shapes, grid=grid, in_specs=specs +...]
    unnamed x57 -> x53, local copies, waits for them, and re-layouts: 7.61 us -> 7.87 us
  transfers between devices with their start and end apart: 45 -> 44, of which waited for: 18 -> 16; matrix products, arithmetic and copies ran while one was open for 4% -> 4% of each run, Pallas kernels for 17% -> 19%
where the time goes in v4:
time: 151 us; the launch traced here: 150 us
  waiting for transfers between devices  51 us (34%)
  starting transfers between devices  46.7 us (31%)
  Pallas kernels  35.9 us (24%)
  local copies, waits for them, and re-layouts  11.5 us (8%)
  other arithmetic  4.13 us (3%)
    ppermute x38, starting transfers between devices, shifted(): return lax.ppermute(values, 'dp', pairs)  39.2 us
    pallas_call x22, Pallas kernels, run(): pl.pallas_call(ordered, out_shape=out_shapes, grid=grid, in_specs=specs +...  35.9 us
    ppermute x38, waiting for transfers between devices, shifted(): return lax.ppermute(values, 'dp', pairs)  35.5 us
    ppermute x6, waiting for transfers between devices, swapped(): return lax.ppermute(values, 'tensor', [(0, 1), (1, 0)])  15.5 us
    unnamed x53, local copies, waits for them, and re-layouts  7.87 us
    ppermute x6, starting transfers between devices, swapped(): return lax.ppermute(values, 'tensor', [(0, 1), (1, 0)])  7.5 us
  transfers between devices with their start and end apart: 44, of which 16 were waited for; matrix products, arithmetic and copies ran while one was open for 4% of the time, Pallas kernels for 19%

profile of v4, /device:TPU:0, one launch (start us, length us, event | category | flops | bytes accessed | tf_op | source)
XLA Modules:
  0.0 150.4 jit_solution(4085711307765743775)
XLA Ops:
  0.6 0.7 convert_bitcast_fusion
  1.4 0.9 fusion.9
  2.3 3.1 %collective-permute-start = (bf16[48,768]{1,0:T(8,128)(2,1)S(1)}, bf16[48,768]{1,0:T(8,128)(2,1)S(1)}, u32[]{:S(2)}, u32[]{:S(2)}) collective-permute-start(bf16[48,768]{1,0:T(8,128)(2,1)S(1)} %pad_maximum_fusion.1.refs_0_.refs_4_), channel_id=1, source_target_pairs={{0,8},{2,10},{4,12},{6,14},{8,16},{10,18},{12,20},{14,22},{16,24},... | collective-permute-start | bytes 221192 | tf_op jit(solution)/shard_map/ppermute | solution.py:58
  5.4 2.6 %collective-permute-start.1 = (bf16[48,768]{1,0:T(8,128)(2,1)S(1)}, bf16[48,768]{1,0:T(8,128)(2,1)S(1)}, u32[]{:S(2)}, u32[]{:S(2)}) collective-permute-start(bf16[48,768]{1,0:T(8,128)(2,1)S(1)} %pad_maximum_fusion.1.refs_0_.refs_4_), channel_id=1, source_target_pairs={{0,16},{2,18},{4,20},{6,22},{8,24},{10,26},{12,28},{14,30},{16,0},... | collective-permute-start | bytes 221192 | tf_op jit(solution)/shard_map/ppermute | solution.py:58
  8.0 1.3 collective-permute-start.2
  9.3 0.8 pad.10.refs_0_
  10.1 1.5 %collective-permute-start.12 = (bf16[48,640]{1,0:T(8,128)(2,1)S(1)}, bf16[48,640]{1,0:T(8,128)(2,1)S(1)}, u32[]{:S(2)}, u32[]{:S(2)}) collective-permute-start(bf16[48,640]{1,0:T(8,128)(2,1)S(1)} %pad.10.refs_0_), channel_id=1, source_target_pairs={{0,4},{2,6},{4,0},{6,2},{8,12},{10,14},{12,8},{14,10},{16,20},{18,... | collective-permute-start | bytes 184328 | tf_op jit(solution)/shard_map/ppermute | solution.py:58
  11.8 1.3 fusion.1
  13.4 1.3 collective-permute-start.6
  14.8 1.9 %collective-permute-start.3 = (bf16[48,768]{1,0:T(8,128)(2,1)S(1)}, bf16[48,768]{1,0:T(8,128)(2,1)S(1)}, u32[]{:S(2)}, u32[]{:S(2)}) collective-permute-start(bf16[48,768]{1,0:T(8,128)(2,1)S(1)} %pad_maximum_fusion.refs_0_.refs_5_), channel_id=1, source_target_pairs={{0,8},{2,10},{4,12},{6,14},{8,16},{10,18},{12,20},{14,22},{16,24},... | collective-permute-start | bytes 221192 | tf_op jit(solution)/shard_map/ppermute | solution.py:58
  16.7 1.9 %collective-permute-start.4 = (bf16[48,768]{1,0:T(8,128)(2,1)S(1)}, bf16[48,768]{1,0:T(8,128)(2,1)S(1)}, u32[]{:S(2)}, u32[]{:S(2)}) collective-permute-start(bf16[48,768]{1,0:T(8,128)(2,1)S(1)} %pad_maximum_fusion.refs_0_.refs_5_), channel_id=1, source_target_pairs={{0,16},{2,18},{4,20},{6,22},{8,24},{10,26},{12,28},{14,30},{16,0},... | collective-permute-start | bytes 221192 | tf_op jit(solution)/shard_map/ppermute | solution.py:58
  19.6 1.9 %collective-permute-done.3.refs_1_ = bf16[48,768]{1,0:T(8,128)(2,1)S(1)} collective-permute-done((bf16[48,768]{1,0:T(8,128)(2,1)S(1)}, bf16[48,768]{1,0:T(8,128)(2,1)S(1)}, u32[]{:S(2)}, u32[]{:S(2)}) %collective-permute-start.3) | collective-permute-done | bytes 73760 | tf_op jit(solution)/shard_map/ppermute | solution.py:58
  21.5 2.2 %collective-permute-done.4.refs_2_ = bf16[48,768]{1,0:T(8,128)(2,1)S(1)} collective-permute-done((bf16[48,768]{1,0:T(8,128)(2,1)S(1)}, bf16[48,768]{1,0:T(8,128)(2,1)S(1)}, u32[]{:S(2)}, u32[]{:S(2)}) %collective-permute-start.4) | collective-permute-done | bytes 73760 | tf_op jit(solution)/shard_map/ppermute | solution.py:58
  23.8 0.7 collective-permute-start.7
  25.2 1.7 %collective-permute-start.13 = (bf16[48,1280]{1,0:T(8,128)(2,1)S(1)}, bf16[48,1280]{1,0:T(8,128)(2,1)S(1)}, u32[]{:S(2)}, u32[]{:S(2)}) collective-permute-start(bf16[48,1280]{1,0:T(8,128)(2,1)S(1)} %fusion.5.refs_0_.refs_1_), channel_id=1, source_target_pairs={{0,8},{2,10},{4,12},{6,14},{8,16},{10,18},{12,20},{14,22},{16,24},... | collective-permute-start | bytes 368648 | tf_op jit(solution)/shard_map/ppermute | solution.py:58
  26.8 1.3 collective-permute-start.14
  28.2 3.8 %collective-permute-done.7.refs_5_.refs_2_.refs_13_ = bf16[192,768]{1,0:T(8,128)(2,1)S(1)} collective-permute-done((bf16[192,768]{1,0:T(8,128)(2,1)S(1)}, bf16[192,768]{1,0:T(8,128)(2,1)S(1)}, u32[]{:S(2)}, u32[]{:S(2)}) %collective-permute-start.7) | collective-permute-done | bytes 294944 | tf_op jit(solution)/shard_map/ppermute | solution.py:58
  32.0 1.3 collective-permute-start.15
  33.2 1.0 fusion.2
  34.2 1.1 copy-done.10
  35.4 1.1 copy-done.11
  36.5 1.5 shard_map.163
  38.6 2.7 %shard_map.165 = (bf16[512,384]{1,0:T(8,128)(2,1)S(1)}, bf16[512,384]{1,0:T(8,128)(2,1)S(1)}, bf16[12,256,256]{2,1,0:T(8,128)(2,1)S(1)}) custom-call(bf16[512,768]{1,0:T(8,128)(2,1)S(1)} %get-tuple-element.72.refs_0_.refs_2_, bf16[192,768]{1,0:T(8,128)(2,1)S(1)} %shard_map.161.refs_4_.refs_1_.refs_8_, ...), custom_call_target="tpu_custom_call" | custom-call | tf_op jit(solution)/shard_map/pallas_call | solution.py:192
  41.5 1.7 %shard_map.167 = (bf16[512,384]{1,0:T(8,128)(2,1)S(1)}, bf16[512,384]{1,0:T(8,128)(2,1)S(1)}, bf16[512,768]{1,0:T(8,128)(2,1)S(1)}) custom-call(bf16[512,768]{1,0:T(8,128)(2,1)S(1)} %get-tuple-element.72.refs_0_.refs_2_, bf16[192,768]{1,0:T(8,128)(2,1)S(1)} %shard_map.162.refs_3_.refs_1_.refs_4_.refs_12_, ...), custom_call_target="tpu_custom_call" | custom-call | tf_op jit(solution)/shard_map/pallas_call | solution.py:192
  43.2 1.6 %collective-permute-start.16 = (bf16[512,768]{1,0:T(8,128)(2,1)S(1)}, bf16[512,768]{1,0:T(8,128)(2,1)S(1)}, u32[]{:S(2)}, u32[]{:S(2)}) collective-permute-start(bf16[512,768]{1,0:T(8,128)(2,1)S(1)} %get-tuple-element.76.refs_2_), channel_id=1, source_target_pairs={{0,1},{1,0},{2,3},{3,2},{4,5},{5,4},{6,7},{7,6},{8,9},{9,8},{10,11... | collective-permute-start | bytes 2359304 | tf_op jit(solution)/shard_map/ppermute | solution.py:62
  45.9 1.5 collective-permute-start.19
  47.3 2.9 %collective-permute-start.20 = (bf16[96,640]{1,0:T(8,128)(2,1)S(1)}, bf16[96,640]{1,0:T(8,128)(2,1)S(1)}, u32[]{:S(2)}, u32[]{:S(2)}) collective-permute-start(bf16[96,640]{1,0:T(8,128)(2,1)S(1)} %shard_map.164.refs_9_.refs_0_), channel_id=1, source_target_pairs={{0,24},{2,26},{4,28},{6,30},{8,0},{10,2},{12,4},{14,6},{16,8},{18,... | collective-permute-start | bytes 368648 | tf_op jit(solution)/shard_map/ppermute | solution.py:58
  50.2 3.1 %collective-permute-done.18.refs_1_ = bf16[96,640]{1,0:T(8,128)(2,1)S(1)} collective-permute-done((bf16[96,640]{1,0:T(8,128)(2,1)S(1)}, bf16[96,640]{1,0:T(8,128)(2,1)S(1)}, u32[]{:S(2)}, u32[]{:S(2)}) %collective-permute-start.18) | collective-permute-done | bytes 122912 | tf_op jit(solution)/shard_map/ppermute | solution.py:58
  53.3 3.9 %collective-permute-done.19.refs_2_ = bf16[96,640]{1,0:T(8,128)(2,1)S(1)} collective-permute-done((bf16[96,640]{1,0:T(8,128)(2,1)S(1)}, bf16[96,640]{1,0:T(8,128)(2,1)S(1)}, u32[]{:S(2)}, u32[]{:S(2)}) %collective-permute-start.19) | collective-permute-done | bytes 122912 | tf_op jit(solution)/shard_map/ppermute | solution.py:58
  57.2 5.5 %collective-permute-done.16.refs_5_.refs_3_ = bf16[512,768]{1,0:T(8,128)(2,1)S(1)} collective-permute-done((bf16[512,768]{1,0:T(8,128)(2,1)S(1)}, bf16[512,768]{1,0:T(8,128)(2,1)S(1)}, u32[]{:S(2)}, u32[]{:S(2)}) %collective-permute-start.16) | collective-permute-done | bytes 786464 | tf_op jit(solution)/shard_map/ppermute | solution.py:62
  63.9 1.9 %collective-permute-done.23.refs_10_ = bf16[192,640]{1,0:T(8,128)(2,1)S(1)} collective-permute-done((bf16[192,640]{1,0:T(8,128)(2,1)S(1)}, bf16[192,640]{1,0:T(8,128)(2,1)S(1)}, u32[]{:S(2)}, u32[]{:S(2)}) %collective-permute-start.23) | collective-permute-done | bytes 245792 | tf_op jit(solution)/shard_map/ppermute | solution.py:58
  66.2 4.5 %shard_map.169 = (f32[512,768]{1,0:T(8,128)S(1)}, bf16[512,768]{1,0:T(8,128)(2,1)S(1)}, bf16[512,640]{1,0:T(8,128)(2,1)S(1)}, bf16[512,1280]{1,0:T(8,128)(2,1)S(...) custom-call(bf16[512,768]{1,0:T(8,128)(2,1)S(1)} %get-tuple-element.70.refs_2_.refs_0_.refs_1_, ...), custom_call_target="tpu_custom_call" | custom-call | tf_op jit(solution)/shard_map/pallas_call | solution.py:192
  70.7 1.6 %collective-permute-start.25 = (bf16[512,768]{1,0:T(8,128)(2,1)S(1)}, bf16[512,768]{1,0:T(8,128)(2,1)S(1)}, u32[]{:S(2)}, u32[]{:S(2)}) collective-permute-start(bf16[512,768]{1,0:T(8,128)(2,1)S(1)} %get-tuple-element.85.refs_2_), channel_id=1, source_target_pairs={{0,1},{1,0},{2,3},{3,2},{4,5},{5,4},{6,7},{7,6},{8,9},{9,8},{10,11... | collective-permute-start | bytes 2359304 | tf_op jit(solution)/shard_map/ppermute | solution.py:62
  72.2 1.8 %shard_map.170 = (bf16[384,640]{1,0:T(8,128)(2,1)S(1)}, bf16[384,640]{1,0:T(8,128)(2,1)S(1)}, bf16[384,640]{1,0:T(8,128)(2,1)S(1)}, bf16[384,640]{1,0:T(8,128)(2...) custom-call(bf16[512,768]{1,0:T(8,128)(2,1)S(1)} %get-tuple-element.89.refs_0_, ...), custom_call_target="tpu_custom_call" | custom-call | tf_op jit(solution)/shard_map/pallas_call | solution.py:192
  74.7 1.3 collective-permute-done.27.refs_3_
  76.0 0.7 collective-permute-done.28.refs_4_
  76.7 0.7 collective-permute-done.29.refs_5_
  78.3 1.5 %collective-permute-start.31 = (bf16[192,640]{1,0:T(8,128)(2,1)S(1)}, bf16[192,640]{1,0:T(8,128)(2,1)S(1)}, u32[]{:S(2)}, u32[]{:S(2)}) collective-permute-start(bf16[192,640]{1,0:T(8,128)(2,1)S(1)} %get-tuple-element.104), channel_id=1, source_target_pairs={{0,4},{2,6},{4,0},{6,2},{8,12},{10,14},{12,8},{14,10},{16,20},{18,... | collective-permute-start | bytes 737288 | tf_op jit(solution)/shard_map/ppermute | solution.py:58
  80.3 10.0 %collective-permute-done.25.refs_3_ = bf16[512,768]{1,0:T(8,128)(2,1)S(1)} collective-permute-done((bf16[512,768]{1,0:T(8,128)(2,1)S(1)}, bf16[512,768]{1,0:T(8,128)(2,1)S(1)}, u32[]{:S(2)}, u32[]{:S(2)}) %collective-permute-start.25) | collective-permute-done | bytes 786464 | tf_op jit(solution)/shard_map/ppermute | solution.py:62
  90.3 1.5 collective-permute-start.26
  91.8 2.0 %shard_map.172 = (f32[512,768]{1,0:T(8,128)S(1)}, bf16[512,768]{1,0:T(8,128)(2,1)S(1)}, bf16[512,384]{1,0:T(8,128)(2,1)S(1)}, bf16[512,384]{1,0:T(8,128)(2,1)S(1)}) custom-call(bf16[512,768]{1,0:T(8,128)(2,1)S(1)} %get-tuple-element.71.refs_1_.refs_3_.refs_0_, f32[512,768]{1,0:T(8,128)S(1)} %get-tuple-element.83.refs_1_.refs_0_, ...), custom_call_target="tpu_custom_call" | custom-call | tf_op jit(solution)/shard_map/pallas_call | solution.py:192
  93.8 1.1 copy-done.5
  95.0 5.2 %shard_map.173 = (bf16[512,768]{1,0:T(8,128)(2,1)S(1)}, bf16[512,768]{1,0:T(8,128)(2,1)S(1)}) custom-call(bf16[512,384]{1,0:T(8,128)(2,1)S(1)} %get-tuple-element.75.refs_4_.refs_0_, bf16[512,384]{1,0:T(8,128)(2,1)S(1)} %get-tuple-element.87.refs_1_, bf16[512,384]{1,0:T(8,128)(2,1)S(1)} %get-tuple-element.78.refs_4_.refs_2_, ...), custom_call_target="tpu_custom_call" | custom-call | tf_op jit(solution)/shard_map/pallas_call | solution.py:192
  100.2 1.6 %shard_map.174 = (bf16[384,1536]{1,0:T(8,128)(2,1)S(1)}, bf16[384,1536]{1,0:T(8,128)(2,1)S(1)}) custom-call(bf16[512,768]{1,0:T(8,128)(2,1)S(1)} %get-tuple-element.72.refs_0_.refs_2_, bf16[512,768]{1,0:T(8,128)(2,1)S(1)} %get-tuple-element.101.refs_1_.refs_6_, bf16[512,768]{1,0:T(8,128)(2,1)S(1)} %get-tuple-element.72.refs_0_.refs_2_, ...), custom_call_target="tpu_custom_call" | custom-call | tf_op jit(solution)/shard_map/pallas_call | solution.py:192
  102.7 1.4 collective-permute-start.35
  104.0 1.1 collective-permute-start.36
  105.1 1.9 %collective-permute-start.37 = (bf16[48,1920]{1,0:T(8,128)(2,1)S(1)}, bf16[48,1920]{1,0:T(8,128)(2,1)S(1)}, u32[]{:S(2)}, u32[]{:S(2)}) collective-permute-start(bf16[48,1920]{1,0:T(8,128)(2,1)S(1)} %get-tuple-element.115), channel_id=1, source_target_pairs={{0,8},{2,10},{4,12},{6,14},{8,16},{10,18},{12,20},{14,22},{16,24},... | collective-permute-start | bytes 552968 | tf_op jit(solution)/shard_map/ppermute | solution.py:58
  107.1 0.9 slice.33
  108.3 0.8 collective-permute-start.34
  109.4 12.4 %collective-permute-done.36.refs_2_ = bf16[48,1920]{1,0:T(8,128)(2,1)S(1)} collective-permute-done((bf16[48,1920]{1,0:T(8,128)(2,1)S(1)}, bf16[48,1920]{1,0:T(8,128)(2,1)S(1)}, u32[]{:S(2)}, u32[]{:S(2)}) %collective-permute-start.36) | collective-permute-done | bytes 184352 | tf_op jit(solution)/shard_map/ppermute | solution.py:58
  122.0 0.8 copy-done.9
  123.7 1.5 collective-permute-start.39
  125.2 2.2 %collective-permute-start.40 = (bf16[48,1536]{1,0:T(8,128)(2,1)S(1)}, bf16[48,1536]{1,0:T(8,128)(2,1)S(1)}, u32[]{:S(2)}, u32[]{:S(2)}) collective-permute-start(bf16[48,1536]{1,0:T(8,128)(2,1)S(1)} %get-tuple-element.119), channel_id=1, source_target_pairs={{0,24},{2,26},{4,28},{6,30},{8,0},{10,2},{12,4},{14,6},{16,8},{18,... | collective-permute-start | bytes 442376 | tf_op jit(solution)/shard_map/ppermute | solution.py:58
  127.3 1.4 collective-permute-start.42
  128.8 0.7 copy.34.refs_2_
  129.5 1.9 %shard_map.179 = (f32[2,48,576]{2,1,0:T(8,128)}, f32[48,576]{1,0:T(8,128)}, f32[48,2]{1,0:T(8,128)}) custom-call(f32[48,1920]{1,0:T(8,128)} %copy-done.6, bf16[48,1280]{1,0:T(8,128)(2,1)} %copy-done.15, f32[48,2]{1,0:T(8,128)} %copy.34.refs_2_, bf16[48,1536]{1,0:T(8,128)(2,1)} %copy-done.14), custom_call_target="tpu_custom_call" | custom-call | tf_op jit(solution)/shard_map/pallas_call | solution.py:192
  131.4 5.9 %shard_map.180.refs_7_ = f32[512,768]{1,0:T(8,128)} custom-call(f32[512,768]{1,0:T(8,128)} %copy-done.5, bf16[512,768]{1,0:T(8,128)(2,1)} %copy-done, bf16[512,768]{1,0:T(8,128)(2,1)} %copy-done.8, bf16[512,768]{1,0:T(8,128)(2,1)} %copy-done.9, bf16[768,768]{1,0:T(8,128)(2,1)} %get-tuple-element.161.refs_4_, f32[48,2]{1,0:T(8,128)} %get-tuple-element.122.refs_5_.refs_6_), custom_call_target="tpu_custom_call" | custom-call | tf_op jit(solution)/shard_map/pallas_call | solution.py:192
  137.3 2.7 %collective-permute-done.41.refs_2_ = bf16[48,1536]{1,0:T(8,128)(2,1)S(1)} collective-permute-done((bf16[48,1536]{1,0:T(8,128)(2,1)S(1)}, bf16[48,1536]{1,0:T(8,128)(2,1)S(1)}, u32[]{:S(2)}, u32[]{:S(2)}) %collective-permute-start.41) | collective-permute-done | bytes 147488 | tf_op jit(solution)/shard_map/ppermute | solution.py:58
  141.3 2.1 %shard_map.181 = (f32[3,48,384]{2,1,0:T(8,128)}, f32[48,384]{1,0:T(8,128)}, f32[48,2]{1,0:T(8,128)}) custom-call(bf16[48,1536]{1,0:T(8,128)(2,1)} %copy-done.14, bf16[48,1536]{1,0:T(8,128)(2,1)} %copy-done.20, bf16[48,1536]{1,0:T(8,128)(2,1)} %copy-done.21, bf16[48,1536]{1,0:T(8,128)(2,1)} %copy-done.22, bf16[48,768]{1,0:T(8,128)(2,1)} %copy-done.12, ...), custom_call_target="tpu_custom_call" | custom-call | tf_op jit(solution)/shard_map/pallas_call | solution.py:192
  143.4 0.8 collective-permute-start.43
  144.2 0.8 copy.35
  145.0 0.8 copy-done.17
  145.8 3.9 %shard_map.182 = bf16[512,768]{1,0:T(8,128)(2,1)} custom-call(f32[512,768]{1,0:T(8,128)} %copy-done.1, bf16[512,768]{1,0:T(8,128)(2,1)} %copy-done.2, bf16[128,768]{1,0:T(8,128)(2,1)} %copy-done.7, bf16[384,768]{1,0:T(8,128)(2,1)} %copy-done.17, bf16[768,768]{1,0:T(8,128)(2,1)} %get-tuple-element.161.refs_4_, f32[48,2]{1,0:T(8,128)} %get-tuple-element.125.refs_5_), custom_call_target="tpu_custom_call" | custom-call | tf_op jit(solution)/shard_map/pallas_call | solution.py:192
  149.7 0.7 slice_reduce_fusion
  (124 shorter events, 11.3 us)
Async XLA Ops:
  0.6 12.5 %copy-start.18 = (bf16[48,2,576]{2,1,0:T(2,128)(2,1)S(1)}, bf16[48,2,576]{2,1,0:T(2,128)(2,1)}, u32[]{:S(2)}) copy-start(bf16[48,2,576]{2,1,0:T(2,128)(2,1)} %param.17) | copy-start | bytes 331780
  2.3 11.1 %copy-start.12 = (bf16[48,768]{1,0:T(8,128)(2,1)}, bf16[48,768]{1,0:T(8,128)(2,1)S(1)}, u32[]{:S(2)}) copy-start(bf16[48,768]{1,0:T(8,128)(2,1)S(1)} %pad_maximum_fusion.1.refs_0_.refs_4_) | copy-start | bytes 221188
  2.3 11.1 %copy-start.24 = (bf16[384,48]{0,1:T(8,128)(2,1)S(1)}, bf16[384,48]{0,1:T(8,128)(2,1)}, u32[]{:S(2)}) copy-start(bf16[384,48]{0,1:T(8,128)(2,1)} %param.15) | copy-start | bytes 110596
  2.3 11.1 %collective-permute-start = (bf16[48,768]{1,0:T(8,128)(2,1)S(1)}, bf16[48,768]{1,0:T(8,128)(2,1)S(1)}, u32[]{:S(2)}, u32[]{:S(2)}) collective-permute-start(bf16[48,768]{1,0:T(8,128)(2,1)S(1)} %pad_maximum_fusion.1.refs_0_.refs_4_), channel_id=1, source_target_pairs={{0,8},{2,10},{4,12},{6,14},{8,16},{10,18},{12,20},{14,22},{16,24},... | collective-permute-start | bytes 221192 | tf_op jit(solution)/shard_map/ppermute | solution.py:58
  5.4 8.0 %collective-permute-start.1 = (bf16[48,768]{1,0:T(8,128)(2,1)S(1)}, bf16[48,768]{1,0:T(8,128)(2,1)S(1)}, u32[]{:S(2)}, u32[]{:S(2)}) collective-permute-start(bf16[48,768]{1,0:T(8,128)(2,1)S(1)} %pad_maximum_fusion.1.refs_0_.refs_4_), channel_id=1, source_target_pairs={{0,16},{2,18},{4,20},{6,22},{8,24},{10,26},{12,28},{14,30},{16,0},... | collective-permute-start | bytes 221192 | tf_op jit(solution)/shard_map/ppermute | solution.py:58
  8.0 5.4 %collective-permute-start.2 = (bf16[48,768]{1,0:T(8,128)(2,1)S(1)}, bf16[48,768]{1,0:T(8,128)(2,1)S(1)}, u32[]{:S(2)}, u32[]{:S(2)}) collective-permute-start(bf16[48,768]{1,0:T(8,128)(2,1)S(1)} %pad_maximum_fusion.1.refs_0_.refs_4_), channel_id=1, source_target_pairs={{0,24},{2,26},{4,28},{6,30},{8,0},{10,2},{12,4},{14,6},{16,8},{18,... | collective-permute-start | bytes 221192 | tf_op jit(solution)/shard_map/ppermute | solution.py:58
  10.1 16.7 %collective-permute-start.12 = (bf16[48,640]{1,0:T(8,128)(2,1)S(1)}, bf16[48,640]{1,0:T(8,128)(2,1)S(1)}, u32[]{:S(2)}, u32[]{:S(2)}) collective-permute-start(bf16[48,640]{1,0:T(8,128)(2,1)S(1)} %pad.10.refs_0_), channel_id=1, source_target_pairs={{0,4},{2,6},{4,0},{6,2},{8,12},{10,14},{12,8},{14,10},{16,20},{18,... | collective-permute-start | bytes 184328 | tf_op jit(solution)/shard_map/ppermute | solution.py:58
  11.8 7.6 %copy-start.25 = (s32[512]{0:T(512)S(1)}, s32[512]{0:T(512)}, u32[]{:S(2)}) copy-start(s32[512]{0:T(512)} %param.12) | copy-start | bytes 6148
  11.8 7.6 %copy-start.16 = (s32[512]{0:T(512)S(1)}, s32[512]{0:T(512)}, u32[]{:S(2)}) copy-start(s32[512]{0:T(512)} %param.11) | copy-start | bytes 6148
  13.3 20.9 %copy-start.13 = (bf16[48,768]{1,0:T(8,128)(2,1)}, bf16[48,768]{1,0:T(8,128)(2,1)S(1)}, u32[]{:S(2)}) copy-start(bf16[48,768]{1,0:T(8,128)(2,1)S(1)} %pad_maximum_fusion.refs_0_.refs_5_) | copy-start | bytes 221188
  13.4 10.4 %collective-permute-start.6 = (bf16[192,768]{1,0:T(8,128)(2,1)S(1)}, bf16[192,768]{1,0:T(8,128)(2,1)S(1)}, u32[]{:S(2)}, u32[]{:S(2)}) collective-permute-start(bf16[192,768]{1,0:T(8,128)(2,1)S(1)} %shard_map.161.refs_4_.refs_1_.refs_8_), channel_id=1, source_target_pairs={{0,4},{2,6},{4,0},{6,2},{8,12},{10,14},{12,8},{14,10},{16,20},{18,... | collective-permute-start | bytes 884744 | tf_op jit(solution)/shard_map/ppermute | solution.py:58
  14.8 6.7 %collective-permute-start.3 = (bf16[48,768]{1,0:T(8,128)(2,1)S(1)}, bf16[48,768]{1,0:T(8,128)(2,1)S(1)}, u32[]{:S(2)}, u32[]{:S(2)}) collective-permute-start(bf16[48,768]{1,0:T(8,128)(2,1)S(1)} %pad_maximum_fusion.refs_0_.refs_5_), channel_id=1, source_target_pairs={{0,8},{2,10},{4,12},{6,14},{8,16},{10,18},{12,20},{14,22},{16,24},... | collective-permute-start | bytes 221192 | tf_op jit(solution)/shard_map/ppermute | solution.py:58
  16.7 7.1 %collective-permute-start.4 = (bf16[48,768]{1,0:T(8,128)(2,1)S(1)}, bf16[48,768]{1,0:T(8,128)(2,1)S(1)}, u32[]{:S(2)}, u32[]{:S(2)}) collective-permute-start(bf16[48,768]{1,0:T(8,128)(2,1)S(1)} %pad_maximum_fusion.refs_0_.refs_5_), channel_id=1, source_target_pairs={{0,16},{2,18},{4,20},{6,22},{8,24},{10,26},{12,28},{14,30},{16,0},... | collective-permute-start | bytes 221192 | tf_op jit(solution)/shard_map/ppermute | solution.py:58
  18.6 5.1 %collective-permute-start.5 = (bf16[48,768]{1,0:T(8,128)(2,1)S(1)}, bf16[48,768]{1,0:T(8,128)(2,1)S(1)}, u32[]{:S(2)}, u32[]{:S(2)}) collective-permute-start(bf16[48,768]{1,0:T(8,128)(2,1)S(1)} %pad_maximum_fusion.refs_0_.refs_5_), channel_id=1, source_target_pairs={{0,24},{2,26},{4,28},{6,30},{8,0},{10,2},{12,4},{14,6},{16,8},{18,... | collective-permute-start | bytes 221192 | tf_op jit(solution)/shard_map/ppermute | solution.py:58
  23.8 14.8 %copy-start.3 = (bf16[192,768]{1,0:T(8,128)(2,1)}, bf16[192,768]{1,0:T(8,128)(2,1)S(1)}, u32[]{:S(2)}) copy-start(bf16[192,768]{1,0:T(8,128)(2,1)S(1)} %collective-permute-done.6.refs_5_.refs_2_.refs_9_) | copy-start | bytes 884740
  23.8 8.1 %collective-permute-start.7 = (bf16[192,768]{1,0:T(8,128)(2,1)S(1)}, bf16[192,768]{1,0:T(8,128)(2,1)S(1)}, u32[]{:S(2)}, u32[]{:S(2)}) collective-permute-start(bf16[192,768]{1,0:T(8,128)(2,1)S(1)} %shard_map.162.refs_3_.refs_1_.refs_4_.refs_12_), channel_id=1, source_target_pairs={{0,4},{2,6},{4,0},{6,2},{8,12},{10,14},{12,8},{14,10},{16,20},{18,... | collective-permute-start | bytes 884744 | tf_op jit(solution)/shard_map/ppermute | solution.py:58
  24.6 16.8 %copy-start.15 = (bf16[48,1280]{1,0:T(8,128)(2,1)}, bf16[48,1280]{1,0:T(8,128)(2,1)S(1)}, u32[]{:S(2)}) copy-start(bf16[48,1280]{1,0:T(8,128)(2,1)S(1)} %fusion.5.refs_0_.refs_1_) | copy-start | bytes 368644
  24.6 13.4 %collective-permute-start.10 = (bf16[192,768]{1,0:T(8,128)(2,1)S(1)}, bf16[192,768]{1,0:T(8,128)(2,1)S(1)}, u32[]{:S(2)}, u32[]{:S(2)}) collective-permute-start(bf16[192,768]{1,0:T(8,128)(2,1)S(1)} %shard_map.161.refs_4_.refs_1_.refs_8_), channel_id=1, source_target_pairs={{0,2},{2,0},{4,6},{6,4},{8,10},{10,8},{12,14},{14,12},{16,18},{18,... | collective-permute-start | bytes 884744 | tf_op jit(solution)/shard_map/ppermute | solution.py:58
  24.7 13.4 %collective-permute-start.11 = (bf16[192,768]{1,0:T(8,128)(2,1)S(1)}, bf16[192,768]{1,0:T(8,128)(2,1)S(1)}, u32[]{:S(2)}, u32[]{:S(2)}) collective-permute-start(bf16[192,768]{1,0:T(8,128)(2,1)S(1)} %collective-permute-done.6.refs_5_.refs_2_.refs_9_), channel_id=1, source_target_pairs={{0,2},{2,0},{4,6},{6,4},{8,10},{10,8},{12,14},{14,12},{16,18},{18,... | collective-permute-start | bytes 884744 | tf_op jit(solution)/shard_map/ppermute | solution.py:58
  25.2 16.2 %collective-permute-start.13 = (bf16[48,1280]{1,0:T(8,128)(2,1)S(1)}, bf16[48,1280]{1,0:T(8,128)(2,1)S(1)}, u32[]{:S(2)}, u32[]{:S(2)}) collective-permute-start(bf16[48,1280]{1,0:T(8,128)(2,1)S(1)} %fusion.5.refs_0_.refs_1_), channel_id=1, source_target_pairs={{0,8},{2,10},{4,12},{6,14},{8,16},{10,18},{12,20},{14,22},{16,24},... | collective-permute-start | bytes 368648 | tf_op jit(solution)/shard_map/ppermute | solution.py:58
  26.8 14.5 %collective-permute-start.14 = (bf16[48,1280]{1,0:T(8,128)(2,1)S(1)}, bf16[48,1280]{1,0:T(8,128)(2,1)S(1)}, u32[]{:S(2)}, u32[]{:S(2)}) collective-permute-start(bf16[48,1280]{1,0:T(8,128)(2,1)S(1)} %fusion.5.refs_0_.refs_1_), channel_id=1, source_target_pairs={{0,16},{2,18},{4,20},{6,22},{8,24},{10,26},{12,28},{14,30},{16,0},... | collective-permute-start | bytes 368648 | tf_op jit(solution)/shard_map/ppermute | solution.py:58
  32.0 9.4 %collective-permute-start.15 = (bf16[48,1280]{1,0:T(8,128)(2,1)S(1)}, bf16[48,1280]{1,0:T(8,128)(2,1)S(1)}, u32[]{:S(2)}, u32[]{:S(2)}) collective-permute-start(bf16[48,1280]{1,0:T(8,128)(2,1)S(1)} %fusion.5.refs_0_.refs_1_), channel_id=1, source_target_pairs={{0,24},{2,26},{4,28},{6,30},{8,0},{10,2},{12,4},{14,6},{16,8},{18,... | collective-permute-start | bytes 368648 | tf_op jit(solution)/shard_map/ppermute | solution.py:58
  34.2 1.1 copy-start.10
  38.0 28.2 %copy-start = (bf16[512,768]{1,0:T(8,128)(2,1)}, bf16[512,768]{1,0:T(8,128)(2,1)S(1)}, u32[]{:S(2)}) copy-start(bf16[512,768]{1,0:T(8,128)(2,1)S(1)} %get-tuple-element.70.refs_2_.refs_0_.refs_1_) | copy-start | bytes 2359300
  38.0 3.4 %collective-permute-start.8 = (bf16[192,768]{1,0:T(8,128)(2,1)S(1)}, bf16[192,768]{1,0:T(8,128)(2,1)S(1)}, u32[]{:S(2)}, u32[]{:S(2)}) collective-permute-start(bf16[192,768]{1,0:T(8,128)(2,1)S(1)} %shard_map.162.refs_3_.refs_1_.refs_4_.refs_12_), channel_id=1, source_target_pairs={{0,2},{2,0},{4,6},{6,4},{8,10},{10,8},{12,14},{14,12},{16,18},{18,... | collective-permute-start | bytes 884744 | tf_op jit(solution)/shard_map/ppermute | solution.py:58
  38.1 3.3 %collective-permute-start.9 = (bf16[192,768]{1,0:T(8,128)(2,1)S(1)}, bf16[192,768]{1,0:T(8,128)(2,1)S(1)}, u32[]{:S(2)}, u32[]{:S(2)}) collective-permute-start(bf16[192,768]{1,0:T(8,128)(2,1)S(1)} %collective-permute-done.7.refs_5_.refs_2_.refs_13_), channel_id=1, source_target_pairs={{0,2},{2,0},{4,6},{6,4},{8,10},{10,8},{12,14},{14,12},{16,18},{18,... | collective-permute-start | bytes 884744 | tf_op jit(solution)/shard_map/ppermute | solution.py:58
  43.2 19.6 %collective-permute-start.16 = (bf16[512,768]{1,0:T(8,128)(2,1)S(1)}, bf16[512,768]{1,0:T(8,128)(2,1)S(1)}, u32[]{:S(2)}, u32[]{:S(2)}) collective-permute-start(bf16[512,768]{1,0:T(8,128)(2,1)S(1)} %get-tuple-element.76.refs_2_), channel_id=1, source_target_pairs={{0,1},{1,0},{2,3},{3,2},{4,5},{5,4},{6,7},{7,6},{8,9},{9,8},{10,11... | collective-permute-start | bytes 2359304 | tf_op jit(solution)/shard_map/ppermute | solution.py:62
  44.7 18.1 %collective-permute-start.17 = (bf16[192,1280]{1,0:T(8,128)(2,1)S(1)}, bf16[192,1280]{1,0:T(8,128)(2,1)S(1)}, u32[]{:S(2)}, u32[]{:S(2)}) collective-permute-start(bf16[192,1280]{1,0:T(8,128)(2,1)S(1)} %shard_map.166.refs_6_.refs_4_), channel_id=1, source_target_pairs={{0,4},{2,6},{4,0},{6,2},{8,12},{10,14},{12,8},{14,10},{16,20},{18,... | collective-permute-start | bytes 1474568 | tf_op jit(solution)/shard_map/ppermute | solution.py:58
  45.2 8.1 %collective-permute-start.18 = (bf16[96,640]{1,0:T(8,128)(2,1)S(1)}, bf16[96,640]{1,0:T(8,128)(2,1)S(1)}, u32[]{:S(2)}, u32[]{:S(2)}) collective-permute-start(bf16[96,640]{1,0:T(8,128)(2,1)S(1)} %shard_map.164.refs_9_.refs_0_), channel_id=1, source_target_pairs={{0,8},{2,10},{4,12},{6,14},{8,16},{10,18},{12,20},{14,22},{16,24},... | collective-permute-start | bytes 368648 | tf_op jit(solution)/shard_map/ppermute | solution.py:58
  45.9 11.3 %collective-permute-start.19 = (bf16[96,640]{1,0:T(8,128)(2,1)S(1)}, bf16[96,640]{1,0:T(8,128)(2,1)S(1)}, u32[]{:S(2)}, u32[]{:S(2)}) collective-permute-start(bf16[96,640]{1,0:T(8,128)(2,1)S(1)} %shard_map.164.refs_9_.refs_0_), channel_id=1, source_target_pairs={{0,16},{2,18},{4,20},{6,22},{8,24},{10,26},{12,28},{14,30},{16,0},... | collective-permute-start | bytes 368648 | tf_op jit(solution)/shard_map/ppermute | solution.py:58
  47.3 9.9 %collective-permute-start.20 = (bf16[96,640]{1,0:T(8,128)(2,1)S(1)}, bf16[96,640]{1,0:T(8,128)(2,1)S(1)}, u32[]{:S(2)}, u32[]{:S(2)}) collective-permute-start(bf16[96,640]{1,0:T(8,128)(2,1)S(1)} %shard_map.164.refs_9_.refs_0_), channel_id=1, source_target_pairs={{0,24},{2,26},{4,28},{6,30},{8,0},{10,2},{12,4},{14,6},{16,8},{18,... | collective-permute-start | bytes 368648 | tf_op jit(solution)/shard_map/ppermute | solution.py:58
  62.8 3.3 %collective-permute-start.22 = (bf16[192,1280]{1,0:T(8,128)(2,1)S(1)}, bf16[192,1280]{1,0:T(8,128)(2,1)S(1)}, u32[]{:S(2)}, u32[]{:S(2)}) collective-permute-start(bf16[192,1280]{1,0:T(8,128)(2,1)S(1)} %collective-permute-done.17.refs_5_), channel_id=1, source_target_pairs={{0,2},{2,0},{4,6},{6,4},{8,10},{10,8},{12,14},{14,12},{16,18},{18,... | collective-permute-start | bytes 1474568 | tf_op jit(solution)/shard_map/ppermute | solution.py:58
  62.9 3.3 %collective-permute-start.21 = (bf16[192,1280]{1,0:T(8,128)(2,1)S(1)}, bf16[192,1280]{1,0:T(8,128)(2,1)S(1)}, u32[]{:S(2)}, u32[]{:S(2)}) collective-permute-start(bf16[192,1280]{1,0:T(8,128)(2,1)S(1)} %shard_map.166.refs_6_.refs_4_), channel_id=1, source_target_pairs={{0,2},{2,0},{4,6},{6,4},{8,10},{10,8},{12,14},{14,12},{16,18},{18,... | collective-permute-start | bytes 1474568 | tf_op jit(solution)/shard_map/ppermute | solution.py:58
  63.4 2.4 %collective-permute-start.23 = (bf16[192,640]{1,0:T(8,128)(2,1)S(1)}, bf16[192,640]{1,0:T(8,128)(2,1)S(1)}, u32[]{:S(2)}, u32[]{:S(2)}) collective-permute-start(bf16[192,640]{1,0:T(8,128)(2,1)S(1)} %get-tuple-element.79.refs_8_.refs_12_), channel_id=1, source_target_pairs={{0,2},{2,0},{4,6},{6,4},{8,10},{10,8},{12,14},{14,12},{16,18},{18,... | collective-permute-start | bytes 737288 | tf_op jit(solution)/shard_map/ppermute | solution.py:58
  63.5 2.7 %collective-permute-start.24 = (bf16[192,640]{1,0:T(8,128)(2,1)S(1)}, bf16[192,640]{1,0:T(8,128)(2,1)S(1)}, u32[]{:S(2)}, u32[]{:S(2)}) collective-permute-start(bf16[192,640]{1,0:T(8,128)(2,1)S(1)} %get-tuple-element.82.refs_9_), channel_id=1, source_target_pairs={{0,2},{2,0},{4,6},{6,4},{8,10},{10,8},{12,14},{14,12},{16,18},{18,... | collective-permute-start | bytes 737288 | tf_op jit(solution)/shard_map/ppermute | solution.py:58
  70.6 21.2 %copy-start.1 = (f32[512,768]{1,0:T(8,128)}, f32[512,768]{1,0:T(8,128)S(1)}, u32[]{:S(2)}) copy-start(f32[512,768]{1,0:T(8,128)S(1)} %get-tuple-element.83.refs_1_.refs_0_) | copy-start | bytes 4718596
  70.6 36.4 %copy-start.2 = (bf16[512,768]{1,0:T(8,128)(2,1)}, bf16[512,768]{1,0:T(8,128)(2,1)S(1)}, u32[]{:S(2)}) copy-start(bf16[512,768]{1,0:T(8,128)(2,1)S(1)} %get-tuple-element.84.refs_1_) | copy-start | bytes 2359300
  70.7 19.6 %collective-permute-start.25 = (bf16[512,768]{1,0:T(8,128)(2,1)S(1)}, bf16[512,768]{1,0:T(8,128)(2,1)S(1)}, u32[]{:S(2)}, u32[]{:S(2)}) collective-permute-start(bf16[512,768]{1,0:T(8,128)(2,1)S(1)} %get-tuple-element.85.refs_2_), channel_id=1, source_target_pairs={{0,1},{1,0},{2,3},{3,2},{4,5},{5,4},{6,7},{7,6},{8,9},{9,8},{10,11... | collective-permute-start | bytes 2359304 | tf_op jit(solution)/shard_map/ppermute | solution.py:62
  74.0 1.9 %collective-permute-start.27 = (bf16[384,640]{1,0:T(8,128)(2,1)S(1)}, bf16[384,640]{1,0:T(8,128)(2,1)S(1)}, u32[]{:S(2)}, u32[]{:S(2)}) collective-permute-start(bf16[384,640]{1,0:T(8,128)(2,1)S(1)} %get-tuple-element.95), channel_id=1, source_target_pairs={{0,2},{2,0},{4,6},{6,4},{8,10},{10,8},{12,14},{14,12},{16,18},{18,... | collective-permute-start | bytes 1474568 | tf_op jit(solution)/shard_map/ppermute | solution.py:58
  74.1 2.6 %collective-permute-start.28 = (bf16[384,640]{1,0:T(8,128)(2,1)S(1)}, bf16[384,640]{1,0:T(8,128)(2,1)S(1)}, u32[]{:S(2)}, u32[]{:S(2)}) collective-permute-start(bf16[384,640]{1,0:T(8,128)(2,1)S(1)} %get-tuple-element.96), channel_id=1, source_target_pairs={{0,2},{2,0},{4,6},{6,4},{8,10},{10,8},{12,14},{14,12},{16,18},{18,... | collective-permute-start | bytes 1474568 | tf_op jit(solution)/shard_map/ppermute | solution.py:58
  74.6 2.8 %collective-permute-start.29 = (bf16[384,640]{1,0:T(8,128)(2,1)S(1)}, bf16[384,640]{1,0:T(8,128)(2,1)S(1)}, u32[]{:S(2)}, u32[]{:S(2)}) collective-permute-start(bf16[384,640]{1,0:T(8,128)(2,1)S(1)} %get-tuple-element.97), channel_id=1, source_target_pairs={{0,2},{2,0},{4,6},{6,4},{8,10},{10,8},{12,14},{14,12},{16,18},{18,... | collective-permute-start | bytes 1474568 | tf_op jit(solution)/shard_map/ppermute | solution.py:58
  77.7 22.4 %collective-permute-start.30 = (bf16[192,640]{1,0:T(8,128)(2,1)S(1)}, bf16[192,640]{1,0:T(8,128)(2,1)S(1)}, u32[]{:S(2)}, u32[]{:S(2)}) collective-permute-start(bf16[192,640]{1,0:T(8,128)(2,1)S(1)} %get-tuple-element.103), channel_id=1, source_target_pairs={{0,4},{2,6},{4,0},{6,2},{8,12},{10,14},{12,8},{14,10},{16,20},{18,... | collective-permute-start | bytes 737288 | tf_op jit(solution)/shard_map/ppermute | solution.py:58
  78.3 21.8 %collective-permute-start.31 = (bf16[192,640]{1,0:T(8,128)(2,1)S(1)}, bf16[192,640]{1,0:T(8,128)(2,1)S(1)}, u32[]{:S(2)}, u32[]{:S(2)}) collective-permute-start(bf16[192,640]{1,0:T(8,128)(2,1)S(1)} %get-tuple-element.104), channel_id=1, source_target_pairs={{0,4},{2,6},{4,0},{6,2},{8,12},{10,14},{12,8},{14,10},{16,20},{18,... | collective-permute-start | bytes 737288 | tf_op jit(solution)/shard_map/ppermute | solution.py:58
  79.8 20.3 %collective-permute-start.32 = (bf16[192,640]{1,0:T(8,128)(2,1)S(1)}, bf16[192,640]{1,0:T(8,128)(2,1)S(1)}, u32[]{:S(2)}, u32[]{:S(2)}) collective-permute-start(bf16[192,640]{1,0:T(8,128)(2,1)S(1)} %get-tuple-element.105), channel_id=1, source_target_pairs={{0,4},{2,6},{4,0},{6,2},{8,12},{10,14},{12,8},{14,10},{16,20},{18,... | collective-permute-start | bytes 737288 | tf_op jit(solution)/shard_map/ppermute | solution.py:58
  90.3 9.9 %collective-permute-start.26 = (bf16[128,768]{1,0:T(8,128)(2,1)S(1)}, bf16[128,768]{1,0:T(8,128)(2,1)S(1)}, u32[]{:S(2)}, u32[]{:S(2)}) collective-permute-start(bf16[128,768]{1,0:T(8,128)(2,1)S(1)} %slice.32), channel_id=1, source_target_pairs={{0,1},{1,0},{2,3},{3,2},{4,5},{5,4},{6,7},{7,6},{8,9},{9,8},{10,11... | collective-permute-start | bytes 589832 | tf_op jit(solution)/shard_map/ppermute | solution.py:62
  91.8 3.2 %copy-start.4 = (bf16[192,768]{1,0:T(8,128)(2,1)S(1)}, bf16[192,768]{1,0:T(8,128)(2,1)}, u32[]{:S(2)}) copy-start(bf16[192,768]{1,0:T(8,128)(2,1)} %copy-done.3) | copy-start | bytes 884740
  93.8 1.1 copy-start.5
  100.1 1.8 %copy-start.8 = (bf16[512,768]{1,0:T(8,128)(2,1)}, bf16[512,768]{1,0:T(8,128)(2,1)S(1)}, u32[]{:S(2)}) copy-start(bf16[512,768]{1,0:T(8,128)(2,1)S(1)} %get-tuple-element.116.refs_2_) | copy-start | bytes 2359300
  100.2 1.6 %copy-start.7 = (bf16[128,768]{1,0:T(8,128)(2,1)}, bf16[128,768]{1,0:T(8,128)(2,1)S(1)}, u32[]{:S(2)}) copy-start(bf16[128,768]{1,0:T(8,128)(2,1)S(1)} %collective-permute-done.26.refs_7_.refs_2_) | copy-start | bytes 589828
  101.8 6.2 %collective-permute-start.33 = (bf16[384,1536]{1,0:T(8,128)(2,1)S(1)}, bf16[384,1536]{1,0:T(8,128)(2,1)S(1)}, u32[]{:S(2)}, u32[]{:S(2)}) collective-permute-start(bf16[384,1536]{1,0:T(8,128)(2,1)S(1)} %get-tuple-element.107), channel_id=1, source_target_pairs={{0,2},{2,0},{4,6},{6,4},{8,10},{10,8},{12,14},{14,12},{16,18},{18,... | collective-permute-start | bytes 3538952 | tf_op jit(solution)/shard_map/ppermute | solution.py:58
  101.9 20.0 %collective-permute-start.38 = (bf16[512,768]{1,0:T(8,128)(2,1)S(1)}, bf16[512,768]{1,0:T(8,128)(2,1)S(1)}, u32[]{:S(2)}, u32[]{:S(2)}) collective-permute-start(bf16[512,768]{1,0:T(8,128)(2,1)S(1)} %get-tuple-element.116.refs_2_), channel_id=1, source_target_pairs={{0,1},{1,0},{2,3},{3,2},{4,5},{5,4},{6,7},{7,6},{8,9},{9,8},{10,11... | collective-permute-start | bytes 2359304 | tf_op jit(solution)/shard_map/ppermute | solution.py:62
  102.7 6.8 %collective-permute-start.35 = (bf16[48,1920]{1,0:T(8,128)(2,1)S(1)}, bf16[48,1920]{1,0:T(8,128)(2,1)S(1)}, u32[]{:S(2)}, u32[]{:S(2)}) collective-permute-start(bf16[48,1920]{1,0:T(8,128)(2,1)S(1)} %get-tuple-element.113), channel_id=1, source_target_pairs={{0,24},{2,26},{4,28},{6,30},{8,0},{10,2},{12,4},{14,6},{16,8},{18,... | collective-permute-start | bytes 552968 | tf_op jit(solution)/shard_map/ppermute | solution.py:58
  104.0 17.8 %collective-permute-start.36 = (bf16[48,1920]{1,0:T(8,128)(2,1)S(1)}, bf16[48,1920]{1,0:T(8,128)(2,1)S(1)}, u32[]{:S(2)}, u32[]{:S(2)}) collective-permute-start(bf16[48,1920]{1,0:T(8,128)(2,1)S(1)} %get-tuple-element.114), channel_id=1, source_target_pairs={{0,16},{2,18},{4,20},{6,22},{8,24},{10,26},{12,28},{14,30},{16,0},... | collective-permute-start | bytes 552968 | tf_op jit(solution)/shard_map/ppermute | solution.py:58
  105.1 16.7 %collective-permute-start.37 = (bf16[48,1920]{1,0:T(8,128)(2,1)S(1)}, bf16[48,1920]{1,0:T(8,128)(2,1)S(1)}, u32[]{:S(2)}, u32[]{:S(2)}) collective-permute-start(bf16[48,1920]{1,0:T(8,128)(2,1)S(1)} %get-tuple-element.115), channel_id=1, source_target_pairs={{0,8},{2,10},{4,12},{6,14},{8,16},{10,18},{12,20},{14,22},{16,24},... | collective-permute-start | bytes 552968 | tf_op jit(solution)/shard_map/ppermute | solution.py:58
  108.3 14.6 %collective-permute-start.34 = (bf16[192,1536]{1,0:T(8,128)(2,1)S(1)}, bf16[192,1536]{1,0:T(8,128)(2,1)S(1)}, u32[]{:S(2)}, u32[]{:S(2)}) collective-permute-start(bf16[192,1536]{1,0:T(8,128)(2,1)S(1)} %get-tuple-element.112), channel_id=1, source_target_pairs={{0,4},{2,6},{4,0},{6,2},{8,12},{10,14},{12,8},{14,10},{16,20},{18,... | collective-permute-start | bytes 1769480 | tf_op jit(solution)/shard_map/ppermute | solution.py:58
  122.8 6.7 %copy-start.6 = (f32[48,1920]{1,0:T(8,128)}, f32[48,1920]{1,0:T(8,128)S(1)}, u32[]{:S(2)}) copy-start(f32[48,1920]{1,0:T(8,128)S(1)} %shard_map.177.refs_2_.refs_0_) | copy-start | bytes 1105924
  123.7 21.3 %collective-permute-start.39 = (bf16[384,768]{1,0:T(8,128)(2,1)}, bf16[384,768]{1,0:T(8,128)(2,1)S(1)}, u32[]{:S(2)}, u32[]{:S(2)}) collective-permute-start(bf16[384,768]{1,0:T(8,128)(2,1)} %slice.33), channel_id=1, source_target_pairs={{0,1},{1,0},{2,3},{3,2},{4,5},{5,4},{6,7},{7,6},{8,9},{9,8},{10,11... | collective-permute-start | bytes 1769480 | tf_op jit(solution)/shard_map/ppermute | solution.py:62
  125.2 12.1 %collective-permute-start.40 = (bf16[48,1536]{1,0:T(8,128)(2,1)S(1)}, bf16[48,1536]{1,0:T(8,128)(2,1)S(1)}, u32[]{:S(2)}, u32[]{:S(2)}) collective-permute-start(bf16[48,1536]{1,0:T(8,128)(2,1)S(1)} %get-tuple-element.119), channel_id=1, source_target_pairs={{0,24},{2,26},{4,28},{6,30},{8,0},{10,2},{12,4},{14,6},{16,8},{18,... | collective-permute-start | bytes 442376 | tf_op jit(solution)/shard_map/ppermute | solution.py:58
  127.3 12.6 %collective-permute-start.41 = (bf16[48,1536]{1,0:T(8,128)(2,1)S(1)}, bf16[48,1536]{1,0:T(8,128)(2,1)S(1)}, u32[]{:S(2)}, u32[]{:S(2)}) collective-permute-start(bf16[48,1536]{1,0:T(8,128)(2,1)S(1)} %get-tuple-element.120), channel_id=1, source_target_pairs={{0,16},{2,18},{4,20},{6,22},{8,24},{10,26},{12,28},{14,30},{16,0},... | collective-permute-start | bytes 442376 | tf_op jit(solution)/shard_map/ppermute | solution.py:58
  127.3 12.6 %collective-permute-start.42 = (bf16[48,1536]{1,0:T(8,128)(2,1)S(1)}, bf16[48,1536]{1,0:T(8,128)(2,1)S(1)}, u32[]{:S(2)}, u32[]{:S(2)}) collective-permute-start(bf16[48,1536]{1,0:T(8,128)(2,1)S(1)} %get-tuple-element.121), channel_id=1, source_target_pairs={{0,8},{2,10},{4,12},{6,14},{8,16},{10,18},{12,20},{14,22},{16,24},... | collective-permute-start | bytes 442376 | tf_op jit(solution)/shard_map/ppermute | solution.py:58
  137.2 6.9 %copy-start.19 = (f32[2,48,576]{2,1,0:T(8,128)S(1)}, f32[2,48,576]{2,1,0:T(8,128)}, u32[]{:S(2)}) copy-start(f32[2,48,576]{2,1,0:T(8,128)} %get-tuple-element.128) | copy-start | bytes 663556
  137.3 2.7 %copy-start.20 = (bf16[48,1536]{1,0:T(8,128)(2,1)}, bf16[48,1536]{1,0:T(8,128)(2,1)S(1)}, u32[]{:S(2)}) copy-start(bf16[48,1536]{1,0:T(8,128)(2,1)S(1)} %collective-permute-done.40.refs_1_) | copy-start | bytes 442372
  143.4 6.3 %collective-permute-start.43 = (f32[48,2]{1,0:T(8,128)}, f32[48,2]{1,0:T(8,128)S(1)}, u32[]{:S(2)}, u32[]{:S(2)}) collective-permute-start(f32[48,2]{1,0:T(8,128)} %get-tuple-element.125.refs_5_), channel_id=1, source_target_pairs={{0,1},{1,0},{2,3},{3,2},{4,5},{5,4},{6,7},{7,6},{8,9},{9,8},{10,11... | collective-permute-start | bytes 1160 | tf_op jit(solution)/shard_map/ppermute | solution.py:62
  145.0 4.7 %copy-start.23 = (f32[48,2]{1,0:T(8,128)S(1)}, f32[48,2]{1,0:T(8,128)}, u32[]{:S(2)}) copy-start(f32[48,2]{1,0:T(8,128)} %get-tuple-element.125.refs_5_) | copy-start | bytes 1156
  (6 other events, 4.8 us)

commit v5 on v4

--- a/solution.py
+++ b/solution.py
@@ -14,7 +14,7 @@
 LANES = 128
 BLOCK = 128
 WINDOW = 256
-EARLY = 4
+EARLY = 2
 WEIGHT = 10**10
 PIECES = 4
 
@@ -104,7 +104,7 @@
         if self.plain:
             _, second, third = self.levels
             if self.late:
-                held, other = stack_rows([self.shard] + self.received, 2)
+                held, other = stack_rows([self.shard] + self.received, 2, weight)
             else:
                 held = stack_rows([self.shard] + self.received, weight=weight)
                 other = self.other = shifted(held, self.count, second, 1)
@@ -116,7 +116,8 @@
     def share(self, *others):
         if self.plain:
             self.pieces += [
-                shifted(after(part, *others), self.count, self.levels[2], 1) for part in self.pieces
+                shifted(after(part, *(array for array in others if array is not part)), self.count, self.levels[2], 1)
+                for part in self.pieces
             ]
 
 
@@ -278,15 +279,15 @@
     def body(total_ref, weights_ref, gains_ref, sum_ref, down_ref, columns_ref):
         gain = gains_ref[:, :1]
         down_ref[...] = total_ref[:, 2 * room : 2 * room + hidden]
-        sum_ref[0] = total_ref[:, :hidden] * gain
-        sum_ref[1] = total_ref[:, room : room + hidden] * gain
+        sum_ref[:, 0, :] = total_ref[:, :hidden] * gain
+        sum_ref[:, 1, :] = total_ref[:, room : room + hidden] * gain
         share = jnp.sum(wide(weights_ref[...]) * total_ref[:, : 2 * room], axis=1, keepdims=True) / gain
         lane = lax.broadcasted_iota(jnp.int32, (rows, 2), 1)
         columns_ref[...] = jnp.where(lane == 0, gains_ref[:, 1:], share)
 
     return run(
         body,
-        [full(2, rows, hidden), full(rows, hidden), full(rows, 2)],
+        [full(rows, 2, hidden), full(rows, hidden), full(rows, 2)],
         [total, weights, gains],
         last=True,
     )
@@ -304,12 +305,14 @@
         share = jnp.sum(wide(query_keys_ref[...]) * total[:, : 2 * inner], axis=1, keepdims=True)
         values = wide(values_out_ref[:, :inner]) * total[:, 2 * inner : 3 * inner]
         share = (share + jnp.sum(values, axis=1, keepdims=True)) / gain
-        lane = lax.broadcasted_iota(jnp.int32, (rows, 2), 1)
-        share_ref[...] = jnp.where(lane == 0, share, columns_ref[...])
-
-    return run(
-        body,
-        [full(3, rows, inner), full(rows, inner), full(rows, 2)],
+        place = lax.broadcasted_iota(jnp.int32, (rows, rows), 0) == lax.broadcasted_iota(jnp.int32, (rows, rows), 1)
+        for number, column in enumerate((share, columns_ref[:, 1:])):
+            spread = jnp.where(place, column, jnp.zeros((rows, rows), jnp.float32))
+            share_ref[number : number + 1, :] = jnp.sum(spread, axis=0, keepdims=True)
+
+    return run(
+        body,
+        [full(3, rows, inner), full(rows, inner), full(2, rows)],
         [*parts, query_keys, values_out, columns],
         last=True,
     )
@@ -368,18 +371,20 @@
             yield number, pair, slice(block * BLOCK, (block + 1) * BLOCK), slice(start, start + WINDOW)
 
 
-def prepare(tokens, cotangent, order):
-    count, width = tokens.shape
-
-    def body(tokens_ref, cotangent_ref, order_ref, inputs_ref, normed_ref, upstream_ref):
+def prepare(tokens, order):
+    def body(tokens_ref, order_ref, inputs_ref, normed_ref):
         inputs = product(tokens_ref[...], order_ref[...])
         inputs_ref[...] = low(inputs)
         normed_ref[...] = low(normalize(inputs)[0])
-        upstream_ref[...] = low(product(cotangent_ref[...], order_ref[...]))
-
-    return run(
-        body, [half(count, width)] * 3, [tokens, cotangent, order]
-    )
+
+    return run(body, [half(*tokens.shape)] * 2, [tokens, order])
+
+
+def reorder(values, order):
+    def body(values_ref, order_ref, out_ref):
+        out_ref[...] = low(product(values_ref[...], order_ref[...]))
+
+    return run(body, [half(*values.shape)], [values, order])[0]
 
 
 def attend_shares(normed, pieces, cosine, sine, column, row):
@@ -435,18 +440,23 @@
     )
 
 
-def feed_forward(inputs, upstream, own, other, gates_in, down):
-    count, width = inputs.shape
-    hidden = down[0].shape[1]
-
-    def body(inputs_ref, upstream_ref, own_ref, other_ref, a, b, c, d, e, f, g, h,
-             middle_ref, normed_ref, mixed_ref, gates_ref, forward_ref, back_ref):
+def settle(inputs, own, other):
+    def body(inputs_ref, own_ref, other_ref, middle_ref, normed_ref):
         middle = wide(inputs_ref[...]) + (wide(own_ref[...]) + wide(other_ref[...]))
         middle_ref[...] = middle
-        normed = low(normalize(middle)[0])
-        normed_ref[...] = normed
+        normed_ref[...] = low(normalize(middle)[0])
+
+    return run(body, [full(*inputs.shape), half(*inputs.shape)], [inputs, own, other], weight=WEIGHT)
+
+
+def feed_forward(normed, upstream, gates_in, down):
+    count, width = normed.shape
+    hidden = down[0].shape[1]
+
+    def body(normed_ref, upstream_ref, a, b, c, d, e, f, g, h,
+             mixed_ref, gates_ref, forward_ref, back_ref):
         matrix, down = rows_of((a, b, c, d)), rows_of((e, f, g, h))
-        gates = product(normed, matrix)
+        gates = product(normed_ref[...], matrix)
         active, factor = gates[:, :hidden], gates[:, hidden:]
         chance = 0.5 + 0.5 * lax.erf(active * 0.7071067811865476)
         bent = active * chance
@@ -461,9 +471,8 @@
 
     return run(
         body,
-        [full(count, width), half(count, width), half(count, hidden), half(count, 2 * hidden)]
-        + [half(count, width)] * 2,
-        [inputs, upstream, own, other, *gates_in, *down],
+        [half(count, hidden), half(count, 2 * hidden), half(count, width), half(count, width)],
+        [normed, upstream, *gates_in, *down],
     )
 
 
@@ -491,7 +500,7 @@
             total = low(middle_ref[part, :] + (wide(own_ref[part, :]) + wide(ref[...])))
             out_ref[part, :] = low(product(total, order_ref[...]))
 
-    return run(body, [half(*middle.shape)], [middle, own, *others, order], last=True)[0]
+    return run(body, [half(*middle.shape)], [middle, own, *others, order])[0]
 
 
 def attend_back_values(upstream, middle, own, other, pieces, context, shares):
@@ -636,11 +645,11 @@
     column, row = seg_ids[:, None], seg_ids[None, :]
     held = query_keys.stack()
     values_out = Gather(after(shard_two, held), devices)
+    inputs, normed_one = prepare(tokens, order)
     wait_for(query_keys.other)
     held = values_out.stack()
     gates_in = Gather(after(shard_three, held), devices, tail=True)
     wait_for(cosine, sine, column)
-    inputs, normed_one, upstream = prepare(tokens, cotangent, order)
     down.join_rows()
     query, keys, shares = attend_shares(normed_one, query_keys.pieces, cosine, sine, column, row)
     wait_for(values_out.other)
@@ -648,17 +657,19 @@
     down.begin(held)
     values, context, own = attend_values(normed_one, values_out.pieces, shares)
     other = swapped(own)
-    wait_for(other)
-    gates_in.share(down.stack())
-    middle, normed_two, mixed, grad_gates, own_out, own_two = feed_forward(
-        inputs, upstream, own, other, gates_in.pieces, down.pieces
+    upstream = reorder(cotangent, order)
+    down.stack()
+    gates_in.share(gates_in.other)
+    middle, normed_two = settle(inputs, own, other)
+    mixed, grad_gates, own_out, own_two = feed_forward(
+        normed_two, upstream, gates_in.pieces, down.pieces
     )
     other_two = swapped(own_two)
     grads_mlp = feed_forward_grads(normed_two, mixed, grad_gates, upstream)
     sums_mlp = Scatter(grads_mlp[:3], grads_mlp[3:], devices, rows)
     sums_mlp.second()
     early = own_out.shape[0] // EARLY
-    upper_out = swapped(after(own_out[:early], other_two))
+    upper_out = swapped(own_out[:early])
     grad_middle, branch, grad_context, grad_values = attend_back_values(
         upstream, middle, own_two, other_two, values_out.pieces, context, shares
     )
@@ -681,11 +692,11 @@
         sum_mlp, shard_three, jnp.concatenate([gain_two, gain_one], axis=1), hidden
     )
     grad_input = input_grads(grad_middle, inputs, own_one, other_one, back)
+    output = add_output(middle, own_out, (upper_out, lower_out), back)
     sum_qkv, sum_out, share = finish_attention(sums.parts, shard_one, shard_two, columns)
-    output = add_output(middle, own_out, (upper_out, lower_out), back)
     gains = after(share, output) + swapped(share)
-    sum_qkv, sum_in = (jnp.transpose(array, (1, 0, 2)) for array in (sum_qkv, sum_in))
-    return (output, grad_input, gains[:, 0], sum_qkv, sum_out.T, gains[:, 1], sum_in, sum_down.T)
+    sum_qkv = jnp.transpose(sum_qkv, (1, 0, 2))
+    return (output, grad_input, gains[0], sum_qkv, sum_out.T, gains[1], sum_in, sum_down.T)
 
 
 def solution(mesh):

time: 151 us -> 143 us (0.947)
  waiting for transfers between devices: 51 us -> 45.7 us
  local copies, waits for them, and re-layouts: 11.5 us -> 8.55 us
    ppermute x38, waiting for transfers between devices: 35.5 us -> 29.1 us  [shifted(): return lax.ppermute(values, 'dp', pairs)]
    unnamed x53 -> x42, local copies, waits for them, and re-layouts: 7.87 us -> 5.2 us
    pallas_call x22 -> x24, Pallas kernels: 35.9 us -> 36.1 us  [run(): pl.pallas_call(ordered, out_shape=out_shapes, grid=grid, in_specs=specs +...]
  transfers between devices with their start and end apart: 44 -> 44, of which waited for: 16 -> 13; matrix products, arithmetic and copies ran while one was open for 4% -> 4% of each run, Pallas kernels for 19% -> 18%
where the time goes in v5:
time: 143 us
  starting transfers between devices  46.6 us (33%)
  waiting for transfers between devices  45.7 us (32%)
  Pallas kernels  36.1 us (25%)
  local copies, waits for them, and re-layouts  8.55 us (6%)
  other arithmetic  4.77 us (3%)
    ppermute x38, starting transfers between devices, shifted(): return lax.ppermute(values, 'dp', pairs)  40.3 us
    pallas_call x24, Pallas kernels, run(): pl.pallas_call(ordered, out_shape=out_shapes, grid=grid, in_specs=specs +...  36.1 us
    ppermute x38, waiting for transfers between devices, shifted(): return lax.ppermute(values, 'dp', pairs)  29.1 us
    ppermute x6, waiting for transfers between devices, swapped(): return lax.ppermute(values, 'tensor', [(0, 1), (1, 0)])  16.6 us
    ppermute x6, starting transfers between devices, swapped(): return lax.ppermute(values, 'tensor', [(0, 1), (1, 0)])  6.33 us
    unnamed x42, local copies, waits for them, and re-layouts  5.2 us
  transfers between devices with their start and end apart: 44, of which 13 were waited for; matrix products, arithmetic and copies ran while one was open for 4% of the time, Pallas kernels for 18%

profile of v5, /device:TPU:0, one launch (start us, length us, event | category | flops | bytes accessed | tf_op | source)
XLA Modules:
  0.0 142.9 jit_solution(16188248675765703628)
XLA Ops:
  0.6 0.7 convert_bitcast_fusion
  1.4 0.9 fusion.8
  2.3 3.1 %collective-permute-start = (bf16[48,768]{1,0:T(8,128)(2,1)S(1)}, bf16[48,768]{1,0:T(8,128)(2,1)S(1)}, u32[]{:S(2)}, u32[]{:S(2)}) collective-permute-start(bf16[48,768]{1,0:T(8,128)(2,1)S(1)} %pad_maximum_fusion.refs_0_.refs_4_), channel_id=1, source_target_pairs={{0,8},{2,10},{4,12},{6,14},{8,16},{10,18},{12,20},{14,22},{16,24},... | collective-permute-start | bytes 221192 | tf_op jit(solution)/shard_map/ppermute | solution.py:58
  5.4 2.6 %collective-permute-start.1 = (bf16[48,768]{1,0:T(8,128)(2,1)S(1)}, bf16[48,768]{1,0:T(8,128)(2,1)S(1)}, u32[]{:S(2)}, u32[]{:S(2)}) collective-permute-start(bf16[48,768]{1,0:T(8,128)(2,1)S(1)} %pad_maximum_fusion.refs_0_.refs_4_), channel_id=1, source_target_pairs={{0,16},{2,18},{4,20},{6,22},{8,24},{10,26},{12,28},{14,30},{16,0},... | collective-permute-start | bytes 221192 | tf_op jit(solution)/shard_map/ppermute | solution.py:58
  8.0 1.3 collective-permute-start.2
  9.3 0.8 pad.10.refs_0_
  10.1 1.5 %collective-permute-start.12 = (bf16[48,640]{1,0:T(8,128)(2,1)S(1)}, bf16[48,640]{1,0:T(8,128)(2,1)S(1)}, u32[]{:S(2)}, u32[]{:S(2)}) collective-permute-start(bf16[48,640]{1,0:T(8,128)(2,1)S(1)} %pad.10.refs_0_), channel_id=1, source_target_pairs={{0,4},{2,6},{4,0},{6,2},{8,12},{10,14},{12,8},{14,10},{16,20},{18,... | collective-permute-start | bytes 184328 | tf_op jit(solution)/shard_map/ppermute | solution.py:58
  11.8 1.3 fusion.1
  13.4 1.3 collective-permute-start.6
  14.8 1.9 %collective-permute-start.3 = (bf16[48,768]{1,0:T(8,128)(2,1)S(1)}, bf16[48,768]{1,0:T(8,128)(2,1)S(1)}, u32[]{:S(2)}, u32[]{:S(2)}) collective-permute-start(bf16[48,768]{1,0:T(8,128)(2,1)S(1)} %pad_maximum_fusion.1.refs_0_.refs_5_), channel_id=1, source_target_pairs={{0,8},{2,10},{4,12},{6,14},{8,16},{10,18},{12,20},{14,22},{16,24},... | collective-permute-start | bytes 221192 | tf_op jit(solution)/shard_map/ppermute | solution.py:58
  16.7 1.9 %collective-permute-start.4 = (bf16[48,768]{1,0:T(8,128)(2,1)S(1)}, bf16[48,768]{1,0:T(8,128)(2,1)S(1)}, u32[]{:S(2)}, u32[]{:S(2)}) collective-permute-start(bf16[48,768]{1,0:T(8,128)(2,1)S(1)} %pad_maximum_fusion.1.refs_0_.refs_5_), channel_id=1, source_target_pairs={{0,16},{2,18},{4,20},{6,22},{8,24},{10,26},{12,28},{14,30},{16,0},... | collective-permute-start | bytes 221192 | tf_op jit(solution)/shard_map/ppermute | solution.py:58
  18.6 0.7 collective-permute-start.5
  19.6 1.1 copy-done.11
  20.7 1.1 shard_map.162
  21.9 1.9 %collective-permute-done.4.refs_2_ = bf16[48,768]{1,0:T(8,128)(2,1)S(1)} collective-permute-done((bf16[48,768]{1,0:T(8,128)(2,1)S(1)}, bf16[48,768]{1,0:T(8,128)(2,1)S(1)}, u32[]{:S(2)}, u32[]{:S(2)}) %collective-permute-start.4) | collective-permute-done | bytes 73760 | tf_op jit(solution)/shard_map/ppermute | solution.py:58
  23.8 0.7 collective-permute-start.7
  25.2 1.7 %collective-permute-start.13 = (bf16[48,1280]{1,0:T(8,128)(2,1)S(1)}, bf16[48,1280]{1,0:T(8,128)(2,1)S(1)}, u32[]{:S(2)}, u32[]{:S(2)}) collective-permute-start(bf16[48,1280]{1,0:T(8,128)(2,1)S(1)} %fusion.5.refs_0_.refs_1_), channel_id=1, source_target_pairs={{0,8},{2,10},{4,12},{6,14},{8,16},{10,18},{12,20},{14,22},{16,24},... | collective-permute-start | bytes 368648 | tf_op jit(solution)/shard_map/ppermute | solution.py:58
  26.9 1.3 collective-permute-start.14
  28.2 3.8 %collective-permute-done.7.refs_5_.refs_2_.refs_13_ = bf16[192,768]{1,0:T(8,128)(2,1)S(1)} collective-permute-done((bf16[192,768]{1,0:T(8,128)(2,1)S(1)}, bf16[192,768]{1,0:T(8,128)(2,1)S(1)}, u32[]{:S(2)}, u32[]{:S(2)}) %collective-permute-start.7) | collective-permute-done | bytes 294944 | tf_op jit(solution)/shard_map/ppermute | solution.py:58
  32.0 1.3 collective-permute-start.15
  33.2 1.0 fusion.2
  34.8 2.7 %shard_map.165 = (bf16[512,384]{1,0:T(8,128)(2,1)S(1)}, bf16[512,384]{1,0:T(8,128)(2,1)S(1)}, bf16[12,256,256]{2,1,0:T(8,128)(2,1)S(1)}) custom-call(bf16[512,768]{1,0:T(8,128)(2,1)S(1)} %get-tuple-element.67.refs_0_.refs_2_, bf16[192,768]{1,0:T(8,128)(2,1)S(1)} %shard_map.161.refs_2_.refs_1_.refs_8_, ...), custom_call_target="tpu_custom_call" | custom-call | tf_op jit(solution)/shard_map/pallas_call | solution.py:193
  37.7 1.2 collective-permute-done.15.refs_3_
  38.9 1.7 %shard_map.167 = (bf16[512,384]{1,0:T(8,128)(2,1)S(1)}, bf16[512,384]{1,0:T(8,128)(2,1)S(1)}, bf16[512,768]{1,0:T(8,128)(2,1)S(1)}) custom-call(bf16[512,768]{1,0:T(8,128)(2,1)S(1)} %get-tuple-element.67.refs_0_.refs_2_, bf16[192,768]{1,0:T(8,128)(2,1)S(1)} %shard_map.163.refs_2_.refs_1_.refs_4_.refs_12_, ...), custom_call_target="tpu_custom_call" | custom-call | tf_op jit(solution)/shard_map/pallas_call | solution.py:193
  40.6 1.6 %collective-permute-start.16 = (bf16[512,768]{1,0:T(8,128)(2,1)S(1)}, bf16[512,768]{1,0:T(8,128)(2,1)S(1)}, u32[]{:S(2)}, u32[]{:S(2)}) collective-permute-start(bf16[512,768]{1,0:T(8,128)(2,1)S(1)} %get-tuple-element.72.refs_1_), channel_id=1, source_target_pairs={{0,1},{1,0},{2,3},{3,2},{4,5},{5,4},{6,7},{7,6},{8,9},{9,8},{10,11... | collective-permute-start | bytes 2359304 | tf_op jit(solution)/shard_map/ppermute | solution.py:62
  42.2 0.7 collective-permute-start.20
  42.9 2.6 %collective-permute-start.17 = (bf16[96,640]{1,0:T(8,128)(2,1)S(1)}, bf16[96,640]{1,0:T(8,128)(2,1)S(1)}, u32[]{:S(2)}, u32[]{:S(2)}) collective-permute-start(bf16[96,640]{1,0:T(8,128)(2,1)S(1)} %shard_map.164.refs_9_.refs_0_), channel_id=1, source_target_pairs={{0,8},{2,10},{4,12},{6,14},{8,16},{10,18},{12,20},{14,22},{16,24},... | collective-permute-start | bytes 368648 | tf_op jit(solution)/shard_map/ppermute | solution.py:58
  45.9 1.9 %collective-permute-start.19 = (bf16[96,640]{1,0:T(8,128)(2,1)S(1)}, bf16[96,640]{1,0:T(8,128)(2,1)S(1)}, u32[]{:S(2)}, u32[]{:S(2)}) collective-permute-start(bf16[96,640]{1,0:T(8,128)(2,1)S(1)} %shard_map.164.refs_9_.refs_0_), channel_id=1, source_target_pairs={{0,24},{2,26},{4,28},{6,30},{8,0},{10,2},{12,4},{14,6},{16,8},{18,... | collective-permute-start | bytes 368648 | tf_op jit(solution)/shard_map/ppermute | solution.py:58
  47.8 0.8 shard_map.168.refs_4_.refs_1_.refs_3_.refs_0_
  48.6 2.3 %collective-permute-done.17.refs_1_ = bf16[96,640]{1,0:T(8,128)(2,1)S(1)} collective-permute-done((bf16[96,640]{1,0:T(8,128)(2,1)S(1)}, bf16[96,640]{1,0:T(8,128)(2,1)S(1)}, u32[]{:S(2)}, u32[]{:S(2)}) %collective-permute-start.17) | collective-permute-done | bytes 122912 | tf_op jit(solution)/shard_map/ppermute | solution.py:58
  50.9 3.6 %collective-permute-done.18.refs_2_ = bf16[96,640]{1,0:T(8,128)(2,1)S(1)} collective-permute-done((bf16[96,640]{1,0:T(8,128)(2,1)S(1)}, bf16[96,640]{1,0:T(8,128)(2,1)S(1)}, u32[]{:S(2)}, u32[]{:S(2)}) %collective-permute-start.18) | collective-permute-done | bytes 122912 | tf_op jit(solution)/shard_map/ppermute | solution.py:58
  55.7 3.3 %collective-permute-done.16.refs_2_ = bf16[512,768]{1,0:T(8,128)(2,1)S(1)} collective-permute-done((bf16[512,768]{1,0:T(8,128)(2,1)S(1)}, bf16[512,768]{1,0:T(8,128)(2,1)S(1)}, u32[]{:S(2)}, u32[]{:S(2)}) %collective-permute-start.16) | collective-permute-done | bytes 786464 | tf_op jit(solution)/shard_map/ppermute | solution.py:62
  59.7 4.0 %shard_map.171 = (bf16[512,640]{1,0:T(8,128)(2,1)S(1)}, bf16[512,1280]{1,0:T(8,128)(2,1)S(1)}, bf16[512,768]{1,0:T(8,128)(2,1)S(1)}, bf16[512,768]{1,0:T(8,128)(2,1)S(1)}) custom-call(bf16[512,768]{1,0:T(8,128)(2,1)S(1)} %get-tuple-element.77.refs_0_, bf16[512,768]{1,0:T(8,128)(2,1)S(1)} %shard_map.168.refs_4_.refs_1_.refs_3_.refs_0_, ...), custom_call_target="tpu_custom_call" | custom-call | tf_op jit(solution)/shard_map/pallas_call | solution.py:193
  63.7 1.6 %collective-permute-start.26 = (bf16[512,768]{1,0:T(8,128)(2,1)S(1)}, bf16[512,768]{1,0:T(8,128)(2,1)S(1)}, u32[]{:S(2)}, u32[]{:S(2)}) collective-permute-start(bf16[512,768]{1,0:T(8,128)(2,1)S(1)} %get-tuple-element.82.refs_2_), channel_id=1, source_target_pairs={{0,1},{1,0},{2,3},{3,2},{4,5},{5,4},{6,7},{7,6},{8,9},{9,8},{10,11... | collective-permute-start | bytes 2359304 | tf_op jit(solution)/shard_map/ppermute | solution.py:62
  65.2 1.8 %shard_map.172 = (bf16[384,640]{1,0:T(8,128)(2,1)S(1)}, bf16[384,640]{1,0:T(8,128)(2,1)S(1)}, bf16[384,640]{1,0:T(8,128)(2,1)S(1)}, bf16[384,640]{1,0:T(8,128)(2...) custom-call(bf16[512,768]{1,0:T(8,128)(2,1)S(1)} %get-tuple-element.77.refs_0_, ...), custom_call_target="tpu_custom_call" | custom-call | tf_op jit(solution)/shard_map/pallas_call | solution.py:193
  67.7 0.8 fusion.27
  69.7 0.7 collective-permute-done.29.refs_5_
  70.7 1.3 collective-permute-start.30
  72.0 0.8 collective-permute-start.31
  72.8 1.3 collective-permute-start.32
  74.1 10.1 %collective-permute-done.26.refs_3_ = bf16[512,768]{1,0:T(8,128)(2,1)S(1)} collective-permute-done((bf16[512,768]{1,0:T(8,128)(2,1)S(1)}, bf16[512,768]{1,0:T(8,128)(2,1)S(1)}, u32[]{:S(2)}, u32[]{:S(2)}) %collective-permute-start.26) | collective-permute-done | bytes 786464 | tf_op jit(solution)/shard_map/ppermute | solution.py:62
  84.2 2.0 %shard_map.174 = (f32[512,768]{1,0:T(8,128)S(1)}, bf16[512,768]{1,0:T(8,128)(2,1)S(1)}, bf16[512,384]{1,0:T(8,128)(2,1)S(1)}, bf16[512,384]{1,0:T(8,128)(2,1)S(1)}) custom-call(bf16[512,768]{1,0:T(8,128)(2,1)S(1)} %shard_map.168.refs_4_.refs_1_.refs_3_.refs_0_, f32[512,768]{1,0:T(8,128)S(1)} %get-tuple-element.76.refs_10_.refs_1_.refs_0_, ...), custom_call_target="tpu_custom_call" | custom-call | tf_op jit(solution)/shard_map/pallas_call | solution.py:193
  86.2 1.1 copy-done.7
  87.4 5.1 %shard_map.175 = (bf16[512,768]{1,0:T(8,128)(2,1)S(1)}, bf16[512,768]{1,0:T(8,128)(2,1)S(1)}) custom-call(bf16[512,384]{1,0:T(8,128)(2,1)S(1)} %get-tuple-element.71.refs_4_.refs_0_, bf16[512,384]{1,0:T(8,128)(2,1)S(1)} %get-tuple-element.81.refs_1_, bf16[512,384]{1,0:T(8,128)(2,1)S(1)} %get-tuple-element.74.refs_2_, ...), custom_call_target="tpu_custom_call" | custom-call | tf_op jit(solution)/shard_map/pallas_call | solution.py:193
  92.6 1.6 %shard_map.176 = (bf16[384,1536]{1,0:T(8,128)(2,1)S(1)}, bf16[384,1536]{1,0:T(8,128)(2,1)S(1)}) custom-call(bf16[512,768]{1,0:T(8,128)(2,1)S(1)} %get-tuple-element.67.refs_0_.refs_2_, bf16[512,768]{1,0:T(8,128)(2,1)S(1)} %get-tuple-element.95.refs_1_.refs_6_, bf16[512,768]{1,0:T(8,128)(2,1)S(1)} %get-tuple-element.67.refs_0_.refs_2_, ...), custom_call_target="tpu_custom_call" | custom-call | tf_op jit(solution)/shard_map/pallas_call | solution.py:193
  94.3 1.6 %collective-permute-start.38 = (bf16[512,768]{1,0:T(8,128)(2,1)S(1)}, bf16[512,768]{1,0:T(8,128)(2,1)S(1)}, u32[]{:S(2)}, u32[]{:S(2)}) collective-permute-start(bf16[512,768]{1,0:T(8,128)(2,1)S(1)} %get-tuple-element.110.refs_2_), channel_id=1, source_target_pairs={{0,1},{1,0},{2,3},{3,2},{4,5},{5,4},{6,7},{7,6},{8,9},{9,8},{10,11... | collective-permute-start | bytes 2359304 | tf_op jit(solution)/shard_map/ppermute | solution.py:62
  96.0 1.4 collective-permute-start.35
  97.4 3.3 %collective-permute-start.36 = (bf16[48,1920]{1,0:T(8,128)(2,1)S(1)}, bf16[48,1920]{1,0:T(8,128)(2,1)S(1)}, u32[]{:S(2)}, u32[]{:S(2)}) collective-permute-start(bf16[48,1920]{1,0:T(8,128)(2,1)S(1)} %get-tuple-element.108), channel_id=1, source_target_pairs={{0,16},{2,18},{4,20},{6,22},{8,24},{10,26},{12,28},{14,30},{16,0},... | collective-permute-start | bytes 552968 | tf_op jit(solution)/shard_map/ppermute | solution.py:58
  101.0 1.4 collective-permute-start.34
  102.3 1.9 %collective-permute-done.35.refs_1_ = bf16[48,1920]{1,0:T(8,128)(2,1)S(1)} collective-permute-done((bf16[48,1920]{1,0:T(8,128)(2,1)S(1)}, bf16[48,1920]{1,0:T(8,128)(2,1)S(1)}, u32[]{:S(2)}, u32[]{:S(2)}) %collective-permute-start.35) | collective-permute-done | bytes 184352 | tf_op jit(solution)/shard_map/ppermute | solution.py:58
  104.2 13.0 %collective-permute-done.36.refs_2_ = bf16[48,1920]{1,0:T(8,128)(2,1)S(1)} collective-permute-done((bf16[48,1920]{1,0:T(8,128)(2,1)S(1)}, bf16[48,1920]{1,0:T(8,128)(2,1)S(1)}, u32[]{:S(2)}, u32[]{:S(2)}) %collective-permute-start.36) | collective-permute-done | bytes 184352 | tf_op jit(solution)/shard_map/ppermute | solution.py:58
  117.3 0.8 copy-done.10
  118.1 0.9 shard_map.180
  120.2 1.2 collective-permute-start.40
  121.3 1.5 %collective-permute-start.41 = (bf16[48,1536]{1,0:T(8,128)(2,1)}, bf16[48,1536]{1,0:T(8,128)(2,1)}, u32[]{:S(2)}, u32[]{:S(2)}) collective-permute-start(bf16[48,1536]{1,0:T(8,128)(2,1)} %get-tuple-element.116), channel_id=1, source_target_pairs={{0,16},{2,18},{4,20},{6,22},{8,24},{10,26},{12,28},{14,30},{16,0},... | collective-permute-start | bytes 442376 | tf_op jit(solution)/shard_map/ppermute | solution.py:58
  123.1 0.7 copy.32.refs_2_
  123.8 1.9 %shard_map.181 = (f32[48,2,576]{2,1,0:T(2,128)}, f32[48,576]{1,0:T(8,128)}, f32[48,2]{1,0:T(8,128)}) custom-call(f32[48,1920]{1,0:T(8,128)} %copy-done.8, bf16[48,1280]{1,0:T(8,128)(2,1)} %copy-done.16, f32[48,2]{1,0:T(8,128)} %copy.32.refs_2_, bf16[48,1536]{1,0:T(8,128)(2,1)} %copy-done.15), custom_call_target="tpu_custom_call" | custom-call | tf_op jit(solution)/shard_map/pallas_call | solution.py:193
  125.7 6.0 %shard_map.182.refs_5_ = f32[512,768]{1,0:T(8,128)} custom-call(f32[512,768]{1,0:T(8,128)} %copy-done.7, bf16[512,768]{1,0:T(8,128)(2,1)} %copy-done.2, bf16[512,768]{1,0:T(8,128)(2,1)} %copy-done.9, bf16[512,768]{1,0:T(8,128)(2,1)} %copy-done.10, bf16[768,768]{1,0:T(8,128)(2,1)} %get-tuple-element.131.refs_4_, f32[48,2]{1,0:T(8,128)} %get-tuple-element.114.refs_5_.refs_6_), custom_call_target="tpu_custom_call" | custom-call | tf_op jit(solution)/shard_map/pallas_call | solution.py:193
  131.7 1.4 copy-done.1
  133.1 2.7 %shard_map.183.refs_7_ = bf16[512,768]{1,0:T(8,128)(2,1)} custom-call(f32[512,768]{1,0:T(8,128)S(1)} %get-tuple-element.76.refs_10_.refs_1_.refs_0_, bf16[512,768]{1,0:T(8,128)(2,1)S(1)} %get-tuple-element.80.refs_1_, bf16[256,768]{1,0:T(8,128)(2,1)S(1)} %copy-done.6, bf16[256,768]{1,0:T(8,128)(2,1)} %collective-permute-done.39.refs_3_, ...), custom_call_target="tpu_custom_call" | custom-call | tf_op jit(solution)/shard_map/pallas_call | solution.py:193
  135.8 2.2 %shard_map.184 = (f32[3,48,384]{2,1,0:T(8,128)}, f32[48,384]{1,0:T(8,128)}, f32[2,48]{1,0:T(2,128)}) custom-call(bf16[48,1536]{1,0:T(8,128)(2,1)} %copy-done.15, bf16[48,1536]{1,0:T(8,128)(2,1)} %collective-permute-done.40.refs_1_, bf16[48,1536]{1,0:T(8,128)(2,1)} %collective-permute-done.41.refs_2_, bf16[48,1536]{1,0:T(8,128)(2,1)} %collective-permute-done.42.refs_3_, ...), custom_call_target="tpu_custom_call" | custom-call | tf_op jit(solution)/shard_map/pallas_call | solution.py:193
  138.0 0.7 collective-permute-start.43
  138.6 3.1 %collective-permute-done.43 = f32[2,48]{1,0:T(2,128)S(1)} collective-permute-done((f32[2,48]{1,0:T(2,128)}, f32[2,48]{1,0:T(2,128)S(1)}, u32[]{:S(2)}, u32[]{:S(2)}) %collective-permute-start.43) | collective-permute-done | bytes 416 | tf_op jit(solution)/shard_map/ppermute | solution.py:62
  141.7 0.7 add.172
  (114 shorter events, 9.0 us)
Async XLA Ops:
  0.6 12.5 %copy-start.18 = (bf16[48,2,576]{2,1,0:T(2,128)(2,1)S(1)}, bf16[48,2,576]{2,1,0:T(2,128)(2,1)}, u32[]{:S(2)}) copy-start(bf16[48,2,576]{2,1,0:T(2,128)(2,1)} %param.17) | copy-start | bytes 331780
  2.3 11.1 %copy-start.13 = (bf16[48,768]{1,0:T(8,128)(2,1)}, bf16[48,768]{1,0:T(8,128)(2,1)S(1)}, u32[]{:S(2)}) copy-start(bf16[48,768]{1,0:T(8,128)(2,1)S(1)} %pad_maximum_fusion.refs_0_.refs_4_) | copy-start | bytes 221188
  2.3 11.0 %copy-start.19 = (bf16[384,48]{0,1:T(8,128)(2,1)S(1)}, bf16[384,48]{0,1:T(8,128)(2,1)}, u32[]{:S(2)}) copy-start(bf16[384,48]{0,1:T(8,128)(2,1)} %param.15) | copy-start | bytes 110596
  2.3 11.1 %collective-permute-start = (bf16[48,768]{1,0:T(8,128)(2,1)S(1)}, bf16[48,768]{1,0:T(8,128)(2,1)S(1)}, u32[]{:S(2)}, u32[]{:S(2)}) collective-permute-start(bf16[48,768]{1,0:T(8,128)(2,1)S(1)} %pad_maximum_fusion.refs_0_.refs_4_), channel_id=1, source_target_pairs={{0,8},{2,10},{4,12},{6,14},{8,16},{10,18},{12,20},{14,22},{16,24},... | collective-permute-start | bytes 221192 | tf_op jit(solution)/shard_map/ppermute | solution.py:58
  5.4 8.0 %collective-permute-start.1 = (bf16[48,768]{1,0:T(8,128)(2,1)S(1)}, bf16[48,768]{1,0:T(8,128)(2,1)S(1)}, u32[]{:S(2)}, u32[]{:S(2)}) collective-permute-start(bf16[48,768]{1,0:T(8,128)(2,1)S(1)} %pad_maximum_fusion.refs_0_.refs_4_), channel_id=1, source_target_pairs={{0,16},{2,18},{4,20},{6,22},{8,24},{10,26},{12,28},{14,30},{16,0},... | collective-permute-start | bytes 221192 | tf_op jit(solution)/shard_map/ppermute | solution.py:58
  8.0 5.4 %collective-permute-start.2 = (bf16[48,768]{1,0:T(8,128)(2,1)S(1)}, bf16[48,768]{1,0:T(8,128)(2,1)S(1)}, u32[]{:S(2)}, u32[]{:S(2)}) collective-permute-start(bf16[48,768]{1,0:T(8,128)(2,1)S(1)} %pad_maximum_fusion.refs_0_.refs_4_), channel_id=1, source_target_pairs={{0,24},{2,26},{4,28},{6,30},{8,0},{10,2},{12,4},{14,6},{16,8},{18,... | collective-permute-start | bytes 221192 | tf_op jit(solution)/shard_map/ppermute | solution.py:58
  10.1 16.7 %collective-permute-start.12 = (bf16[48,640]{1,0:T(8,128)(2,1)S(1)}, bf16[48,640]{1,0:T(8,128)(2,1)S(1)}, u32[]{:S(2)}, u32[]{:S(2)}) collective-permute-start(bf16[48,640]{1,0:T(8,128)(2,1)S(1)} %pad.10.refs_0_), channel_id=1, source_target_pairs={{0,4},{2,6},{4,0},{6,2},{8,12},{10,14},{12,8},{14,10},{16,20},{18,... | collective-permute-start | bytes 184328 | tf_op jit(solution)/shard_map/ppermute | solution.py:58
  11.8 7.6 %copy-start.20 = (s32[512]{0:T(512)S(1)}, s32[512]{0:T(512)}, u32[]{:S(2)}) copy-start(s32[512]{0:T(512)} %param.12) | copy-start | bytes 6148
  11.8 7.6 %copy-start.17 = (s32[512]{0:T(512)S(1)}, s32[512]{0:T(512)}, u32[]{:S(2)}) copy-start(s32[512]{0:T(512)} %param.11) | copy-start | bytes 6148
  13.3 10.5 %copy-start.14 = (bf16[48,768]{1,0:T(8,128)(2,1)}, bf16[48,768]{1,0:T(8,128)(2,1)S(1)}, u32[]{:S(2)}) copy-start(bf16[48,768]{1,0:T(8,128)(2,1)S(1)} %pad_maximum_fusion.1.refs_0_.refs_5_) | copy-start | bytes 221188
  13.4 10.4 %collective-permute-start.6 = (bf16[192,768]{1,0:T(8,128)(2,1)S(1)}, bf16[192,768]{1,0:T(8,128)(2,1)S(1)}, u32[]{:S(2)}, u32[]{:S(2)}) collective-permute-start(bf16[192,768]{1,0:T(8,128)(2,1)S(1)} %shard_map.161.refs_2_.refs_1_.refs_8_), channel_id=1, source_target_pairs={{0,4},{2,6},{4,0},{6,2},{8,12},{10,14},{12,8},{14,10},{16,20},{18,... | collective-permute-start | bytes 884744 | tf_op jit(solution)/shard_map/ppermute | solution.py:58
  14.8 7.0 %collective-permute-start.3 = (bf16[48,768]{1,0:T(8,128)(2,1)S(1)}, bf16[48,768]{1,0:T(8,128)(2,1)S(1)}, u32[]{:S(2)}, u32[]{:S(2)}) collective-permute-start(bf16[48,768]{1,0:T(8,128)(2,1)S(1)} %pad_maximum_fusion.1.refs_0_.refs_5_), channel_id=1, source_target_pairs={{0,8},{2,10},{4,12},{6,14},{8,16},{10,18},{12,20},{14,22},{16,24},... | collective-permute-start | bytes 221192 | tf_op jit(solution)/shard_map/ppermute | solution.py:58
  16.7 7.1 %collective-permute-start.4 = (bf16[48,768]{1,0:T(8,128)(2,1)S(1)}, bf16[48,768]{1,0:T(8,128)(2,1)S(1)}, u32[]{:S(2)}, u32[]{:S(2)}) collective-permute-start(bf16[48,768]{1,0:T(8,128)(2,1)S(1)} %pad_maximum_fusion.1.refs_0_.refs_5_), channel_id=1, source_target_pairs={{0,16},{2,18},{4,20},{6,22},{8,24},{10,26},{12,28},{14,30},{16,0},... | collective-permute-start | bytes 221192 | tf_op jit(solution)/shard_map/ppermute | solution.py:58
  18.6 5.1 %collective-permute-start.5 = (bf16[48,768]{1,0:T(8,128)(2,1)S(1)}, bf16[48,768]{1,0:T(8,128)(2,1)S(1)}, u32[]{:S(2)}, u32[]{:S(2)}) collective-permute-start(bf16[48,768]{1,0:T(8,128)(2,1)S(1)} %pad_maximum_fusion.1.refs_0_.refs_5_), channel_id=1, source_target_pairs={{0,24},{2,26},{4,28},{6,30},{8,0},{10,2},{12,4},{14,6},{16,8},{18,... | collective-permute-start | bytes 221192 | tf_op jit(solution)/shard_map/ppermute | solution.py:58
  19.6 1.1 copy-start.11
  21.8 37.2 %copy-start.2 = (bf16[512,768]{1,0:T(8,128)(2,1)}, bf16[512,768]{1,0:T(8,128)(2,1)S(1)}, u32[]{:S(2)}) copy-start(bf16[512,768]{1,0:T(8,128)(2,1)S(1)} %get-tuple-element.66.refs_4_.refs_0_.refs_1_) | copy-start | bytes 2359300
  23.8 11.1 %copy-start.3 = (bf16[192,768]{1,0:T(8,128)(2,1)}, bf16[192,768]{1,0:T(8,128)(2,1)S(1)}, u32[]{:S(2)}) copy-start(bf16[192,768]{1,0:T(8,128)(2,1)S(1)} %collective-permute-done.6.refs_5_.refs_2_.refs_9_) | copy-start | bytes 884740
  23.8 8.1 %collective-permute-start.7 = (bf16[192,768]{1,0:T(8,128)(2,1)S(1)}, bf16[192,768]{1,0:T(8,128)(2,1)S(1)}, u32[]{:S(2)}, u32[]{:S(2)}) collective-permute-start(bf16[192,768]{1,0:T(8,128)(2,1)S(1)} %shard_map.163.refs_2_.refs_1_.refs_4_.refs_12_), channel_id=1, source_target_pairs={{0,4},{2,6},{4,0},{6,2},{8,12},{10,14},{12,8},{14,10},{16,20},{18,... | collective-permute-start | bytes 884744 | tf_op jit(solution)/shard_map/ppermute | solution.py:58
  24.6 14.3 %copy-start.16 = (bf16[48,1280]{1,0:T(8,128)(2,1)}, bf16[48,1280]{1,0:T(8,128)(2,1)S(1)}, u32[]{:S(2)}) copy-start(bf16[48,1280]{1,0:T(8,128)(2,1)S(1)} %fusion.5.refs_0_.refs_1_) | copy-start | bytes 368644
  24.6 9.7 %collective-permute-start.10 = (bf16[192,768]{1,0:T(8,128)(2,1)S(1)}, bf16[192,768]{1,0:T(8,128)(2,1)S(1)}, u32[]{:S(2)}, u32[]{:S(2)}) collective-permute-start(bf16[192,768]{1,0:T(8,128)(2,1)S(1)} %shard_map.161.refs_2_.refs_1_.refs_8_), channel_id=1, source_target_pairs={{0,2},{2,0},{4,6},{6,4},{8,10},{10,8},{12,14},{14,12},{16,18},{18,... | collective-permute-start | bytes 884744 | tf_op jit(solution)/shard_map/ppermute | solution.py:58
  24.7 9.7 %collective-permute-start.11 = (bf16[192,768]{1,0:T(8,128)(2,1)S(1)}, bf16[192,768]{1,0:T(8,128)(2,1)S(1)}, u32[]{:S(2)}, u32[]{:S(2)}) collective-permute-start(bf16[192,768]{1,0:T(8,128)(2,1)S(1)} %collective-permute-done.6.refs_5_.refs_2_.refs_9_), channel_id=1, source_target_pairs={{0,2},{2,0},{4,6},{6,4},{8,10},{10,8},{12,14},{14,12},{16,18},{18,... | collective-permute-start | bytes 884744 | tf_op jit(solution)/shard_map/ppermute | solution.py:58
  25.2 12.4 %collective-permute-start.13 = (bf16[48,1280]{1,0:T(8,128)(2,1)S(1)}, bf16[48,1280]{1,0:T(8,128)(2,1)S(1)}, u32[]{:S(2)}, u32[]{:S(2)}) collective-permute-start(bf16[48,1280]{1,0:T(8,128)(2,1)S(1)} %fusion.5.refs_0_.refs_1_), channel_id=1, source_target_pairs={{0,8},{2,10},{4,12},{6,14},{8,16},{10,18},{12,20},{14,22},{16,24},... | collective-permute-start | bytes 368648 | tf_op jit(solution)/shard_map/ppermute | solution.py:58
  26.9 10.8 %collective-permute-start.14 = (bf16[48,1280]{1,0:T(8,128)(2,1)S(1)}, bf16[48,1280]{1,0:T(8,128)(2,1)S(1)}, u32[]{:S(2)}, u32[]{:S(2)}) collective-permute-start(bf16[48,1280]{1,0:T(8,128)(2,1)S(1)} %fusion.5.refs_0_.refs_1_), channel_id=1, source_target_pairs={{0,16},{2,18},{4,20},{6,22},{8,24},{10,26},{12,28},{14,30},{16,0},... | collective-permute-start | bytes 368648 | tf_op jit(solution)/shard_map/ppermute | solution.py:58
  32.0 6.9 %collective-permute-start.15 = (bf16[48,1280]{1,0:T(8,128)(2,1)S(1)}, bf16[48,1280]{1,0:T(8,128)(2,1)S(1)}, u32[]{:S(2)}, u32[]{:S(2)}) collective-permute-start(bf16[48,1280]{1,0:T(8,128)(2,1)S(1)} %fusion.5.refs_0_.refs_1_), channel_id=1, source_target_pairs={{0,24},{2,26},{4,28},{6,30},{8,0},{10,2},{12,4},{14,6},{16,8},{18,... | collective-permute-start | bytes 368648 | tf_op jit(solution)/shard_map/ppermute | solution.py:58
  34.3 4.6 %collective-permute-start.8 = (bf16[192,768]{1,0:T(8,128)(2,1)S(1)}, bf16[192,768]{1,0:T(8,128)(2,1)S(1)}, u32[]{:S(2)}, u32[]{:S(2)}) collective-permute-start(bf16[192,768]{1,0:T(8,128)(2,1)S(1)} %shard_map.163.refs_2_.refs_1_.refs_4_.refs_12_), channel_id=1, source_target_pairs={{0,2},{2,0},{4,6},{6,4},{8,10},{10,8},{12,14},{14,12},{16,18},{18,... | collective-permute-start | bytes 884744 | tf_op jit(solution)/shard_map/ppermute | solution.py:58
  34.4 4.5 %collective-permute-start.9 = (bf16[192,768]{1,0:T(8,128)(2,1)S(1)}, bf16[192,768]{1,0:T(8,128)(2,1)S(1)}, u32[]{:S(2)}, u32[]{:S(2)}) collective-permute-start(bf16[192,768]{1,0:T(8,128)(2,1)S(1)} %collective-permute-done.7.refs_5_.refs_2_.refs_13_), channel_id=1, source_target_pairs={{0,2},{2,0},{4,6},{6,4},{8,10},{10,8},{12,14},{14,12},{16,18},{18,... | collective-permute-start | bytes 884744 | tf_op jit(solution)/shard_map/ppermute | solution.py:58
  38.9 8.9 %copy-start.12 = (bf16[512,768]{1,0:T(8,128)(2,1)S(1)}, bf16[512,768]{1,0:T(8,128)(2,1)}, u32[]{:S(2)}) copy-start(bf16[512,768]{1,0:T(8,128)(2,1)} %refs_0_.3) | copy-start | bytes 2359300
  40.6 18.4 %collective-permute-start.16 = (bf16[512,768]{1,0:T(8,128)(2,1)S(1)}, bf16[512,768]{1,0:T(8,128)(2,1)S(1)}, u32[]{:S(2)}, u32[]{:S(2)}) collective-permute-start(bf16[512,768]{1,0:T(8,128)(2,1)S(1)} %get-tuple-element.72.refs_1_), channel_id=1, source_target_pairs={{0,1},{1,0},{2,3},{3,2},{4,5},{5,4},{6,7},{7,6},{8,9},{9,8},{10,11... | collective-permute-start | bytes 2359304 | tf_op jit(solution)/shard_map/ppermute | solution.py:62
  42.2 13.0 %collective-permute-start.20 = (bf16[192,1280]{1,0:T(8,128)(2,1)S(1)}, bf16[192,1280]{1,0:T(8,128)(2,1)S(1)}, u32[]{:S(2)}, u32[]{:S(2)}) collective-permute-start(bf16[192,1280]{1,0:T(8,128)(2,1)S(1)} %shard_map.166.refs_6_.refs_2_), channel_id=1, source_target_pairs={{0,4},{2,6},{4,0},{6,2},{8,12},{10,14},{12,8},{14,10},{16,20},{18,... | collective-permute-start | bytes 1474568 | tf_op jit(solution)/shard_map/ppermute | solution.py:58
  42.9 8.0 %collective-permute-start.17 = (bf16[96,640]{1,0:T(8,128)(2,1)S(1)}, bf16[96,640]{1,0:T(8,128)(2,1)S(1)}, u32[]{:S(2)}, u32[]{:S(2)}) collective-permute-start(bf16[96,640]{1,0:T(8,128)(2,1)S(1)} %shard_map.164.refs_9_.refs_0_), channel_id=1, source_target_pairs={{0,8},{2,10},{4,12},{6,14},{8,16},{10,18},{12,20},{14,22},{16,24},... | collective-permute-start | bytes 368648 | tf_op jit(solution)/shard_map/ppermute | solution.py:58
  45.5 9.1 %collective-permute-start.18 = (bf16[96,640]{1,0:T(8,128)(2,1)S(1)}, bf16[96,640]{1,0:T(8,128)(2,1)S(1)}, u32[]{:S(2)}, u32[]{:S(2)}) collective-permute-start(bf16[96,640]{1,0:T(8,128)(2,1)S(1)} %shard_map.164.refs_9_.refs_0_), channel_id=1, source_target_pairs={{0,16},{2,18},{4,20},{6,22},{8,24},{10,26},{12,28},{14,30},{16,0},... | collective-permute-start | bytes 368648 | tf_op jit(solution)/shard_map/ppermute | solution.py:58
  45.9 8.6 %collective-permute-start.19 = (bf16[96,640]{1,0:T(8,128)(2,1)S(1)}, bf16[96,640]{1,0:T(8,128)(2,1)S(1)}, u32[]{:S(2)}, u32[]{:S(2)}) collective-permute-start(bf16[96,640]{1,0:T(8,128)(2,1)S(1)} %shard_map.164.refs_9_.refs_0_), channel_id=1, source_target_pairs={{0,24},{2,26},{4,28},{6,30},{8,0},{10,2},{12,4},{14,6},{16,8},{18,... | collective-permute-start | bytes 368648 | tf_op jit(solution)/shard_map/ppermute | solution.py:58
  54.6 5.0 %collective-permute-start.23 = (bf16[192,640]{1,0:T(8,128)(2,1)S(1)}, bf16[192,640]{1,0:T(8,128)(2,1)S(1)}, u32[]{:S(2)}, u32[]{:S(2)}) collective-permute-start(bf16[192,640]{1,0:T(8,128)(2,1)S(1)} %get-tuple-element.75.refs_3_.refs_6_), channel_id=1, source_target_pairs={{0,2},{2,0},{4,6},{6,4},{8,10},{10,8},{12,14},{14,12},{16,18},{18,... | collective-permute-start | bytes 737288 | tf_op jit(solution)/shard_map/ppermute | solution.py:58
  54.7 5.0 %collective-permute-start.24 = (bf16[192,640]{1,0:T(8,128)(2,1)S(1)}, bf16[192,640]{1,0:T(8,128)(2,1)S(1)}, u32[]{:S(2)}, u32[]{:S(2)}) collective-permute-start(bf16[192,640]{1,0:T(8,128)(2,1)S(1)} %get-tuple-element.79.refs_7_), channel_id=1, source_target_pairs={{0,2},{2,0},{4,6},{6,4},{8,10},{10,8},{12,14},{14,12},{16,18},{18,... | collective-permute-start | bytes 737288 | tf_op jit(solution)/shard_map/ppermute | solution.py:58
  55.2 4.5 %collective-permute-start.21 = (bf16[192,1280]{1,0:T(8,128)(2,1)S(1)}, bf16[192,1280]{1,0:T(8,128)(2,1)S(1)}, u32[]{:S(2)}, u32[]{:S(2)}) collective-permute-start(bf16[192,1280]{1,0:T(8,128)(2,1)S(1)} %shard_map.166.refs_6_.refs_2_), channel_id=1, source_target_pairs={{0,2},{2,0},{4,6},{6,4},{8,10},{10,8},{12,14},{14,12},{16,18},{18,... | collective-permute-start | bytes 1474568 | tf_op jit(solution)/shard_map/ppermute | solution.py:58
  55.2 4.4 %collective-permute-start.22 = (bf16[192,1280]{1,0:T(8,128)(2,1)S(1)}, bf16[192,1280]{1,0:T(8,128)(2,1)S(1)}, u32[]{:S(2)}, u32[]{:S(2)}) collective-permute-start(bf16[192,1280]{1,0:T(8,128)(2,1)S(1)} %collective-permute-done.20.refs_3_), channel_id=1, source_target_pairs={{0,2},{2,0},{4,6},{6,4},{8,10},{10,8},{12,14},{14,12},{16,18},{18,... | collective-permute-start | bytes 1474568 | tf_op jit(solution)/shard_map/ppermute | solution.py:58
  63.7 20.5 %collective-permute-start.26 = (bf16[512,768]{1,0:T(8,128)(2,1)S(1)}, bf16[512,768]{1,0:T(8,128)(2,1)S(1)}, u32[]{:S(2)}, u32[]{:S(2)}) collective-permute-start(bf16[512,768]{1,0:T(8,128)(2,1)S(1)} %get-tuple-element.82.refs_2_), channel_id=1, source_target_pairs={{0,1},{1,0},{2,3},{3,2},{4,5},{5,4},{6,7},{7,6},{8,9},{9,8},{10,11... | collective-permute-start | bytes 2359304 | tf_op jit(solution)/shard_map/ppermute | solution.py:62
  67.0 2.0 %collective-permute-start.27 = (bf16[384,640]{1,0:T(8,128)(2,1)S(1)}, bf16[384,640]{1,0:T(8,128)(2,1)S(1)}, u32[]{:S(2)}, u32[]{:S(2)}) collective-permute-start(bf16[384,640]{1,0:T(8,128)(2,1)S(1)} %get-tuple-element.89), channel_id=1, source_target_pairs={{0,2},{2,0},{4,6},{6,4},{8,10},{10,8},{12,14},{14,12},{16,18},{18,... | collective-permute-start | bytes 1474568 | tf_op jit(solution)/shard_map/ppermute | solution.py:58
  67.1 2.6 %collective-permute-start.28 = (bf16[384,640]{1,0:T(8,128)(2,1)S(1)}, bf16[384,640]{1,0:T(8,128)(2,1)S(1)}, u32[]{:S(2)}, u32[]{:S(2)}) collective-permute-start(bf16[384,640]{1,0:T(8,128)(2,1)S(1)} %get-tuple-element.90), channel_id=1, source_target_pairs={{0,2},{2,0},{4,6},{6,4},{8,10},{10,8},{12,14},{14,12},{16,18},{18,... | collective-permute-start | bytes 1474568 | tf_op jit(solution)/shard_map/ppermute | solution.py:58
  67.6 2.8 %collective-permute-start.29 = (bf16[384,640]{1,0:T(8,128)(2,1)S(1)}, bf16[384,640]{1,0:T(8,128)(2,1)S(1)}, u32[]{:S(2)}, u32[]{:S(2)}) collective-permute-start(bf16[384,640]{1,0:T(8,128)(2,1)S(1)} %get-tuple-element.91), channel_id=1, source_target_pairs={{0,2},{2,0},{4,6},{6,4},{8,10},{10,8},{12,14},{14,12},{16,18},{18,... | collective-permute-start | bytes 1474568 | tf_op jit(solution)/shard_map/ppermute | solution.py:58
  68.5 24.0 %collective-permute-start.25 = (bf16[256,768]{1,0:T(8,128)(2,1)S(1)}, bf16[256,768]{1,0:T(8,128)(2,1)S(1)}, u32[]{:S(2)}, u32[]{:S(2)}) collective-permute-start(bf16[256,768]{1,0:T(8,128)(2,1)S(1)} %get-tuple-element.125), channel_id=1, source_target_pairs={{0,1},{1,0},{2,3},{3,2},{4,5},{5,4},{6,7},{7,6},{8,9},{9,8},{10,11... | collective-permute-start | bytes 1179656 | tf_op jit(solution)/shard_map/ppermute | solution.py:62
  70.7 21.8 %collective-permute-start.30 = (bf16[192,640]{1,0:T(8,128)(2,1)S(1)}, bf16[192,640]{1,0:T(8,128)(2,1)S(1)}, u32[]{:S(2)}, u32[]{:S(2)}) collective-permute-start(bf16[192,640]{1,0:T(8,128)(2,1)S(1)} %get-tuple-element.97), channel_id=1, source_target_pairs={{0,4},{2,6},{4,0},{6,2},{8,12},{10,14},{12,8},{14,10},{16,20},{18,... | collective-permute-start | bytes 737288 | tf_op jit(solution)/shard_map/ppermute | solution.py:58
  72.0 20.5 %collective-permute-start.31 = (bf16[192,640]{1,0:T(8,128)(2,1)S(1)}, bf16[192,640]{1,0:T(8,128)(2,1)S(1)}, u32[]{:S(2)}, u32[]{:S(2)}) collective-permute-start(bf16[192,640]{1,0:T(8,128)(2,1)S(1)} %get-tuple-element.98), channel_id=1, source_target_pairs={{0,4},{2,6},{4,0},{6,2},{8,12},{10,14},{12,8},{14,10},{16,20},{18,... | collective-permute-start | bytes 737288 | tf_op jit(solution)/shard_map/ppermute | solution.py:58
  72.8 19.7 %collective-permute-start.32 = (bf16[192,640]{1,0:T(8,128)(2,1)S(1)}, bf16[192,640]{1,0:T(8,128)(2,1)S(1)}, u32[]{:S(2)}, u32[]{:S(2)}) collective-permute-start(bf16[192,640]{1,0:T(8,128)(2,1)S(1)} %get-tuple-element.99), channel_id=1, source_target_pairs={{0,4},{2,6},{4,0},{6,2},{8,12},{10,14},{12,8},{14,10},{16,20},{18,... | collective-permute-start | bytes 737288 | tf_op jit(solution)/shard_map/ppermute | solution.py:58
  84.2 3.2 %copy-start.4 = (bf16[192,768]{1,0:T(8,128)(2,1)S(1)}, bf16[192,768]{1,0:T(8,128)(2,1)}, u32[]{:S(2)}) copy-start(bf16[192,768]{1,0:T(8,128)(2,1)} %copy-done.3) | copy-start | bytes 884740
  86.2 1.1 copy-start.7
  92.5 1.8 %copy-start.9 = (bf16[512,768]{1,0:T(8,128)(2,1)}, bf16[512,768]{1,0:T(8,128)(2,1)S(1)}, u32[]{:S(2)}) copy-start(bf16[512,768]{1,0:T(8,128)(2,1)S(1)} %get-tuple-element.110.refs_2_) | copy-start | bytes 2359300
  92.5 1.7 %copy-start.5 = (bf16[256,768]{1,0:T(8,128)(2,1)}, bf16[256,768]{1,0:T(8,128)(2,1)S(1)}, u32[]{:S(2)}) copy-start(bf16[256,768]{1,0:T(8,128)(2,1)S(1)} %collective-permute-done.25.refs_7_.refs_2_) | copy-start | bytes 1179652
  94.2 6.5 %collective-permute-start.33 = (bf16[384,1536]{1,0:T(8,128)(2,1)S(1)}, bf16[384,1536]{1,0:T(8,128)(2,1)S(1)}, u32[]{:S(2)}, u32[]{:S(2)}) collective-permute-start(bf16[384,1536]{1,0:T(8,128)(2,1)S(1)} %get-tuple-element.101), channel_id=1, source_target_pairs={{0,2},{2,0},{4,6},{6,4},{8,10},{10,8},{12,14},{14,12},{16,18},{18,... | collective-permute-start | bytes 3538952 | tf_op jit(solution)/shard_map/ppermute | solution.py:58
  94.3 22.9 %collective-permute-start.38 = (bf16[512,768]{1,0:T(8,128)(2,1)S(1)}, bf16[512,768]{1,0:T(8,128)(2,1)S(1)}, u32[]{:S(2)}, u32[]{:S(2)}) collective-permute-start(bf16[512,768]{1,0:T(8,128)(2,1)S(1)} %get-tuple-element.110.refs_2_), channel_id=1, source_target_pairs={{0,1},{1,0},{2,3},{3,2},{4,5},{5,4},{6,7},{7,6},{8,9},{9,8},{10,11... | collective-permute-start | bytes 2359304 | tf_op jit(solution)/shard_map/ppermute | solution.py:62
  96.0 8.2 %collective-permute-start.35 = (bf16[48,1920]{1,0:T(8,128)(2,1)S(1)}, bf16[48,1920]{1,0:T(8,128)(2,1)S(1)}, u32[]{:S(2)}, u32[]{:S(2)}) collective-permute-start(bf16[48,1920]{1,0:T(8,128)(2,1)S(1)} %get-tuple-element.107), channel_id=1, source_target_pairs={{0,24},{2,26},{4,28},{6,30},{8,0},{10,2},{12,4},{14,6},{16,8},{18,... | collective-permute-start | bytes 552968 | tf_op jit(solution)/shard_map/ppermute | solution.py:58
  97.4 19.8 %collective-permute-start.36 = (bf16[48,1920]{1,0:T(8,128)(2,1)S(1)}, bf16[48,1920]{1,0:T(8,128)(2,1)S(1)}, u32[]{:S(2)}, u32[]{:S(2)}) collective-permute-start(bf16[48,1920]{1,0:T(8,128)(2,1)S(1)} %get-tuple-element.108), channel_id=1, source_target_pairs={{0,16},{2,18},{4,20},{6,22},{8,24},{10,26},{12,28},{14,30},{16,0},... | collective-permute-start | bytes 552968 | tf_op jit(solution)/shard_map/ppermute | solution.py:58
  100.7 16.5 %collective-permute-start.37 = (bf16[48,1920]{1,0:T(8,128)(2,1)S(1)}, bf16[48,1920]{1,0:T(8,128)(2,1)S(1)}, u32[]{:S(2)}, u32[]{:S(2)}) collective-permute-start(bf16[48,1920]{1,0:T(8,128)(2,1)S(1)} %get-tuple-element.109), channel_id=1, source_target_pairs={{0,8},{2,10},{4,12},{6,14},{8,16},{10,18},{12,20},{14,22},{16,24},... | collective-permute-start | bytes 552968 | tf_op jit(solution)/shard_map/ppermute | solution.py:58
  101.0 17.2 %collective-permute-start.34 = (bf16[192,1536]{1,0:T(8,128)(2,1)S(1)}, bf16[192,1536]{1,0:T(8,128)(2,1)S(1)}, u32[]{:S(2)}, u32[]{:S(2)}) collective-permute-start(bf16[192,1536]{1,0:T(8,128)(2,1)S(1)} %get-tuple-element.106), channel_id=1, source_target_pairs={{0,4},{2,6},{4,0},{6,2},{8,12},{10,14},{12,8},{14,10},{16,20},{18,... | collective-permute-start | bytes 1769480 | tf_op jit(solution)/shard_map/ppermute | solution.py:58
  117.2 0.9 copy-start.10
  118.1 5.7 %copy-start.8 = (f32[48,1920]{1,0:T(8,128)}, f32[48,1920]{1,0:T(8,128)S(1)}, u32[]{:S(2)}) copy-start(f32[48,1920]{1,0:T(8,128)S(1)} %shard_map.179.refs_2_.refs_0_) | copy-start | bytes 1105924
  119.7 12.0 %collective-permute-start.39 = (bf16[256,768]{1,0:T(8,128)(2,1)}, bf16[256,768]{1,0:T(8,128)(2,1)}, u32[]{:S(2)}, u32[]{:S(2)}) collective-permute-start(bf16[256,768]{1,0:T(8,128)(2,1)} %get-tuple-element.112), channel_id=1, source_target_pairs={{0,1},{1,0},{2,3},{3,2},{4,5},{5,4},{6,7},{7,6},{8,9},{9,8},{10,11... | collective-permute-start | bytes 1179656 | tf_op jit(solution)/shard_map/ppermute | solution.py:62
  120.2 15.6 %collective-permute-start.40 = (bf16[48,1536]{1,0:T(8,128)(2,1)}, bf16[48,1536]{1,0:T(8,128)(2,1)}, u32[]{:S(2)}, u32[]{:S(2)}) collective-permute-start(bf16[48,1536]{1,0:T(8,128)(2,1)} %get-tuple-element.115), channel_id=1, source_target_pairs={{0,24},{2,26},{4,28},{6,30},{8,0},{10,2},{12,4},{14,6},{16,8},{18,... | collective-permute-start | bytes 442376 | tf_op jit(solution)/shard_map/ppermute | solution.py:58
  121.3 14.5 %collective-permute-start.41 = (bf16[48,1536]{1,0:T(8,128)(2,1)}, bf16[48,1536]{1,0:T(8,128)(2,1)}, u32[]{:S(2)}, u32[]{:S(2)}) collective-permute-start(bf16[48,1536]{1,0:T(8,128)(2,1)} %get-tuple-element.116), channel_id=1, source_target_pairs={{0,16},{2,18},{4,20},{6,22},{8,24},{10,26},{12,28},{14,30},{16,0},... | collective-permute-start | bytes 442376 | tf_op jit(solution)/shard_map/ppermute | solution.py:58
  122.8 13.0 %collective-permute-start.42 = (bf16[48,1536]{1,0:T(8,128)(2,1)}, bf16[48,1536]{1,0:T(8,128)(2,1)}, u32[]{:S(2)}, u32[]{:S(2)}) collective-permute-start(bf16[48,1536]{1,0:T(8,128)(2,1)} %get-tuple-element.117), channel_id=1, source_target_pairs={{0,8},{2,10},{4,12},{6,14},{8,16},{10,18},{12,20},{14,22},{16,24},... | collective-permute-start | bytes 442376 | tf_op jit(solution)/shard_map/ppermute | solution.py:58
  125.7 6.0 %copy-start = (bf16[768,768]{1,0:T(8,128)(2,1)S(1)}, bf16[768,768]{1,0:T(8,128)(2,1)}, u32[]{:S(2)}) copy-start(bf16[768,768]{1,0:T(8,128)(2,1)} %get-tuple-element.131.refs_4_) | copy-start | bytes 3538948
  125.7 6.0 %copy-start.6 = (bf16[256,768]{1,0:T(8,128)(2,1)S(1)}, bf16[256,768]{1,0:T(8,128)(2,1)}, u32[]{:S(2)}) copy-start(bf16[256,768]{1,0:T(8,128)(2,1)} %copy-done.5) | copy-start | bytes 1179652
  131.7 1.4 copy-start.1
  138.0 3.8 %collective-permute-start.43 = (f32[2,48]{1,0:T(2,128)}, f32[2,48]{1,0:T(2,128)S(1)}, u32[]{:S(2)}, u32[]{:S(2)}) collective-permute-start(f32[2,48]{1,0:T(2,128)} %get-tuple-element.119), channel_id=1, source_target_pairs={{0,1},{1,0},{2,3},{3,2},{4,5},{5,4},{6,7},{7,6},{8,9},{9,8},{10,11... | collective-permute-start | bytes 1160 | tf_op jit(solution)/shard_map/ppermute | solution.py:62
  (1 other events, 0.7 us)

commit v6 on v5

--- a/solution.py
+++ b/solution.py
@@ -273,24 +273,27 @@
     return run(body, [full(*parts[0].shape)], parts, limit=SMALL, weight=WEIGHT)[0]
 
 
-def finish_feed_forward(total, weights, gains, hidden):
+def gain_columns(total, weights, gains):
+    rows, room = total.shape[0], weights.shape[1]
+
+    def body(total_ref, weights_ref, gains_ref, columns_ref):
+        share = jnp.sum(wide(weights_ref[...]) * total_ref[:, :room], axis=1, keepdims=True)
+        lane = lax.broadcasted_iota(jnp.int32, (rows, 2), 1)
+        columns_ref[...] = jnp.where(lane == 0, gains_ref[:, 1:], share / gains_ref[:, :1])
+
+    return run(body, [full(rows, 2)], [total, weights, gains], limit=SMALL)[0]
+
+
+def finish_feed_forward(total, gains, hidden):
     rows, room = total.shape[0], total.shape[1] // 3
 
-    def body(total_ref, weights_ref, gains_ref, sum_ref, down_ref, columns_ref):
+    def body(total_ref, gains_ref, sum_ref, down_ref):
         gain = gains_ref[:, :1]
         down_ref[...] = total_ref[:, 2 * room : 2 * room + hidden]
         sum_ref[:, 0, :] = total_ref[:, :hidden] * gain
         sum_ref[:, 1, :] = total_ref[:, room : room + hidden] * gain
-        share = jnp.sum(wide(weights_ref[...]) * total_ref[:, : 2 * room], axis=1, keepdims=True) / gain
-        lane = lax.broadcasted_iota(jnp.int32, (rows, 2), 1)
-        columns_ref[...] = jnp.where(lane == 0, gains_ref[:, 1:], share)
-
-    return run(
-        body,
-        [full(rows, 2, hidden), full(rows, hidden), full(rows, 2)],
-        [total, weights, gains],
-        last=True,
-    )
+
+    return run(body, [full(rows, 2, hidden), full(rows, hidden)], [total, gains], last=True)
 
 
 def finish_attention(parts, query_keys, values_out, columns):
@@ -509,12 +512,11 @@
     tiles = list(tiles_of(count, inner))
 
     def body(upstream_ref, middle_ref, own_ref, other_ref, a, b, c, d, context_ref, shares_ref,
-             grad_middle_ref, branch_ref, grad_context_ref, grad_values_ref, total_ref):
+             branch_ref, grad_context_ref, grad_values_ref, total_ref):
         matrix = rows_of((a, b, c, d))
         normed, inverse = normalize(middle_ref[...])
         scaled = wide(own_ref[...]) + wide(other_ref[...])
         grad_middle = wide(upstream_ref[...]) + norm_back(scaled, normed, inverse)
-        grad_middle_ref[...] = grad_middle
         branch_ref[...] = low(grad_middle)
         grad_context_ref[...] = low(product(branch_ref[...], matrix))
         total_ref[...] = jnp.zeros_like(total_ref)
@@ -525,7 +527,7 @@
 
     return run(
         body,
-        [full(count, width), half(count, width), half(count, inner), half(count, inner)],
+        [half(count, width), half(count, inner), half(count, inner)],
         [upstream, middle, own, other, *pieces, context, shares],
         [None] * 4 + [spec((width // PIECES, inner), 0, 1)] * PIECES + [None] * 2,
         scratch=[pltpu.VMEM((count, inner), jnp.float32)],
@@ -593,21 +595,19 @@
     )
 
 
-def input_grads(grad_middle, inputs, own, other, order):
+def input_grads(branch, inputs, own, other, order):
     count, width = inputs.shape
 
-    def body(grad_middle_ref, inputs_ref, own_ref, other_ref, order_ref, out_ref):
+    def body(branch_ref, inputs_ref, own_ref, other_ref, order_ref, out_ref):
         normed, inverse = normalize(wide(inputs_ref[...]))
         scaled = wide(own_ref[...]) + wide(other_ref[...])
-        total = grad_middle_ref[...] + norm_back(scaled, normed, inverse)
-        high = low(total)
-        rest = low(total - wide(high))
-        out_ref[...] = product(high, order_ref[...]) + product(rest, order_ref[...])
+        total = wide(branch_ref[...]) + norm_back(scaled, normed, inverse)
+        out_ref[...] = product(low(total), order_ref[...])
 
     return run(
         body,
         [full(count, width)],
-        [grad_middle, inputs, own, other, order],
+        [branch, inputs, own, other, order],
         last=True,
     )[0]
 
@@ -646,7 +646,7 @@
     held = query_keys.stack()
     values_out = Gather(after(shard_two, held), devices)
     inputs, normed_one = prepare(tokens, order)
-    wait_for(query_keys.other)
+    wait_for(query_keys.other, query_keys.pieces[2])
     held = values_out.stack()
     gates_in = Gather(after(shard_three, held), devices, tail=True)
     wait_for(cosine, sine, column)
@@ -657,6 +657,8 @@
     down.begin(held)
     values, context, own = attend_values(normed_one, values_out.pieces, shares)
     other = swapped(own)
+    gains = jnp.concatenate([gain_two, gain_one], axis=1)
+
     upstream = reorder(cotangent, order)
     down.stack()
     gates_in.share(gates_in.other)
@@ -670,7 +672,7 @@
     sums_mlp.second()
     early = own_out.shape[0] // EARLY
     upper_out = swapped(own_out[:early])
-    grad_middle, branch, grad_context, grad_values = attend_back_values(
+    branch, grad_context, grad_values = attend_back_values(
         upstream, middle, own_two, other_two, values_out.pieces, context, shares
     )
     grad_query_keys, own_one = attend_back_shares(
@@ -684,17 +686,15 @@
     sums = Scatter([kept], [sent], devices, rows)
     sums_mlp.third()
     sums.second()
-    wait_for(other_one)
     sum_mlp = add_all(sums_mlp.parts)
     sums.third()
     lower_out = swapped(after(own_out[early:], sums.begun))
-    sum_in, sum_down, columns = finish_feed_forward(
-        sum_mlp, shard_three, jnp.concatenate([gain_two, gain_one], axis=1), hidden
-    )
-    grad_input = input_grads(grad_middle, inputs, own_one, other_one, back)
+    columns = gain_columns(sum_mlp, shard_three, gains)
+    grad_input = input_grads(branch, inputs, own_one, other_one, back)
     output = add_output(middle, own_out, (upper_out, lower_out), back)
     sum_qkv, sum_out, share = finish_attention(sums.parts, shard_one, shard_two, columns)
-    gains = after(share, output) + swapped(share)
+    sum_in, sum_down = finish_feed_forward(sum_mlp, gains, hidden)
+    gains = after(share, sum_down) + swapped(share)
     sum_qkv = jnp.transpose(sum_qkv, (1, 0, 2))
     return (output, grad_input, gains[0], sum_qkv, sum_out.T, gains[1], sum_in, sum_down.T)
 

time: 143 us -> 141 us (0.986)
  waiting for transfers between devices: 45.7 us -> 41.8 us
  starting transfers between devices: 46.6 us -> 49.7 us
  local copies, waits for them, and re-layouts: 8.55 us -> 5.97 us
    ppermute x6, waiting for transfers between devices: 16.6 us -> 14.1 us  [swapped(): return lax.ppermute(values, 'tensor', [(0, 1), (1, 0)])]
    unnamed x42 -> x40, local copies, waits for them, and re-layouts: 5.2 us -> 3.23 us
    ppermute x6, starting transfers between devices: 6.33 us -> 8.1 us  [swapped(): return lax.ppermute(values, 'tensor', [(0, 1), (1, 0)])]
    ppermute x38, waiting for transfers between devices: 29.1 us -> 27.7 us  [shifted(): return lax.ppermute(values, 'dp', pairs)]
    pallas_call x24 -> x25, Pallas kernels: 36.1 us -> 37 us  [run(): pl.pallas_call(ordered, out_shape=out_shapes, grid=grid, in_specs=specs +...]
  transfers between devices with their start and end apart: 44 -> 44, of which waited for: 13 -> 16; matrix products, arithmetic and copies ran while one was open for 4% -> 3% of each run, Pallas kernels for 18% -> 20%
where the time goes in v6:
time: 141 us; the launch traced here: 140 us
  starting transfers between devices  49.7 us (35%)
  waiting for transfers between devices  41.8 us (30%)
  Pallas kernels  37 us (26%)
  local copies, waits for them, and re-layouts  5.97 us (4%)
  other arithmetic  4.71 us (3%)
    ppermute x38, starting transfers between devices, shifted(): return lax.ppermute(values, 'dp', pairs)  41.6 us
    pallas_call x25, Pallas kernels, run(): pl.pallas_call(ordered, out_shape=out_shapes, grid=grid, in_specs=specs +...  37 us
    ppermute x38, waiting for transfers between devices, shifted(): return lax.ppermute(values, 'dp', pairs)  27.7 us
    ppermute x6, waiting for transfers between devices, swapped(): return lax.ppermute(values, 'tensor', [(0, 1), (1, 0)])  14.1 us
    ppermute x6, starting transfers between devices, swapped(): return lax.ppermute(values, 'tensor', [(0, 1), (1, 0)])  8.1 us
    unnamed x40, local copies, waits for them, and re-layouts  3.23 us
  transfers between devices with their start and end apart: 44, of which 16 were waited for; matrix products, arithmetic and copies ran while one was open for 3% of the time, Pallas kernels for 20%

profile of v6, /device:TPU:0, one launch (start us, length us, event | category | flops | bytes accessed | tf_op | source)
XLA Modules:
  0.0 140.3 jit_solution(14304935354556369504)
XLA Ops:
  0.6 0.7 convert_bitcast_fusion
  1.3 0.9 fusion.8
  2.2 3.1 %collective-permute-start = (bf16[48,768]{1,0:T(8,128)(2,1)S(1)}, bf16[48,768]{1,0:T(8,128)(2,1)S(1)}, u32[]{:S(2)}, u32[]{:S(2)}) collective-permute-start(bf16[48,768]{1,0:T(8,128)(2,1)S(1)} %pad_maximum_fusion.refs_0_.refs_4_), channel_id=1, source_target_pairs={{0,8},{2,10},{4,12},{6,14},{8,16},{10,18},{12,20},{14,22},{16,24},... | collective-permute-start | bytes 221192 | tf_op jit(solution)/shard_map/ppermute | solution.py:58
  5.3 2.6 %collective-permute-start.1 = (bf16[48,768]{1,0:T(8,128)(2,1)S(1)}, bf16[48,768]{1,0:T(8,128)(2,1)S(1)}, u32[]{:S(2)}, u32[]{:S(2)}) collective-permute-start(bf16[48,768]{1,0:T(8,128)(2,1)S(1)} %pad_maximum_fusion.refs_0_.refs_4_), channel_id=1, source_target_pairs={{0,16},{2,18},{4,20},{6,22},{8,24},{10,26},{12,28},{14,30},{16,0},... | collective-permute-start | bytes 221192 | tf_op jit(solution)/shard_map/ppermute | solution.py:58
  7.9 1.3 collective-permute-start.2
  9.4 1.3 fusion.1
  11.0 1.8 %collective-permute-done.1.refs_2_ = bf16[48,768]{1,0:T(8,128)(2,1)S(1)} collective-permute-done((bf16[48,768]{1,0:T(8,128)(2,1)S(1)}, bf16[48,768]{1,0:T(8,128)(2,1)S(1)}, u32[]{:S(2)}, u32[]{:S(2)}) %collective-permute-start.1) | collective-permute-done | bytes 73760 | tf_op jit(solution)/shard_map/ppermute | solution.py:58
  13.1 1.6 %collective-permute-start.6 = (bf16[192,768]{1,0:T(8,128)(2,1)S(1)}, bf16[192,768]{1,0:T(8,128)(2,1)S(1)}, u32[]{:S(2)}, u32[]{:S(2)}) collective-permute-start(bf16[192,768]{1,0:T(8,128)(2,1)S(1)} %shard_map.161.refs_2_.refs_1_.refs_8_), channel_id=1, source_target_pairs={{0,4},{2,6},{4,0},{6,2},{8,12},{10,14},{12,8},{14,10},{16,20},{18,... | collective-permute-start | bytes 884744 | tf_op jit(solution)/shard_map/ppermute | solution.py:58
  14.7 1.9 %collective-permute-start.3 = (bf16[48,768]{1,0:T(8,128)(2,1)S(1)}, bf16[48,768]{1,0:T(8,128)(2,1)S(1)}, u32[]{:S(2)}, u32[]{:S(2)}) collective-permute-start(bf16[48,768]{1,0:T(8,128)(2,1)S(1)} %pad_maximum_fusion.1.refs_0_.refs_5_), channel_id=1, source_target_pairs={{0,8},{2,10},{4,12},{6,14},{8,16},{10,18},{12,20},{14,22},{16,24},... | collective-permute-start | bytes 221192 | tf_op jit(solution)/shard_map/ppermute | solution.py:58
  16.6 1.9 %collective-permute-start.4 = (bf16[48,768]{1,0:T(8,128)(2,1)S(1)}, bf16[48,768]{1,0:T(8,128)(2,1)S(1)}, u32[]{:S(2)}, u32[]{:S(2)}) collective-permute-start(bf16[48,768]{1,0:T(8,128)(2,1)S(1)} %pad_maximum_fusion.1.refs_0_.refs_5_), channel_id=1, source_target_pairs={{0,16},{2,18},{4,20},{6,22},{8,24},{10,26},{12,28},{14,30},{16,0},... | collective-permute-start | bytes 221192 | tf_op jit(solution)/shard_map/ppermute | solution.py:58
  18.5 0.7 collective-permute-start.5
  19.5 0.8 pad.10.refs_0_
  20.3 1.1 shard_map.162
  21.8 1.3 collective-permute-start.12
  23.1 1.4 collective-permute-done.4.refs_2_
  24.5 0.9 shard_map.163.refs_2_.refs_1_.refs_4_.refs_12_
  25.4 0.6 collective-permute-start.8
  26.0 2.2 %collective-permute-start.13 = (bf16[48,1280]{1,0:T(8,128)(2,1)S(1)}, bf16[48,1280]{1,0:T(8,128)(2,1)S(1)}, u32[]{:S(2)}, u32[]{:S(2)}) collective-permute-start(bf16[48,1280]{1,0:T(8,128)(2,1)S(1)} %fusion.5.refs_0_.refs_1_), channel_id=1, source_target_pairs={{0,8},{2,10},{4,12},{6,14},{8,16},{10,18},{12,20},{14,22},{16,24},... | collective-permute-start | bytes 368648 | tf_op jit(solution)/shard_map/ppermute | solution.py:58
  28.2 1.0 collective-permute-start.14
  29.1 1.4 %collective-permute-start.15 = (bf16[48,1280]{1,0:T(8,128)(2,1)S(1)}, bf16[48,1280]{1,0:T(8,128)(2,1)S(1)}, u32[]{:S(2)}, u32[]{:S(2)}) collective-permute-start(bf16[48,1280]{1,0:T(8,128)(2,1)S(1)} %fusion.5.refs_0_.refs_1_), channel_id=1, source_target_pairs={{0,24},{2,26},{4,28},{6,30},{8,0},{10,2},{12,4},{14,6},{16,8},{18,... | collective-permute-start | bytes 368648 | tf_op jit(solution)/shard_map/ppermute | solution.py:58
  30.5 1.0 fusion.2
  31.6 2.8 %collective-permute-done.8.refs_5_.refs_2_.refs_13_ = bf16[192,768]{1,0:T(8,128)(2,1)S(1)} collective-permute-done((bf16[192,768]{1,0:T(8,128)(2,1)S(1)}, bf16[192,768]{1,0:T(8,128)(2,1)S(1)}, u32[]{:S(2)}, u32[]{:S(2)}) %collective-permute-start.8) | collective-permute-done | bytes 294944 | tf_op jit(solution)/shard_map/ppermute | solution.py:58
  34.9 2.7 %shard_map.165 = (bf16[512,384]{1,0:T(8,128)(2,1)S(1)}, bf16[512,384]{1,0:T(8,128)(2,1)S(1)}, bf16[12,256,256]{2,1,0:T(8,128)(2,1)S(1)}) custom-call(bf16[512,768]{1,0:T(8,128)(2,1)S(1)} %get-tuple-element.65.refs_0_.refs_2_, bf16[192,768]{1,0:T(8,128)(2,1)S(1)} %shard_map.161.refs_2_.refs_1_.refs_8_, ...), custom_call_target="tpu_custom_call" | custom-call | tf_op jit(solution)/shard_map/pallas_call | solution.py:193
  38.2 1.7 %shard_map.167 = (bf16[512,384]{1,0:T(8,128)(2,1)S(1)}, bf16[512,384]{1,0:T(8,128)(2,1)S(1)}, bf16[512,768]{1,0:T(8,128)(2,1)S(1)}) custom-call(bf16[512,768]{1,0:T(8,128)(2,1)S(1)} %get-tuple-element.65.refs_0_.refs_2_, bf16[192,768]{1,0:T(8,128)(2,1)S(1)} %shard_map.163.refs_2_.refs_1_.refs_4_.refs_12_, ...), custom_call_target="tpu_custom_call" | custom-call | tf_op jit(solution)/shard_map/pallas_call | solution.py:193
  39.9 1.5 %collective-permute-start.16 = (bf16[512,768]{1,0:T(8,128)(2,1)S(1)}, bf16[512,768]{1,0:T(8,128)(2,1)S(1)}, u32[]{:S(2)}, u32[]{:S(2)}) collective-permute-start(bf16[512,768]{1,0:T(8,128)(2,1)S(1)} %get-tuple-element.70.refs_1_), channel_id=1, source_target_pairs={{0,1},{1,0},{2,3},{3,2},{4,5},{5,4},{6,7},{7,6},{8,9},{9,8},{10,11... | collective-permute-start | bytes 2359304 | tf_op jit(solution)/shard_map/ppermute | solution.py:62
  41.4 1.5 %collective-permute-start.20 = (bf16[192,1280]{1,0:T(8,128)(2,1)S(1)}, bf16[192,1280]{1,0:T(8,128)(2,1)S(1)}, u32[]{:S(2)}, u32[]{:S(2)}) collective-permute-start(bf16[192,1280]{1,0:T(8,128)(2,1)S(1)} %shard_map.166.refs_6_.refs_2_), channel_id=1, source_target_pairs={{0,4},{2,6},{4,0},{6,2},{8,12},{10,14},{12,8},{14,10},{16,20},{18,... | collective-permute-start | bytes 1474568 | tf_op jit(solution)/shard_map/ppermute | solution.py:58
  42.9 3.1 %collective-permute-start.17 = (bf16[96,640]{1,0:T(8,128)(2,1)S(1)}, bf16[96,640]{1,0:T(8,128)(2,1)S(1)}, u32[]{:S(2)}, u32[]{:S(2)}) collective-permute-start(bf16[96,640]{1,0:T(8,128)(2,1)S(1)} %shard_map.164.refs_9_.refs_0_), channel_id=1, source_target_pairs={{0,8},{2,10},{4,12},{6,14},{8,16},{10,18},{12,20},{14,22},{16,24},... | collective-permute-start | bytes 368648 | tf_op jit(solution)/shard_map/ppermute | solution.py:58
  46.0 1.1 collective-permute-start.18
  47.1 1.3 collective-permute-start.19
  48.4 0.8 shard_map.168.refs_4_.refs_1_.refs_3_.refs_0_
  49.2 1.7 %collective-permute-done.17.refs_1_ = bf16[96,640]{1,0:T(8,128)(2,1)S(1)} collective-permute-done((bf16[96,640]{1,0:T(8,128)(2,1)S(1)}, bf16[96,640]{1,0:T(8,128)(2,1)S(1)}, u32[]{:S(2)}, u32[]{:S(2)}) %collective-permute-start.17) | collective-permute-done | bytes 122912 | tf_op jit(solution)/shard_map/ppermute | solution.py:58
  50.9 4.1 %collective-permute-done.18.refs_2_ = bf16[96,640]{1,0:T(8,128)(2,1)S(1)} collective-permute-done((bf16[96,640]{1,0:T(8,128)(2,1)S(1)}, bf16[96,640]{1,0:T(8,128)(2,1)S(1)}, u32[]{:S(2)}, u32[]{:S(2)}) %collective-permute-start.18) | collective-permute-done | bytes 122912 | tf_op jit(solution)/shard_map/ppermute | solution.py:58
  56.1 3.2 %collective-permute-done.16.refs_2_ = bf16[512,768]{1,0:T(8,128)(2,1)S(1)} collective-permute-done((bf16[512,768]{1,0:T(8,128)(2,1)S(1)}, bf16[512,768]{1,0:T(8,128)(2,1)S(1)}, u32[]{:S(2)}, u32[]{:S(2)}) %collective-permute-start.16) | collective-permute-done | bytes 786464 | tf_op jit(solution)/shard_map/ppermute | solution.py:62
  59.3 0.6 shard_map.170
  59.9 4.0 %shard_map.171 = (bf16[512,640]{1,0:T(8,128)(2,1)S(1)}, bf16[512,1280]{1,0:T(8,128)(2,1)S(1)}, bf16[512,768]{1,0:T(8,128)(2,1)S(1)}, bf16[512,768]{1,0:T(8,128)(2,1)S(1)}) custom-call(bf16[512,768]{1,0:T(8,128)(2,1)S(1)} %get-tuple-element.75.refs_0_, bf16[512,768]{1,0:T(8,128)(2,1)S(1)} %shard_map.168.refs_4_.refs_1_.refs_3_.refs_0_, ...), custom_call_target="tpu_custom_call" | custom-call | tf_op jit(solution)/shard_map/pallas_call | solution.py:193
  64.0 1.5 %collective-permute-start.26 = (bf16[512,768]{1,0:T(8,128)(2,1)S(1)}, bf16[512,768]{1,0:T(8,128)(2,1)S(1)}, u32[]{:S(2)}, u32[]{:S(2)}) collective-permute-start(bf16[512,768]{1,0:T(8,128)(2,1)S(1)} %get-tuple-element.80.refs_2_), channel_id=1, source_target_pairs={{0,1},{1,0},{2,3},{3,2},{4,5},{5,4},{6,7},{7,6},{8,9},{9,8},{10,11... | collective-permute-start | bytes 2359304 | tf_op jit(solution)/shard_map/ppermute | solution.py:62
  65.5 1.8 %shard_map.172 = (bf16[384,640]{1,0:T(8,128)(2,1)S(1)}, bf16[384,640]{1,0:T(8,128)(2,1)S(1)}, bf16[384,640]{1,0:T(8,128)(2,1)S(1)}, bf16[384,640]{1,0:T(8,128)(2...) custom-call(bf16[512,768]{1,0:T(8,128)(2,1)S(1)} %get-tuple-element.75.refs_0_, ...), custom_call_target="tpu_custom_call" | custom-call | tf_op jit(solution)/shard_map/pallas_call | solution.py:193
  68.0 0.8 fusion.27
  69.3 0.6 collective-permute-done.28.refs_4_
  70.0 0.7 collective-permute-done.29.refs_5_
  71.0 1.6 %collective-permute-start.30 = (bf16[192,640]{1,0:T(8,128)(2,1)S(1)}, bf16[192,640]{1,0:T(8,128)(2,1)S(1)}, u32[]{:S(2)}, u32[]{:S(2)}) collective-permute-start(bf16[192,640]{1,0:T(8,128)(2,1)S(1)} %get-tuple-element.95), channel_id=1, source_target_pairs={{0,4},{2,6},{4,0},{6,2},{8,12},{10,14},{12,8},{14,10},{16,20},{18,... | collective-permute-start | bytes 737288 | tf_op jit(solution)/shard_map/ppermute | solution.py:58
  73.1 1.5 %collective-permute-start.32 = (bf16[192,640]{1,0:T(8,128)(2,1)S(1)}, bf16[192,640]{1,0:T(8,128)(2,1)S(1)}, u32[]{:S(2)}, u32[]{:S(2)}) collective-permute-start(bf16[192,640]{1,0:T(8,128)(2,1)S(1)} %get-tuple-element.97), channel_id=1, source_target_pairs={{0,4},{2,6},{4,0},{6,2},{8,12},{10,14},{12,8},{14,10},{16,20},{18,... | collective-permute-start | bytes 737288 | tf_op jit(solution)/shard_map/ppermute | solution.py:58
  74.6 9.9 %collective-permute-done.26.refs_3_ = bf16[512,768]{1,0:T(8,128)(2,1)S(1)} collective-permute-done((bf16[512,768]{1,0:T(8,128)(2,1)S(1)}, bf16[512,768]{1,0:T(8,128)(2,1)S(1)}, u32[]{:S(2)}, u32[]{:S(2)}) %collective-permute-start.26) | collective-permute-done | bytes 786464 | tf_op jit(solution)/shard_map/ppermute | solution.py:62
  84.5 2.0 %shard_map.174 = (bf16[512,768]{1,0:T(8,128)(2,1)S(1)}, bf16[512,384]{1,0:T(8,128)(2,1)S(1)}, bf16[512,384]{1,0:T(8,128)(2,1)S(1)}) custom-call(bf16[512,768]{1,0:T(8,128)(2,1)S(1)} %shard_map.168.refs_4_.refs_1_.refs_3_.refs_0_, f32[512,768]{1,0:T(8,128)S(1)} %get-tuple-element.74.refs_10_.refs_1_.refs_0_, bf16[512,768]{1,0:T(8,128)(2,1)S(1)} %get-tuple-element.80.refs_2_, ...), custom_call_target="tpu_custom_call" | custom-call | tf_op jit(solution)/shard_map/pallas_call | solution.py:193
  86.5 6.0 %shard_map.175 = (bf16[512,768]{1,0:T(8,128)(2,1)S(1)}, bf16[512,768]{1,0:T(8,128)(2,1)}) custom-call(bf16[512,384]{1,0:T(8,128)(2,1)S(1)} %get-tuple-element.69.refs_4_.refs_0_, bf16[512,384]{1,0:T(8,128)(2,1)S(1)} %get-tuple-element.79.refs_1_, bf16[512,384]{1,0:T(8,128)(2,1)S(1)} %get-tuple-element.72.refs_2_, ...), custom_call_target="tpu_custom_call" | custom-call | tf_op jit(solution)/shard_map/pallas_call | solution.py:193
  92.6 1.6 %shard_map.176 = (bf16[384,1536]{1,0:T(8,128)(2,1)S(1)}, bf16[384,1536]{1,0:T(8,128)(2,1)S(1)}) custom-call(bf16[512,768]{1,0:T(8,128)(2,1)S(1)} %get-tuple-element.65.refs_0_.refs_2_, bf16[512,768]{1,0:T(8,128)(2,1)S(1)} %get-tuple-element.93.refs_1_.refs_6_, bf16[512,768]{1,0:T(8,128)(2,1)S(1)} %get-tuple-element.65.refs_0_.refs_2_, ...), custom_call_target="tpu_custom_call" | custom-call | tf_op jit(solution)/shard_map/pallas_call | solution.py:193
  94.5 2.9 %collective-permute-start.35 = (bf16[48,1920]{1,0:T(8,128)(2,1)S(1)}, bf16[48,1920]{1,0:T(8,128)(2,1)S(1)}, u32[]{:S(2)}, u32[]{:S(2)}) collective-permute-start(bf16[48,1920]{1,0:T(8,128)(2,1)S(1)} %get-tuple-element.105), channel_id=1, source_target_pairs={{0,24},{2,26},{4,28},{6,30},{8,0},{10,2},{12,4},{14,6},{16,8},{18,... | collective-permute-start | bytes 552968 | tf_op jit(solution)/shard_map/ppermute | solution.py:58
  97.3 1.8 %collective-permute-start.36 = (bf16[48,1920]{1,0:T(8,128)(2,1)S(1)}, bf16[48,1920]{1,0:T(8,128)(2,1)S(1)}, u32[]{:S(2)}, u32[]{:S(2)}) collective-permute-start(bf16[48,1920]{1,0:T(8,128)(2,1)S(1)} %get-tuple-element.106), channel_id=1, source_target_pairs={{0,16},{2,18},{4,20},{6,22},{8,24},{10,26},{12,28},{14,30},{16,0},... | collective-permute-start | bytes 552968 | tf_op jit(solution)/shard_map/ppermute | solution.py:58
  99.2 1.5 %collective-permute-start.39 = (bf16[512,768]{1,0:T(8,128)(2,1)}, bf16[512,768]{1,0:T(8,128)(2,1)}, u32[]{:S(2)}, u32[]{:S(2)}) collective-permute-start(bf16[512,768]{1,0:T(8,128)(2,1)} %get-tuple-element.110.refs_2_), channel_id=1, source_target_pairs={{0,1},{1,0},{2,3},{3,2},{4,5},{5,4},{6,7},{7,6},{8,9},{9,8},{10,11... | collective-permute-start | bytes 2359304 | tf_op jit(solution)/shard_map/ppermute | solution.py:62
  100.9 1.6 %collective-permute-start.34 = (bf16[192,1536]{1,0:T(8,128)(2,1)S(1)}, bf16[192,1536]{1,0:T(8,128)(2,1)S(1)}, u32[]{:S(2)}, u32[]{:S(2)}) collective-permute-start(bf16[192,1536]{1,0:T(8,128)(2,1)S(1)} %get-tuple-element.104), channel_id=1, source_target_pairs={{0,4},{2,6},{4,0},{6,2},{8,12},{10,14},{12,8},{14,10},{16,20},{18,... | collective-permute-start | bytes 1769480 | tf_op jit(solution)/shard_map/ppermute | solution.py:58
  103.0 13.0 %collective-permute-done.36.refs_2_ = bf16[48,1920]{1,0:T(8,128)(2,1)S(1)} collective-permute-done((bf16[48,1920]{1,0:T(8,128)(2,1)S(1)}, bf16[48,1920]{1,0:T(8,128)(2,1)S(1)}, u32[]{:S(2)}, u32[]{:S(2)}) %collective-permute-start.36) | collective-permute-done | bytes 184352 | tf_op jit(solution)/shard_map/ppermute | solution.py:58
  116.2 0.8 shard_map.180
  117.0 1.5 %collective-permute-start.38 = (bf16[256,768]{1,0:T(8,128)(2,1)}, bf16[256,768]{1,0:T(8,128)(2,1)}, u32[]{:S(2)}, u32[]{:S(2)}) collective-permute-start(bf16[256,768]{1,0:T(8,128)(2,1)} %get-tuple-element.109), channel_id=1, source_target_pairs={{0,1},{1,0},{2,3},{3,2},{4,5},{5,4},{6,7},{7,6},{8,9},{9,8},{10,11... | collective-permute-start | bytes 1179656 | tf_op jit(solution)/shard_map/ppermute | solution.py:62
  118.4 2.3 %collective-permute-start.40 = (bf16[48,1536]{1,0:T(8,128)(2,1)}, bf16[48,1536]{1,0:T(8,128)(2,1)}, u32[]{:S(2)}, u32[]{:S(2)}) collective-permute-start(bf16[48,1536]{1,0:T(8,128)(2,1)} %get-tuple-element.111), channel_id=1, source_target_pairs={{0,24},{2,26},{4,28},{6,30},{8,0},{10,2},{12,4},{14,6},{16,8},{18,... | collective-permute-start | bytes 442376 | tf_op jit(solution)/shard_map/ppermute | solution.py:58
  121.6 0.6 copy-done.14
  122.2 5.2 %shard_map.182.refs_5_ = f32[512,768]{1,0:T(8,128)} custom-call(bf16[512,768]{1,0:T(8,128)(2,1)} %copy-done.6, bf16[512,768]{1,0:T(8,128)(2,1)} %copy-done.5, bf16[512,768]{1,0:T(8,128)(2,1)} %get-tuple-element.110.refs_2_, bf16[512,768]{1,0:T(8,128)(2,1)} %collective-permute-done.39.refs_3_, bf16[768,768]{1,0:T(8,128)(2,1)} %get-tuple-element.127.refs_4_, ...), custom_call_target="tpu_custom_call" | custom-call | tf_op jit(solution)/shard_map/pallas_call | solution.py:193
  127.4 0.6 collective-permute-done.38.refs_3_
  128.0 1.4 %copy-done.1 = f32[512,768]{1,0:T(8,128)S(1)} copy-done((f32[512,768]{1,0:T(8,128)S(1)}, f32[512,768]{1,0:T(8,128)}, u32[]{:S(2)}) %copy-start.1) | copy-done | bytes 1572888
  129.4 1.1 copy-done.4
  130.6 2.7 %shard_map.183.refs_7_ = bf16[512,768]{1,0:T(8,128)(2,1)} custom-call(f32[512,768]{1,0:T(8,128)S(1)} %get-tuple-element.74.refs_10_.refs_1_.refs_0_, bf16[512,768]{1,0:T(8,128)(2,1)S(1)} %copy-done.4, bf16[256,768]{1,0:T(8,128)(2,1)S(1)} %collective-permute-done.25.refs_7_.refs_2_, bf16[256,768]{1,0:T(8,128)(2,1)} %collective-permute-done.38.refs_3_, ...), custom_call_target="tpu_custom_call" | custom-call | tf_op jit(solution)/shard_map/pallas_call | solution.py:193
  133.2 2.2 %shard_map.184 = (f32[3,48,384]{2,1,0:T(8,128)}, f32[48,384]{1,0:T(8,128)}, f32[2,48]{1,0:T(2,128)}) custom-call(bf16[48,1536]{1,0:T(8,128)(2,1)} %copy-done.11, bf16[48,1536]{1,0:T(8,128)(2,1)} %collective-permute-done.40.refs_1_, bf16[48,1536]{1,0:T(8,128)(2,1)} %collective-permute-done.41.refs_2_, bf16[48,1536]{1,0:T(8,128)(2,1)} %collective-permute-done.42.refs_3_, ...), custom_call_target="tpu_custom_call" | custom-call | tf_op jit(solution)/shard_map/pallas_call | solution.py:193
  135.4 1.5 %collective-permute-start.43 = (f32[2,48]{1,0:T(2,128)}, f32[2,48]{1,0:T(2,128)S(1)}, u32[]{:S(2)}, u32[]{:S(2)}) collective-permute-start(f32[2,48]{1,0:T(2,128)} %get-tuple-element.116.refs_2_), channel_id=1, source_target_pairs={{0,1},{1,0},{2,3},{3,2},{4,5},{5,4},{6,7},{7,6},{8,9},{9,8},{10,11... | collective-permute-start | bytes 1160 | tf_op jit(solution)/shard_map/ppermute | solution.py:62
  136.9 1.8 %shard_map.185 = (f32[48,2,576]{2,1,0:T(2,128)}, f32[48,576]{1,0:T(8,128)}) custom-call(f32[48,1920]{1,0:T(8,128)} %copy-done.2, f32[48,2]{1,0:T(8,128)} %copy-done.15, f32[2,48]{1,0:T(2,128)} %get-tuple-element.116.refs_2_), custom_call_target="tpu_custom_call" | custom-call | tf_op jit(solution)/shard_map/pallas_call | solution.py:193
  139.2 0.6 add.172
  (113 shorter events, 8.5 us)
Async XLA Ops:
  2.2 8.5 %copy-start.17 = (bf16[48,2,576]{2,1,0:T(2,128)(2,1)S(1)}, bf16[48,2,576]{2,1,0:T(2,128)(2,1)}, u32[]{:S(2)}) copy-start(bf16[48,2,576]{2,1,0:T(2,128)(2,1)} %param.17) | copy-start | bytes 331780
  2.2 10.9 %copy-start.9 = (bf16[48,768]{1,0:T(8,128)(2,1)}, bf16[48,768]{1,0:T(8,128)(2,1)S(1)}, u32[]{:S(2)}) copy-start(bf16[48,768]{1,0:T(8,128)(2,1)S(1)} %pad_maximum_fusion.refs_0_.refs_4_) | copy-start | bytes 221188
  2.2 8.8 %collective-permute-start = (bf16[48,768]{1,0:T(8,128)(2,1)S(1)}, bf16[48,768]{1,0:T(8,128)(2,1)S(1)}, u32[]{:S(2)}, u32[]{:S(2)}) collective-permute-start(bf16[48,768]{1,0:T(8,128)(2,1)S(1)} %pad_maximum_fusion.refs_0_.refs_4_), channel_id=1, source_target_pairs={{0,8},{2,10},{4,12},{6,14},{8,16},{10,18},{12,20},{14,22},{16,24},... | collective-permute-start | bytes 221192 | tf_op jit(solution)/shard_map/ppermute | solution.py:58
  5.3 7.5 %collective-permute-start.1 = (bf16[48,768]{1,0:T(8,128)(2,1)S(1)}, bf16[48,768]{1,0:T(8,128)(2,1)S(1)}, u32[]{:S(2)}, u32[]{:S(2)}) collective-permute-start(bf16[48,768]{1,0:T(8,128)(2,1)S(1)} %pad_maximum_fusion.refs_0_.refs_4_), channel_id=1, source_target_pairs={{0,16},{2,18},{4,20},{6,22},{8,24},{10,26},{12,28},{14,30},{16,0},... | collective-permute-start | bytes 221192 | tf_op jit(solution)/shard_map/ppermute | solution.py:58
  7.9 5.2 %collective-permute-start.2 = (bf16[48,768]{1,0:T(8,128)(2,1)S(1)}, bf16[48,768]{1,0:T(8,128)(2,1)S(1)}, u32[]{:S(2)}, u32[]{:S(2)}) collective-permute-start(bf16[48,768]{1,0:T(8,128)(2,1)S(1)} %pad_maximum_fusion.refs_0_.refs_4_), channel_id=1, source_target_pairs={{0,24},{2,26},{4,28},{6,30},{8,0},{10,2},{12,4},{14,6},{16,8},{18,... | collective-permute-start | bytes 221192 | tf_op jit(solution)/shard_map/ppermute | solution.py:58
  9.4 1.6 %copy-start.18 = (bf16[384,48]{0,1:T(8,128)(2,1)S(1)}, bf16[384,48]{0,1:T(8,128)(2,1)}, u32[]{:S(2)}) copy-start(bf16[384,48]{0,1:T(8,128)(2,1)} %param.15) | copy-start | bytes 110596
  10.7 8.6 %copy-start.19 = (s32[512]{0:T(512)S(1)}, s32[512]{0:T(512)}, u32[]{:S(2)}) copy-start(s32[512]{0:T(512)} %param.12) | copy-start | bytes 6148
  10.7 8.6 %copy-start.16 = (s32[512]{0:T(512)S(1)}, s32[512]{0:T(512)}, u32[]{:S(2)}) copy-start(s32[512]{0:T(512)} %param.11) | copy-start | bytes 6148
  10.7 9.6 %copy-start.7 = (bf16[512,768]{1,0:T(8,128)(2,1)S(1)}, bf16[512,768]{1,0:T(8,128)(2,1)}, u32[]{:S(2)}) copy-start(bf16[512,768]{1,0:T(8,128)(2,1)} %refs_0_.2) | copy-start | bytes 2359300
  11.0 13.5 %copy-start.10 = (bf16[48,768]{1,0:T(8,128)(2,1)}, bf16[48,768]{1,0:T(8,128)(2,1)S(1)}, u32[]{:S(2)}) copy-start(bf16[48,768]{1,0:T(8,128)(2,1)S(1)} %pad_maximum_fusion.1.refs_0_.refs_5_) | copy-start | bytes 221188
  13.1 8.7 %collective-permute-start.6 = (bf16[192,768]{1,0:T(8,128)(2,1)S(1)}, bf16[192,768]{1,0:T(8,128)(2,1)S(1)}, u32[]{:S(2)}, u32[]{:S(2)}) collective-permute-start(bf16[192,768]{1,0:T(8,128)(2,1)S(1)} %shard_map.161.refs_2_.refs_1_.refs_8_), channel_id=1, source_target_pairs={{0,4},{2,6},{4,0},{6,2},{8,12},{10,14},{12,8},{14,10},{16,20},{18,... | collective-permute-start | bytes 884744 | tf_op jit(solution)/shard_map/ppermute | solution.py:58
  14.7 9.8 %collective-permute-start.7 = (bf16[192,768]{1,0:T(8,128)(2,1)S(1)}, bf16[192,768]{1,0:T(8,128)(2,1)S(1)}, u32[]{:S(2)}, u32[]{:S(2)}) collective-permute-start(bf16[192,768]{1,0:T(8,128)(2,1)S(1)} %shard_map.161.refs_2_.refs_1_.refs_8_), channel_id=1, source_target_pairs={{0,2},{2,0},{4,6},{6,4},{8,10},{10,8},{12,14},{14,12},{16,18},{18,... | collective-permute-start | bytes 884744 | tf_op jit(solution)/shard_map/ppermute | solution.py:58
  14.7 23.4 %copy-start.12 = (bf16[48,1280]{1,0:T(8,128)(2,1)}, bf16[48,1280]{1,0:T(8,128)(2,1)S(1)}, u32[]{:S(2)}) copy-start(bf16[48,1280]{1,0:T(8,128)(2,1)S(1)} %fusion.5.refs_0_.refs_1_) | copy-start | bytes 368644
  14.7 8.4 %collective-permute-start.3 = (bf16[48,768]{1,0:T(8,128)(2,1)S(1)}, bf16[48,768]{1,0:T(8,128)(2,1)S(1)}, u32[]{:S(2)}, u32[]{:S(2)}) collective-permute-start(bf16[48,768]{1,0:T(8,128)(2,1)S(1)} %pad_maximum_fusion.1.refs_0_.refs_5_), channel_id=1, source_target_pairs={{0,8},{2,10},{4,12},{6,14},{8,16},{10,18},{12,20},{14,22},{16,24},... | collective-permute-start | bytes 221192 | tf_op jit(solution)/shard_map/ppermute | solution.py:58
  16.6 7.9 %collective-permute-start.4 = (bf16[48,768]{1,0:T(8,128)(2,1)S(1)}, bf16[48,768]{1,0:T(8,128)(2,1)S(1)}, u32[]{:S(2)}, u32[]{:S(2)}) collective-permute-start(bf16[48,768]{1,0:T(8,128)(2,1)S(1)} %pad_maximum_fusion.1.refs_0_.refs_5_), channel_id=1, source_target_pairs={{0,16},{2,18},{4,20},{6,22},{8,24},{10,26},{12,28},{14,30},{16,0},... | collective-permute-start | bytes 221192 | tf_op jit(solution)/shard_map/ppermute | solution.py:58
  18.5 6.0 %collective-permute-start.5 = (bf16[48,768]{1,0:T(8,128)(2,1)S(1)}, bf16[48,768]{1,0:T(8,128)(2,1)}, u32[]{:S(2)}, u32[]{:S(2)}) collective-permute-start(bf16[48,768]{1,0:T(8,128)(2,1)S(1)} %pad_maximum_fusion.1.refs_0_.refs_5_), channel_id=1, source_target_pairs={{0,24},{2,26},{4,28},{6,30},{8,0},{10,2},{12,4},{14,6},{16,8},{18,... | collective-permute-start | bytes 221192 | tf_op jit(solution)/shard_map/ppermute | solution.py:58
  21.4 37.9 %copy-start.5 = (bf16[512,768]{1,0:T(8,128)(2,1)}, bf16[512,768]{1,0:T(8,128)(2,1)S(1)}, u32[]{:S(2)}) copy-start(bf16[512,768]{1,0:T(8,128)(2,1)S(1)} %get-tuple-element.64.refs_4_.refs_0_.refs_1_) | copy-start | bytes 2359300
  21.8 7.3 %collective-permute-start.12 = (bf16[48,640]{1,0:T(8,128)(2,1)S(1)}, bf16[48,640]{1,0:T(8,128)(2,1)S(1)}, u32[]{:S(2)}, u32[]{:S(2)}) collective-permute-start(bf16[48,640]{1,0:T(8,128)(2,1)S(1)} %pad.10.refs_0_), channel_id=1, source_target_pairs={{0,4},{2,6},{4,0},{6,2},{8,12},{10,14},{12,8},{14,10},{16,20},{18,... | collective-permute-start | bytes 184328 | tf_op jit(solution)/shard_map/ppermute | solution.py:58
  23.1 11.2 %collective-permute-start.11 = (bf16[192,768]{1,0:T(8,128)(2,1)S(1)}, bf16[192,768]{1,0:T(8,128)(2,1)S(1)}, u32[]{:S(2)}, u32[]{:S(2)}) collective-permute-start(bf16[192,768]{1,0:T(8,128)(2,1)S(1)} %collective-permute-done.6.refs_5_.refs_2_.refs_9_), channel_id=1, source_target_pairs={{0,2},{2,0},{4,6},{6,4},{8,10},{10,8},{12,14},{14,12},{16,18},{18,... | collective-permute-start | bytes 884744 | tf_op jit(solution)/shard_map/ppermute | solution.py:58
  25.4 9.0 %collective-permute-start.8 = (bf16[192,768]{1,0:T(8,128)(2,1)S(1)}, bf16[192,768]{1,0:T(8,128)(2,1)S(1)}, u32[]{:S(2)}, u32[]{:S(2)}) collective-permute-start(bf16[192,768]{1,0:T(8,128)(2,1)S(1)} %shard_map.163.refs_2_.refs_1_.refs_4_.refs_12_), channel_id=1, source_target_pairs={{0,4},{2,6},{4,0},{6,2},{8,12},{10,14},{12,8},{14,10},{16,20},{18,... | collective-permute-start | bytes 884744 | tf_op jit(solution)/shard_map/ppermute | solution.py:58
  26.0 11.6 %collective-permute-start.13 = (bf16[48,1280]{1,0:T(8,128)(2,1)S(1)}, bf16[48,1280]{1,0:T(8,128)(2,1)S(1)}, u32[]{:S(2)}, u32[]{:S(2)}) collective-permute-start(bf16[48,1280]{1,0:T(8,128)(2,1)S(1)} %fusion.5.refs_0_.refs_1_), channel_id=1, source_target_pairs={{0,8},{2,10},{4,12},{6,14},{8,16},{10,18},{12,20},{14,22},{16,24},... | collective-permute-start | bytes 368648 | tf_op jit(solution)/shard_map/ppermute | solution.py:58
  28.2 9.9 %collective-permute-start.14 = (bf16[48,1280]{1,0:T(8,128)(2,1)S(1)}, bf16[48,1280]{1,0:T(8,128)(2,1)S(1)}, u32[]{:S(2)}, u32[]{:S(2)}) collective-permute-start(bf16[48,1280]{1,0:T(8,128)(2,1)S(1)} %fusion.5.refs_0_.refs_1_), channel_id=1, source_target_pairs={{0,16},{2,18},{4,20},{6,22},{8,24},{10,26},{12,28},{14,30},{16,0},... | collective-permute-start | bytes 368648 | tf_op jit(solution)/shard_map/ppermute | solution.py:58
  29.1 9.0 %collective-permute-start.15 = (bf16[48,1280]{1,0:T(8,128)(2,1)S(1)}, bf16[48,1280]{1,0:T(8,128)(2,1)S(1)}, u32[]{:S(2)}, u32[]{:S(2)}) collective-permute-start(bf16[48,1280]{1,0:T(8,128)(2,1)S(1)} %fusion.5.refs_0_.refs_1_), channel_id=1, source_target_pairs={{0,24},{2,26},{4,28},{6,30},{8,0},{10,2},{12,4},{14,6},{16,8},{18,... | collective-permute-start | bytes 368648 | tf_op jit(solution)/shard_map/ppermute | solution.py:58
  34.4 3.8 %collective-permute-start.9 = (bf16[192,768]{1,0:T(8,128)(2,1)S(1)}, bf16[192,768]{1,0:T(8,128)(2,1)S(1)}, u32[]{:S(2)}, u32[]{:S(2)}) collective-permute-start(bf16[192,768]{1,0:T(8,128)(2,1)S(1)} %shard_map.163.refs_2_.refs_1_.refs_4_.refs_12_), channel_id=1, source_target_pairs={{0,2},{2,0},{4,6},{6,4},{8,10},{10,8},{12,14},{14,12},{16,18},{18,... | collective-permute-start | bytes 884744 | tf_op jit(solution)/shard_map/ppermute | solution.py:58
  34.4 3.8 %collective-permute-start.10 = (bf16[192,768]{1,0:T(8,128)(2,1)S(1)}, bf16[192,768]{1,0:T(8,128)(2,1)S(1)}, u32[]{:S(2)}, u32[]{:S(2)}) collective-permute-start(bf16[192,768]{1,0:T(8,128)(2,1)S(1)} %collective-permute-done.8.refs_5_.refs_2_.refs_13_), channel_id=1, source_target_pairs={{0,2},{2,0},{4,6},{6,4},{8,10},{10,8},{12,14},{14,12},{16,18},{18,... | collective-permute-start | bytes 884744 | tf_op jit(solution)/shard_map/ppermute | solution.py:58
  38.1 10.2 %copy-start.8 = (bf16[512,768]{1,0:T(8,128)(2,1)S(1)}, bf16[512,768]{1,0:T(8,128)(2,1)}, u32[]{:S(2)}) copy-start(bf16[512,768]{1,0:T(8,128)(2,1)} %refs_0_.3) | copy-start | bytes 2359300
  39.9 19.4 %collective-permute-start.16 = (bf16[512,768]{1,0:T(8,128)(2,1)S(1)}, bf16[512,768]{1,0:T(8,128)(2,1)S(1)}, u32[]{:S(2)}, u32[]{:S(2)}) collective-permute-start(bf16[512,768]{1,0:T(8,128)(2,1)S(1)} %get-tuple-element.70.refs_1_), channel_id=1, source_target_pairs={{0,1},{1,0},{2,3},{3,2},{4,5},{5,4},{6,7},{7,6},{8,9},{9,8},{10,11... | collective-permute-start | bytes 2359304 | tf_op jit(solution)/shard_map/ppermute | solution.py:62
  41.4 14.2 %collective-permute-start.20 = (bf16[192,1280]{1,0:T(8,128)(2,1)S(1)}, bf16[192,1280]{1,0:T(8,128)(2,1)S(1)}, u32[]{:S(2)}, u32[]{:S(2)}) collective-permute-start(bf16[192,1280]{1,0:T(8,128)(2,1)S(1)} %shard_map.166.refs_6_.refs_2_), channel_id=1, source_target_pairs={{0,4},{2,6},{4,0},{6,2},{8,12},{10,14},{12,8},{14,10},{16,20},{18,... | collective-permute-start | bytes 1474568 | tf_op jit(solution)/shard_map/ppermute | solution.py:58
  42.9 8.0 %collective-permute-start.17 = (bf16[96,640]{1,0:T(8,128)(2,1)S(1)}, bf16[96,640]{1,0:T(8,128)(2,1)S(1)}, u32[]{:S(2)}, u32[]{:S(2)}) collective-permute-start(bf16[96,640]{1,0:T(8,128)(2,1)S(1)} %shard_map.164.refs_9_.refs_0_), channel_id=1, source_target_pairs={{0,8},{2,10},{4,12},{6,14},{8,16},{10,18},{12,20},{14,22},{16,24},... | collective-permute-start | bytes 368648 | tf_op jit(solution)/shard_map/ppermute | solution.py:58
  46.0 8.9 %collective-permute-start.18 = (bf16[96,640]{1,0:T(8,128)(2,1)S(1)}, bf16[96,640]{1,0:T(8,128)(2,1)S(1)}, u32[]{:S(2)}, u32[]{:S(2)}) collective-permute-start(bf16[96,640]{1,0:T(8,128)(2,1)S(1)} %shard_map.164.refs_9_.refs_0_), channel_id=1, source_target_pairs={{0,16},{2,18},{4,20},{6,22},{8,24},{10,26},{12,28},{14,30},{16,0},... | collective-permute-start | bytes 368648 | tf_op jit(solution)/shard_map/ppermute | solution.py:58
  47.1 7.9 %collective-permute-start.19 = (bf16[96,640]{1,0:T(8,128)(2,1)S(1)}, bf16[96,640]{1,0:T(8,128)(2,1)S(1)}, u32[]{:S(2)}, u32[]{:S(2)}) collective-permute-start(bf16[96,640]{1,0:T(8,128)(2,1)S(1)} %shard_map.164.refs_9_.refs_0_), channel_id=1, source_target_pairs={{0,24},{2,26},{4,28},{6,30},{8,0},{10,2},{12,4},{14,6},{16,8},{18,... | collective-permute-start | bytes 368648 | tf_op jit(solution)/shard_map/ppermute | solution.py:58
  55.0 4.9 %collective-permute-start.23 = (bf16[192,640]{1,0:T(8,128)(2,1)S(1)}, bf16[192,640]{1,0:T(8,128)(2,1)S(1)}, u32[]{:S(2)}, u32[]{:S(2)}) collective-permute-start(bf16[192,640]{1,0:T(8,128)(2,1)S(1)} %get-tuple-element.73.refs_3_.refs_6_), channel_id=1, source_target_pairs={{0,2},{2,0},{4,6},{6,4},{8,10},{10,8},{12,14},{14,12},{16,18},{18,... | collective-permute-start | bytes 737288 | tf_op jit(solution)/shard_map/ppermute | solution.py:58
  55.1 4.8 %collective-permute-start.24 = (bf16[192,640]{1,0:T(8,128)(2,1)S(1)}, bf16[192,640]{1,0:T(8,128)(2,1)S(1)}, u32[]{:S(2)}, u32[]{:S(2)}) collective-permute-start(bf16[192,640]{1,0:T(8,128)(2,1)S(1)} %get-tuple-element.77.refs_7_), channel_id=1, source_target_pairs={{0,2},{2,0},{4,6},{6,4},{8,10},{10,8},{12,14},{14,12},{16,18},{18,... | collective-permute-start | bytes 737288 | tf_op jit(solution)/shard_map/ppermute | solution.py:58
  55.6 4.3 %collective-permute-start.21 = (bf16[192,1280]{1,0:T(8,128)(2,1)S(1)}, bf16[192,1280]{1,0:T(8,128)(2,1)S(1)}, u32[]{:S(2)}, u32[]{:S(2)}) collective-permute-start(bf16[192,1280]{1,0:T(8,128)(2,1)S(1)} %shard_map.166.refs_6_.refs_2_), channel_id=1, source_target_pairs={{0,2},{2,0},{4,6},{6,4},{8,10},{10,8},{12,14},{14,12},{16,18},{18,... | collective-permute-start | bytes 1474568 | tf_op jit(solution)/shard_map/ppermute | solution.py:58
  55.7 4.3 %collective-permute-start.22 = (bf16[192,1280]{1,0:T(8,128)(2,1)S(1)}, bf16[192,1280]{1,0:T(8,128)(2,1)S(1)}, u32[]{:S(2)}, u32[]{:S(2)}) collective-permute-start(bf16[192,1280]{1,0:T(8,128)(2,1)S(1)} %collective-permute-done.20.refs_3_), channel_id=1, source_target_pairs={{0,2},{2,0},{4,6},{6,4},{8,10},{10,8},{12,14},{14,12},{16,18},{18,... | collective-permute-start | bytes 1474568 | tf_op jit(solution)/shard_map/ppermute | solution.py:58
  63.9 4.0 %copy-start.3 = (bf16[512,768]{1,0:T(8,128)(2,1)}, bf16[512,768]{1,0:T(8,128)(2,1)S(1)}, u32[]{:S(2)}) copy-start(bf16[512,768]{1,0:T(8,128)(2,1)S(1)} %get-tuple-element.78.refs_1_) | copy-start | bytes 2359300
  64.0 20.5 %collective-permute-start.26 = (bf16[512,768]{1,0:T(8,128)(2,1)S(1)}, bf16[512,768]{1,0:T(8,128)(2,1)S(1)}, u32[]{:S(2)}, u32[]{:S(2)}) collective-permute-start(bf16[512,768]{1,0:T(8,128)(2,1)S(1)} %get-tuple-element.80.refs_2_), channel_id=1, source_target_pairs={{0,1},{1,0},{2,3},{3,2},{4,5},{5,4},{6,7},{7,6},{8,9},{9,8},{10,11... | collective-permute-start | bytes 2359304 | tf_op jit(solution)/shard_map/ppermute | solution.py:62
  67.3 2.0 %collective-permute-start.27 = (bf16[384,640]{1,0:T(8,128)(2,1)S(1)}, bf16[384,640]{1,0:T(8,128)(2,1)S(1)}, u32[]{:S(2)}, u32[]{:S(2)}) collective-permute-start(bf16[384,640]{1,0:T(8,128)(2,1)S(1)} %get-tuple-element.87), channel_id=1, source_target_pairs={{0,2},{2,0},{4,6},{6,4},{8,10},{10,8},{12,14},{14,12},{16,18},{18,... | collective-permute-start | bytes 1474568 | tf_op jit(solution)/shard_map/ppermute | solution.py:58
  67.4 2.6 %collective-permute-start.28 = (bf16[384,640]{1,0:T(8,128)(2,1)S(1)}, bf16[384,640]{1,0:T(8,128)(2,1)S(1)}, u32[]{:S(2)}, u32[]{:S(2)}) collective-permute-start(bf16[384,640]{1,0:T(8,128)(2,1)S(1)} %get-tuple-element.88), channel_id=1, source_target_pairs={{0,2},{2,0},{4,6},{6,4},{8,10},{10,8},{12,14},{14,12},{16,18},{18,... | collective-permute-start | bytes 1474568 | tf_op jit(solution)/shard_map/ppermute | solution.py:58
  67.9 2.8 %collective-permute-start.29 = (bf16[384,640]{1,0:T(8,128)(2,1)S(1)}, bf16[384,640]{1,0:T(8,128)(2,1)S(1)}, u32[]{:S(2)}, u32[]{:S(2)}) collective-permute-start(bf16[384,640]{1,0:T(8,128)(2,1)S(1)} %get-tuple-element.89), channel_id=1, source_target_pairs={{0,2},{2,0},{4,6},{6,4},{8,10},{10,8},{12,14},{14,12},{16,18},{18,... | collective-permute-start | bytes 1474568 | tf_op jit(solution)/shard_map/ppermute | solution.py:58
  68.8 23.8 %collective-permute-start.25 = (bf16[256,768]{1,0:T(8,128)(2,1)S(1)}, bf16[256,768]{1,0:T(8,128)(2,1)S(1)}, u32[]{:S(2)}, u32[]{:S(2)}) collective-permute-start(bf16[256,768]{1,0:T(8,128)(2,1)S(1)} %get-tuple-element.121), channel_id=1, source_target_pairs={{0,1},{1,0},{2,3},{3,2},{4,5},{5,4},{6,7},{7,6},{8,9},{9,8},{10,11... | collective-permute-start | bytes 1179656 | tf_op jit(solution)/shard_map/ppermute | solution.py:62
  71.0 21.5 %collective-permute-start.30 = (bf16[192,640]{1,0:T(8,128)(2,1)S(1)}, bf16[192,640]{1,0:T(8,128)(2,1)S(1)}, u32[]{:S(2)}, u32[]{:S(2)}) collective-permute-start(bf16[192,640]{1,0:T(8,128)(2,1)S(1)} %get-tuple-element.95), channel_id=1, source_target_pairs={{0,4},{2,6},{4,0},{6,2},{8,12},{10,14},{12,8},{14,10},{16,20},{18,... | collective-permute-start | bytes 737288 | tf_op jit(solution)/shard_map/ppermute | solution.py:58
  72.6 19.9 %collective-permute-start.31 = (bf16[192,640]{1,0:T(8,128)(2,1)S(1)}, bf16[192,640]{1,0:T(8,128)(2,1)S(1)}, u32[]{:S(2)}, u32[]{:S(2)}) collective-permute-start(bf16[192,640]{1,0:T(8,128)(2,1)S(1)} %get-tuple-element.96), channel_id=1, source_target_pairs={{0,4},{2,6},{4,0},{6,2},{8,12},{10,14},{12,8},{14,10},{16,20},{18,... | collective-permute-start | bytes 737288 | tf_op jit(solution)/shard_map/ppermute | solution.py:58
  73.1 19.5 %collective-permute-start.32 = (bf16[192,640]{1,0:T(8,128)(2,1)S(1)}, bf16[192,640]{1,0:T(8,128)(2,1)S(1)}, u32[]{:S(2)}, u32[]{:S(2)}) collective-permute-start(bf16[192,640]{1,0:T(8,128)(2,1)S(1)} %get-tuple-element.97), channel_id=1, source_target_pairs={{0,4},{2,6},{4,0},{6,2},{8,12},{10,14},{12,8},{14,10},{16,20},{18,... | collective-permute-start | bytes 737288 | tf_op jit(solution)/shard_map/ppermute | solution.py:58
  86.5 6.1 %copy-start.6 = (bf16[512,768]{1,0:T(8,128)(2,1)}, bf16[512,768]{1,0:T(8,128)(2,1)S(1)}, u32[]{:S(2)}) copy-start(bf16[512,768]{1,0:T(8,128)(2,1)S(1)} %get-tuple-element.94.refs_4_.refs_0_) | copy-start | bytes 2359300
  94.2 6.5 %collective-permute-start.33 = (bf16[384,1536]{1,0:T(8,128)(2,1)S(1)}, bf16[384,1536]{1,0:T(8,128)(2,1)S(1)}, u32[]{:S(2)}, u32[]{:S(2)}) collective-permute-start(bf16[384,1536]{1,0:T(8,128)(2,1)S(1)} %get-tuple-element.99), channel_id=1, source_target_pairs={{0,2},{2,0},{4,6},{6,4},{8,10},{10,8},{12,14},{14,12},{16,18},{18,... | collective-permute-start | bytes 3538952 | tf_op jit(solution)/shard_map/ppermute | solution.py:58
  94.5 8.5 %collective-permute-start.35 = (bf16[48,1920]{1,0:T(8,128)(2,1)S(1)}, bf16[48,1920]{1,0:T(8,128)(2,1)S(1)}, u32[]{:S(2)}, u32[]{:S(2)}) collective-permute-start(bf16[48,1920]{1,0:T(8,128)(2,1)S(1)} %get-tuple-element.105), channel_id=1, source_target_pairs={{0,24},{2,26},{4,28},{6,30},{8,0},{10,2},{12,4},{14,6},{16,8},{18,... | collective-permute-start | bytes 552968 | tf_op jit(solution)/shard_map/ppermute | solution.py:58
  97.3 18.7 %collective-permute-start.36 = (bf16[48,1920]{1,0:T(8,128)(2,1)S(1)}, bf16[48,1920]{1,0:T(8,128)(2,1)S(1)}, u32[]{:S(2)}, u32[]{:S(2)}) collective-permute-start(bf16[48,1920]{1,0:T(8,128)(2,1)S(1)} %get-tuple-element.106), channel_id=1, source_target_pairs={{0,16},{2,18},{4,20},{6,22},{8,24},{10,26},{12,28},{14,30},{16,0},... | collective-permute-start | bytes 552968 | tf_op jit(solution)/shard_map/ppermute | solution.py:58
  99.2 16.9 %collective-permute-start.37 = (bf16[48,1920]{1,0:T(8,128)(2,1)S(1)}, bf16[48,1920]{1,0:T(8,128)(2,1)S(1)}, u32[]{:S(2)}, u32[]{:S(2)}) collective-permute-start(bf16[48,1920]{1,0:T(8,128)(2,1)S(1)} %get-tuple-element.107), channel_id=1, source_target_pairs={{0,8},{2,10},{4,12},{6,14},{8,16},{10,18},{12,20},{14,22},{16,24},... | collective-permute-start | bytes 552968 | tf_op jit(solution)/shard_map/ppermute | solution.py:58
  99.2 23.1 %collective-permute-start.39 = (bf16[512,768]{1,0:T(8,128)(2,1)}, bf16[512,768]{1,0:T(8,128)(2,1)}, u32[]{:S(2)}, u32[]{:S(2)}) collective-permute-start(bf16[512,768]{1,0:T(8,128)(2,1)} %get-tuple-element.110.refs_2_), channel_id=1, source_target_pairs={{0,1},{1,0},{2,3},{3,2},{4,5},{5,4},{6,7},{7,6},{8,9},{9,8},{10,11... | collective-permute-start | bytes 2359304 | tf_op jit(solution)/shard_map/ppermute | solution.py:62
  100.9 15.2 %collective-permute-start.34 = (bf16[192,1536]{1,0:T(8,128)(2,1)S(1)}, bf16[192,1536]{1,0:T(8,128)(2,1)S(1)}, u32[]{:S(2)}, u32[]{:S(2)}) collective-permute-start(bf16[192,1536]{1,0:T(8,128)(2,1)S(1)} %get-tuple-element.104), channel_id=1, source_target_pairs={{0,4},{2,6},{4,0},{6,2},{8,12},{10,14},{12,8},{14,10},{16,20},{18,... | collective-permute-start | bytes 1769480 | tf_op jit(solution)/shard_map/ppermute | solution.py:58
  116.1 11.3 %copy-start.2 = (f32[48,1920]{1,0:T(8,128)}, f32[48,1920]{1,0:T(8,128)S(1)}, u32[]{:S(2)}) copy-start(f32[48,1920]{1,0:T(8,128)S(1)} %shard_map.179.refs_2_.refs_0_) | copy-start | bytes 1105924
  116.1 5.3 %copy-start.13 = (bf16[48,1280]{1,0:T(8,128)(2,1)S(1)}, bf16[48,1280]{1,0:T(8,128)(2,1)}, u32[]{:S(2)}) copy-start(bf16[48,1280]{1,0:T(8,128)(2,1)} %copy-done.12) | copy-start | bytes 368644
  117.0 5.3 %copy-start.11 = (bf16[48,1536]{1,0:T(8,128)(2,1)}, bf16[48,1536]{1,0:T(8,128)(2,1)S(1)}, u32[]{:S(2)}) copy-start(bf16[48,1536]{1,0:T(8,128)(2,1)S(1)} %get-tuple-element.108.refs_3_.refs_0_) | copy-start | bytes 442372
  117.0 11.0 %collective-permute-start.38 = (bf16[256,768]{1,0:T(8,128)(2,1)}, bf16[256,768]{1,0:T(8,128)(2,1)}, u32[]{:S(2)}, u32[]{:S(2)}) collective-permute-start(bf16[256,768]{1,0:T(8,128)(2,1)} %get-tuple-element.109), channel_id=1, source_target_pairs={{0,1},{1,0},{2,3},{3,2},{4,5},{5,4},{6,7},{7,6},{8,9},{9,8},{10,11... | collective-permute-start | bytes 1179656 | tf_op jit(solution)/shard_map/ppermute | solution.py:62
  118.4 14.8 %collective-permute-start.40 = (bf16[48,1536]{1,0:T(8,128)(2,1)}, bf16[48,1536]{1,0:T(8,128)(2,1)}, u32[]{:S(2)}, u32[]{:S(2)}) collective-permute-start(bf16[48,1536]{1,0:T(8,128)(2,1)} %get-tuple-element.111), channel_id=1, source_target_pairs={{0,24},{2,26},{4,28},{6,30},{8,0},{10,2},{12,4},{14,6},{16,8},{18,... | collective-permute-start | bytes 442376 | tf_op jit(solution)/shard_map/ppermute | solution.py:58
  120.8 12.5 %collective-permute-start.41 = (bf16[48,1536]{1,0:T(8,128)(2,1)}, bf16[48,1536]{1,0:T(8,128)(2,1)}, u32[]{:S(2)}, u32[]{:S(2)}) collective-permute-start(bf16[48,1536]{1,0:T(8,128)(2,1)} %get-tuple-element.112), channel_id=1, source_target_pairs={{0,16},{2,18},{4,20},{6,22},{8,24},{10,26},{12,28},{14,30},{16,0},... | collective-permute-start | bytes 442376 | tf_op jit(solution)/shard_map/ppermute | solution.py:58
  120.8 12.5 %collective-permute-start.42 = (bf16[48,1536]{1,0:T(8,128)(2,1)}, bf16[48,1536]{1,0:T(8,128)(2,1)}, u32[]{:S(2)}, u32[]{:S(2)}) collective-permute-start(bf16[48,1536]{1,0:T(8,128)(2,1)} %get-tuple-element.113), channel_id=1, source_target_pairs={{0,8},{2,10},{4,12},{6,14},{8,16},{10,18},{12,20},{14,22},{16,24},... | collective-permute-start | bytes 442376 | tf_op jit(solution)/shard_map/ppermute | solution.py:58
  121.4 6.0 %copy-start.15 = (f32[48,2]{1,0:T(8,128)}, f32[48,2]{1,0:T(8,128)S(1)}, u32[]{:S(2)}) copy-start(f32[48,2]{1,0:T(8,128)S(1)} %copy.32.refs_2_.refs_1_) | copy-start | bytes 1156
  121.6 0.6 copy-start.14
  122.2 5.8 %copy-start = (bf16[768,768]{1,0:T(8,128)(2,1)S(1)}, bf16[768,768]{1,0:T(8,128)(2,1)}, u32[]{:S(2)}) copy-start(bf16[768,768]{1,0:T(8,128)(2,1)} %get-tuple-element.127.refs_4_) | copy-start | bytes 3538948
  128.0 1.4 %copy-start.1 = (f32[512,768]{1,0:T(8,128)S(1)}, f32[512,768]{1,0:T(8,128)}, u32[]{:S(2)}) copy-start(f32[512,768]{1,0:T(8,128)} %shard_map.182.refs_5_) | copy-start | bytes 4718596
  129.4 1.1 copy-start.4
  135.4 3.8 %collective-permute-start.43 = (f32[2,48]{1,0:T(2,128)}, f32[2,48]{1,0:T(2,128)S(1)}, u32[]{:S(2)}, u32[]{:S(2)}) collective-permute-start(f32[2,48]{1,0:T(2,128)} %get-tuple-element.116.refs_2_), channel_id=1, source_target_pairs={{0,1},{1,0},{2,3},{3,2},{4,5},{5,4},{6,7},{7,6},{8,9},{9,8},{10,11... | collective-permute-start | bytes 1160 | tf_op jit(solution)/shard_map/ppermute | solution.py:62

commit v7 on v6

--- a/solution.py
+++ b/solution.py
@@ -688,7 +688,7 @@
     sums.second()
     sum_mlp = add_all(sums_mlp.parts)
     sums.third()
-    lower_out = swapped(after(own_out[early:], sums.begun))
+    lower_out = swapped(after(own_out[early:], sum_mlp))
     columns = gain_columns(sum_mlp, shard_three, gains)
     grad_input = input_grads(branch, inputs, own_one, other_one, back)
     output = add_output(middle, own_out, (upper_out, lower_out), back)

time: 141 us -> 140 us (level)
  transfers between devices with their start and end apart: 44 -> 44, of which waited for: 16 -> 15; matrix products, arithmetic and copies ran while one was open for 3% -> 3% of each run, Pallas kernels for 20% -> 20%
where the time goes in v7:
time: 140 us
  starting transfers between devices  49.6 us (35%)
  waiting for transfers between devices  41.3 us (30%)
  Pallas kernels  37 us (26%)
  local copies, waits for them, and re-layouts  5.97 us (4%)
  other arithmetic  4.71 us (3%)
    ppermute x38, starting transfers between devices, shifted(): return lax.ppermute(values, 'dp', pairs)  41.5 us
    pallas_call x25, Pallas kernels, run(): pl.pallas_call(ordered, out_shape=out_shapes, grid=grid, in_specs=specs +...  37 us
    ppermute x38, waiting for transfers between devices, shifted(): return lax.ppermute(values, 'dp', pairs)  27.7 us
    ppermute x6, waiting for transfers between devices, swapped(): return lax.ppermute(values, 'tensor', [(0, 1), (1, 0)])  13.6 us
    ppermute x6, starting transfers between devices, swapped(): return lax.ppermute(values, 'tensor', [(0, 1), (1, 0)])  8.08 us
    unnamed x40, local copies, waits for them, and re-layouts  3.23 us
  transfers between devices with their start and end apart: 44, of which 15 were waited for; matrix products, arithmetic and copies ran while one was open for 3% of the time, Pallas kernels for 20%

profile of v7, /device:TPU:0, one launch (start us, length us, event | category | flops | bytes accessed | tf_op | source)
XLA Modules:
  0.0 139.7 jit_solution(11350496991400504096)
XLA Ops:
  0.6 0.7 convert_bitcast_fusion
  1.3 0.9 fusion.8
  2.2 3.1 %collective-permute-start = (bf16[48,768]{1,0:T(8,128)(2,1)S(1)}, bf16[48,768]{1,0:T(8,128)(2,1)S(1)}, u32[]{:S(2)}, u32[]{:S(2)}) collective-permute-start(bf16[48,768]{1,0:T(8,128)(2,1)S(1)} %pad_maximum_fusion.refs_0_.refs_4_), channel_id=1, source_target_pairs={{0,8},{2,10},{4,12},{6,14},{8,16},{10,18},{12,20},{14,22},{16,24},... | collective-permute-start | bytes 221192 | tf_op jit(solution)/shard_map/ppermute | solution.py:58
  5.3 2.6 %collective-permute-start.1 = (bf16[48,768]{1,0:T(8,128)(2,1)S(1)}, bf16[48,768]{1,0:T(8,128)(2,1)S(1)}, u32[]{:S(2)}, u32[]{:S(2)}) collective-permute-start(bf16[48,768]{1,0:T(8,128)(2,1)S(1)} %pad_maximum_fusion.refs_0_.refs_4_), channel_id=1, source_target_pairs={{0,16},{2,18},{4,20},{6,22},{8,24},{10,26},{12,28},{14,30},{16,0},... | collective-permute-start | bytes 221192 | tf_op jit(solution)/shard_map/ppermute | solution.py:58
  7.9 1.3 collective-permute-start.2
  9.4 1.3 fusion.1
  11.0 1.8 %collective-permute-done.1.refs_2_ = bf16[48,768]{1,0:T(8,128)(2,1)S(1)} collective-permute-done((bf16[48,768]{1,0:T(8,128)(2,1)S(1)}, bf16[48,768]{1,0:T(8,128)(2,1)S(1)}, u32[]{:S(2)}, u32[]{:S(2)}) %collective-permute-start.1) | collective-permute-done | bytes 73760 | tf_op jit(solution)/shard_map/ppermute | solution.py:58
  13.1 1.6 %collective-permute-start.6 = (bf16[192,768]{1,0:T(8,128)(2,1)S(1)}, bf16[192,768]{1,0:T(8,128)(2,1)S(1)}, u32[]{:S(2)}, u32[]{:S(2)}) collective-permute-start(bf16[192,768]{1,0:T(8,128)(2,1)S(1)} %shard_map.161.refs_2_.refs_1_.refs_8_), channel_id=1, source_target_pairs={{0,4},{2,6},{4,0},{6,2},{8,12},{10,14},{12,8},{14,10},{16,20},{18,... | collective-permute-start | bytes 884744 | tf_op jit(solution)/shard_map/ppermute | solution.py:58
  14.7 1.9 %collective-permute-start.3 = (bf16[48,768]{1,0:T(8,128)(2,1)S(1)}, bf16[48,768]{1,0:T(8,128)(2,1)S(1)}, u32[]{:S(2)}, u32[]{:S(2)}) collective-permute-start(bf16[48,768]{1,0:T(8,128)(2,1)S(1)} %pad_maximum_fusion.1.refs_0_.refs_5_), channel_id=1, source_target_pairs={{0,8},{2,10},{4,12},{6,14},{8,16},{10,18},{12,20},{14,22},{16,24},... | collective-permute-start | bytes 221192 | tf_op jit(solution)/shard_map/ppermute | solution.py:58
  16.6 1.9 %collective-permute-start.4 = (bf16[48,768]{1,0:T(8,128)(2,1)S(1)}, bf16[48,768]{1,0:T(8,128)(2,1)S(1)}, u32[]{:S(2)}, u32[]{:S(2)}) collective-permute-start(bf16[48,768]{1,0:T(8,128)(2,1)S(1)} %pad_maximum_fusion.1.refs_0_.refs_5_), channel_id=1, source_target_pairs={{0,16},{2,18},{4,20},{6,22},{8,24},{10,26},{12,28},{14,30},{16,0},... | collective-permute-start | bytes 221192 | tf_op jit(solution)/shard_map/ppermute | solution.py:58
  18.5 0.7 collective-permute-start.5
  19.5 0.8 pad.10.refs_0_
  20.3 1.1 shard_map.162
  21.8 1.3 collective-permute-start.12
  23.1 1.4 collective-permute-done.4.refs_2_
  24.5 0.9 shard_map.163.refs_2_.refs_1_.refs_4_.refs_12_
  25.4 0.6 collective-permute-start.8
  26.0 2.2 %collective-permute-start.13 = (bf16[48,1280]{1,0:T(8,128)(2,1)S(1)}, bf16[48,1280]{1,0:T(8,128)(2,1)S(1)}, u32[]{:S(2)}, u32[]{:S(2)}) collective-permute-start(bf16[48,1280]{1,0:T(8,128)(2,1)S(1)} %fusion.5.refs_0_.refs_1_), channel_id=1, source_target_pairs={{0,8},{2,10},{4,12},{6,14},{8,16},{10,18},{12,20},{14,22},{16,24},... | collective-permute-start | bytes 368648 | tf_op jit(solution)/shard_map/ppermute | solution.py:58
  28.2 1.0 collective-permute-start.14
  29.1 1.4 %collective-permute-start.15 = (bf16[48,1280]{1,0:T(8,128)(2,1)S(1)}, bf16[48,1280]{1,0:T(8,128)(2,1)S(1)}, u32[]{:S(2)}, u32[]{:S(2)}) collective-permute-start(bf16[48,1280]{1,0:T(8,128)(2,1)S(1)} %fusion.5.refs_0_.refs_1_), channel_id=1, source_target_pairs={{0,24},{2,26},{4,28},{6,30},{8,0},{10,2},{12,4},{14,6},{16,8},{18,... | collective-permute-start | bytes 368648 | tf_op jit(solution)/shard_map/ppermute | solution.py:58
  30.5 1.0 fusion.2
  31.6 2.8 %collective-permute-done.8.refs_5_.refs_2_.refs_13_ = bf16[192,768]{1,0:T(8,128)(2,1)S(1)} collective-permute-done((bf16[192,768]{1,0:T(8,128)(2,1)S(1)}, bf16[192,768]{1,0:T(8,128)(2,1)S(1)}, u32[]{:S(2)}, u32[]{:S(2)}) %collective-permute-start.8) | collective-permute-done | bytes 294944 | tf_op jit(solution)/shard_map/ppermute | solution.py:58
  34.9 2.7 %shard_map.165 = (bf16[512,384]{1,0:T(8,128)(2,1)S(1)}, bf16[512,384]{1,0:T(8,128)(2,1)S(1)}, bf16[12,256,256]{2,1,0:T(8,128)(2,1)S(1)}) custom-call(bf16[512,768]{1,0:T(8,128)(2,1)S(1)} %get-tuple-element.65.refs_0_.refs_2_, bf16[192,768]{1,0:T(8,128)(2,1)S(1)} %shard_map.161.refs_2_.refs_1_.refs_8_, ...), custom_call_target="tpu_custom_call" | custom-call | tf_op jit(solution)/shard_map/pallas_call | solution.py:193
  38.2 1.7 %shard_map.167 = (bf16[512,384]{1,0:T(8,128)(2,1)S(1)}, bf16[512,384]{1,0:T(8,128)(2,1)S(1)}, bf16[512,768]{1,0:T(8,128)(2,1)S(1)}) custom-call(bf16[512,768]{1,0:T(8,128)(2,1)S(1)} %get-tuple-element.65.refs_0_.refs_2_, bf16[192,768]{1,0:T(8,128)(2,1)S(1)} %shard_map.163.refs_2_.refs_1_.refs_4_.refs_12_, ...), custom_call_target="tpu_custom_call" | custom-call | tf_op jit(solution)/shard_map/pallas_call | solution.py:193
  39.9 1.5 %collective-permute-start.16 = (bf16[512,768]{1,0:T(8,128)(2,1)S(1)}, bf16[512,768]{1,0:T(8,128)(2,1)S(1)}, u32[]{:S(2)}, u32[]{:S(2)}) collective-permute-start(bf16[512,768]{1,0:T(8,128)(2,1)S(1)} %get-tuple-element.70.refs_1_), channel_id=1, source_target_pairs={{0,1},{1,0},{2,3},{3,2},{4,5},{5,4},{6,7},{7,6},{8,9},{9,8},{10,11... | collective-permute-start | bytes 2359304 | tf_op jit(solution)/shard_map/ppermute | solution.py:62
  41.4 1.5 %collective-permute-start.20 = (bf16[192,1280]{1,0:T(8,128)(2,1)S(1)}, bf16[192,1280]{1,0:T(8,128)(2,1)S(1)}, u32[]{:S(2)}, u32[]{:S(2)}) collective-permute-start(bf16[192,1280]{1,0:T(8,128)(2,1)S(1)} %shard_map.166.refs_6_.refs_2_), channel_id=1, source_target_pairs={{0,4},{2,6},{4,0},{6,2},{8,12},{10,14},{12,8},{14,10},{16,20},{18,... | collective-permute-start | bytes 1474568 | tf_op jit(solution)/shard_map/ppermute | solution.py:58
  42.9 3.1 %collective-permute-start.17 = (bf16[96,640]{1,0:T(8,128)(2,1)S(1)}, bf16[96,640]{1,0:T(8,128)(2,1)S(1)}, u32[]{:S(2)}, u32[]{:S(2)}) collective-permute-start(bf16[96,640]{1,0:T(8,128)(2,1)S(1)} %shard_map.164.refs_9_.refs_0_), channel_id=1, source_target_pairs={{0,8},{2,10},{4,12},{6,14},{8,16},{10,18},{12,20},{14,22},{16,24},... | collective-permute-start | bytes 368648 | tf_op jit(solution)/shard_map/ppermute | solution.py:58
  46.0 1.1 collective-permute-start.18
  47.1 1.3 collective-permute-start.19
  48.4 0.8 shard_map.168.refs_4_.refs_1_.refs_3_.refs_0_
  49.2 1.7 %collective-permute-done.17.refs_1_ = bf16[96,640]{1,0:T(8,128)(2,1)S(1)} collective-permute-done((bf16[96,640]{1,0:T(8,128)(2,1)S(1)}, bf16[96,640]{1,0:T(8,128)(2,1)S(1)}, u32[]{:S(2)}, u32[]{:S(2)}) %collective-permute-start.17) | collective-permute-done | bytes 122912 | tf_op jit(solution)/shard_map/ppermute | solution.py:58
  50.9 4.1 %collective-permute-done.18.refs_2_ = bf16[96,640]{1,0:T(8,128)(2,1)S(1)} collective-permute-done((bf16[96,640]{1,0:T(8,128)(2,1)S(1)}, bf16[96,640]{1,0:T(8,128)(2,1)S(1)}, u32[]{:S(2)}, u32[]{:S(2)}) %collective-permute-start.18) | collective-permute-done | bytes 122912 | tf_op jit(solution)/shard_map/ppermute | solution.py:58
  56.1 3.2 %collective-permute-done.16.refs_2_ = bf16[512,768]{1,0:T(8,128)(2,1)S(1)} collective-permute-done((bf16[512,768]{1,0:T(8,128)(2,1)S(1)}, bf16[512,768]{1,0:T(8,128)(2,1)S(1)}, u32[]{:S(2)}, u32[]{:S(2)}) %collective-permute-start.16) | collective-permute-done | bytes 786464 | tf_op jit(solution)/shard_map/ppermute | solution.py:62
  59.3 0.6 shard_map.170
  59.9 4.0 %shard_map.171 = (bf16[512,640]{1,0:T(8,128)(2,1)S(1)}, bf16[512,1280]{1,0:T(8,128)(2,1)S(1)}, bf16[512,768]{1,0:T(8,128)(2,1)S(1)}, bf16[512,768]{1,0:T(8,128)(2,1)S(1)}) custom-call(bf16[512,768]{1,0:T(8,128)(2,1)S(1)} %get-tuple-element.75.refs_0_, bf16[512,768]{1,0:T(8,128)(2,1)S(1)} %shard_map.168.refs_4_.refs_1_.refs_3_.refs_0_, ...), custom_call_target="tpu_custom_call" | custom-call | tf_op jit(solution)/shard_map/pallas_call | solution.py:193
  64.0 1.5 %collective-permute-start.32 = (bf16[512,768]{1,0:T(8,128)(2,1)S(1)}, bf16[512,768]{1,0:T(8,128)(2,1)S(1)}, u32[]{:S(2)}, u32[]{:S(2)}) collective-permute-start(bf16[512,768]{1,0:T(8,128)(2,1)S(1)} %get-tuple-element.94.refs_2_), channel_id=1, source_target_pairs={{0,1},{1,0},{2,3},{3,2},{4,5},{5,4},{6,7},{7,6},{8,9},{9,8},{10,11... | collective-permute-start | bytes 2359304 | tf_op jit(solution)/shard_map/ppermute | solution.py:62
  65.5 1.8 %shard_map.172 = (bf16[384,640]{1,0:T(8,128)(2,1)S(1)}, bf16[384,640]{1,0:T(8,128)(2,1)S(1)}, bf16[384,640]{1,0:T(8,128)(2,1)S(1)}, bf16[384,640]{1,0:T(8,128)(2...) custom-call(bf16[512,768]{1,0:T(8,128)(2,1)S(1)} %get-tuple-element.75.refs_0_, ...), custom_call_target="tpu_custom_call" | custom-call | tf_op jit(solution)/shard_map/pallas_call | solution.py:193
  68.0 0.8 fusion.27
  69.3 0.6 collective-permute-done.27.refs_4_
  70.0 0.7 collective-permute-done.28.refs_5_
  71.0 1.6 %collective-permute-start.29 = (bf16[192,640]{1,0:T(8,128)(2,1)S(1)}, bf16[192,640]{1,0:T(8,128)(2,1)S(1)}, u32[]{:S(2)}, u32[]{:S(2)}) collective-permute-start(bf16[192,640]{1,0:T(8,128)(2,1)S(1)} %get-tuple-element.90), channel_id=1, source_target_pairs={{0,4},{2,6},{4,0},{6,2},{8,12},{10,14},{12,8},{14,10},{16,20},{18,... | collective-permute-start | bytes 737288 | tf_op jit(solution)/shard_map/ppermute | solution.py:58
  73.1 1.5 %collective-permute-start.31 = (bf16[192,640]{1,0:T(8,128)(2,1)S(1)}, bf16[192,640]{1,0:T(8,128)(2,1)S(1)}, u32[]{:S(2)}, u32[]{:S(2)}) collective-permute-start(bf16[192,640]{1,0:T(8,128)(2,1)S(1)} %get-tuple-element.92), channel_id=1, source_target_pairs={{0,4},{2,6},{4,0},{6,2},{8,12},{10,14},{12,8},{14,10},{16,20},{18,... | collective-permute-start | bytes 737288 | tf_op jit(solution)/shard_map/ppermute | solution.py:58
  74.6 9.9 %collective-permute-done.32.refs_3_ = bf16[512,768]{1,0:T(8,128)(2,1)S(1)} collective-permute-done((bf16[512,768]{1,0:T(8,128)(2,1)S(1)}, bf16[512,768]{1,0:T(8,128)(2,1)S(1)}, u32[]{:S(2)}, u32[]{:S(2)}) %collective-permute-start.32) | collective-permute-done | bytes 786464 | tf_op jit(solution)/shard_map/ppermute | solution.py:62
  84.5 2.0 %shard_map.174 = (bf16[512,768]{1,0:T(8,128)(2,1)S(1)}, bf16[512,384]{1,0:T(8,128)(2,1)S(1)}, bf16[512,384]{1,0:T(8,128)(2,1)S(1)}) custom-call(bf16[512,768]{1,0:T(8,128)(2,1)S(1)} %shard_map.168.refs_4_.refs_1_.refs_3_.refs_0_, f32[512,768]{1,0:T(8,128)S(1)} %get-tuple-element.74.refs_10_.refs_1_.refs_0_, bf16[512,768]{1,0:T(8,128)(2,1)S(1)} %get-tuple-element.94.refs_2_, ...), custom_call_target="tpu_custom_call" | custom-call | tf_op jit(solution)/shard_map/pallas_call | solution.py:193
  86.5 6.0 %shard_map.175 = (bf16[512,768]{1,0:T(8,128)(2,1)S(1)}, bf16[512,768]{1,0:T(8,128)(2,1)}) custom-call(bf16[512,384]{1,0:T(8,128)(2,1)S(1)} %get-tuple-element.69.refs_4_.refs_0_, bf16[512,384]{1,0:T(8,128)(2,1)S(1)} %get-tuple-element.93.refs_1_, bf16[512,384]{1,0:T(8,128)(2,1)S(1)} %get-tuple-element.72.refs_2_, ...), custom_call_target="tpu_custom_call" | custom-call | tf_op jit(solution)/shard_map/pallas_call | solution.py:193
  92.6 1.6 %shard_map.176 = (bf16[384,1536]{1,0:T(8,128)(2,1)S(1)}, bf16[384,1536]{1,0:T(8,128)(2,1)S(1)}) custom-call(bf16[512,768]{1,0:T(8,128)(2,1)S(1)} %get-tuple-element.65.refs_0_.refs_2_, bf16[512,768]{1,0:T(8,128)(2,1)S(1)} %get-tuple-element.98.refs_1_.refs_6_, bf16[512,768]{1,0:T(8,128)(2,1)S(1)} %get-tuple-element.65.refs_0_.refs_2_, ...), custom_call_target="tpu_custom_call" | custom-call | tf_op jit(solution)/shard_map/pallas_call | solution.py:193
  94.5 2.9 %collective-permute-start.33 = (bf16[48,1920]{1,0:T(8,128)(2,1)S(1)}, bf16[48,1920]{1,0:T(8,128)(2,1)S(1)}, u32[]{:S(2)}, u32[]{:S(2)}) collective-permute-start(bf16[48,1920]{1,0:T(8,128)(2,1)S(1)} %get-tuple-element.102), channel_id=1, source_target_pairs={{0,24},{2,26},{4,28},{6,30},{8,0},{10,2},{12,4},{14,6},{16,8},{18,... | collective-permute-start | bytes 552968 | tf_op jit(solution)/shard_map/ppermute | solution.py:58
  97.3 1.8 %collective-permute-start.34 = (bf16[48,1920]{1,0:T(8,128)(2,1)S(1)}, bf16[48,1920]{1,0:T(8,128)(2,1)S(1)}, u32[]{:S(2)}, u32[]{:S(2)}) collective-permute-start(bf16[48,1920]{1,0:T(8,128)(2,1)S(1)} %get-tuple-element.103), channel_id=1, source_target_pairs={{0,16},{2,18},{4,20},{6,22},{8,24},{10,26},{12,28},{14,30},{16,0},... | collective-permute-start | bytes 552968 | tf_op jit(solution)/shard_map/ppermute | solution.py:58
  99.2 1.5 %collective-permute-start.38 = (bf16[512,768]{1,0:T(8,128)(2,1)}, bf16[512,768]{1,0:T(8,128)(2,1)}, u32[]{:S(2)}, u32[]{:S(2)}) collective-permute-start(bf16[512,768]{1,0:T(8,128)(2,1)} %get-tuple-element.108.refs_2_), channel_id=1, source_target_pairs={{0,1},{1,0},{2,3},{3,2},{4,5},{5,4},{6,7},{7,6},{8,9},{9,8},{10,11... | collective-permute-start | bytes 2359304 | tf_op jit(solution)/shard_map/ppermute | solution.py:62
  100.9 1.6 %collective-permute-start.39 = (bf16[192,1536]{1,0:T(8,128)(2,1)S(1)}, bf16[192,1536]{1,0:T(8,128)(2,1)S(1)}, u32[]{:S(2)}, u32[]{:S(2)}) collective-permute-start(bf16[192,1536]{1,0:T(8,128)(2,1)S(1)} %get-tuple-element.109), channel_id=1, source_target_pairs={{0,4},{2,6},{4,0},{6,2},{8,12},{10,14},{12,8},{14,10},{16,20},{18,... | collective-permute-start | bytes 1769480 | tf_op jit(solution)/shard_map/ppermute | solution.py:58
  103.0 13.0 %collective-permute-done.34.refs_2_ = bf16[48,1920]{1,0:T(8,128)(2,1)S(1)} collective-permute-done((bf16[48,1920]{1,0:T(8,128)(2,1)S(1)}, bf16[48,1920]{1,0:T(8,128)(2,1)S(1)}, u32[]{:S(2)}, u32[]{:S(2)}) %collective-permute-start.34) | collective-permute-done | bytes 184352 | tf_op jit(solution)/shard_map/ppermute | solution.py:58
  116.2 1.6 %collective-permute-start.37 = (bf16[256,768]{1,0:T(8,128)(2,1)}, bf16[256,768]{1,0:T(8,128)(2,1)}, u32[]{:S(2)}, u32[]{:S(2)}) collective-permute-start(bf16[256,768]{1,0:T(8,128)(2,1)} %get-tuple-element.107), channel_id=1, source_target_pairs={{0,1},{1,0},{2,3},{3,2},{4,5},{5,4},{6,7},{7,6},{8,9},{9,8},{10,11... | collective-permute-start | bytes 1179656 | tf_op jit(solution)/shard_map/ppermute | solution.py:62
  117.7 0.8 shard_map.180
  118.5 1.7 %collective-permute-start.40 = (bf16[48,1536]{1,0:T(8,128)(2,1)}, bf16[48,1536]{1,0:T(8,128)(2,1)}, u32[]{:S(2)}, u32[]{:S(2)}) collective-permute-start(bf16[48,1536]{1,0:T(8,128)(2,1)} %get-tuple-element.111), channel_id=1, source_target_pairs={{0,24},{2,26},{4,28},{6,30},{8,0},{10,2},{12,4},{14,6},{16,8},{18,... | collective-permute-start | bytes 442376 | tf_op jit(solution)/shard_map/ppermute | solution.py:58
  120.2 1.1 collective-permute-start.42
  121.6 0.6 copy-done.14
  122.2 5.2 %shard_map.182.refs_5_ = f32[512,768]{1,0:T(8,128)} custom-call(bf16[512,768]{1,0:T(8,128)(2,1)} %copy-done.6, bf16[512,768]{1,0:T(8,128)(2,1)} %copy-done.5, bf16[512,768]{1,0:T(8,128)(2,1)} %get-tuple-element.108.refs_2_, bf16[512,768]{1,0:T(8,128)(2,1)} %collective-permute-done.38.refs_3_, bf16[768,768]{1,0:T(8,128)(2,1)} %get-tuple-element.127.refs_4_, ...), custom_call_target="tpu_custom_call" | custom-call | tf_op jit(solution)/shard_map/pallas_call | solution.py:193
  127.4 1.4 %copy-done.1 = f32[512,768]{1,0:T(8,128)S(1)} copy-done((f32[512,768]{1,0:T(8,128)S(1)}, f32[512,768]{1,0:T(8,128)}, u32[]{:S(2)}) %copy-start.1) | copy-done | bytes 1572888
  128.8 1.1 copy-done.4
  129.9 2.7 %shard_map.183.refs_7_ = bf16[512,768]{1,0:T(8,128)(2,1)} custom-call(f32[512,768]{1,0:T(8,128)S(1)} %get-tuple-element.74.refs_10_.refs_1_.refs_0_, bf16[512,768]{1,0:T(8,128)(2,1)S(1)} %copy-done.4, bf16[256,768]{1,0:T(8,128)(2,1)S(1)} %collective-permute-done.25.refs_7_.refs_2_, bf16[256,768]{1,0:T(8,128)(2,1)} %collective-permute-done.37.refs_3_, ...), custom_call_target="tpu_custom_call" | custom-call | tf_op jit(solution)/shard_map/pallas_call | solution.py:193
  132.6 2.2 %shard_map.184 = (f32[3,48,384]{2,1,0:T(8,128)}, f32[48,384]{1,0:T(8,128)}, f32[2,48]{1,0:T(2,128)}) custom-call(bf16[48,1536]{1,0:T(8,128)(2,1)} %copy-done.11, bf16[48,1536]{1,0:T(8,128)(2,1)} %collective-permute-done.40.refs_1_, bf16[48,1536]{1,0:T(8,128)(2,1)} %collective-permute-done.41.refs_2_, bf16[48,1536]{1,0:T(8,128)(2,1)} %collective-permute-done.42.refs_3_, ...), custom_call_target="tpu_custom_call" | custom-call | tf_op jit(solution)/shard_map/pallas_call | solution.py:193
  134.8 1.4 collective-permute-start.43
  136.2 1.8 %shard_map.185 = (f32[48,2,576]{2,1,0:T(2,128)}, f32[48,576]{1,0:T(8,128)}) custom-call(f32[48,1920]{1,0:T(8,128)} %copy-done.2, f32[48,2]{1,0:T(8,128)} %copy-done.15, f32[2,48]{1,0:T(2,128)} %get-tuple-element.116.refs_2_), custom_call_target="tpu_custom_call" | custom-call | tf_op jit(solution)/shard_map/pallas_call | solution.py:193
  138.6 0.6 add.172
  (113 shorter events, 8.0 us)
Async XLA Ops:
  2.2 8.5 %copy-start.17 = (bf16[48,2,576]{2,1,0:T(2,128)(2,1)S(1)}, bf16[48,2,576]{2,1,0:T(2,128)(2,1)}, u32[]{:S(2)}) copy-start(bf16[48,2,576]{2,1,0:T(2,128)(2,1)} %param.17) | copy-start | bytes 331780
  2.2 10.9 %copy-start.9 = (bf16[48,768]{1,0:T(8,128)(2,1)}, bf16[48,768]{1,0:T(8,128)(2,1)S(1)}, u32[]{:S(2)}) copy-start(bf16[48,768]{1,0:T(8,128)(2,1)S(1)} %pad_maximum_fusion.refs_0_.refs_4_) | copy-start | bytes 221188
  2.2 8.8 %collective-permute-start = (bf16[48,768]{1,0:T(8,128)(2,1)S(1)}, bf16[48,768]{1,0:T(8,128)(2,1)S(1)}, u32[]{:S(2)}, u32[]{:S(2)}) collective-permute-start(bf16[48,768]{1,0:T(8,128)(2,1)S(1)} %pad_maximum_fusion.refs_0_.refs_4_), channel_id=1, source_target_pairs={{0,8},{2,10},{4,12},{6,14},{8,16},{10,18},{12,20},{14,22},{16,24},... | collective-permute-start | bytes 221192 | tf_op jit(solution)/shard_map/ppermute | solution.py:58
  5.3 7.5 %collective-permute-start.1 = (bf16[48,768]{1,0:T(8,128)(2,1)S(1)}, bf16[48,768]{1,0:T(8,128)(2,1)S(1)}, u32[]{:S(2)}, u32[]{:S(2)}) collective-permute-start(bf16[48,768]{1,0:T(8,128)(2,1)S(1)} %pad_maximum_fusion.refs_0_.refs_4_), channel_id=1, source_target_pairs={{0,16},{2,18},{4,20},{6,22},{8,24},{10,26},{12,28},{14,30},{16,0},... | collective-permute-start | bytes 221192 | tf_op jit(solution)/shard_map/ppermute | solution.py:58
  7.9 5.2 %collective-permute-start.2 = (bf16[48,768]{1,0:T(8,128)(2,1)S(1)}, bf16[48,768]{1,0:T(8,128)(2,1)S(1)}, u32[]{:S(2)}, u32[]{:S(2)}) collective-permute-start(bf16[48,768]{1,0:T(8,128)(2,1)S(1)} %pad_maximum_fusion.refs_0_.refs_4_), channel_id=1, source_target_pairs={{0,24},{2,26},{4,28},{6,30},{8,0},{10,2},{12,4},{14,6},{16,8},{18,... | collective-permute-start | bytes 221192 | tf_op jit(solution)/shard_map/ppermute | solution.py:58
  9.4 1.6 %copy-start.18 = (bf16[384,48]{0,1:T(8,128)(2,1)S(1)}, bf16[384,48]{0,1:T(8,128)(2,1)}, u32[]{:S(2)}) copy-start(bf16[384,48]{0,1:T(8,128)(2,1)} %param.15) | copy-start | bytes 110596
  10.7 8.6 %copy-start.19 = (s32[512]{0:T(512)S(1)}, s32[512]{0:T(512)}, u32[]{:S(2)}) copy-start(s32[512]{0:T(512)} %param.12) | copy-start | bytes 6148
  10.7 8.6 %copy-start.16 = (s32[512]{0:T(512)S(1)}, s32[512]{0:T(512)}, u32[]{:S(2)}) copy-start(s32[512]{0:T(512)} %param.11) | copy-start | bytes 6148
  10.7 9.6 %copy-start.7 = (bf16[512,768]{1,0:T(8,128)(2,1)S(1)}, bf16[512,768]{1,0:T(8,128)(2,1)}, u32[]{:S(2)}) copy-start(bf16[512,768]{1,0:T(8,128)(2,1)} %refs_0_.2) | copy-start | bytes 2359300
  11.0 13.5 %copy-start.10 = (bf16[48,768]{1,0:T(8,128)(2,1)}, bf16[48,768]{1,0:T(8,128)(2,1)S(1)}, u32[]{:S(2)}) copy-start(bf16[48,768]{1,0:T(8,128)(2,1)S(1)} %pad_maximum_fusion.1.refs_0_.refs_5_) | copy-start | bytes 221188
  13.1 8.7 %collective-permute-start.6 = (bf16[192,768]{1,0:T(8,128)(2,1)S(1)}, bf16[192,768]{1,0:T(8,128)(2,1)S(1)}, u32[]{:S(2)}, u32[]{:S(2)}) collective-permute-start(bf16[192,768]{1,0:T(8,128)(2,1)S(1)} %shard_map.161.refs_2_.refs_1_.refs_8_), channel_id=1, source_target_pairs={{0,4},{2,6},{4,0},{6,2},{8,12},{10,14},{12,8},{14,10},{16,20},{18,... | collective-permute-start | bytes 884744 | tf_op jit(solution)/shard_map/ppermute | solution.py:58
  14.7 9.8 %collective-permute-start.7 = (bf16[192,768]{1,0:T(8,128)(2,1)S(1)}, bf16[192,768]{1,0:T(8,128)(2,1)S(1)}, u32[]{:S(2)}, u32[]{:S(2)}) collective-permute-start(bf16[192,768]{1,0:T(8,128)(2,1)S(1)} %shard_map.161.refs_2_.refs_1_.refs_8_), channel_id=1, source_target_pairs={{0,2},{2,0},{4,6},{6,4},{8,10},{10,8},{12,14},{14,12},{16,18},{18,... | collective-permute-start | bytes 884744 | tf_op jit(solution)/shard_map/ppermute | solution.py:58
  14.7 23.4 %copy-start.12 = (bf16[48,1280]{1,0:T(8,128)(2,1)}, bf16[48,1280]{1,0:T(8,128)(2,1)S(1)}, u32[]{:S(2)}) copy-start(bf16[48,1280]{1,0:T(8,128)(2,1)S(1)} %fusion.5.refs_0_.refs_1_) | copy-start | bytes 368644
  14.7 8.4 %collective-permute-start.3 = (bf16[48,768]{1,0:T(8,128)(2,1)S(1)}, bf16[48,768]{1,0:T(8,128)(2,1)S(1)}, u32[]{:S(2)}, u32[]{:S(2)}) collective-permute-start(bf16[48,768]{1,0:T(8,128)(2,1)S(1)} %pad_maximum_fusion.1.refs_0_.refs_5_), channel_id=1, source_target_pairs={{0,8},{2,10},{4,12},{6,14},{8,16},{10,18},{12,20},{14,22},{16,24},... | collective-permute-start | bytes 221192 | tf_op jit(solution)/shard_map/ppermute | solution.py:58
  16.6 7.9 %collective-permute-start.4 = (bf16[48,768]{1,0:T(8,128)(2,1)S(1)}, bf16[48,768]{1,0:T(8,128)(2,1)S(1)}, u32[]{:S(2)}, u32[]{:S(2)}) collective-permute-start(bf16[48,768]{1,0:T(8,128)(2,1)S(1)} %pad_maximum_fusion.1.refs_0_.refs_5_), channel_id=1, source_target_pairs={{0,16},{2,18},{4,20},{6,22},{8,24},{10,26},{12,28},{14,30},{16,0},... | collective-permute-start | bytes 221192 | tf_op jit(solution)/shard_map/ppermute | solution.py:58
  18.5 6.0 %collective-permute-start.5 = (bf16[48,768]{1,0:T(8,128)(2,1)S(1)}, bf16[48,768]{1,0:T(8,128)(2,1)}, u32[]{:S(2)}, u32[]{:S(2)}) collective-permute-start(bf16[48,768]{1,0:T(8,128)(2,1)S(1)} %pad_maximum_fusion.1.refs_0_.refs_5_), channel_id=1, source_target_pairs={{0,24},{2,26},{4,28},{6,30},{8,0},{10,2},{12,4},{14,6},{16,8},{18,... | collective-permute-start | bytes 221192 | tf_op jit(solution)/shard_map/ppermute | solution.py:58
  21.4 37.9 %copy-start.5 = (bf16[512,768]{1,0:T(8,128)(2,1)}, bf16[512,768]{1,0:T(8,128)(2,1)S(1)}, u32[]{:S(2)}) copy-start(bf16[512,768]{1,0:T(8,128)(2,1)S(1)} %get-tuple-element.64.refs_4_.refs_0_.refs_1_) | copy-start | bytes 2359300
  21.8 7.3 %collective-permute-start.12 = (bf16[48,640]{1,0:T(8,128)(2,1)S(1)}, bf16[48,640]{1,0:T(8,128)(2,1)S(1)}, u32[]{:S(2)}, u32[]{:S(2)}) collective-permute-start(bf16[48,640]{1,0:T(8,128)(2,1)S(1)} %pad.10.refs_0_), channel_id=1, source_target_pairs={{0,4},{2,6},{4,0},{6,2},{8,12},{10,14},{12,8},{14,10},{16,20},{18,... | collective-permute-start | bytes 184328 | tf_op jit(solution)/shard_map/ppermute | solution.py:58
  23.1 11.2 %collective-permute-start.11 = (bf16[192,768]{1,0:T(8,128)(2,1)S(1)}, bf16[192,768]{1,0:T(8,128)(2,1)S(1)}, u32[]{:S(2)}, u32[]{:S(2)}) collective-permute-start(bf16[192,768]{1,0:T(8,128)(2,1)S(1)} %collective-permute-done.6.refs_5_.refs_2_.refs_9_), channel_id=1, source_target_pairs={{0,2},{2,0},{4,6},{6,4},{8,10},{10,8},{12,14},{14,12},{16,18},{18,... | collective-permute-start | bytes 884744 | tf_op jit(solution)/shard_map/ppermute | solution.py:58
  25.4 9.0 %collective-permute-start.8 = (bf16[192,768]{1,0:T(8,128)(2,1)S(1)}, bf16[192,768]{1,0:T(8,128)(2,1)S(1)}, u32[]{:S(2)}, u32[]{:S(2)}) collective-permute-start(bf16[192,768]{1,0:T(8,128)(2,1)S(1)} %shard_map.163.refs_2_.refs_1_.refs_4_.refs_12_), channel_id=1, source_target_pairs={{0,4},{2,6},{4,0},{6,2},{8,12},{10,14},{12,8},{14,10},{16,20},{18,... | collective-permute-start | bytes 884744 | tf_op jit(solution)/shard_map/ppermute | solution.py:58
  26.0 11.6 %collective-permute-start.13 = (bf16[48,1280]{1,0:T(8,128)(2,1)S(1)}, bf16[48,1280]{1,0:T(8,128)(2,1)S(1)}, u32[]{:S(2)}, u32[]{:S(2)}) collective-permute-start(bf16[48,1280]{1,0:T(8,128)(2,1)S(1)} %fusion.5.refs_0_.refs_1_), channel_id=1, source_target_pairs={{0,8},{2,10},{4,12},{6,14},{8,16},{10,18},{12,20},{14,22},{16,24},... | collective-permute-start | bytes 368648 | tf_op jit(solution)/shard_map/ppermute | solution.py:58
  28.2 9.9 %collective-permute-start.14 = (bf16[48,1280]{1,0:T(8,128)(2,1)S(1)}, bf16[48,1280]{1,0:T(8,128)(2,1)S(1)}, u32[]{:S(2)}, u32[]{:S(2)}) collective-permute-start(bf16[48,1280]{1,0:T(8,128)(2,1)S(1)} %fusion.5.refs_0_.refs_1_), channel_id=1, source_target_pairs={{0,16},{2,18},{4,20},{6,22},{8,24},{10,26},{12,28},{14,30},{16,0},... | collective-permute-start | bytes 368648 | tf_op jit(solution)/shard_map/ppermute | solution.py:58
  29.1 9.0 %collective-permute-start.15 = (bf16[48,1280]{1,0:T(8,128)(2,1)S(1)}, bf16[48,1280]{1,0:T(8,128)(2,1)S(1)}, u32[]{:S(2)}, u32[]{:S(2)}) collective-permute-start(bf16[48,1280]{1,0:T(8,128)(2,1)S(1)} %fusion.5.refs_0_.refs_1_), channel_id=1, source_target_pairs={{0,24},{2,26},{4,28},{6,30},{8,0},{10,2},{12,4},{14,6},{16,8},{18,... | collective-permute-start | bytes 368648 | tf_op jit(solution)/shard_map/ppermute | solution.py:58
  34.4 3.8 %collective-permute-start.9 = (bf16[192,768]{1,0:T(8,128)(2,1)S(1)}, bf16[192,768]{1,0:T(8,128)(2,1)S(1)}, u32[]{:S(2)}, u32[]{:S(2)}) collective-permute-start(bf16[192,768]{1,0:T(8,128)(2,1)S(1)} %shard_map.163.refs_2_.refs_1_.refs_4_.refs_12_), channel_id=1, source_target_pairs={{0,2},{2,0},{4,6},{6,4},{8,10},{10,8},{12,14},{14,12},{16,18},{18,... | collective-permute-start | bytes 884744 | tf_op jit(solution)/shard_map/ppermute | solution.py:58
  34.4 3.8 %collective-permute-start.10 = (bf16[192,768]{1,0:T(8,128)(2,1)S(1)}, bf16[192,768]{1,0:T(8,128)(2,1)S(1)}, u32[]{:S(2)}, u32[]{:S(2)}) collective-permute-start(bf16[192,768]{1,0:T(8,128)(2,1)S(1)} %collective-permute-done.8.refs_5_.refs_2_.refs_13_), channel_id=1, source_target_pairs={{0,2},{2,0},{4,6},{6,4},{8,10},{10,8},{12,14},{14,12},{16,18},{18,... | collective-permute-start | bytes 884744 | tf_op jit(solution)/shard_map/ppermute | solution.py:58
  38.1 10.2 %copy-start.8 = (bf16[512,768]{1,0:T(8,128)(2,1)S(1)}, bf16[512,768]{1,0:T(8,128)(2,1)}, u32[]{:S(2)}) copy-start(bf16[512,768]{1,0:T(8,128)(2,1)} %refs_0_.3) | copy-start | bytes 2359300
  39.9 19.4 %collective-permute-start.16 = (bf16[512,768]{1,0:T(8,128)(2,1)S(1)}, bf16[512,768]{1,0:T(8,128)(2,1)S(1)}, u32[]{:S(2)}, u32[]{:S(2)}) collective-permute-start(bf16[512,768]{1,0:T(8,128)(2,1)S(1)} %get-tuple-element.70.refs_1_), channel_id=1, source_target_pairs={{0,1},{1,0},{2,3},{3,2},{4,5},{5,4},{6,7},{7,6},{8,9},{9,8},{10,11... | collective-permute-start | bytes 2359304 | tf_op jit(solution)/shard_map/ppermute | solution.py:62
  41.4 14.2 %collective-permute-start.20 = (bf16[192,1280]{1,0:T(8,128)(2,1)S(1)}, bf16[192,1280]{1,0:T(8,128)(2,1)S(1)}, u32[]{:S(2)}, u32[]{:S(2)}) collective-permute-start(bf16[192,1280]{1,0:T(8,128)(2,1)S(1)} %shard_map.166.refs_6_.refs_2_), channel_id=1, source_target_pairs={{0,4},{2,6},{4,0},{6,2},{8,12},{10,14},{12,8},{14,10},{16,20},{18,... | collective-permute-start | bytes 1474568 | tf_op jit(solution)/shard_map/ppermute | solution.py:58
  42.9 8.0 %collective-permute-start.17 = (bf16[96,640]{1,0:T(8,128)(2,1)S(1)}, bf16[96,640]{1,0:T(8,128)(2,1)S(1)}, u32[]{:S(2)}, u32[]{:S(2)}) collective-permute-start(bf16[96,640]{1,0:T(8,128)(2,1)S(1)} %shard_map.164.refs_9_.refs_0_), channel_id=1, source_target_pairs={{0,8},{2,10},{4,12},{6,14},{8,16},{10,18},{12,20},{14,22},{16,24},... | collective-permute-start | bytes 368648 | tf_op jit(solution)/shard_map/ppermute | solution.py:58
  46.0 8.9 %collective-permute-start.18 = (bf16[96,640]{1,0:T(8,128)(2,1)S(1)}, bf16[96,640]{1,0:T(8,128)(2,1)S(1)}, u32[]{:S(2)}, u32[]{:S(2)}) collective-permute-start(bf16[96,640]{1,0:T(8,128)(2,1)S(1)} %shard_map.164.refs_9_.refs_0_), channel_id=1, source_target_pairs={{0,16},{2,18},{4,20},{6,22},{8,24},{10,26},{12,28},{14,30},{16,0},... | collective-permute-start | bytes 368648 | tf_op jit(solution)/shard_map/ppermute | solution.py:58
  47.1 7.9 %collective-permute-start.19 = (bf16[96,640]{1,0:T(8,128)(2,1)S(1)}, bf16[96,640]{1,0:T(8,128)(2,1)S(1)}, u32[]{:S(2)}, u32[]{:S(2)}) collective-permute-start(bf16[96,640]{1,0:T(8,128)(2,1)S(1)} %shard_map.164.refs_9_.refs_0_), channel_id=1, source_target_pairs={{0,24},{2,26},{4,28},{6,30},{8,0},{10,2},{12,4},{14,6},{16,8},{18,... | collective-permute-start | bytes 368648 | tf_op jit(solution)/shard_map/ppermute | solution.py:58
  55.0 4.9 %collective-permute-start.23 = (bf16[192,640]{1,0:T(8,128)(2,1)S(1)}, bf16[192,640]{1,0:T(8,128)(2,1)S(1)}, u32[]{:S(2)}, u32[]{:S(2)}) collective-permute-start(bf16[192,640]{1,0:T(8,128)(2,1)S(1)} %get-tuple-element.73.refs_3_.refs_6_), channel_id=1, source_target_pairs={{0,2},{2,0},{4,6},{6,4},{8,10},{10,8},{12,14},{14,12},{16,18},{18,... | collective-permute-start | bytes 737288 | tf_op jit(solution)/shard_map/ppermute | solution.py:58
  55.1 4.8 %collective-permute-start.24 = (bf16[192,640]{1,0:T(8,128)(2,1)S(1)}, bf16[192,640]{1,0:T(8,128)(2,1)S(1)}, u32[]{:S(2)}, u32[]{:S(2)}) collective-permute-start(bf16[192,640]{1,0:T(8,128)(2,1)S(1)} %get-tuple-element.77.refs_7_), channel_id=1, source_target_pairs={{0,2},{2,0},{4,6},{6,4},{8,10},{10,8},{12,14},{14,12},{16,18},{18,... | collective-permute-start | bytes 737288 | tf_op jit(solution)/shard_map/ppermute | solution.py:58
  55.6 4.3 %collective-permute-start.21 = (bf16[192,1280]{1,0:T(8,128)(2,1)S(1)}, bf16[192,1280]{1,0:T(8,128)(2,1)S(1)}, u32[]{:S(2)}, u32[]{:S(2)}) collective-permute-start(bf16[192,1280]{1,0:T(8,128)(2,1)S(1)} %shard_map.166.refs_6_.refs_2_), channel_id=1, source_target_pairs={{0,2},{2,0},{4,6},{6,4},{8,10},{10,8},{12,14},{14,12},{16,18},{18,... | collective-permute-start | bytes 1474568 | tf_op jit(solution)/shard_map/ppermute | solution.py:58
  55.7 4.3 %collective-permute-start.22 = (bf16[192,1280]{1,0:T(8,128)(2,1)S(1)}, bf16[192,1280]{1,0:T(8,128)(2,1)S(1)}, u32[]{:S(2)}, u32[]{:S(2)}) collective-permute-start(bf16[192,1280]{1,0:T(8,128)(2,1)S(1)} %collective-permute-done.20.refs_3_), channel_id=1, source_target_pairs={{0,2},{2,0},{4,6},{6,4},{8,10},{10,8},{12,14},{14,12},{16,18},{18,... | collective-permute-start | bytes 1474568 | tf_op jit(solution)/shard_map/ppermute | solution.py:58
  63.9 4.0 %copy-start.3 = (bf16[512,768]{1,0:T(8,128)(2,1)}, bf16[512,768]{1,0:T(8,128)(2,1)S(1)}, u32[]{:S(2)}) copy-start(bf16[512,768]{1,0:T(8,128)(2,1)S(1)} %get-tuple-element.78.refs_1_) | copy-start | bytes 2359300
  64.0 20.5 %collective-permute-start.32 = (bf16[512,768]{1,0:T(8,128)(2,1)S(1)}, bf16[512,768]{1,0:T(8,128)(2,1)S(1)}, u32[]{:S(2)}, u32[]{:S(2)}) collective-permute-start(bf16[512,768]{1,0:T(8,128)(2,1)S(1)} %get-tuple-element.94.refs_2_), channel_id=1, source_target_pairs={{0,1},{1,0},{2,3},{3,2},{4,5},{5,4},{6,7},{7,6},{8,9},{9,8},{10,11... | collective-permute-start | bytes 2359304 | tf_op jit(solution)/shard_map/ppermute | solution.py:62
  67.3 2.0 %collective-permute-start.26 = (bf16[384,640]{1,0:T(8,128)(2,1)S(1)}, bf16[384,640]{1,0:T(8,128)(2,1)S(1)}, u32[]{:S(2)}, u32[]{:S(2)}) collective-permute-start(bf16[384,640]{1,0:T(8,128)(2,1)S(1)} %get-tuple-element.84), channel_id=1, source_target_pairs={{0,2},{2,0},{4,6},{6,4},{8,10},{10,8},{12,14},{14,12},{16,18},{18,... | collective-permute-start | bytes 1474568 | tf_op jit(solution)/shard_map/ppermute | solution.py:58
  67.4 2.6 %collective-permute-start.27 = (bf16[384,640]{1,0:T(8,128)(2,1)S(1)}, bf16[384,640]{1,0:T(8,128)(2,1)S(1)}, u32[]{:S(2)}, u32[]{:S(2)}) collective-permute-start(bf16[384,640]{1,0:T(8,128)(2,1)S(1)} %get-tuple-element.85), channel_id=1, source_target_pairs={{0,2},{2,0},{4,6},{6,4},{8,10},{10,8},{12,14},{14,12},{16,18},{18,... | collective-permute-start | bytes 1474568 | tf_op jit(solution)/shard_map/ppermute | solution.py:58
  67.9 2.8 %collective-permute-start.28 = (bf16[384,640]{1,0:T(8,128)(2,1)S(1)}, bf16[384,640]{1,0:T(8,128)(2,1)S(1)}, u32[]{:S(2)}, u32[]{:S(2)}) collective-permute-start(bf16[384,640]{1,0:T(8,128)(2,1)S(1)} %get-tuple-element.86), channel_id=1, source_target_pairs={{0,2},{2,0},{4,6},{6,4},{8,10},{10,8},{12,14},{14,12},{16,18},{18,... | collective-permute-start | bytes 1474568 | tf_op jit(solution)/shard_map/ppermute | solution.py:58
  68.8 23.8 %collective-permute-start.25 = (bf16[256,768]{1,0:T(8,128)(2,1)S(1)}, bf16[256,768]{1,0:T(8,128)(2,1)S(1)}, u32[]{:S(2)}, u32[]{:S(2)}) collective-permute-start(bf16[256,768]{1,0:T(8,128)(2,1)S(1)} %get-tuple-element.121), channel_id=1, source_target_pairs={{0,1},{1,0},{2,3},{3,2},{4,5},{5,4},{6,7},{7,6},{8,9},{9,8},{10,11... | collective-permute-start | bytes 1179656 | tf_op jit(solution)/shard_map/ppermute | solution.py:62
  71.0 21.5 %collective-permute-start.29 = (bf16[192,640]{1,0:T(8,128)(2,1)S(1)}, bf16[192,640]{1,0:T(8,128)(2,1)S(1)}, u32[]{:S(2)}, u32[]{:S(2)}) collective-permute-start(bf16[192,640]{1,0:T(8,128)(2,1)S(1)} %get-tuple-element.90), channel_id=1, source_target_pairs={{0,4},{2,6},{4,0},{6,2},{8,12},{10,14},{12,8},{14,10},{16,20},{18,... | collective-permute-start | bytes 737288 | tf_op jit(solution)/shard_map/ppermute | solution.py:58
  72.6 19.9 %collective-permute-start.30 = (bf16[192,640]{1,0:T(8,128)(2,1)S(1)}, bf16[192,640]{1,0:T(8,128)(2,1)S(1)}, u32[]{:S(2)}, u32[]{:S(2)}) collective-permute-start(bf16[192,640]{1,0:T(8,128)(2,1)S(1)} %get-tuple-element.91), channel_id=1, source_target_pairs={{0,4},{2,6},{4,0},{6,2},{8,12},{10,14},{12,8},{14,10},{16,20},{18,... | collective-permute-start | bytes 737288 | tf_op jit(solution)/shard_map/ppermute | solution.py:58
  73.1 19.5 %collective-permute-start.31 = (bf16[192,640]{1,0:T(8,128)(2,1)S(1)}, bf16[192,640]{1,0:T(8,128)(2,1)S(1)}, u32[]{:S(2)}, u32[]{:S(2)}) collective-permute-start(bf16[192,640]{1,0:T(8,128)(2,1)S(1)} %get-tuple-element.92), channel_id=1, source_target_pairs={{0,4},{2,6},{4,0},{6,2},{8,12},{10,14},{12,8},{14,10},{16,20},{18,... | collective-permute-start | bytes 737288 | tf_op jit(solution)/shard_map/ppermute | solution.py:58
  86.5 6.1 %copy-start.6 = (bf16[512,768]{1,0:T(8,128)(2,1)}, bf16[512,768]{1,0:T(8,128)(2,1)S(1)}, u32[]{:S(2)}) copy-start(bf16[512,768]{1,0:T(8,128)(2,1)S(1)} %get-tuple-element.99.refs_4_.refs_0_) | copy-start | bytes 2359300
  94.2 6.5 %collective-permute-start.36 = (bf16[384,1536]{1,0:T(8,128)(2,1)S(1)}, bf16[384,1536]{1,0:T(8,128)(2,1)S(1)}, u32[]{:S(2)}, u32[]{:S(2)}) collective-permute-start(bf16[384,1536]{1,0:T(8,128)(2,1)S(1)} %get-tuple-element.105), channel_id=1, source_target_pairs={{0,2},{2,0},{4,6},{6,4},{8,10},{10,8},{12,14},{14,12},{16,18},{18,... | collective-permute-start | bytes 3538952 | tf_op jit(solution)/shard_map/ppermute | solution.py:58
  94.5 8.5 %collective-permute-start.33 = (bf16[48,1920]{1,0:T(8,128)(2,1)S(1)}, bf16[48,1920]{1,0:T(8,128)(2,1)S(1)}, u32[]{:S(2)}, u32[]{:S(2)}) collective-permute-start(bf16[48,1920]{1,0:T(8,128)(2,1)S(1)} %get-tuple-element.102), channel_id=1, source_target_pairs={{0,24},{2,26},{4,28},{6,30},{8,0},{10,2},{12,4},{14,6},{16,8},{18,... | collective-permute-start | bytes 552968 | tf_op jit(solution)/shard_map/ppermute | solution.py:58
  97.3 18.7 %collective-permute-start.34 = (bf16[48,1920]{1,0:T(8,128)(2,1)S(1)}, bf16[48,1920]{1,0:T(8,128)(2,1)S(1)}, u32[]{:S(2)}, u32[]{:S(2)}) collective-permute-start(bf16[48,1920]{1,0:T(8,128)(2,1)S(1)} %get-tuple-element.103), channel_id=1, source_target_pairs={{0,16},{2,18},{4,20},{6,22},{8,24},{10,26},{12,28},{14,30},{16,0},... | collective-permute-start | bytes 552968 | tf_op jit(solution)/shard_map/ppermute | solution.py:58
  99.2 16.9 %collective-permute-start.35 = (bf16[48,1920]{1,0:T(8,128)(2,1)S(1)}, bf16[48,1920]{1,0:T(8,128)(2,1)S(1)}, u32[]{:S(2)}, u32[]{:S(2)}) collective-permute-start(bf16[48,1920]{1,0:T(8,128)(2,1)S(1)} %get-tuple-element.104), channel_id=1, source_target_pairs={{0,8},{2,10},{4,12},{6,14},{8,16},{10,18},{12,20},{14,22},{16,24},... | collective-permute-start | bytes 552968 | tf_op jit(solution)/shard_map/ppermute | solution.py:58
  99.2 23.0 %collective-permute-start.38 = (bf16[512,768]{1,0:T(8,128)(2,1)}, bf16[512,768]{1,0:T(8,128)(2,1)}, u32[]{:S(2)}, u32[]{:S(2)}) collective-permute-start(bf16[512,768]{1,0:T(8,128)(2,1)} %get-tuple-element.108.refs_2_), channel_id=1, source_target_pairs={{0,1},{1,0},{2,3},{3,2},{4,5},{5,4},{6,7},{7,6},{8,9},{9,8},{10,11... | collective-permute-start | bytes 2359304 | tf_op jit(solution)/shard_map/ppermute | solution.py:62
  100.9 16.8 %collective-permute-start.39 = (bf16[192,1536]{1,0:T(8,128)(2,1)S(1)}, bf16[192,1536]{1,0:T(8,128)(2,1)S(1)}, u32[]{:S(2)}, u32[]{:S(2)}) collective-permute-start(bf16[192,1536]{1,0:T(8,128)(2,1)S(1)} %get-tuple-element.109), channel_id=1, source_target_pairs={{0,4},{2,6},{4,0},{6,2},{8,12},{10,14},{12,8},{14,10},{16,20},{18,... | collective-permute-start | bytes 1769480 | tf_op jit(solution)/shard_map/ppermute | solution.py:58
  116.1 11.2 %copy-start.2 = (f32[48,1920]{1,0:T(8,128)}, f32[48,1920]{1,0:T(8,128)S(1)}, u32[]{:S(2)}) copy-start(f32[48,1920]{1,0:T(8,128)S(1)} %shard_map.179.refs_2_.refs_0_) | copy-start | bytes 1105924
  116.1 5.3 %copy-start.13 = (bf16[48,1280]{1,0:T(8,128)(2,1)S(1)}, bf16[48,1280]{1,0:T(8,128)(2,1)}, u32[]{:S(2)}) copy-start(bf16[48,1280]{1,0:T(8,128)(2,1)} %copy-done.12) | copy-start | bytes 368644
  116.2 11.2 %collective-permute-start.37 = (bf16[256,768]{1,0:T(8,128)(2,1)}, bf16[256,768]{1,0:T(8,128)(2,1)}, u32[]{:S(2)}, u32[]{:S(2)}) collective-permute-start(bf16[256,768]{1,0:T(8,128)(2,1)} %get-tuple-element.107), channel_id=1, source_target_pairs={{0,1},{1,0},{2,3},{3,2},{4,5},{5,4},{6,7},{7,6},{8,9},{9,8},{10,11... | collective-permute-start | bytes 1179656 | tf_op jit(solution)/shard_map/ppermute | solution.py:62
  118.5 3.7 %copy-start.11 = (bf16[48,1536]{1,0:T(8,128)(2,1)}, bf16[48,1536]{1,0:T(8,128)(2,1)S(1)}, u32[]{:S(2)}) copy-start(bf16[48,1536]{1,0:T(8,128)(2,1)S(1)} %get-tuple-element.110.refs_3_.refs_0_) | copy-start | bytes 442372
  118.5 14.1 %collective-permute-start.40 = (bf16[48,1536]{1,0:T(8,128)(2,1)}, bf16[48,1536]{1,0:T(8,128)(2,1)}, u32[]{:S(2)}, u32[]{:S(2)}) collective-permute-start(bf16[48,1536]{1,0:T(8,128)(2,1)} %get-tuple-element.111), channel_id=1, source_target_pairs={{0,24},{2,26},{4,28},{6,30},{8,0},{10,2},{12,4},{14,6},{16,8},{18,... | collective-permute-start | bytes 442376 | tf_op jit(solution)/shard_map/ppermute | solution.py:58
  120.2 12.4 %collective-permute-start.41 = (bf16[48,1536]{1,0:T(8,128)(2,1)}, bf16[48,1536]{1,0:T(8,128)(2,1)}, u32[]{:S(2)}, u32[]{:S(2)}) collective-permute-start(bf16[48,1536]{1,0:T(8,128)(2,1)} %get-tuple-element.112), channel_id=1, source_target_pairs={{0,16},{2,18},{4,20},{6,22},{8,24},{10,26},{12,28},{14,30},{16,0},... | collective-permute-start | bytes 442376 | tf_op jit(solution)/shard_map/ppermute | solution.py:58
  120.2 12.4 %collective-permute-start.42 = (bf16[48,1536]{1,0:T(8,128)(2,1)}, bf16[48,1536]{1,0:T(8,128)(2,1)}, u32[]{:S(2)}, u32[]{:S(2)}) collective-permute-start(bf16[48,1536]{1,0:T(8,128)(2,1)} %get-tuple-element.113), channel_id=1, source_target_pairs={{0,8},{2,10},{4,12},{6,14},{8,16},{10,18},{12,20},{14,22},{16,24},... | collective-permute-start | bytes 442376 | tf_op jit(solution)/shard_map/ppermute | solution.py:58
  121.4 6.0 %copy-start.15 = (f32[48,2]{1,0:T(8,128)}, f32[48,2]{1,0:T(8,128)S(1)}, u32[]{:S(2)}) copy-start(f32[48,2]{1,0:T(8,128)S(1)} %copy.32.refs_2_.refs_1_) | copy-start | bytes 1156
  121.6 0.6 copy-start.14
  122.2 5.2 %copy-start = (bf16[768,768]{1,0:T(8,128)(2,1)S(1)}, bf16[768,768]{1,0:T(8,128)(2,1)}, u32[]{:S(2)}) copy-start(bf16[768,768]{1,0:T(8,128)(2,1)} %get-tuple-element.127.refs_4_) | copy-start | bytes 3538948
  127.4 1.4 %copy-start.1 = (f32[512,768]{1,0:T(8,128)S(1)}, f32[512,768]{1,0:T(8,128)}, u32[]{:S(2)}) copy-start(f32[512,768]{1,0:T(8,128)} %shard_map.182.refs_5_) | copy-start | bytes 4718596
  128.8 1.1 copy-start.4
  134.8 3.8 %collective-permute-start.43 = (f32[2,48]{1,0:T(2,128)}, f32[2,48]{1,0:T(2,128)S(1)}, u32[]{:S(2)}, u32[]{:S(2)}) collective-permute-start(f32[2,48]{1,0:T(2,128)} %get-tuple-element.116.refs_2_), channel_id=1, source_target_pairs={{0,1},{1,0},{2,3},{3,2},{4,5},{5,4},{6,7},{7,6},{8,9},{9,8},{10,11... | collective-permute-start | bytes 1160 | tf_op jit(solution)/shard_map/ppermute | solution.py:62
